TPU v7x, 32 devices: a whole 2x2x4 slice. The times are simulated.
32 devices in a mesh: blk: 8 (over z, y), pb: 4 (over x, core).
Axes of the slice: x: 2, y: 2, z: 4, core: 2. Of those that a mesh axis runs over, the one named last changes fastest.
Arguments:
- query_rows: bfloat16 [10240, 1024], P(('blk', 'pb')), may hold values from -64 to 64
- key_rows: bfloat16 [10240, 1024], P(('blk', 'pb')), may hold values from -64 to 64
- partner: int32 [8, 1280], P('blk', 'pb'), may hold values from 0 to 1279, each once within a row
Outputs:
- pair_loss: float32 [10240], P(('blk', 'pb'))
- grad_queries: float32 [10240, 1024], P(('blk', 'pb'))
- grad_keys: float32 [10240, 1024], P(('blk', 'pb'))
Inputs may be any that keep to these rules, and one draw needn't show every extreme that they name: Each row of partner is a permutation of 0 .. 1279.
All inputs are finite; a program needn't handle non-finite values.
Results may differ from a plain program's by a relative error of at most 0.0015.
Values may be sent and summed in bfloat16 or wider, within the bound.
No kernel may reach another device: no remote copies, remote signals or barrier semaphores. Data moves between devices by JAX's collectives and lax.ppermute only.
A program may use at most 192 MiB of HBM per device.

v0:
```python
import jax
import jax.numpy as jnp
from jax import lax
from jax.sharding import PartitionSpec as P

WIN = 4


def from_behind(array, axis, by):
    peers = lax.axis_size(axis)
    return lax.ppermute(array, axis, [(i, (i + by) % peers) for i in range(peers)])


def joined(array, axis, combine):
    everything = jax.tree.map(lambda part: lax.all_gather(part, axis), array)
    leading = jax.tree.map(lambda part: part[0], everything)

    def hop(k, so_far):
        return combine(so_far, jax.tree.map(lambda part: part[k], everything))

    return lax.fori_loop(1, lax.axis_size(axis), hop, leading)


def merge_pairs(first, second):
    first_max, first_sum = first
    second_max, second_sum = second
    top = jnp.maximum(first_max, second_max)
    return (top, first_sum * jnp.exp(first_max - top) + second_sum * jnp.exp(second_max - top))


def add_logs(first, second):
    top = jnp.maximum(first, second)
    return top + jnp.log(jnp.exp(first - top) + jnp.exp(second - top))


def local(query_rows, key_rows, partner):
    features = query_rows.shape[1]
    factor = float(features) ** (-0.5)
    block_keys = lax.all_gather(key_rows, "pb", axis=0, tiled=True)
    pieces = [block_keys]
    arrived = block_keys
    for step in range(1, WIN):
        arrived = from_behind(arrived, "blk", 1)
        pieces.append(arrived)
    window_keys = jnp.stack(pieces)
    block_size = window_keys.shape[1]
    scores = (
        jnp.einsum("qd,skd->sqk", query_rows, window_keys, preferred_element_type=jnp.float32)
        * factor
    )
    row_max = jnp.max(scores, axis=(0, 2))
    row_lse = row_max + jnp.log(jnp.sum(jnp.exp(scores - row_max[None, :, None]), axis=(0, 2)))
    col_max = jnp.max(scores, axis=1)
    col_sum = jnp.sum(jnp.exp(scores - col_max[:, None, :]), axis=1)
    col_max, col_sum = joined((col_max, col_sum), "pb", merge_pairs)
    partial_lse = col_max + jnp.log(col_sum)
    carried = partial_lse[WIN - 1]
    for step in range(WIN - 2, -1, -1):
        arrived_lse = from_behind(carried, "blk", -1)
        carried = add_logs(arrived_lse, partial_lse[step])
    lse_list = [carried]
    travelling = carried
    for step in range(1, WIN):
        travelling = from_behind(travelling, "blk", 1)
        lse_list.append(travelling)
    col_lse = jnp.stack(lse_list)
    chosen = partner[0]
    columns = jnp.arange(block_size, dtype=jnp.int32)
    mask = (columns[None, :] == chosen[:, None]).astype(jnp.float32)
    first_only = (jnp.arange(WIN, dtype=jnp.int32) == 0).astype(jnp.float32)
    weights = 0.5 * jnp.exp(scores - row_lse[None, :, None]) + 0.5 * jnp.exp(
        scores - col_lse[:, None, :]
    )
    weights = (weights - first_only[:, None, None] * mask[None, :, :]).astype(jnp.bfloat16)
    positive = jnp.take_along_axis(scores[0], chosen[:, None], axis=1)[:, 0]
    pair_loss = 0.5 * row_lse + 0.5 * jnp.take(col_lse[0], chosen) - positive
    grad_queries = (
        jnp.einsum("sqk,skd->qd", weights, window_keys, preferred_element_type=jnp.float32) * factor
    )
    query_pieces = [query_rows]
    lse_pieces = [row_lse]
    moving_queries = query_rows
    moving_sums = row_lse
    for step in range(1, WIN):
        moving_queries = from_behind(moving_queries, "blk", -1)
        moving_sums = from_behind(moving_sums, "blk", -1)
        query_pieces.append(moving_queries)
        lse_pieces.append(moving_sums)
    window_queries = lax.all_gather(jnp.stack(query_pieces), "pb", axis=1, tiled=True)
    window_sums = lax.all_gather(jnp.stack(lse_pieces), "pb", axis=1, tiled=True)
    block_partner = lax.all_gather(partner, "pb", axis=1, tiled=True)[0]
    quarter = key_rows.shape[0]
    offset = lax.axis_index("pb") * quarter
    own_lse = lax.dynamic_slice_in_dim(carried, offset, quarter, 0)
    own_columns = offset + jnp.arange(quarter, dtype=jnp.int32)
    own_mask = (block_partner[:, None] == own_columns[None, :]).astype(jnp.float32)
    own_scores = (
        jnp.einsum("sqd,kd->sqk", window_queries, key_rows, preferred_element_type=jnp.float32)
        * factor
    )
    own_weights = 0.5 * jnp.exp(own_scores - window_sums[:, :, None]) + 0.5 * jnp.exp(
        own_scores - own_lse[None, None, :]
    )
    own_weights = (own_weights - first_only[:, None, None] * own_mask[None, :, :]).astype(
        jnp.bfloat16
    )
    grad_keys = jnp.einsum(
        "sqk,sqd->kd", own_weights, window_queries, preferred_element_type=jnp.float32
    )
    return (pair_loss, grad_queries, grad_keys * factor)


def solution(mesh):
    return jax.shard_map(
        local,
        mesh=mesh,
        in_specs=(P(("blk", "pb"), None), P(("blk", "pb"), None), P("blk", "pb")),
        out_specs=(P(("blk", "pb")), P(("blk", "pb"), None), P(("blk", "pb"), None)),
        check_vma=False,
    )
```

profile of v0, /device:TPU:0, one launch (start us, length us, event | category | flops | bytes accessed | tf_op | source)
XLA Modules:
  0.0 378.8 jit_solution(17885681990535260808)
XLA Ops:
  7.2 0.7 all-gather.8.cloned.1.call-update
  7.9 0.0 all-gather.10.cloned.1.call-start
  8.0 29.9 %all-gather.8.cloned.1.call-done = bf16[1280,1024]{1,0:T(8,128)(2,1)} async-done(((bf16[320,1024]{1,0:T(8,128)(2,1)}), bf16[1280,1024]{1,0:T(8,128)(2,1)}) %all-gather.8.cloned.1.call-update) | async-done | bytes 2621456 | tf_op jit(solution)/shard_map/all_gather | solution.py:39
  37.9 1.5 collective-permute-start
  39.3 3.2 collective-permute-start.9
  42.6 69.7 %collective-permute-done.9 = bf16[320,1024]{1,0:T(8,128)(2,1)S(1)} collective-permute-done((bf16[320,1024]{1,0:T(8,128)(2,1)}, bf16[320,1024]{1,0:T(8,128)(2,1)S(1)}, u32[]{:S(2)}, u32[]{:S(2)}) %collective-permute-start.9) | collective-permute-done | bytes 655392 | tf_op jit(solution)/shard_map/ppermute | solution.py:11
  112.3 2.1 collective-permute-start.10
  114.4 14.2 %collective-permute-done.10 = bf16[320,1024]{1,0:T(8,128)(2,1)S(1)} collective-permute-done((bf16[320,1024]{1,0:T(8,128)(2,1)S(1)}, bf16[320,1024]{1,0:T(8,128)(2,1)S(1)}, u32[]{:S(2)}, u32[]{:S(2)}) %collective-permute-start.10) | collective-permute-done | bytes 655392 | tf_op jit(solution)/shard_map/ppermute | solution.py:11
  128.6 5.2 %collective-permute-start.11 = (bf16[320,1024]{1,0:T(8,128)(2,1)S(1)}, bf16[320,1024]{1,0:T(8,128)(2,1)S(1)}, u32[]{:S(2)}, u32[]{:S(2)}) collective-permute-start(bf16[320,1024]{1,0:T(8,128)(2,1)S(1)} %collective-permute-done.10), channel_id=1, source_target_pairs={{0,28},{4,0},{8,4},{12,8},{16,12},{20,16},{24,20},{28,24},{1,29},{... | collective-permute-start | bytes 1966088 | tf_op jit(solution)/shard_map/ppermute | solution.py:11
  133.8 13.3 %collective-permute-done.11 = bf16[320,1024]{1,0:T(8,128)(2,1)S(1)} collective-permute-done((bf16[320,1024]{1,0:T(8,128)(2,1)S(1)}, bf16[320,1024]{1,0:T(8,128)(2,1)S(1)}, u32[]{:S(2)}, u32[]{:S(2)}) %collective-permute-start.11) | collective-permute-done | bytes 655392 | tf_op jit(solution)/shard_map/ppermute | solution.py:11
  147.1 3.0 pad_maximum_fusion.1
  150.1 0.1 collective-permute-start.1
  150.2 60.8 %collective-permute-done.1 = bf16[1280,1024]{1,0:T(8,128)(2,1)} collective-permute-done((bf16[1280,1024]{1,0:T(8,128)(2,1)}, bf16[1280,1024]{1,0:T(8,128)(2,1)}, u32[]{:S(2)}, u32[]{:S(2)}) %collective-permute-start.1) | collective-permute-done | bytes 2621472 | tf_op jit(solution)/shard_map/ppermute | solution.py:11
  211.1 59.3 %collective-permute-done.2 = bf16[1280,1024]{1,0:T(8,128)(2,1)} collective-permute-done((bf16[1280,1024]{1,0:T(8,128)(2,1)}, bf16[1280,1024]{1,0:T(8,128)(2,1)}, u32[]{:S(2)}, u32[]{:S(2)}) %collective-permute-start.2) | collective-permute-done | bytes 2621472 | tf_op jit(solution)/shard_map/ppermute | solution.py:11
  270.3 6.9 %fusion.26 = (f32[4,1280]{1,0:T(4,128)S(1)}, f32[4,1280,320]{1,2,0:T(8,128)S(1)}) fusion(bf16[320,1024]{1,0:T(8,128)(2,1)S(1)} %copy-done.1, bf16[1,1280,1024]{2,1,0:T(8,128)(2,1)} %bitcast.5, bf16[1,1280,1024]{2,1,0:T(8,128)(2,1)} %bitcast.4, bf16[1,1280,1024]{2,1,0:T(8,128)(2,1)} %bitcast.3, bf16[1,1280,1024]{2,1,0:T(8,128)(2,1)S(1)} %bitcast.90), kind=kOutput, calls=%fused_computation.69 | convolution fusion | flops 3374443520 | bytes 17715200 | tf_op jit(solution)/shard_map/qd,skd->sqk/dot_general | solution.py:48
  277.3 5.3 %all-gather.2 = f32[4,4,1280]{2,1,0:T(4,128)S(1)} all-gather(f32[1,4,1280]{2,1,0:T(4,128)S(1)} %bitcast.86), channel_id=2, replica_groups=mesh['blk'=8,'pb'=4] {'pb'}, dimensions={0}, use_global_device_ids=true | all-gather | bytes 102400 | tf_op jit(solution)/shard_map/all_gather | solution.py:15
  282.6 3.5 multiply_reduce_fusion
  286.0 2.6 exponential_reduce_fusion
  288.6 5.3 %all-gather.3 = f32[4,4,1280]{2,1,0:T(4,128)S(1)} all-gather(f32[1,4,1280]{2,1,0:T(4,128)S(1)} %bitcast.87), channel_id=3, replica_groups=mesh['blk'=8,'pb'=4] {'pb'}, dimensions={0}, use_global_device_ids=true | all-gather | bytes 102400 | tf_op jit(solution)/shard_map/all_gather | solution.py:15
  293.9 0.2 while.17
  294.1 0.1 slice_reduce_fusion.3
  294.2 0.1 collective-permute-start.3
  294.3 0.6 dynamic-slice
  295.5 0.3 dynamic-update-slice
  295.8 2.1 collective-permute-done.3
  297.9 2.7 collective-permute-start.4
  300.7 4.3 %all-reduce = s32[1280]{0:T(1024)S(1)} all-reduce(s32[1280]{0:T(1024)S(1)} %dynamic-update-slice), channel_id=1, replica_groups=mesh['blk'=8,'pb'=4] {'pb'}, use_global_device_ids=true, to_apply=%add | all-reduce | flops 1280 | bytes 10240
  305.0 2.1 collective-permute-start.5
  307.1 1.5 slice_bitcast_fusion
  308.6 3.0 gather_fusion.1
  311.6 2.2 gather_fusion
  313.9 0.6 select_subtract_fusion
  314.5 1.8 collective-permute-start.12
  316.3 0.2 compare_convert_fusion
  316.5 1.6 collective-permute-done.12
  318.1 4.5 %collective-permute-start.13 = (f32[320]{0:T(512)S(1)}, f32[320]{0:T(512)S(1)}, u32[]{:S(2)}, u32[]{:S(2)}) collective-permute-start(f32[320]{0:T(512)S(1)} %collective-permute-done.12), channel_id=1, source_target_pairs={{0,28},{4,0},{8,4},{12,8},{16,12},{20,16},{24,20},{28,24},{1,29},{... | collective-permute-start | bytes 3848 | tf_op jit(solution)/shard_map/ppermute | solution.py:11
  322.6 0.2 fusion.9
  322.7 0.1 collective-permute-start.6
  322.8 1.1 collective-permute-done.13
  323.9 5.0 %collective-permute-start.14 = (f32[320]{0:T(512)S(1)}, f32[320]{0:T(512)S(1)}, u32[]{:S(2)}, u32[]{:S(2)}) collective-permute-start(f32[320]{0:T(512)S(1)} %collective-permute-done.13), channel_id=1, source_target_pairs={{0,28},{4,0},{8,4},{12,8},{16,12},{20,16},{24,20},{28,24},{1,29},{... | collective-permute-start | bytes 3848 | tf_op jit(solution)/shard_map/ppermute | solution.py:11
  328.9 0.1 dynamic_slice.23
  328.9 1.2 collective-permute-done.14
  330.2 6.6 %collective-permute-done.7 = f32[1280]{0:T(1024)S(1)} collective-permute-done((f32[1280]{0:T(1024)S(1)}, f32[1280]{0:T(1024)S(1)}, u32[]{:S(2)}, u32[]{:S(2)}) %collective-permute-start.7) | collective-permute-done | bytes 5152 | tf_op jit(solution)/shard_map/ppermute | solution.py:11
  336.8 5.4 %all-gather.4 = f32[4,320,4]{1,2,0:T(4,128)S(1)} all-gather(f32[1,320,4]{1,2,0:T(4,128)S(1)} %maximum_bitcast_fusion), channel_id=1, replica_groups=mesh['blk'=8,'pb'=4] {'pb'}, dimensions={0}, use_global_device_ids=true | all-gather | bytes 25600 | tf_op jit(solution)/shard_map/all_gather | solution.py:90
  342.1 0.1 reshape.238
  342.2 0.9 collective-permute-done.8
  343.1 12.0 %fusion.12 = f32[320,1024]{1,0:T(8,128)} fusion(bf16[1,1280,1024]{2,1,0:T(8,128)(2,1)} %bitcast.5, bf16[1,1280,1024]{2,1,0:T(8,128)(2,1)} %bitcast.4, bf16[1,1280,1024]{2,1,0:T(8,128)(2,1)} %bitcast.3, bf16[1,1280,1024]{2,1,0:T(8,128)(2,1)} %bitcast.89, f32[320,1280]{1,0:T(8,128)S(1)} %fusion.9, f32[4]{0:T(128)S(1)} %compare_convert_fusion.1, ...), kind=kOutput, calls=%fused_computation.29 | convolution fusion | flops 3384606720 | bytes 20010256 | tf_op jit(solution)/shard_map/sqk,skd->qd/dot_general | solution.py:78
  355.2 16.7 %fusion.11 = f32[320,1024]{1,0:T(8,128)} fusion(bf16[4,1280,1024]{2,1,0:T(8,128)(2,1)} %all-gather.10.cloned.1.call-done, f32[1280,320]{0,1:T(8,128)S(1)} %compare_convert_fusion, f32[4]{0:T(128)S(1)} %compare_convert_fusion.1, f32[320]{0:T(512)S(1)} %dynamic_slice.23, f32[4,1280]{1,0:T(4,128)S(1)} %bitcast.88, bf16[320,1024]{1,0:T(8,128)(2,1)} %param.6), kind=kOutput, calls=%fused_computation.28 | convolution fusion | flops 6724321280 | bytes 14112016 | tf_op jit(solution)/shard_map/sqk,sqd->kd/dot_general | solution.py:107
  (50 shorter events, 0.5 us)
Async XLA Ops:
  7.2 263.2 %copy-start.1 = (bf16[320,1024]{1,0:T(8,128)(2,1)S(1)}, bf16[320,1024]{1,0:T(8,128)(2,1)}, u32[]{:S(2)}) copy-start(bf16[320,1024]{1,0:T(8,128)(2,1)} %param.5) | copy-start | bytes 1966084
  7.2 203.8 %copy-start.2 = (s32[1,320]{1,0:T(1,128)S(1)}, s32[1,320]{1,0:T(1,128)}, u32[]{:S(2)}) copy-start(s32[1,320]{1,0:T(1,128)} %param.7) | copy-start | bytes 3844
  7.2 30.7 %all-gather.8.cloned.1.call-start = ((), (), s32[]{:S(2)}) async-start(), calls=%async_computation | async-start | bytes 3276800 | tf_op jit(solution)/shard_map/all_gather | solution.py:39
  7.9 347.3 %all-gather.10.cloned.1.call-start = ((), (), s32[]{:S(2)}) async-start(), calls=%async_computation.1 | async-start | bytes 13107200 | tf_op jit(solution)/shard_map/all_gather | solution.py:89
  37.9 232.5 %copy-start.3 = (bf16[1280,1024]{1,0:T(8,128)(2,1)S(1)}, bf16[1280,1024]{1,0:T(8,128)(2,1)}, u32[]{:S(2)}) copy-start(bf16[1280,1024]{1,0:T(8,128)(2,1)} %all-gather.8.cloned.1.call-done) | copy-start | bytes 7864324
  37.9 112.2 %collective-permute-start = (bf16[1280,1024]{1,0:T(8,128)(2,1)}, bf16[1280,1024]{1,0:T(8,128)(2,1)}, u32[]{:S(2)}, u32[]{:S(2)}) collective-permute-start(bf16[1280,1024]{1,0:T(8,128)(2,1)} %all-gather.8.cloned.1.call-done), channel_id=1, source_target_pairs={{0,4},{4,8},{8,12},{12,16},{16,20},{20,24},{24,28},{28,0},{1,5},{5... | collective-permute-start | bytes 7864328 | tf_op jit(solution)/shard_map/ppermute | solution.py:11
  39.3 73.0 %collective-permute-start.9 = (bf16[320,1024]{1,0:T(8,128)(2,1)}, bf16[320,1024]{1,0:T(8,128)(2,1)S(1)}, u32[]{:S(2)}, u32[]{:S(2)}) collective-permute-start(bf16[320,1024]{1,0:T(8,128)(2,1)} %param.5), channel_id=1, source_target_pairs={{0,28},{4,0},{8,4},{12,8},{16,12},{20,16},{24,20},{28,24},{1,29},{... | collective-permute-start | bytes 1966088 | tf_op jit(solution)/shard_map/ppermute | solution.py:11
  112.3 16.3 %collective-permute-start.10 = (bf16[320,1024]{1,0:T(8,128)(2,1)S(1)}, bf16[320,1024]{1,0:T(8,128)(2,1)S(1)}, u32[]{:S(2)}, u32[]{:S(2)}) collective-permute-start(bf16[320,1024]{1,0:T(8,128)(2,1)S(1)} %collective-permute-done.9), channel_id=1, source_target_pairs={{0,28},{4,0},{8,4},{12,8},{16,12},{20,16},{24,20},{28,24},{1,29},{... | collective-permute-start | bytes 1966088 | tf_op jit(solution)/shard_map/ppermute | solution.py:11
  128.6 18.5 %collective-permute-start.11 = (bf16[320,1024]{1,0:T(8,128)(2,1)S(1)}, bf16[320,1024]{1,0:T(8,128)(2,1)S(1)}, u32[]{:S(2)}, u32[]{:S(2)}) collective-permute-start(bf16[320,1024]{1,0:T(8,128)(2,1)S(1)} %collective-permute-done.10), channel_id=1, source_target_pairs={{0,28},{4,0},{8,4},{12,8},{16,12},{20,16},{24,20},{28,24},{1,29},{... | collective-permute-start | bytes 1966088 | tf_op jit(solution)/shard_map/ppermute | solution.py:11
  150.1 60.8 %collective-permute-start.1 = (bf16[1280,1024]{1,0:T(8,128)(2,1)}, bf16[1280,1024]{1,0:T(8,128)(2,1)}, u32[]{:S(2)}, u32[]{:S(2)}) collective-permute-start(bf16[1280,1024]{1,0:T(8,128)(2,1)} %collective-permute-done), channel_id=1, source_target_pairs={{0,4},{4,8},{8,12},{12,16},{16,20},{20,24},{24,28},{28,0},{1,5},{5... | collective-permute-start | bytes 7864328 | tf_op jit(solution)/shard_map/ppermute | solution.py:11
  210.9 59.4 %collective-permute-start.2 = (bf16[1280,1024]{1,0:T(8,128)(2,1)}, bf16[1280,1024]{1,0:T(8,128)(2,1)}, u32[]{:S(2)}, u32[]{:S(2)}) collective-permute-start(bf16[1280,1024]{1,0:T(8,128)(2,1)} %collective-permute-done.1), channel_id=1, source_target_pairs={{0,4},{4,8},{8,12},{12,16},{16,20},{20,24},{24,28},{28,0},{1,5},{5... | collective-permute-start | bytes 7864328 | tf_op jit(solution)/shard_map/ppermute | solution.py:11
  277.3 8.8 %copy-start = (f32[4,1280,320]{1,2,0:T(8,128)}, f32[4,1280,320]{1,2,0:T(8,128)S(1)}, u32[]{:S(2)}) copy-start(f32[4,1280,320]{1,2,0:T(8,128)S(1)} %get-tuple-element.161) | copy-start | bytes 19660804
  286.0 8.2 %copy-start.4 = (u32[32]{0:T(128)S(1)}, u32[32]{0:T(128)}, u32[]{:S(2)}) copy-start(u32[32]{0:T(128)} %constant.101) | copy-start | bytes 388
  294.2 3.7 collective-permute-start.3
  297.9 7.0 %collective-permute-start.4 = (f32[1280]{0:T(1024)S(1)}, f32[1280]{0:T(1024)S(1)}, u32[]{:S(2)}, u32[]{:S(2)}) collective-permute-start(f32[1280]{0:T(1024)S(1)} %log_add_fusion.3), channel_id=1, source_target_pairs={{0,28},{4,0},{8,4},{12,8},{16,12},{20,16},{24,20},{28,24},{1,29},{... | collective-permute-start | bytes 15368 | tf_op jit(solution)/shard_map/ppermute | solution.py:11
  305.0 6.6 %collective-permute-start.5 = (f32[1280]{0:T(1024)S(1)}, f32[1280]{0:T(1024)S(1)}, u32[]{:S(2)}, u32[]{:S(2)}) collective-permute-start(f32[1280]{0:T(1024)S(1)} %log_add_fusion.2), channel_id=1, source_target_pairs={{0,28},{4,0},{8,4},{12,8},{16,12},{20,16},{24,20},{28,24},{1,29},{... | collective-permute-start | bytes 15368 | tf_op jit(solution)/shard_map/ppermute | solution.py:11
  314.5 3.6 collective-permute-start.12
  318.1 5.8 %collective-permute-start.13 = (f32[320]{0:T(512)S(1)}, f32[320]{0:T(512)S(1)}, u32[]{:S(2)}, u32[]{:S(2)}) collective-permute-start(f32[320]{0:T(512)S(1)} %collective-permute-done.12), channel_id=1, source_target_pairs={{0,28},{4,0},{8,4},{12,8},{16,12},{20,16},{24,20},{28,24},{1,29},{... | collective-permute-start | bytes 3848 | tf_op jit(solution)/shard_map/ppermute | solution.py:11
  322.7 7.4 %collective-permute-start.6 = (f32[1280]{0:T(1024)S(1)}, f32[1280]{0:T(1024)S(1)}, u32[]{:S(2)}, u32[]{:S(2)}) collective-permute-start(f32[1280]{0:T(1024)S(1)} %log_add_fusion.1), channel_id=1, source_target_pairs={{0,4},{4,8},{8,12},{12,16},{16,20},{20,24},{24,28},{28,0},{1,5},{5... | collective-permute-start | bytes 15368 | tf_op jit(solution)/shard_map/ppermute | solution.py:11
  323.9 6.3 %collective-permute-start.14 = (f32[320]{0:T(512)S(1)}, f32[320]{0:T(512)S(1)}, u32[]{:S(2)}, u32[]{:S(2)}) collective-permute-start(f32[320]{0:T(512)S(1)} %collective-permute-done.13), channel_id=1, source_target_pairs={{0,28},{4,0},{8,4},{12,8},{16,12},{20,16},{24,20},{28,24},{1,29},{... | collective-permute-start | bytes 3848 | tf_op jit(solution)/shard_map/ppermute | solution.py:11
  330.2 6.6 %collective-permute-start.7 = (f32[1280]{0:T(1024)S(1)}, f32[1280]{0:T(1024)S(1)}, u32[]{:S(2)}, u32[]{:S(2)}) collective-permute-start(f32[1280]{0:T(1024)S(1)} %collective-permute-done.6), channel_id=1, source_target_pairs={{0,4},{4,8},{8,12},{12,16},{16,20},{20,24},{24,28},{28,0},{1,5},{5... | collective-permute-start | bytes 15368 | tf_op jit(solution)/shard_map/ppermute | solution.py:11
  336.8 6.3 %collective-permute-start.8 = (f32[1280]{0:T(1024)S(1)}, f32[1280]{0:T(1024)S(1)}, u32[]{:S(2)}, u32[]{:S(2)}) collective-permute-start(f32[1280]{0:T(1024)S(1)} %collective-permute-done.7), channel_id=1, source_target_pairs={{0,4},{4,8},{8,12},{12,16},{16,20},{20,24},{24,28},{28,0},{1,5},{5... | collective-permute-start | bytes 15368 | tf_op jit(solution)/shard_map/ppermute | solution.py:11
Sparse Core Ops, SparseCore 0:
  9.6 28.2 all-gather.7
  150.2 71.1 all-gather.9
where the time goes:
time: 379 us
  waiting for transfers between devices  261 us (69%)
  matrix products  35.7 us (9%)
  starting transfers between devices  28.4 us (7%)
  blocking collectives  20.2 us (5%)
  between operations  14.9 us (4%)
  other arithmetic  10.3 us (3%)
  local copies, waits for them, and re-layouts  7.93 us (2%)
    ppermute x15, waiting for transfers between devices, from_behind(): lax.ppermute(array, axis, [(i, (i + by) % peers) for i in range(peers)])  231 us
    all_gather x1, waiting for transfers between devices, local(): block_keys = lax.all_gather(key_rows, 'pb', axis=0, tiled=True)  29.9 us
    ppermute x15, starting transfers between devices, from_behind(): lax.ppermute(array, axis, [(i, (i + by) % peers) for i in range(peers)])  28.3 us
    dot_general x1, matrix products, local(): jnp.einsum('sqk,sqd->kd', own_weights, window_queries, preferred_element_...  16.7 us
    dot_general x1, matrix products, local(): jnp.einsum('sqk,skd->qd', weights, window_keys, preferred_element_type=jn...  12 us
    all_gather x2, blocking collectives, joined(): everything = jax.tree.map(lambda part: lax.all_gather(part, axis), array)  10.6 us
  transfers between devices with their start and end apart: 17, of which 12 were waited for; matrix products, arithmetic and copies ran while one was open for 10% of the time, Pallas kernels for 0%

commit v1 on v0

v1 whole, which is shorter than its diff:
```python
import functools

import jax
import jax.numpy as jnp
from jax import lax
from jax.experimental import pallas as pl
from jax.experimental.pallas import tpu as pltpu
from jax.sharding import PartitionSpec as P

F32 = jnp.float32
VMEM_LIMIT = 48 * 1024 * 1024
NT = (((1,), (1,)), ((), ()))


def shift(array, axis, move):
    peers = lax.axis_size(axis)
    return lax.ppermute(array, axis, [(i, move(i) % peers) for i in range(peers)])


def as_column(row):
    return jnp.broadcast_to(row, (128, row.shape[1])).T[:, 0:1]


def as_row(column):
    return jnp.broadcast_to(column, (column.shape[0], 128)).T[0:1, :]


def log_join(*parts):
    top = functools.reduce(jnp.maximum, parts)
    return top + jnp.log(sum(jnp.exp(part - top) for part in parts))


def fetch(sources, target, sems):
    rows = sources[0].shape[0]
    copies = []
    for i, source in enumerate(sources):
        copy = pltpu.make_async_copy(source, target.at[pl.ds(i * rows, rows)], sems.at[i])
        copy.start()
        copies.append(copy)
    return copies


def score_kernel(tokens, early, stats, factor, *refs):
    mine = refs[:2]
    shards = refs[2 : 2 + tokens]
    rest = list(refs[2 + tokens :])
    if stats:
        side = [rest.pop(0) for _ in range(2 if early else 1)]
    out = rest.pop(0)
    if stats:
        info = rest.pop(0)
    left, right, sems = rest
    copies = fetch(mine, left, sems) + fetch(shards, right, sems.at[pl.ds(2, tokens)])
    for copy in copies[:2]:
        copy.wait()
    rows = mine[0].shape[0]
    pair = 2 * rows
    lhs = left[...]
    row_parts = []
    for p in range(tokens // 2):
        copies[2 + 2 * p].wait()
        copies[3 + 2 * p].wait()
        s = lax.dot_general(
            lhs, right[pl.ds(p * pair, pair), :], NT, preferred_element_type=F32
        ) * factor
        out[:, pl.ds(p * pair, pair)] = s
        if stats:
            col_max = jnp.max(s, axis=0, keepdims=True)
            col = col_max + jnp.log(jnp.sum(jnp.exp(s - col_max), axis=0, keepdims=True))
            row_max = jnp.max(s, axis=1, keepdims=True)
            row_sum = jnp.sum(jnp.exp(s - row_max), axis=1, keepdims=True)
            row_parts.append(row_max + jnp.log(row_sum))
            info[pl.ds(p if early else 3, 1), :] = col
            if early and p == 0:
                hit = as_column(side[0][...]) == side[1][...]
                info[pl.ds(5, 1), :] = as_row(jnp.sum(jnp.where(hit, s, 0.0), axis=1, keepdims=True))
    if stats:
        row = as_row(log_join(*row_parts) if len(row_parts) > 1 else row_parts[0])
        if early:
            info[pl.ds(3, 1), :] = jnp.zeros((1, pair), F32)
            info[pl.ds(4, 1), :] = row
            info[pl.ds(6, 2), :] = jnp.zeros((2, pair), F32)
        else:
            info[pl.ds(0, 3), :] = side[0][pl.ds(0, 3), :]
            info[pl.ds(4, 1), :] = log_join(row, side[0][pl.ds(4, 1), :])
            info[pl.ds(5, 3), :] = side[0][pl.ds(5, 3), :]


def score(mine, shards, early, stats, factor, side=()):
    rows, width = mine[0].shape
    tokens = len(shards)
    anywhere = pl.BlockSpec(memory_space=pl.ANY)
    whole = pl.BlockSpec(memory_space=pltpu.VMEM)
    shapes = [jax.ShapeDtypeStruct((2 * rows, tokens * rows), F32)]
    if stats:
        shapes.append(jax.ShapeDtypeStruct((8, 2 * rows), F32))
    return pl.pallas_call(
        functools.partial(score_kernel, tokens, early, stats, factor),
        out_shape=tuple(shapes),
        in_specs=[anywhere] * (2 + tokens) + [whole] * len(side),
        out_specs=(whole,) * len(shapes),
        scratch_shapes=[
            pltpu.VMEM((2 * rows, width), jnp.bfloat16),
            pltpu.VMEM((tokens * rows, width), jnp.bfloat16),
            pltpu.SemaphoreType.DMA((2 + tokens,)),
        ],
        compiler_params=pltpu.CompilerParams(vmem_limit_bytes=VMEM_LIMIT),
        cost_estimate=pl.CostEstimate(
            flops=4 * rows * rows * tokens * width,
            bytes_accessed=(tokens + 2) * rows * width * 2 + 8 * rows * rows * tokens,
            transcendentals=4 * rows * rows * tokens if stats else 0,
        ),
    )(*mine, *shards, *side)


def halves(ref, row):
    n = ref.shape[1] // 2
    both = ref[pl.ds(row, 1), :]
    return both[:, :n], both[:, n:]


def by_shard(ref):
    a, b, early, late = (halves(ref, i) for i in range(4))
    return [a[0], a[1], b[0], b[1], early[0], late[0], early[1], late[1]]


def block_kernel(own, across, core, corner, out):
    for base, near, far in ((0, own, across), (8, core, corner)):
        near, far = by_shard(near), by_shard(far)
        for i in range(8):
            out[pl.ds(base + i, 1), :] = log_join(near[i], far[i ^ 1])
    own_row, core_row = halves(own, 4), halves(core, 4)
    across_row, corner_row = halves(across, 4), halves(corner, 4)
    out[pl.ds(16, 1), :] = log_join(own_row[0], core_row[1])
    out[pl.ds(17, 1), :] = log_join(across_row[0], corner_row[1])
    out[pl.ds(18, 1), :] = log_join(own_row[1], core_row[0])
    out[pl.ds(19, 1), :] = halves(own, 5)[0] + halves(core, 5)[1]
    out[pl.ds(20, 4), :] = jnp.zeros((4, out.shape[1]), F32)


def window_kernel(even_ref, ids, partner, *refs):
    around = dict(zip((0, 1, 2, 3, -1, -2, -3), refs[:7]))
    col_out, row_out, loss_out = refs[7:]
    even = even_ref[0] == 1

    def line(d, i):
        return around[d][pl.ds(i, 1), :]

    def pick(first, second):
        return jnp.where(even, first, second)

    def total(step, base, half):
        parts = []
        for other in range(4):
            d = other - step
            if other % 2 == 0:
                parts.append(line(d, base + other + half))
            else:
                c, e = line(d, base + 4 + half), line(d, base + 6 + half)
                c_first = (other == 1) == (d % 2 == 0)
                parts.append(pick(c, e) if c_first else pick(e, c))
        return log_join(*parts)

    sums = [[total(step, 0, half) for half in range(2)] for step in range(4)]
    core_sums = [total(0, 8, half) for half in range(2)]
    join = lambda first, second: jnp.concatenate([first, second], axis=1)
    c = [pick(sums[1][h], sums[3][h]) for h in range(2)]
    e = [pick(sums[3][h], sums[1][h]) for h in range(2)]
    col_out[pl.ds(0, 1), :] = join(*sums[0])
    col_out[pl.ds(1, 1), :] = join(*sums[2])
    col_out[pl.ds(2, 1), :] = join(c[0], e[0])
    col_out[pl.ds(3, 1), :] = join(c[1], e[1])
    col_out[pl.ds(4, 1), :] = join(sums[0][0], core_sums[0])
    near = [line(1, 16 + h) for h in range(2)]
    far = [line(3, 16 + h) for h in range(2)]
    c = [pick(far[h], near[h]) for h in range(2)]
    e = [pick(near[h], far[h]) for h in range(2)]
    row_out[pl.ds(0, 1), :] = join(line(0, 16), line(0, 17))
    row_out[pl.ds(1, 1), :] = join(line(2, 16), line(2, 17))
    row_out[pl.ds(2, 1), :] = join(c[0], e[0])
    row_out[pl.ds(3, 1), :] = join(c[1], e[1])
    row_out[pl.ds(4, 1), :] = join(line(0, 16), line(0, 18))
    zeros = jnp.zeros((3, col_out.shape[1]), F32)
    col_out[pl.ds(5, 3), :] = zeros
    row_out[pl.ds(5, 3), :] = zeros
    chosen = as_column(partner[...])
    found = jnp.zeros(chosen.shape, F32)
    for i, value in enumerate((sums[0][0], sums[0][1], core_sums[0], core_sums[1])):
        hit = chosen == ids[pl.ds(i, 1), :]
        found = found + jnp.sum(jnp.where(hit, value, 0.0), axis=1, keepdims=True)
    loss_out[...] = 0.5 * line(0, 16) + 0.5 * as_row(found) - line(0, 19)


def small_call(kernel, shapes, *args, scalars=0):
    whole = pl.BlockSpec(memory_space=pltpu.VMEM)
    return pl.pallas_call(
        kernel,
        out_shape=tuple(jax.ShapeDtypeStruct(s, F32) for s in shapes),
        in_specs=[pl.BlockSpec(memory_space=pltpu.SMEM)] * scalars + [whole] * (len(args) - scalars),
        out_specs=(whole,) * len(shapes),
        cost_estimate=pl.CostEstimate(flops=100000, bytes_accessed=400000, transcendentals=20000),
    )(*args)


def grad_kernel(group, factor, add, *refs):
    early, late, row_info, col_info, row_ids, col_ids = refs[:6]
    shards = refs[6:14]
    rest = list(refs[14:])
    received = rest.pop(0) if add else None
    out, s_early, s_late, held, weights, sems, s_sems = rest
    rows = out.shape[0]
    pair = 2 * rows
    here = pl.ds(group * rows, rows)
    s_copies = [
        pltpu.make_async_copy(early.at[here], s_early, s_sems.at[0]),
        pltpu.make_async_copy(late.at[here], s_late, s_sems.at[1]),
    ]
    for copy in s_copies:
        copy.start()
    copies = fetch(shards, held, sems)
    row = as_column(row_info[pl.ds(4, 1), :])[group * rows : (group + 1) * rows]
    own = as_column(row_ids[...])[group * rows : (group + 1) * rows]
    s_copies[0].wait()
    for p in range(4):
        if p < 3:
            s = s_early[:, pl.ds(p * pair, pair)]
        else:
            s_copies[1].wait()
            s = s_late[...]
        w = 0.5 * jnp.exp(s - row) + 0.5 * jnp.exp(s - col_info[pl.ds(p, 1), :])
        if p == 0:
            w = w - jnp.where(own == col_ids[...], 1.0, 0.0)
        weights[:, pl.ds(p * pair, pair)] = w.astype(jnp.bfloat16)
    for copy in copies:
        copy.wait()
    total = jnp.dot(weights[...], held[...], preferred_element_type=F32) * factor
    if add:
        total = total + received[...]
    out[...] = total


def grad(group, factor, early, late, row_info, col_info, row_ids, col_ids, shards, received=None):
    rows, width = shards[0].shape
    anywhere = pl.BlockSpec(memory_space=pl.ANY)
    whole = pl.BlockSpec(memory_space=pltpu.VMEM)
    add = received is not None
    return pl.pallas_call(
        functools.partial(grad_kernel, group, factor, add),
        out_shape=jax.ShapeDtypeStruct((rows, width), F32),
        in_specs=[anywhere] * 2 + [whole] * 4 + [anywhere] * 8 + ([whole] if add else []),
        out_specs=whole,
        scratch_shapes=[
            pltpu.VMEM((rows, 6 * rows), F32),
            pltpu.VMEM((rows, 2 * rows), F32),
            pltpu.VMEM((8 * rows, width), jnp.bfloat16),
            pltpu.VMEM((rows, 8 * rows), jnp.bfloat16),
            pltpu.SemaphoreType.DMA((8,)),
            pltpu.SemaphoreType.DMA((2,)),
        ],
        compiler_params=pltpu.CompilerParams(vmem_limit_bytes=VMEM_LIMIT),
        cost_estimate=pl.CostEstimate(
            flops=16 * rows * rows * width,
            bytes_accessed=8 * rows * width * 2 + 32 * rows * rows + rows * width * 4,
            transcendentals=16 * rows * rows,
        ),
    )(early, late, row_info, col_info, row_ids, col_ids, *shards, *((received,) if add else ()))


def local(query_rows, key_rows, partner):
    rows, features = query_rows.shape
    factor = float(features) ** (-0.5)
    block = lax.axis_index("blk")
    place = lax.axis_index("pb")
    even = block % 2 == 0

    across = lambda a: shift(a, "pb", lambda i: i ^ 2)
    core = lambda a: shift(a, "pb", lambda i: i ^ 1)
    corner = lambda a: shift(a, "pb", lambda i: i ^ 3)
    beside = lambda a: shift(a, "blk", lambda i: i ^ 1)
    ahead = lambda a: shift(a, "blk", lambda i: i + 2)
    back = lambda a: shift(a, "blk", lambda i: i - 2)
    apart = lambda a: shift(a, "blk", lambda i: i + 2 if i % 2 == 0 else i - 2)
    pick = lambda first, second: jnp.where(even, first, second)

    k0, q0 = key_rows, query_rows
    y1_in = pick(k0, q0)
    kx = across(k0)
    y1 = beside(y1_in)
    kz = ahead(k0)
    ks, qs = core(k0), core(q0)
    partner_core, partner_across = core(partner), across(partner)

    qx = across(q0)
    kzy = beside(kz)
    qz = back(q0)

    kzx = across(kz)
    qzy = beside(qz)
    m1 = apart(pick(kzy, qx))

    kd0 = pick(m1, y1)
    kd1 = across(kd0)
    kzxy = beside(kzx)
    m2 = back(pick(qx, qzy))

    qzx = pick(m2, m1)
    qd0 = pick(y1, m2)
    qd1 = across(qd0)
    qzxy = beside(qzx)

    lanes = jnp.arange(rows, dtype=jnp.int32)[None, :]
    id_own = place * rows + lanes
    id_across = (place ^ 2) * rows + lanes
    id_core = (place ^ 1) * rows + lanes
    id_corner = (place ^ 3) * rows + lanes
    q_row_ids = jnp.concatenate([partner, partner_core], axis=1)
    q_col_ids = jnp.concatenate([id_own, id_across], axis=1)
    k_row_ids = jnp.concatenate([id_own, id_core], axis=1)
    k_col_ids = jnp.concatenate([partner, partner_across], axis=1)
    ids = jnp.concatenate([id_own, id_across, id_core, id_corner], axis=0)

    k_shards = (k0, kx, kz, kzx, kzy, kd0, kzxy, kd1)
    q_shards = (q0, qx, qz, qzx, qzy, qd0, qzxy, qd1)
    s_early, info = score((q0, qs), k_shards[:6], True, True, factor, (q_row_ids, q_col_ids))
    s_late, info = score((q0, qs), k_shards[6:], False, True, factor, (info,))

    in_block = small_call(
        block_kernel, [(24, rows)], info, across(info), core(info), corner(info)
    )[0]
    near = [in_block] + [shift(in_block, "blk", lambda i, d=d: i - d) for d in (1, 2, 3, -1, -2, -3)]
    even_flag = even.astype(jnp.int32)[None]
    col_info, row_info, loss = small_call(
        window_kernel, [(8, 2 * rows), (8, 2 * rows), (1, rows)], even_flag, ids, partner, *near, scalars=1
    )
    (t_early,) = score((k0, ks), q_shards[:6], True, False, factor)
    (t_late,) = score((k0, ks), q_shards[6:], False, False, factor)

    q_args = (factor, s_early, s_late, row_info, col_info, q_row_ids, q_col_ids, k_shards)
    k_args = (factor, t_early, t_late, col_info, row_info, k_row_ids, k_col_ids, q_shards)
    q_other = core(grad(1, *q_args))
    k_other = core(grad(1, *k_args))
    grad_queries = grad(0, *q_args, q_other)
    grad_keys = grad(0, *k_args, k_other)
    return (loss[0], grad_queries, grad_keys)


def solution(mesh):
    return jax.shard_map(
        local,
        mesh=mesh,
        in_specs=(P(("blk", "pb"), None), P(("blk", "pb"), None), P("blk", "pb")),
        out_specs=(P(("blk", "pb")), P(("blk", "pb"), None), P(("blk", "pb"), None)),
        check_vma=False,
    )
```

time: 379 us -> 177 us (0.47)
  waiting for transfers between devices: 261 us -> 74.2 us
  Pallas kernels: 0 us -> 54.4 us
  matrix products: 35.7 us -> 0 us
  blocking collectives: 20.2 us -> 0 us
  between operations: 14.9 us -> 1.13 us
    ppermute x15 -> x29, waiting for transfers between devices: 231 us -> 74.2 us  [shift(): lax.ppermute(array, axis, [(i, move(i) % peers) for i in range(peers)])]
    pallas_call x0 -> x10, Pallas kernels: none -> 54.4 us  [the longest x4 27.1 us: grad(): pl.pallas_call(functools.partial(grad_kernel, group, factor, add), out_sh...]
    dot_general x3 -> x0, matrix products: 35.7 us -> none  [the longest x1 16.7 us: local(): jnp.einsum('sqk,sqd->kd', own_weights, window_queries, preferred_element_...]
    all_gather x2 -> x0, waiting for transfers between devices: 29.9 us -> none  [the longest x1 29.9 us: local(): block_keys = lax.all_gather(key_rows, 'pb', axis=0, tiled=True)]
    all_gather x3 -> x0, blocking collectives: 15.9 us -> none  [the longest x2 10.6 us: joined(): everything = jax.tree.map(lambda part: lax.all_gather(part, axis), array)]
    select_n x2 -> x3, other arithmetic: 0.02 us -> 6.9 us  [local(): pick = lambda first, second: jnp.where(even, first, second)]
    unnamed x15 -> x58, local copies, waits for them, and re-layouts: 0.99 us -> 7.67 us
    gather x2 -> x0, local copies, waits for them, and re-layouts: 5.22 us -> none  [the longest x1 2.99 us: local(): positive = jnp.take_along_axis(scores[0], chosen[:, None], axis=1)[:, 0]]
  transfers between devices with their start and end apart: 17 -> 29, of which waited for: 12 -> 10; matrix products, arithmetic and copies ran while one was open for 10% -> 5% of each run, Pallas kernels for 0% -> 22%
where the time goes in v1:
time: 177 us
  waiting for transfers between devices  74.2 us (42%)
  Pallas kernels  54.4 us (31%)
  starting transfers between devices  31 us (18%)
  other arithmetic  8.27 us (5%)
  local copies, waits for them, and re-layouts  7.67 us (4%)
    ppermute x29, waiting for transfers between devices, shift(): lax.ppermute(array, axis, [(i, move(i) % peers) for i in range(peers)])  74.2 us
    ppermute x29, starting transfers between devices, shift(): lax.ppermute(array, axis, [(i, move(i) % peers) for i in range(peers)])  31 us
    pallas_call x4, Pallas kernels, grad(): pl.pallas_call(functools.partial(grad_kernel, group, factor, add), out_sh...  27.1 us
    pallas_call x4, Pallas kernels, score(): pl.pallas_call(functools.partial(score_kernel, tokens, early, stats, fact...  23.8 us
    unnamed x58, local copies, waits for them, and re-layouts  7.67 us
    select_n x3, other arithmetic, local(): pick = lambda first, second: jnp.where(even, first, second)  6.9 us
  transfers between devices with their start and end apart: 29, of which 10 were waited for; matrix products, arithmetic and copies ran while one was open for 5% of the time, Pallas kernels for 22%

profile of v1, /device:TPU:0, one launch (start us, length us, event | category | flops | bytes accessed | tf_op | source)
XLA Modules:
  0.0 176.6 jit_solution(13575490096925660805)
XLA Ops:
  0.6 5.1 %collective-permute-start.22 = (bf16[320,1024]{1,0:T(8,128)(2,1)}, bf16[320,1024]{1,0:T(8,128)(2,1)S(1)}, u32[]{:S(2)}, u32[]{:S(2)}) collective-permute-start(bf16[320,1024]{1,0:T(8,128)(2,1)} %refs_6_.7), channel_id=1, source_target_pairs={{0,24},{4,28},{8,0},{12,4},{16,8},{20,12},{24,16},{28,20},{1,25},{... | collective-permute-start | bytes 1966088 | tf_op jit(solution)/shard_map/ppermute | solution.py:17
  5.7 1.5 collective-permute-start.5
  7.2 14.0 %collective-permute-done.22.refs_4_.refs_8_ = bf16[320,1024]{1,0:T(8,128)(2,1)S(1)} collective-permute-done((bf16[320,1024]{1,0:T(8,128)(2,1)}, bf16[320,1024]{1,0:T(8,128)(2,1)S(1)}, u32[]{:S(2)}, u32[]{:S(2)}) %collective-permute-start.22) | collective-permute-done | bytes 655392 | tf_op jit(solution)/shard_map/ppermute | solution.py:17
  21.2 1.5 collective-permute-start.23
  22.7 12.3 %collective-permute-done.1.refs_4_.refs_8_ = bf16[320,1024]{1,0:T(8,128)(2,1)} collective-permute-done((bf16[320,1024]{1,0:T(8,128)(2,1)}, bf16[320,1024]{1,0:T(8,128)(2,1)}, u32[]{:S(2)}, u32[]{:S(2)}) %collective-permute-start.1) | collective-permute-done | bytes 655392 | tf_op jit(solution)/shard_map/ppermute | solution.py:17
  35.0 1.5 collective-permute-start.4
  36.5 2.0 %broadcast_select_fusion.4 = bf16[320,1024]{1,0:T(8,128)(2,1)} fusion(bf16[320,1024]{1,0:T(8,128)(2,1)} %refs_0_.7, bf16[320,1024]{1,0:T(8,128)(2,1)} %refs_6_.7, pred[]{:T(512)S(6)} %eq.5), kind=kLoop, calls=%fused_computation.4 | loop fusion | flops 327680 | bytes 1966081 | tf_op jit(solution)/shard_map/jit(_where)/select_n | solution.py:283
  39.0 1.5 collective-permute-start.2
  40.5 12.5 %collective-permute-done.4.refs_6_.refs_10_ = bf16[320,1024]{1,0:T(8,128)(2,1)} collective-permute-done((bf16[320,1024]{1,0:T(8,128)(2,1)}, bf16[320,1024]{1,0:T(8,128)(2,1)}, u32[]{:S(2)}, u32[]{:S(2)}) %collective-permute-start.4) | collective-permute-done | bytes 655392 | tf_op jit(solution)/shard_map/ppermute | solution.py:17
  53.0 2.3 %broadcast_select_fusion.2 = (bf16[320,1024]{1,0:T(8,128)(2,1)}, bf16[320,1024]{1,0:T(8,128)(2,1)}) fusion(bf16[320,1024]{1,0:T(8,128)(2,1)S(1)} %collective-permute-done.5.refs_3_.refs_7_, bf16[320,1024]{1,0:T(8,128)(2,1)S(1)} %collective-permute-done.23.refs_6_.refs_10_, pred[]{:T(512)S(6)} %eq.5, bf16[320,1024]{1,0:T(8,128)(2,1)} %collective-permute-done.4.refs_6_.refs_10_), kind=kLoop, calls=%fused_computation.2 | loop fusion | flops 655360 | bytes 3276801 | tf_op jit(solution)/shard_map/jit(_where)/select_n | solution.py:283
  55.2 2.7 %collective-permute-start.24 = (bf16[320,1024]{1,0:T(8,128)(2,1)}, bf16[320,1024]{1,0:T(8,128)(2,1)S(1)}, u32[]{:S(2)}, u32[]{:S(2)}) collective-permute-start(bf16[320,1024]{1,0:T(8,128)(2,1)} %get-tuple-element.20), channel_id=1, source_target_pairs={{0,24},{4,28},{8,0},{12,4},{16,8},{20,12},{24,16},{28,20},{1,25},{... | collective-permute-start | bytes 1966088 | tf_op jit(solution)/shard_map/ppermute | solution.py:17
  58.0 7.0 %collective-permute-done.7 = bf16[320,1024]{1,0:T(8,128)(2,1)} collective-permute-done((bf16[320,1024]{1,0:T(8,128)(2,1)}, bf16[320,1024]{1,0:T(8,128)(2,1)}, u32[]{:S(2)}, u32[]{:S(2)}) %collective-permute-start.7) | collective-permute-done | bytes 655392 | tf_op jit(solution)/shard_map/ppermute | solution.py:17
  65.0 1.5 collective-permute-start.9
  67.0 6.5 %collective-permute-done.24 = bf16[320,1024]{1,0:T(8,128)(2,1)S(1)} collective-permute-done((bf16[320,1024]{1,0:T(8,128)(2,1)}, bf16[320,1024]{1,0:T(8,128)(2,1)S(1)}, u32[]{:S(2)}, u32[]{:S(2)}) %collective-permute-start.24) | collective-permute-done | bytes 655392 | tf_op jit(solution)/shard_map/ppermute | solution.py:17
  74.3 9.7 %collective-permute-done.6 = bf16[320,1024]{1,0:T(8,128)(2,1)} collective-permute-done((bf16[320,1024]{1,0:T(8,128)(2,1)}, bf16[320,1024]{1,0:T(8,128)(2,1)}, u32[]{:S(2)}, u32[]{:S(2)}) %collective-permute-start.6) | collective-permute-done | bytes 655392 | tf_op jit(solution)/shard_map/ppermute | solution.py:17
  84.0 2.7 %broadcast_select_fusion = (bf16[320,1024]{1,0:T(8,128)(2,1)S(1)}, bf16[320,1024]{1,0:T(8,128)(2,1)}, bf16[320,1024]{1,0:T(8,128)(2,1)}) fusion(bf16[320,1024]{1,0:T(8,128)(2,1)} %collective-permute-done.7, bf16[320,1024]{1,0:T(8,128)(2,1)} %copy-done.16, pred[]{:T(512)S(6)} %eq.5, bf16[320,1024]{1,0:T(8,128)(2,1)} %collective-permute-done.6), kind=kLoop, calls=%fused_computation | loop fusion | flops 983040 | bytes 3932161 | tf_op jit(solution)/shard_map/jit(_where)/select_n | solution.py:283
  86.7 1.5 collective-permute-start.8
  88.3 1.1 collective-permute-done.10
  89.8 0.6 collective-permute-start.26
  90.4 9.2 %shard_map.58 = (f32[640,1920]{1,0:T(8,128)}, f32[8,640]{1,0:T(8,128)S(1)}) custom-call(bf16[320,1024]{1,0:T(8,128)(2,1)S(1)} %copy-done.2, bf16[320,1024]{1,0:T(8,128)(2,1)} %collective-permute-done.refs_1_, bf16[320,1024]{1,0:T(8,128)(2,1)S(1)} %copy-done, bf16[320,1024]{1,0:T(8,128)(2,1)} %collective-permute-done.9.refs_3_.refs_7_, ...), custom_call_target="tpu_custom_call" | custom-call | flops 2516582400 | bytes 10158080 | tf_op jit(solution)/shard_map/pallas_call | solution.py:97
  99.6 5.1 %collective-permute-done.8.refs_3_.refs_13_ = bf16[320,1024]{1,0:T(8,128)(2,1)} collective-permute-done((bf16[320,1024]{1,0:T(8,128)(2,1)}, bf16[320,1024]{1,0:T(8,128)(2,1)}, u32[]{:S(2)}, u32[]{:S(2)}) %collective-permute-start.8) | collective-permute-done | bytes 655392 | tf_op jit(solution)/shard_map/ppermute | solution.py:17
  104.7 3.5 %shard_map.59 = (f32[640,640]{1,0:T(8,128)S(1)}, f32[8,640]{1,0:T(8,128)S(1)}) custom-call(bf16[320,1024]{1,0:T(8,128)(2,1)S(1)} %copy-done.2, bf16[320,1024]{1,0:T(8,128)(2,1)} %collective-permute-done.refs_1_, bf16[320,1024]{1,0:T(8,128)(2,1)} %collective-permute-done.3.refs_2_.refs_12_, bf16[320,1024]{1,0:T(8,128)(2,1)} %collective-permute-done.8.refs_3_.refs_13_, ...), custom_call_target="tpu_custom_call" | custom-call | flops 838860800 | bytes 4259840 | tf_op jit(solution)/shard_map/pallas_call | solution.py:97
  108.2 1.1 copy-done.6
  109.4 1.5 collective-permute-start.11
  110.9 3.3 %collective-permute-done.11.across = f32[8,640]{1,0:T(8,128)S(1)} collective-permute-done((f32[8,640]{1,0:T(8,128)S(1)}, f32[8,640]{1,0:T(8,128)S(1)}, u32[]{:S(2)}, u32[]{:S(2)}) %collective-permute-start.11) | collective-permute-done | bytes 20512 | tf_op jit(solution)/shard_map/ppermute | solution.py:17
  114.2 0.6 pad_add_fusion.ids
  114.8 2.8 %collective-permute-done.13.corner = f32[8,640]{1,0:T(8,128)S(1)} collective-permute-done((f32[8,640]{1,0:T(8,128)S(1)}, f32[8,640]{1,0:T(8,128)S(1)}, u32[]{:S(2)}, u32[]{:S(2)}) %collective-permute-start.13) | collective-permute-done | bytes 20512 | tf_op jit(solution)/shard_map/ppermute | solution.py:17
  117.6 0.6 copy-done.26
  118.2 1.5 shard_map.60.refs_0_
  119.7 3.1 %collective-permute-start.14 = (f32[24,320]{1,0:T(8,128)}, f32[24,320]{1,0:T(8,128)S(1)}, u32[]{:S(2)}, u32[]{:S(2)}) collective-permute-start(f32[24,320]{1,0:T(8,128)} %shard_map.60.refs_0_), channel_id=1, source_target_pairs={{0,28},{4,0},{8,4},{12,8},{16,12},{20,16},{24,20},{28,24},{1,29},{... | collective-permute-start | bytes 92168 | tf_op jit(solution)/shard_map/ppermute | solution.py:17
  122.8 1.1 copy-done.3
  123.9 1.1 copy-done.8
  125.0 8.2 %shard_map.64.refs_0_ = f32[640,1920]{1,0:T(8,128)} custom-call(bf16[320,1024]{1,0:T(8,128)(2,1)S(1)} %copy-done, bf16[320,1024]{1,0:T(8,128)(2,1)} %collective-permute-done.21.refs_1_, bf16[320,1024]{1,0:T(8,128)(2,1)S(1)} %copy-done.2, bf16[320,1024]{1,0:T(8,128)(2,1)S(1)} %collective-permute-done.5.refs_3_.refs_7_, bf16[320,1024]{1,0:T(8,128)(2,1)S(1)} %copy-done.8, ...), custom_call_target="tpu_custom_call" | custom-call | flops 2516582400 | bytes 10158080 | tf_op jit(solution)/shard_map/pallas_call | solution.py:97
  133.2 0.6 collective-permute-start.15
  133.8 1.1 collective-permute-start.16
  134.9 1.4 collective-permute-start.17
  136.3 1.0 collective-permute-start.18
  137.3 2.4 %collective-permute-start.19 = (f32[24,320]{1,0:T(8,128)S(1)}, f32[24,320]{1,0:T(8,128)S(1)}, u32[]{:S(2)}, u32[]{:S(2)}) collective-permute-start(f32[24,320]{1,0:T(8,128)S(1)} %copy-done.17), channel_id=1, source_target_pairs={{0,12},{4,16},{8,20},{12,24},{16,28},{20,0},{24,4},{28,8},{1,13},{... | collective-permute-start | bytes 92168 | tf_op jit(solution)/shard_map/ppermute | solution.py:17
  139.7 2.9 %shard_map.65.refs_1_ = f32[640,640]{1,0:T(8,128)S(1)} custom-call(bf16[320,1024]{1,0:T(8,128)(2,1)S(1)} %copy-done, bf16[320,1024]{1,0:T(8,128)(2,1)} %collective-permute-done.21.refs_1_, bf16[320,1024]{1,0:T(8,128)(2,1)} %collective-permute-done.25.refs_2_.refs_12_, bf16[320,1024]{1,0:T(8,128)(2,1)} %collective-permute-done.26.refs_3_.refs_13_), custom_call_target="tpu_custom_call" | custom-call | flops 838860800 | bytes 4259840 | tf_op jit(solution)/shard_map/pallas_call | solution.py:97
  142.7 1.2 copy-done.1
  144.6 2.0 %shard_map.61 = (f32[8,640]{1,0:T(8,128)}, f32[8,640]{1,0:T(8,128)}, f32[1,320]{1,0:T(1,128)}) custom-call(s32[1]{0:T(128)} %bitcast.even_ref, s32[4,320]{1,0:T(4,128)} %pad_add_fusion.ids, s32[1,320]{1,0:T(1,128)} %partner.1, f32[24,320]{1,0:T(8,128)} %shard_map.60.refs_0_, f32[24,320]{1,0:T(8,128)} %copy-done.18, f32[24,320]{1,0:T(8,128)} %copy-done.19, ...), custom_call_target="tpu_custom_call" | custom-call | flops 100000 | bytes 400000 | tf_op jit(solution)/shard_map/pallas_call | solution.py:196
  146.6 0.7 copy-done.11
  147.3 0.7 copy-done.13
  148.0 6.3 %shard_map.62 = f32[320,1024]{1,0:T(8,128)} custom-call(f32[640,1920]{1,0:T(8,128)} %get-tuple-element.13.refs_0_, f32[640,640]{1,0:T(8,128)} %copy-done.6, f32[8,640]{1,0:T(8,128)S(1)} %copy-done.13, f32[8,640]{1,0:T(8,128)S(1)} %copy-done.11, s32[1,640]{1,0:T(1,128)S(1)} %get-tuple-element.23.refs_8_.refs_4_, ...), custom_call_target="tpu_custom_call" | custom-call | flops 1677721600 | bytes 9830400 | tf_op jit(solution)/shard_map/pallas_call | solution.py:247
  154.5 5.9 %shard_map.66 = f32[320,1024]{1,0:T(8,128)} custom-call(f32[640,1920]{1,0:T(8,128)} %shard_map.64.refs_0_, f32[640,640]{1,0:T(8,128)} %copy-done.1, f32[8,640]{1,0:T(8,128)S(1)} %copy-done.11, f32[8,640]{1,0:T(8,128)S(1)} %copy-done.13, s32[1,640]{1,0:T(1,128)S(1)} %get-tuple-element.24.refs_4_, s32[1,640]{1,0:T(1,128)S(1)} %get-tuple-element.22.refs_5_, ...), custom_call_target="tpu_custom_call" | custom-call | flops 1677721600 | bytes 9830400 | tf_op jit(solution)/shard_map/pallas_call | solution.py:247
  161.0 0.6 reduce
  161.6 7.7 %shard_map.63 = f32[320,1024]{1,0:T(8,128)} custom-call(f32[640,1920]{1,0:T(8,128)} %get-tuple-element.13.refs_0_, f32[640,640]{1,0:T(8,128)} %copy-done.6, f32[8,640]{1,0:T(8,128)S(1)} %copy-done.14, f32[8,640]{1,0:T(8,128)S(1)} %copy-done.12, s32[1,640]{1,0:T(1,128)S(1)} %get-tuple-element.23.refs_8_.refs_4_, ...), custom_call_target="tpu_custom_call" | custom-call | flops 1677721600 | bytes 9830400 | tf_op jit(solution)/shard_map/pallas_call | solution.py:247
  169.3 7.2 %shard_map.67 = f32[320,1024]{1,0:T(8,128)} custom-call(f32[640,1920]{1,0:T(8,128)} %shard_map.64.refs_0_, f32[640,640]{1,0:T(8,128)} %copy-done.1, f32[8,640]{1,0:T(8,128)S(1)} %copy-done.12, f32[8,640]{1,0:T(8,128)S(1)} %copy-done.14, s32[1,640]{1,0:T(1,128)S(1)} %get-tuple-element.24.refs_4_, s32[1,640]{1,0:T(1,128)S(1)} %get-tuple-element.22.refs_5_, ...), custom_call_target="tpu_custom_call" | custom-call | flops 1677721600 | bytes 9830400 | tf_op jit(solution)/shard_map/pallas_call | solution.py:247
  (88 shorter events, 3.7 us)
Async XLA Ops:
  0.6 20.6 %collective-permute-start.22 = (bf16[320,1024]{1,0:T(8,128)(2,1)}, bf16[320,1024]{1,0:T(8,128)(2,1)S(1)}, u32[]{:S(2)}, u32[]{:S(2)}) collective-permute-start(bf16[320,1024]{1,0:T(8,128)(2,1)} %refs_6_.7), channel_id=1, source_target_pairs={{0,24},{4,28},{8,0},{12,4},{16,8},{20,12},{24,16},{28,20},{1,25},{... | collective-permute-start | bytes 1966088 | tf_op jit(solution)/shard_map/ppermute | solution.py:17
  5.7 29.3 %collective-permute-start.1 = (bf16[320,1024]{1,0:T(8,128)(2,1)}, bf16[320,1024]{1,0:T(8,128)(2,1)}, u32[]{:S(2)}, u32[]{:S(2)}) collective-permute-start(bf16[320,1024]{1,0:T(8,128)(2,1)} %refs_0_.7), channel_id=1, source_target_pairs={{0,8},{4,12},{8,16},{12,20},{16,24},{20,28},{24,0},{28,4},{1,9},{5... | collective-permute-start | bytes 1966088 | tf_op jit(solution)/shard_map/ppermute | solution.py:17
  5.7 34.8 %collective-permute-start.5 = (bf16[320,1024]{1,0:T(8,128)(2,1)}, bf16[320,1024]{1,0:T(8,128)(2,1)S(1)}, u32[]{:S(2)}, u32[]{:S(2)}) collective-permute-start(bf16[320,1024]{1,0:T(8,128)(2,1)} %refs_6_.7), channel_id=1, source_target_pairs={{0,2},{1,3},{2,0},{3,1},{4,6},{5,7},{6,4},{7,5},{8,10},{9,11},{10,... | collective-permute-start | bytes 1966088 | tf_op jit(solution)/shard_map/ppermute | solution.py:17
  21.2 34.0 %copy-start.7 = (bf16[320,1024]{1,0:T(8,128)(2,1)}, bf16[320,1024]{1,0:T(8,128)(2,1)S(1)}, u32[]{:S(2)}) copy-start(bf16[320,1024]{1,0:T(8,128)(2,1)S(1)} %collective-permute-done.22.refs_4_.refs_8_) | copy-start | bytes 1966084
  21.2 19.3 %collective-permute-start.23 = (bf16[320,1024]{1,0:T(8,128)(2,1)S(1)}, bf16[320,1024]{1,0:T(8,128)(2,1)S(1)}, u32[]{:S(2)}, u32[]{:S(2)}) collective-permute-start(bf16[320,1024]{1,0:T(8,128)(2,1)S(1)} %collective-permute-done.22.refs_4_.refs_8_), channel_id=1, source_target_pairs={{0,4},{4,0},{8,12},{12,8},{16,20},{20,16},{24,28},{28,24},{1,5},{5... | collective-permute-start | bytes 1966088 | tf_op jit(solution)/shard_map/ppermute | solution.py:17
  35.0 18.0 %collective-permute-start.4 = (bf16[320,1024]{1,0:T(8,128)(2,1)}, bf16[320,1024]{1,0:T(8,128)(2,1)}, u32[]{:S(2)}, u32[]{:S(2)}) collective-permute-start(bf16[320,1024]{1,0:T(8,128)(2,1)} %collective-permute-done.1.refs_4_.refs_8_), channel_id=1, source_target_pairs={{0,4},{4,0},{8,12},{12,8},{16,20},{20,16},{24,28},{28,24},{1,5},{5... | collective-permute-start | bytes 1966088 | tf_op jit(solution)/shard_map/ppermute | solution.py:17
  38.5 19.5 %copy-start.2 = (bf16[320,1024]{1,0:T(8,128)(2,1)S(1)}, bf16[320,1024]{1,0:T(8,128)(2,1)}, u32[]{:S(2)}) copy-start(bf16[320,1024]{1,0:T(8,128)(2,1)} %refs_6_.7) | copy-start | bytes 1966084
  38.5 26.4 %copy-start = (bf16[320,1024]{1,0:T(8,128)(2,1)S(1)}, bf16[320,1024]{1,0:T(8,128)(2,1)}, u32[]{:S(2)}) copy-start(bf16[320,1024]{1,0:T(8,128)(2,1)} %refs_0_.7) | copy-start | bytes 1966084
  38.5 27.9 %copy-start.27 = (s32[1,320]{1,0:T(1,128)S(1)}, s32[1,320]{1,0:T(1,128)}, u32[]{:S(2)}) copy-start(s32[1,320]{1,0:T(1,128)} %partner.1) | copy-start | bytes 3844
  38.5 26.4 %collective-permute-start.7 = (bf16[320,1024]{1,0:T(8,128)(2,1)}, bf16[320,1024]{1,0:T(8,128)(2,1)}, u32[]{:S(2)}, u32[]{:S(2)}) collective-permute-start(bf16[320,1024]{1,0:T(8,128)(2,1)} %broadcast_select_fusion.4), channel_id=1, source_target_pairs={{0,4},{4,0},{8,12},{12,8},{16,20},{20,16},{24,28},{28,24},{1,5},{5... | collective-permute-start | bytes 1966088 | tf_op jit(solution)/shard_map/ppermute | solution.py:17
  39.0 27.4 %collective-permute-start.2 = (bf16[320,1024]{1,0:T(8,128)(2,1)}, bf16[320,1024]{1,0:T(8,128)(2,1)}, u32[]{:S(2)}, u32[]{:S(2)}) collective-permute-start(bf16[320,1024]{1,0:T(8,128)(2,1)} %collective-permute-done.1.refs_4_.refs_8_), channel_id=1, source_target_pairs={{0,2},{1,3},{2,0},{3,1},{4,6},{5,7},{6,4},{7,5},{8,10},{9,11},{10,... | collective-permute-start | bytes 1966088 | tf_op jit(solution)/shard_map/ppermute | solution.py:17
  55.2 18.2 %collective-permute-start.24 = (bf16[320,1024]{1,0:T(8,128)(2,1)}, bf16[320,1024]{1,0:T(8,128)(2,1)S(1)}, u32[]{:S(2)}, u32[]{:S(2)}) collective-permute-start(bf16[320,1024]{1,0:T(8,128)(2,1)} %get-tuple-element.20), channel_id=1, source_target_pairs={{0,24},{4,28},{8,0},{12,4},{16,8},{20,12},{24,16},{28,20},{1,25},{... | collective-permute-start | bytes 1966088 | tf_op jit(solution)/shard_map/ppermute | solution.py:17
  58.0 26.1 %collective-permute-start.6 = (bf16[320,1024]{1,0:T(8,128)(2,1)}, bf16[320,1024]{1,0:T(8,128)(2,1)}, u32[]{:S(2)}, u32[]{:S(2)}) collective-permute-start(bf16[320,1024]{1,0:T(8,128)(2,1)} %get-tuple-element.21), channel_id=1, source_target_pairs={{0,8},{4,28},{8,16},{12,4},{16,24},{20,12},{24,0},{28,20},{1,9},{5... | collective-permute-start | bytes 1966088 | tf_op jit(solution)/shard_map/ppermute | solution.py:17
  58.0 31.7 %collective-permute-start = (bf16[320,1024]{1,0:T(8,128)(2,1)S(1)}, bf16[320,1024]{1,0:T(8,128)(2,1)}, u32[]{:S(2)}, u32[]{:S(2)}) collective-permute-start(bf16[320,1024]{1,0:T(8,128)(2,1)S(1)} %copy-done.2), channel_id=1, source_target_pairs={{0,1},{1,0},{2,3},{3,2},{4,5},{5,4},{6,7},{7,6},{8,9},{9,8},{10,11... | collective-permute-start | bytes 1966088 | tf_op jit(solution)/shard_map/ppermute | solution.py:17
  65.0 24.8 %collective-permute-start.9 = (bf16[320,1024]{1,0:T(8,128)(2,1)S(1)}, bf16[320,1024]{1,0:T(8,128)(2,1)}, u32[]{:S(2)}, u32[]{:S(2)}) collective-permute-start(bf16[320,1024]{1,0:T(8,128)(2,1)S(1)} %copy-done), channel_id=1, source_target_pairs={{0,2},{1,3},{2,0},{3,1},{4,6},{5,7},{6,4},{7,5},{8,10},{9,11},{10,... | collective-permute-start | bytes 1966088 | tf_op jit(solution)/shard_map/ppermute | solution.py:17
  66.4 21.7 %collective-permute-start.27 = (s32[1,320]{1,0:T(1,128)S(1)}, s32[1,320]{1,0:T(1,128)S(1)}, u32[]{:S(2)}, u32[]{:S(2)}) collective-permute-start(s32[1,320]{1,0:T(1,128)S(1)} %copy-done.27), channel_id=1, source_target_pairs={{0,2},{1,3},{2,0},{3,1},{4,6},{5,7},{6,4},{7,5},{8,10},{9,11},{10,... | collective-permute-start | bytes 3848 | tf_op jit(solution)/shard_map/ppermute | solution.py:17
  73.5 26.1 %collective-permute-start.3 = (bf16[320,1024]{1,0:T(8,128)(2,1)}, bf16[320,1024]{1,0:T(8,128)(2,1)}, u32[]{:S(2)}, u32[]{:S(2)}) collective-permute-start(bf16[320,1024]{1,0:T(8,128)(2,1)} %collective-permute-done.2.refs_5_.refs_9_), channel_id=1, source_target_pairs={{0,4},{4,0},{8,12},{12,8},{16,20},{20,16},{24,28},{28,24},{1,5},{5... | collective-permute-start | bytes 1966088 | tf_op jit(solution)/shard_map/ppermute | solution.py:17
  86.7 18.0 %collective-permute-start.8 = (bf16[320,1024]{1,0:T(8,128)(2,1)}, bf16[320,1024]{1,0:T(8,128)(2,1)}, u32[]{:S(2)}, u32[]{:S(2)}) collective-permute-start(bf16[320,1024]{1,0:T(8,128)(2,1)} %get-tuple-element.19.refs_7_.refs_11_), channel_id=1, source_target_pairs={{0,2},{1,3},{2,0},{3,1},{4,6},{5,7},{6,4},{7,5},{8,10},{9,11},{10,... | collective-permute-start | bytes 1966088 | tf_op jit(solution)/shard_map/ppermute | solution.py:17
  88.2 1.2 collective-permute-start.10
  89.4 33.4 %collective-permute-start.21 = (bf16[320,1024]{1,0:T(8,128)(2,1)S(1)}, bf16[320,1024]{1,0:T(8,128)(2,1)}, u32[]{:S(2)}, u32[]{:S(2)}) collective-permute-start(bf16[320,1024]{1,0:T(8,128)(2,1)S(1)} %copy-done), channel_id=1, source_target_pairs={{0,1},{1,0},{2,3},{3,2},{4,5},{5,4},{6,7},{7,6},{8,9},{9,8},{10,11... | collective-permute-start | bytes 1966088 | tf_op jit(solution)/shard_map/ppermute | solution.py:17
  89.7 45.2 %collective-permute-start.25 = (bf16[320,1024]{1,0:T(8,128)(2,1)}, bf16[320,1024]{1,0:T(8,128)(2,1)}, u32[]{:S(2)}, u32[]{:S(2)}) collective-permute-start(bf16[320,1024]{1,0:T(8,128)(2,1)} %get-tuple-element.18.refs_5_.refs_9_), channel_id=1, source_target_pairs={{0,4},{4,0},{8,12},{12,8},{16,20},{20,16},{24,28},{28,24},{1,5},{5... | collective-permute-start | bytes 1966088 | tf_op jit(solution)/shard_map/ppermute | solution.py:17
  89.8 46.6 %collective-permute-start.26 = (bf16[320,1024]{1,0:T(8,128)(2,1)S(1)}, bf16[320,1024]{1,0:T(8,128)(2,1)}, u32[]{:S(2)}, u32[]{:S(2)}) collective-permute-start(bf16[320,1024]{1,0:T(8,128)(2,1)S(1)} %get-tuple-element.17.refs_7_.refs_11_), channel_id=1, source_target_pairs={{0,2},{1,3},{2,0},{3,1},{4,6},{5,7},{6,4},{7,5},{8,10},{9,11},{10,... | collective-permute-start | bytes 1966088 | tf_op jit(solution)/shard_map/ppermute | solution.py:17
  108.2 1.2 copy-start.6
  109.4 8.2 %copy-start.15 = (f32[8,640]{1,0:T(8,128)}, f32[8,640]{1,0:T(8,128)S(1)}, u32[]{:S(2)}) copy-start(f32[8,640]{1,0:T(8,128)S(1)} %get-tuple-element.11.own) | copy-start | bytes 61444
  109.4 4.8 %collective-permute-start.11 = (f32[8,640]{1,0:T(8,128)S(1)}, f32[8,640]{1,0:T(8,128)S(1)}, u32[]{:S(2)}, u32[]{:S(2)}) collective-permute-start(f32[8,640]{1,0:T(8,128)S(1)} %get-tuple-element.11.own), channel_id=1, source_target_pairs={{0,2},{1,3},{2,0},{3,1},{4,6},{5,7},{6,4},{7,5},{8,10},{9,11},{10,... | collective-permute-start | bytes 61448 | tf_op jit(solution)/shard_map/ppermute | solution.py:17
  110.9 3.9 %collective-permute-start.12 = (f32[8,640]{1,0:T(8,128)S(1)}, f32[8,640]{1,0:T(8,128)S(1)}, u32[]{:S(2)}, u32[]{:S(2)}) collective-permute-start(f32[8,640]{1,0:T(8,128)S(1)} %get-tuple-element.11.own), channel_id=1, source_target_pairs={{0,1},{1,0},{2,3},{3,2},{4,5},{5,4},{6,7},{7,6},{8,9},{9,8},{10,11... | collective-permute-start | bytes 61448 | tf_op jit(solution)/shard_map/ppermute | solution.py:17
  114.2 3.4 %copy-start.24 = (f32[8,640]{1,0:T(8,128)}, f32[8,640]{1,0:T(8,128)S(1)}, u32[]{:S(2)}) copy-start(f32[8,640]{1,0:T(8,128)S(1)} %collective-permute-done.11.across) | copy-start | bytes 61444
  114.2 3.4 %collective-permute-start.13 = (f32[8,640]{1,0:T(8,128)S(1)}, f32[8,640]{1,0:T(8,128)S(1)}, u32[]{:S(2)}, u32[]{:S(2)}) collective-permute-start(f32[8,640]{1,0:T(8,128)S(1)} %get-tuple-element.11.own), channel_id=1, source_target_pairs={{0,3},{1,2},{2,1},{3,0},{4,7},{5,6},{6,5},{7,4},{8,11},{9,10},{10,... | collective-permute-start | bytes 61448 | tf_op jit(solution)/shard_map/ppermute | solution.py:17
  114.8 2.8 %copy-start.25 = (f32[8,640]{1,0:T(8,128)}, f32[8,640]{1,0:T(8,128)S(1)}, u32[]{:S(2)}) copy-start(f32[8,640]{1,0:T(8,128)S(1)} %collective-permute-done.12.core) | copy-start | bytes 61444
  119.7 17.6 %collective-permute-start.14 = (f32[24,320]{1,0:T(8,128)}, f32[24,320]{1,0:T(8,128)S(1)}, u32[]{:S(2)}, u32[]{:S(2)}) collective-permute-start(f32[24,320]{1,0:T(8,128)} %shard_map.60.refs_0_), channel_id=1, source_target_pairs={{0,28},{4,0},{8,4},{12,8},{16,12},{20,16},{24,20},{28,24},{1,29},{... | collective-permute-start | bytes 92168 | tf_op jit(solution)/shard_map/ppermute | solution.py:17
  122.8 1.1 copy-start.3
  125.0 8.2 %copy-start.17 = (f32[24,320]{1,0:T(8,128)S(1)}, f32[24,320]{1,0:T(8,128)}, u32[]{:S(2)}) copy-start(f32[24,320]{1,0:T(8,128)} %shard_map.60.refs_0_) | copy-start | bytes 92164
  133.2 10.7 %collective-permute-start.15 = (f32[24,320]{1,0:T(8,128)S(1)}, f32[24,320]{1,0:T(8,128)S(1)}, u32[]{:S(2)}, u32[]{:S(2)}) collective-permute-start(f32[24,320]{1,0:T(8,128)S(1)} %copy-done.17), channel_id=1, source_target_pairs={{0,24},{4,28},{8,0},{12,4},{16,8},{20,12},{24,16},{28,20},{1,25},{... | collective-permute-start | bytes 92168 | tf_op jit(solution)/shard_map/ppermute | solution.py:17
  133.8 10.1 %collective-permute-start.16 = (f32[24,320]{1,0:T(8,128)S(1)}, f32[24,320]{1,0:T(8,128)S(1)}, u32[]{:S(2)}, u32[]{:S(2)}) collective-permute-start(f32[24,320]{1,0:T(8,128)S(1)} %copy-done.17), channel_id=1, source_target_pairs={{0,20},{4,24},{8,28},{12,0},{16,4},{20,8},{24,12},{28,16},{1,21},{... | collective-permute-start | bytes 92168 | tf_op jit(solution)/shard_map/ppermute | solution.py:17
  134.9 9.0 %collective-permute-start.17 = (f32[24,320]{1,0:T(8,128)S(1)}, f32[24,320]{1,0:T(8,128)S(1)}, u32[]{:S(2)}, u32[]{:S(2)}) collective-permute-start(f32[24,320]{1,0:T(8,128)S(1)} %copy-done.17), channel_id=1, source_target_pairs={{0,4},{4,8},{8,12},{12,16},{16,20},{20,24},{24,28},{28,0},{1,5},{5... | collective-permute-start | bytes 92168 | tf_op jit(solution)/shard_map/ppermute | solution.py:17
  136.3 7.6 %collective-permute-start.18 = (f32[24,320]{1,0:T(8,128)S(1)}, f32[24,320]{1,0:T(8,128)S(1)}, u32[]{:S(2)}, u32[]{:S(2)}) collective-permute-start(f32[24,320]{1,0:T(8,128)S(1)} %copy-done.17), channel_id=1, source_target_pairs={{0,8},{4,12},{8,16},{12,20},{16,24},{20,28},{24,0},{28,4},{1,9},{5... | collective-permute-start | bytes 92168 | tf_op jit(solution)/shard_map/ppermute | solution.py:17
  137.3 5.4 %copy-start.18 = (f32[24,320]{1,0:T(8,128)}, f32[24,320]{1,0:T(8,128)S(1)}, u32[]{:S(2)}) copy-start(f32[24,320]{1,0:T(8,128)S(1)} %collective-permute-done.14.refs_1_) | copy-start | bytes 92164
  137.3 6.7 %collective-permute-start.19 = (f32[24,320]{1,0:T(8,128)S(1)}, f32[24,320]{1,0:T(8,128)S(1)}, u32[]{:S(2)}, u32[]{:S(2)}) collective-permute-start(f32[24,320]{1,0:T(8,128)S(1)} %copy-done.17), channel_id=1, source_target_pairs={{0,12},{4,16},{8,20},{12,24},{16,28},{20,0},{24,4},{28,8},{1,13},{... | collective-permute-start | bytes 92168 | tf_op jit(solution)/shard_map/ppermute | solution.py:17
  142.7 1.2 copy-start.1
  148.0 6.4 %copy-start.4 = (bf16[320,1024]{1,0:T(8,128)(2,1)S(1)}, bf16[320,1024]{1,0:T(8,128)(2,1)}, u32[]{:S(2)}) copy-start(bf16[320,1024]{1,0:T(8,128)(2,1)} %get-tuple-element.18.refs_5_.refs_9_) | copy-start | bytes 1966084
  148.0 6.4 %copy-start.9 = (bf16[320,1024]{1,0:T(8,128)(2,1)S(1)}, bf16[320,1024]{1,0:T(8,128)(2,1)}, u32[]{:S(2)}) copy-start(bf16[320,1024]{1,0:T(8,128)(2,1)} %copy-done.7) | copy-start | bytes 1966084
  154.4 7.2 %collective-permute-start.20 = (f32[320,1024]{1,0:T(8,128)}, f32[320,1024]{1,0:T(8,128)}, u32[]{:S(2)}, u32[]{:S(2)}) collective-permute-start(f32[320,1024]{1,0:T(8,128)} %shard_map.62), channel_id=1, source_target_pairs={{0,1},{1,0},{2,3},{3,2},{4,5},{5,4},{6,7},{7,6},{8,9},{9,8},{10,11... | collective-permute-start | bytes 3932168 | tf_op jit(solution)/shard_map/ppermute | solution.py:17
  154.5 6.5 %copy-start.28 = (f32[1,320]{1,0:T(1,128)S(1)}, f32[1,320]{1,0:T(1,128)}, u32[]{:S(2)}) copy-start(f32[1,320]{1,0:T(1,128)} %get-tuple-element.12) | copy-start | bytes 3844
  154.5 7.1 %copy-start.12 = (f32[8,640]{1,0:T(8,128)S(1)}, f32[8,640]{1,0:T(8,128)}, u32[]{:S(2)}) copy-start(f32[8,640]{1,0:T(8,128)} %get-tuple-element.16.refs_3_.refs_2_) | copy-start | bytes 61444
  154.5 7.1 %copy-start.14 = (f32[8,640]{1,0:T(8,128)S(1)}, f32[8,640]{1,0:T(8,128)}, u32[]{:S(2)}) copy-start(f32[8,640]{1,0:T(8,128)} %get-tuple-element.15.refs_2_.refs_3_) | copy-start | bytes 61444
  160.4 8.9 %collective-permute-start.28 = (f32[320,1024]{1,0:T(8,128)}, f32[320,1024]{1,0:T(8,128)}, u32[]{:S(2)}, u32[]{:S(2)}) collective-permute-start(f32[320,1024]{1,0:T(8,128)} %shard_map.66), channel_id=1, source_target_pairs={{0,1},{1,0},{2,3},{3,2},{4,5},{5,4},{6,7},{7,6},{8,9},{9,8},{10,11... | collective-permute-start | bytes 3932168 | tf_op jit(solution)/shard_map/ppermute | solution.py:17
  161.6 7.7 %copy-start.5 = (bf16[320,1024]{1,0:T(8,128)(2,1)S(1)}, bf16[320,1024]{1,0:T(8,128)(2,1)}, u32[]{:S(2)}) copy-start(bf16[320,1024]{1,0:T(8,128)(2,1)} %get-tuple-element.18.refs_5_.refs_9_) | copy-start | bytes 1966084
  161.6 7.7 %copy-start.10 = (bf16[320,1024]{1,0:T(8,128)(2,1)S(1)}, bf16[320,1024]{1,0:T(8,128)(2,1)}, u32[]{:S(2)}) copy-start(bf16[320,1024]{1,0:T(8,128)(2,1)} %copy-done.7) | copy-start | bytes 1966084
  (10 other events, 7.1 us)

commit v2 on v1

--- a/solution.py
+++ b/solution.py
@@ -38,6 +38,35 @@
         copy.start()
         copies.append(copy)
     return copies
+
+
+def choose_kernel(flag, first, second, out, sem):
+    @pl.when(flag[0] == 1)
+    def _():
+        pltpu.make_async_copy(first, out, sem).start()
+
+    @pl.when(flag[0] != 1)
+    def _():
+        pltpu.make_async_copy(second, out, sem).start()
+
+    pltpu.make_async_copy(first, out, sem).wait()
+
+
+def choose(flag, first, second):
+    anywhere = pl.BlockSpec(memory_space=pl.ANY)
+    return pl.pallas_call(
+        choose_kernel,
+        out_shape=jax.ShapeDtypeStruct(first.shape, first.dtype),
+        in_specs=[pl.BlockSpec(memory_space=pltpu.SMEM), anywhere, anywhere],
+        out_specs=anywhere,
+        scratch_shapes=[pltpu.SemaphoreType.DMA],
+        cost_estimate=pl.CostEstimate(flops=0, bytes_accessed=2 * first.size * 2, transcendentals=0),
+    )(flag, first, second)
+
+
+def after(values, landed):
+    done = lax.optimization_barrier((values, landed))
+    return done[0], done[1]
 
 
 def score_kernel(tokens, early, stats, factor, *refs):
@@ -280,33 +309,23 @@
     ahead = lambda a: shift(a, "blk", lambda i: i + 2)
     back = lambda a: shift(a, "blk", lambda i: i - 2)
     apart = lambda a: shift(a, "blk", lambda i: i + 2 if i % 2 == 0 else i - 2)
-    pick = lambda first, second: jnp.where(even, first, second)
+    flag = even.astype(jnp.int32)[None]
+    pick = functools.partial(choose, flag)
 
     k0, q0 = key_rows, query_rows
-    y1_in = pick(k0, q0)
-    kx = across(k0)
-    y1 = beside(y1_in)
-    kz = ahead(k0)
+    kx, kz, y1 = across(k0), ahead(k0), beside(pick(k0, q0))
     ks, qs = core(k0), core(q0)
     partner_core, partner_across = core(partner), across(partner)
-
-    qx = across(q0)
-    kzy = beside(kz)
-    qz = back(q0)
-
-    kzx = across(kz)
-    qzy = beside(qz)
-    m1 = apart(pick(kzy, qx))
-
-    kd0 = pick(m1, y1)
-    kd1 = across(kd0)
-    kzxy = beside(kzx)
-    m2 = back(pick(qx, qzy))
-
-    qzx = pick(m2, m1)
-    qd0 = pick(y1, m2)
-    qd1 = across(qd0)
-    qzxy = beside(qzx)
+    (q0b, kzb), (kx, kz, y1) = after((q0, kz), (kx, kz, y1))
+    qx, kzy, qz = across(q0b), beside(kzb), back(q0b)
+    (kzb, qzb, kzyb, qxb), (qx, kzy, qz) = after((kz, qz, kzy, qx), (qx, kzy, qz))
+    kzx, qzy, m1 = across(kzb), beside(qzb), apart(pick(kzyb, qxb))
+    (m1b, y1b, kzxb, qxb, qzyb), (kzx, qzy, m1) = after((m1, y1, kzx, qx, qzy), (kzx, qzy, m1))
+    kd0 = pick(m1b, y1b)
+    kd1, kzxy, m2 = across(kd0), beside(kzxb), back(pick(qxb, qzyb))
+    (y1b, m1b, m2b), (kd1, kzxy, m2) = after((y1, m1, m2), (kd1, kzxy, m2))
+    qd0, qzx = pick(y1b, m2b), pick(m2b, m1b)
+    qd1, qzxy = across(qd0), beside(qzx)
 
     lanes = jnp.arange(rows, dtype=jnp.int32)[None, :]
     id_own = place * rows + lanes
@@ -328,9 +347,8 @@
         block_kernel, [(24, rows)], info, across(info), core(info), corner(info)
     )[0]
     near = [in_block] + [shift(in_block, "blk", lambda i, d=d: i - d) for d in (1, 2, 3, -1, -2, -3)]
-    even_flag = even.astype(jnp.int32)[None]
     col_info, row_info, loss = small_call(
-        window_kernel, [(8, 2 * rows), (8, 2 * rows), (1, rows)], even_flag, ids, partner, *near, scalars=1
+        window_kernel, [(8, 2 * rows), (8, 2 * rows), (1, rows)], flag, ids, partner, *near, scalars=1
     )
     (t_early,) = score((k0, ks), q_shards[:6], True, False, factor)
     (t_late,) = score((k0, ks), q_shards[6:], False, False, factor)

time: 177 us -> 294 us (1.66)
  Pallas kernels: 54.4 us -> 179 us
  waiting for transfers between devices: 74.2 us -> 52.7 us
  local copies, waits for them, and re-layouts: 7.67 us -> 26.1 us
  other arithmetic: 8.27 us -> 1.36 us
    pallas_call x0 -> x6, Pallas kernels: none -> 126 us  [choose(): pl.pallas_call(choose_kernel, out_shape=jax.ShapeDtypeStruct(first.shape,...]
    ppermute x29, waiting for transfers between devices: 74.2 us -> 52.7 us  [shift(): lax.ppermute(array, axis, [(i, move(i) % peers) for i in range(peers)])]
    unnamed x58 -> x102, local copies, waits for them, and re-layouts: 7.67 us -> 26.1 us
    select_n x3 -> x0, other arithmetic: 6.9 us -> none  [local(): pick = lambda first, second: jnp.where(even, first, second)]
  transfers between devices with their start and end apart: 29 -> 29, of which waited for: 10 -> 9; matrix products, arithmetic and copies ran while one was open for 5% -> 0% of each run, Pallas kernels for 22% -> 52%
where the time goes in v2:
time: 294 us; the launch traced here: 293 us
  Pallas kernels  179 us (61%)
  waiting for transfers between devices  52.7 us (18%)
  starting transfers between devices  32.2 us (11%)
  local copies, waits for them, and re-layouts  26.1 us (9%)
    pallas_call x6, Pallas kernels, choose(): pl.pallas_call(choose_kernel, out_shape=jax.ShapeDtypeStruct(first.shape,...  126 us
    ppermute x29, waiting for transfers between devices, shift(): lax.ppermute(array, axis, [(i, move(i) % peers) for i in range(peers)])  52.7 us
    ppermute x29, starting transfers between devices, shift(): lax.ppermute(array, axis, [(i, move(i) % peers) for i in range(peers)])  32.2 us
    unnamed x102, local copies, waits for them, and re-layouts  26.1 us
    pallas_call x4, Pallas kernels, grad(): pl.pallas_call(functools.partial(grad_kernel, group, factor, add), out_sh...  26.1 us
    pallas_call x4, Pallas kernels, score(): pl.pallas_call(functools.partial(score_kernel, tokens, early, stats, fact...  24 us
  transfers between devices with their start and end apart: 29, of which 9 were waited for; matrix products, arithmetic and copies ran while one was open for 0% of the time, Pallas kernels for 52%

profile of v2, /device:TPU:0, one launch (start us, length us, event | category | flops | bytes accessed | tf_op | source)
XLA Modules:
  0.0 292.9 jit_solution(12820924400086116087)
XLA Ops:
  0.6 3.1 %collective-permute-start.1 = (bf16[320,1024]{1,0:T(8,128)(2,1)}, bf16[320,1024]{1,0:T(8,128)(2,1)S(1)}, u32[]{:S(2)}, u32[]{:S(2)}) collective-permute-start(bf16[320,1024]{1,0:T(8,128)(2,1)} %refs_0_.7), channel_id=1, source_target_pairs={{0,8},{4,12},{8,16},{12,20},{16,24},{20,28},{24,0},{28,4},{1,9},{5... | collective-permute-start | bytes 1966088 | tf_op jit(solution)/shard_map/ppermute | solution.py:17
  3.7 1.5 collective-permute-start.2
  5.2 21.0 %shard_map.58 = bf16[320,1024]{1,0:T(8,128)(2,1)} custom-call(s32[1]{0:T(128)} %bitcast.flag.even_ref, bf16[320,1024]{1,0:T(8,128)(2,1)} %refs_0_.7, bf16[320,1024]{1,0:T(8,128)(2,1)} %refs_6_.7), custom_call_target="tpu_custom_call" | custom-call | bytes 1310720 | tf_op jit(solution)/shard_map/pallas_call | solution.py:57
  26.2 1.6 collective-permute-start.3
  28.6 13.7 %collective-permute-done.3.second.first = bf16[320,1024]{1,0:T(8,128)(2,1)S(1)} collective-permute-done((bf16[320,1024]{1,0:T(8,128)(2,1)}, bf16[320,1024]{1,0:T(8,128)(2,1)S(1)}, u32[]{:S(2)}, u32[]{:S(2)}) %collective-permute-start.3) | collective-permute-done | bytes 655392 | tf_op jit(solution)/shard_map/ppermute | solution.py:17
  42.4 2.4 collective-permute-start.4
  44.8 1.5 collective-permute-start.5
  46.8 10.6 %collective-permute-done.4.refs_4_.refs_8_ = bf16[320,1024]{1,0:T(8,128)(2,1)S(1)} collective-permute-done((bf16[320,1024]{1,0:T(8,128)(2,1)S(1)}, bf16[320,1024]{1,0:T(8,128)(2,1)S(1)}, u32[]{:S(2)}, u32[]{:S(2)}) %collective-permute-start.4) | collective-permute-done | bytes 655392 | tf_op jit(solution)/shard_map/ppermute | solution.py:17
  57.4 2.2 collective-permute-done.5.first.refs_6_.refs_10_
  59.6 1.2 collective-permute-done.6.second.first.refs_3_.refs_7_
  61.7 21.0 %shard_map.59 = bf16[320,1024]{1,0:T(8,128)(2,1)} custom-call(s32[1]{0:T(128)} %bitcast.flag.even_ref, bf16[320,1024]{1,0:T(8,128)(2,1)} %copy-done.16, bf16[320,1024]{1,0:T(8,128)(2,1)} %copy-done), custom_call_target="tpu_custom_call" | custom-call | bytes 1310720 | tf_op jit(solution)/shard_map/pallas_call | solution.py:57
  83.3 3.1 %collective-permute-start.9 = (bf16[320,1024]{1,0:T(8,128)(2,1)S(1)}, bf16[320,1024]{1,0:T(8,128)(2,1)S(1)}, u32[]{:S(2)}, u32[]{:S(2)}) collective-permute-start(bf16[320,1024]{1,0:T(8,128)(2,1)S(1)} %collective-permute-done.4.refs_4_.refs_8_), channel_id=1, source_target_pairs={{0,4},{4,0},{8,12},{12,8},{16,20},{20,16},{24,28},{28,24},{1,5},{5... | collective-permute-start | bytes 1966088 | tf_op jit(solution)/shard_map/ppermute | solution.py:17
  87.3 1.5 collective-permute-start.27
  88.8 9.7 %collective-permute-done.7.first.second = bf16[320,1024]{1,0:T(8,128)(2,1)} collective-permute-done((bf16[320,1024]{1,0:T(8,128)(2,1)}, bf16[320,1024]{1,0:T(8,128)(2,1)}, u32[]{:S(2)}, u32[]{:S(2)}) %collective-permute-start.7) | collective-permute-done | bytes 655392 | tf_op jit(solution)/shard_map/ppermute | solution.py:17
  100.2 21.0 %shard_map.60 = bf16[320,1024]{1,0:T(8,128)(2,1)} custom-call(s32[1]{0:T(128)} %bitcast.flag.even_ref, bf16[320,1024]{1,0:T(8,128)(2,1)} %copy-done, bf16[320,1024]{1,0:T(8,128)(2,1)} %copy-done.5), custom_call_target="tpu_custom_call" | custom-call | bytes 1310720 | tf_op jit(solution)/shard_map/pallas_call | solution.py:57
  121.2 1.5 collective-permute-start.10
  122.7 21.0 %shard_map.61.refs_7_.refs_11_ = bf16[320,1024]{1,0:T(8,128)(2,1)} custom-call(s32[1]{0:T(128)} %bitcast.flag.even_ref, bf16[320,1024]{1,0:T(8,128)(2,1)} %collective-permute-done.7.first.second, bf16[320,1024]{1,0:T(8,128)(2,1)} %copy-done.39), custom_call_target="tpu_custom_call" | custom-call | bytes 1310720 | tf_op jit(solution)/shard_map/pallas_call | solution.py:57
  144.6 2.0 collective-permute-start.12
  146.7 1.1 collective-permute-done.13
  149.2 1.1 copy-done.31
  150.3 9.2 %shard_map.62 = (f32[640,1920]{1,0:T(8,128)}, f32[8,640]{1,0:T(8,128)S(1)}) custom-call(bf16[320,1024]{1,0:T(8,128)(2,1)S(1)} %copy-done.4, bf16[320,1024]{1,0:T(8,128)(2,1)} %collective-permute-done.refs_1_, bf16[320,1024]{1,0:T(8,128)(2,1)S(1)} %copy-done.2, bf16[320,1024]{1,0:T(8,128)(2,1)S(1)} %copy-done.27, ...), custom_call_target="tpu_custom_call" | custom-call | flops 2516582400 | bytes 10158080 | tf_op jit(solution)/shard_map/pallas_call | solution.py:126
  160.3 21.0 %shard_map.68.refs_5_.refs_9_ = bf16[320,1024]{1,0:T(8,128)(2,1)} custom-call(s32[1]{0:T(128)} %bitcast.flag.even_ref, bf16[320,1024]{1,0:T(8,128)(2,1)} %collective-permute-done.10.first.second, bf16[320,1024]{1,0:T(8,128)(2,1)} %collective-permute-done.7.first.second), custom_call_target="tpu_custom_call" | custom-call | bytes 1310720 | tf_op jit(solution)/shard_map/pallas_call | solution.py:57
  181.3 21.0 %shard_map.69.refs_7_.refs_11_ = bf16[320,1024]{1,0:T(8,128)(2,1)} custom-call(s32[1]{0:T(128)} %bitcast.flag.even_ref, bf16[320,1024]{1,0:T(8,128)(2,1)} %copy-done.39, bf16[320,1024]{1,0:T(8,128)(2,1)} %collective-permute-done.10.first.second), custom_call_target="tpu_custom_call" | custom-call | bytes 1310720 | tf_op jit(solution)/shard_map/pallas_call | solution.py:57
  202.5 1.5 collective-permute-start.26
  203.9 3.6 %shard_map.63 = (f32[640,640]{1,0:T(8,128)S(1)}, f32[8,640]{1,0:T(8,128)S(1)}) custom-call(bf16[320,1024]{1,0:T(8,128)(2,1)S(1)} %copy-done.4, bf16[320,1024]{1,0:T(8,128)(2,1)} %collective-permute-done.refs_1_, bf16[320,1024]{1,0:T(8,128)(2,1)} %collective-permute-done.12.refs_2_.refs_12_, bf16[320,1024]{1,0:T(8,128)(2,1)} %collective-permute-done.11.refs_3_.refs_13_, ...), custom_call_target="tpu_custom_call" | custom-call | flops 838860800 | bytes 4259840 | tf_op jit(solution)/shard_map/pallas_call | solution.py:126
  207.6 1.2 copy-done.11
  209.3 10.8 %collective-permute-done.14.across = f32[8,640]{1,0:T(8,128)S(1)} collective-permute-done((f32[8,640]{1,0:T(8,128)S(1)}, f32[8,640]{1,0:T(8,128)S(1)}, u32[]{:S(2)}, u32[]{:S(2)}) %collective-permute-start.14) | collective-permute-done | bytes 20512 | tf_op jit(solution)/shard_map/ppermute | solution.py:17
  220.8 2.6 collective-permute-done.16.corner
  224.1 1.5 shard_map.64.refs_0_
  225.6 1.1 collective-permute-start.17
  227.1 1.5 collective-permute-start.19
  229.8 2.6 collective-permute-start.20
  233.1 1.9 collective-permute-start.22
  235.1 1.1 copy-done.8
  236.2 1.1 copy-done.13
  237.2 8.2 %shard_map.70.refs_0_ = f32[640,1920]{1,0:T(8,128)} custom-call(bf16[320,1024]{1,0:T(8,128)(2,1)S(1)} %copy-done.2, bf16[320,1024]{1,0:T(8,128)(2,1)} %collective-permute-done.24.refs_1_, bf16[320,1024]{1,0:T(8,128)(2,1)S(1)} %copy-done.4, bf16[320,1024]{1,0:T(8,128)(2,1)S(1)} %copy-done.1, bf16[320,1024]{1,0:T(8,128)(2,1)S(1)} %copy-done.13, ...), custom_call_target="tpu_custom_call" | custom-call | flops 2516582400 | bytes 10158080 | tf_op jit(solution)/shard_map/pallas_call | solution.py:126
  246.7 2.0 shard_map.65
  248.7 1.1 copy-done.18
  249.8 1.1 copy-done.21
  250.9 1.1 copy-done.24
  255.6 5.8 %shard_map.66 = f32[320,1024]{1,0:T(8,128)} custom-call(f32[640,1920]{1,0:T(8,128)} %get-tuple-element.58.refs_0_, f32[640,640]{1,0:T(8,128)} %copy-done.11, f32[8,640]{1,0:T(8,128)S(1)} %copy-done.36, f32[8,640]{1,0:T(8,128)S(1)} %copy-done.34, s32[1,640]{1,0:T(1,128)S(1)} %get-tuple-element.68.refs_8_.refs_4_, ...), custom_call_target="tpu_custom_call" | custom-call | flops 1677721600 | bytes 9830400 | tf_op jit(solution)/shard_map/pallas_call | solution.py:276
  261.6 3.0 %shard_map.71.refs_1_ = f32[640,640]{1,0:T(8,128)S(1)} custom-call(bf16[320,1024]{1,0:T(8,128)(2,1)S(1)} %copy-done.2, bf16[320,1024]{1,0:T(8,128)(2,1)} %collective-permute-done.24.refs_1_, bf16[320,1024]{1,0:T(8,128)(2,1)} %collective-permute-done.25.refs_2_.refs_12_, bf16[320,1024]{1,0:T(8,128)(2,1)} %collective-permute-done.26.refs_3_.refs_13_), custom_call_target="tpu_custom_call" | custom-call | flops 838860800 | bytes 4259840 | tf_op jit(solution)/shard_map/pallas_call | solution.py:126
  264.6 1.2 copy-done.3
  265.9 5.9 %shard_map.72 = f32[320,1024]{1,0:T(8,128)} custom-call(f32[640,1920]{1,0:T(8,128)} %shard_map.70.refs_0_, f32[640,640]{1,0:T(8,128)} %copy-done.3, f32[8,640]{1,0:T(8,128)S(1)} %copy-done.35, f32[8,640]{1,0:T(8,128)S(1)} %copy-done.37, s32[1,640]{1,0:T(1,128)S(1)} %get-tuple-element.69.refs_4_, s32[1,640]{1,0:T(1,128)S(1)} %get-tuple-element.67.refs_5_, ...), custom_call_target="tpu_custom_call" | custom-call | flops 1677721600 | bytes 9830400 | tf_op jit(solution)/shard_map/pallas_call | solution.py:276
  272.8 1.2 copy-done.19
  277.3 1.1 copy-done.33
  278.4 7.2 %shard_map.67 = f32[320,1024]{1,0:T(8,128)} custom-call(f32[640,1920]{1,0:T(8,128)} %get-tuple-element.58.refs_0_, f32[640,640]{1,0:T(8,128)} %copy-done.11, f32[8,640]{1,0:T(8,128)S(1)} %copy-done.37, f32[8,640]{1,0:T(8,128)S(1)} %copy-done.35, s32[1,640]{1,0:T(1,128)S(1)} %get-tuple-element.68.refs_8_.refs_4_, ...), custom_call_target="tpu_custom_call" | custom-call | flops 1677721600 | bytes 9830400 | tf_op jit(solution)/shard_map/pallas_call | solution.py:276
  285.6 7.2 %shard_map.73 = f32[320,1024]{1,0:T(8,128)} custom-call(f32[640,1920]{1,0:T(8,128)} %shard_map.70.refs_0_, f32[640,640]{1,0:T(8,128)} %copy-done.3, f32[8,640]{1,0:T(8,128)S(1)} %copy-done.35, f32[8,640]{1,0:T(8,128)S(1)} %copy-done.37, s32[1,640]{1,0:T(1,128)S(1)} %get-tuple-element.69.refs_4_, s32[1,640]{1,0:T(1,128)S(1)} %get-tuple-element.67.refs_5_, ...), custom_call_target="tpu_custom_call" | custom-call | flops 1677721600 | bytes 9830400 | tf_op jit(solution)/shard_map/pallas_call | solution.py:276
  (135 shorter events, 22.5 us)
Async XLA Ops:
  0.6 41.7 %copy-start.4 = (bf16[320,1024]{1,0:T(8,128)(2,1)S(1)}, bf16[320,1024]{1,0:T(8,128)(2,1)}, u32[]{:S(2)}) copy-start(bf16[320,1024]{1,0:T(8,128)(2,1)} %refs_6_.7) | copy-start | bytes 1966084
  0.6 27.1 %collective-permute-start.1 = (bf16[320,1024]{1,0:T(8,128)(2,1)}, bf16[320,1024]{1,0:T(8,128)(2,1)S(1)}, u32[]{:S(2)}, u32[]{:S(2)}) collective-permute-start(bf16[320,1024]{1,0:T(8,128)(2,1)} %refs_0_.7), channel_id=1, source_target_pairs={{0,8},{4,12},{8,16},{12,20},{16,24},{20,28},{24,0},{28,4},{1,9},{5... | collective-permute-start | bytes 1966088 | tf_op jit(solution)/shard_map/ppermute | solution.py:17
  3.7 24.1 %collective-permute-start.2 = (bf16[320,1024]{1,0:T(8,128)(2,1)}, bf16[320,1024]{1,0:T(8,128)(2,1)S(1)}, u32[]{:S(2)}, u32[]{:S(2)}) collective-permute-start(bf16[320,1024]{1,0:T(8,128)(2,1)} %refs_0_.7), channel_id=1, source_target_pairs={{0,2},{1,3},{2,0},{3,1},{4,6},{5,7},{6,4},{7,5},{8,10},{9,11},{10,... | collective-permute-start | bytes 1966088 | tf_op jit(solution)/shard_map/ppermute | solution.py:17
  26.2 61.1 %copy-start.49 = (s32[1,320]{1,0:T(1,128)S(1)}, s32[1,320]{1,0:T(1,128)}, u32[]{:S(2)}) copy-start(s32[1,320]{1,0:T(1,128)} %partner.1) | copy-start | bytes 3844
  26.2 16.2 %collective-permute-start.3 = (bf16[320,1024]{1,0:T(8,128)(2,1)}, bf16[320,1024]{1,0:T(8,128)(2,1)S(1)}, u32[]{:S(2)}, u32[]{:S(2)}) collective-permute-start(bf16[320,1024]{1,0:T(8,128)(2,1)} %shard_map.58), channel_id=1, source_target_pairs={{0,4},{4,0},{8,12},{12,8},{16,20},{20,16},{24,28},{28,24},{1,5},{5... | collective-permute-start | bytes 1966088 | tf_op jit(solution)/shard_map/ppermute | solution.py:17
  42.4 17.2 %copy-start.39 = (bf16[320,1024]{1,0:T(8,128)(2,1)}, bf16[320,1024]{1,0:T(8,128)(2,1)S(1)}, u32[]{:S(2)}) copy-start(bf16[320,1024]{1,0:T(8,128)(2,1)S(1)} %collective-permute-done.3.second.first) | copy-start | bytes 1966084
  42.4 15.0 %collective-permute-start.4 = (bf16[320,1024]{1,0:T(8,128)(2,1)S(1)}, bf16[320,1024]{1,0:T(8,128)(2,1)S(1)}, u32[]{:S(2)}, u32[]{:S(2)}) collective-permute-start(bf16[320,1024]{1,0:T(8,128)(2,1)S(1)} %copy-done.4), channel_id=1, source_target_pairs={{0,24},{4,28},{8,0},{12,4},{16,8},{20,12},{24,16},{28,20},{1,25},{... | collective-permute-start | bytes 1966088 | tf_op jit(solution)/shard_map/ppermute | solution.py:17
  44.8 14.8 %collective-permute-start.5 = (bf16[320,1024]{1,0:T(8,128)(2,1)S(1)}, bf16[320,1024]{1,0:T(8,128)(2,1)S(1)}, u32[]{:S(2)}, u32[]{:S(2)}) collective-permute-start(bf16[320,1024]{1,0:T(8,128)(2,1)S(1)} %collective-permute-done.1.refs_4_.refs_8_), channel_id=1, source_target_pairs={{0,4},{4,0},{8,12},{12,8},{16,20},{20,16},{24,28},{28,24},{1,5},{5... | collective-permute-start | bytes 1966088 | tf_op jit(solution)/shard_map/ppermute | solution.py:17
  46.3 14.6 %collective-permute-start.6 = (bf16[320,1024]{1,0:T(8,128)(2,1)S(1)}, bf16[320,1024]{1,0:T(8,128)(2,1)S(1)}, u32[]{:S(2)}, u32[]{:S(2)}) collective-permute-start(bf16[320,1024]{1,0:T(8,128)(2,1)S(1)} %copy-done.4), channel_id=1, source_target_pairs={{0,2},{1,3},{2,0},{3,1},{4,6},{5,7},{6,4},{7,5},{8,10},{9,11},{10,... | collective-permute-start | bytes 1966088 | tf_op jit(solution)/shard_map/ppermute | solution.py:17
  82.7 15.8 %collective-permute-start.7 = (bf16[320,1024]{1,0:T(8,128)(2,1)}, bf16[320,1024]{1,0:T(8,128)(2,1)}, u32[]{:S(2)}, u32[]{:S(2)}) collective-permute-start(bf16[320,1024]{1,0:T(8,128)(2,1)} %shard_map.59), channel_id=1, source_target_pairs={{0,8},{4,28},{8,16},{12,4},{16,24},{20,12},{24,0},{28,20},{1,9},{5... | collective-permute-start | bytes 1966088 | tf_op jit(solution)/shard_map/ppermute | solution.py:17
  82.7 15.7 %collective-permute-start.8 = (bf16[320,1024]{1,0:T(8,128)(2,1)S(1)}, bf16[320,1024]{1,0:T(8,128)(2,1)S(1)}, u32[]{:S(2)}, u32[]{:S(2)}) collective-permute-start(bf16[320,1024]{1,0:T(8,128)(2,1)S(1)} %collective-permute-done.1.refs_4_.refs_8_), channel_id=1, source_target_pairs={{0,2},{1,3},{2,0},{3,1},{4,6},{5,7},{6,4},{7,5},{8,10},{9,11},{10,... | collective-permute-start | bytes 1966088 | tf_op jit(solution)/shard_map/ppermute | solution.py:17
  83.3 15.2 %collective-permute-start.9 = (bf16[320,1024]{1,0:T(8,128)(2,1)S(1)}, bf16[320,1024]{1,0:T(8,128)(2,1)S(1)}, u32[]{:S(2)}, u32[]{:S(2)}) collective-permute-start(bf16[320,1024]{1,0:T(8,128)(2,1)S(1)} %collective-permute-done.4.refs_4_.refs_8_), channel_id=1, source_target_pairs={{0,4},{4,0},{8,12},{12,8},{16,20},{20,16},{24,28},{28,24},{1,5},{5... | collective-permute-start | bytes 1966088 | tf_op jit(solution)/shard_map/ppermute | solution.py:17
  87.3 60.8 %collective-permute-start = (bf16[320,1024]{1,0:T(8,128)(2,1)S(1)}, bf16[320,1024]{1,0:T(8,128)(2,1)}, u32[]{:S(2)}, u32[]{:S(2)}) collective-permute-start(bf16[320,1024]{1,0:T(8,128)(2,1)S(1)} %copy-done.4), channel_id=1, source_target_pairs={{0,1},{1,0},{2,3},{3,2},{4,5},{5,4},{6,7},{7,6},{8,9},{9,8},{10,11... | collective-permute-start | bytes 1966088 | tf_op jit(solution)/shard_map/ppermute | solution.py:17
  87.3 59.3 %collective-permute-start.27 = (s32[1,320]{1,0:T(1,128)S(1)}, s32[1,320]{1,0:T(1,128)S(1)}, u32[]{:S(2)}, u32[]{:S(2)}) collective-permute-start(s32[1,320]{1,0:T(1,128)S(1)} %copy-done.49), channel_id=1, source_target_pairs={{0,2},{1,3},{2,0},{3,1},{4,6},{5,7},{6,4},{7,5},{8,10},{9,11},{10,... | collective-permute-start | bytes 3848 | tf_op jit(solution)/shard_map/ppermute | solution.py:17
  121.1 26.6 %copy-start.2 = (bf16[320,1024]{1,0:T(8,128)(2,1)S(1)}, bf16[320,1024]{1,0:T(8,128)(2,1)}, u32[]{:S(2)}) copy-start(bf16[320,1024]{1,0:T(8,128)(2,1)} %refs_0_.7) | copy-start | bytes 1966084
  121.1 27.0 %copy-start.17 = (bf16[320,1024]{1,0:T(8,128)(2,1)S(1)}, bf16[320,1024]{1,0:T(8,128)(2,1)}, u32[]{:S(2)}) copy-start(bf16[320,1024]{1,0:T(8,128)(2,1)} %copy-done.16) | copy-start | bytes 1966084
  121.2 27.0 %copy-start.27 = (bf16[320,1024]{1,0:T(8,128)(2,1)S(1)}, bf16[320,1024]{1,0:T(8,128)(2,1)}, u32[]{:S(2)}) copy-start(bf16[320,1024]{1,0:T(8,128)(2,1)} %copy-done.26) | copy-start | bytes 1966084
  121.2 39.2 %collective-permute-start.10 = (bf16[320,1024]{1,0:T(8,128)(2,1)}, bf16[320,1024]{1,0:T(8,128)(2,1)}, u32[]{:S(2)}, u32[]{:S(2)}) collective-permute-start(bf16[320,1024]{1,0:T(8,128)(2,1)} %shard_map.60), channel_id=1, source_target_pairs={{0,24},{4,28},{8,0},{12,4},{16,8},{20,12},{24,16},{28,20},{1,25},{... | collective-permute-start | bytes 1966088 | tf_op jit(solution)/shard_map/ppermute | solution.py:17
  143.6 16.7 %collective-permute-start.11 = (bf16[320,1024]{1,0:T(8,128)(2,1)}, bf16[320,1024]{1,0:T(8,128)(2,1)}, u32[]{:S(2)}, u32[]{:S(2)}) collective-permute-start(bf16[320,1024]{1,0:T(8,128)(2,1)} %shard_map.61.refs_7_.refs_11_), channel_id=1, source_target_pairs={{0,2},{1,3},{2,0},{3,1},{4,6},{5,7},{6,4},{7,5},{8,10},{9,11},{10,... | collective-permute-start | bytes 1966088 | tf_op jit(solution)/shard_map/ppermute | solution.py:17
  144.6 15.7 %collective-permute-start.12 = (bf16[320,1024]{1,0:T(8,128)(2,1)}, bf16[320,1024]{1,0:T(8,128)(2,1)}, u32[]{:S(2)}, u32[]{:S(2)}) collective-permute-start(bf16[320,1024]{1,0:T(8,128)(2,1)} %copy-done.30), channel_id=1, source_target_pairs={{0,4},{4,0},{8,12},{12,8},{16,20},{20,16},{24,28},{28,24},{1,5},{5... | collective-permute-start | bytes 1966088 | tf_op jit(solution)/shard_map/ppermute | solution.py:17
  146.6 1.2 collective-permute-start.13
  147.8 79.3 %collective-permute-start.24 = (bf16[320,1024]{1,0:T(8,128)(2,1)S(1)}, bf16[320,1024]{1,0:T(8,128)(2,1)}, u32[]{:S(2)}, u32[]{:S(2)}) collective-permute-start(bf16[320,1024]{1,0:T(8,128)(2,1)S(1)} %copy-done.2), channel_id=1, source_target_pairs={{0,1},{1,0},{2,3},{3,2},{4,5},{5,4},{6,7},{7,6},{8,9},{9,8},{10,11... | collective-permute-start | bytes 1966088 | tf_op jit(solution)/shard_map/ppermute | solution.py:17
  181.3 21.0 %copy-start.7 = (bf16[320,1024]{1,0:T(8,128)(2,1)S(1)}, bf16[320,1024]{1,0:T(8,128)(2,1)}, u32[]{:S(2)}) copy-start(bf16[320,1024]{1,0:T(8,128)(2,1)} %shard_map.68.refs_5_.refs_9_) | copy-start | bytes 1966084
  202.3 59.3 %collective-permute-start.25 = (bf16[320,1024]{1,0:T(8,128)(2,1)S(1)}, bf16[320,1024]{1,0:T(8,128)(2,1)}, u32[]{:S(2)}, u32[]{:S(2)}) collective-permute-start(bf16[320,1024]{1,0:T(8,128)(2,1)S(1)} %copy-done.7), channel_id=1, source_target_pairs={{0,4},{4,0},{8,12},{12,8},{16,20},{20,16},{24,28},{28,24},{1,5},{5... | collective-permute-start | bytes 1966088 | tf_op jit(solution)/shard_map/ppermute | solution.py:17
  202.5 59.1 %collective-permute-start.26 = (bf16[320,1024]{1,0:T(8,128)(2,1)}, bf16[320,1024]{1,0:T(8,128)(2,1)}, u32[]{:S(2)}, u32[]{:S(2)}) collective-permute-start(bf16[320,1024]{1,0:T(8,128)(2,1)} %shard_map.69.refs_7_.refs_11_), channel_id=1, source_target_pairs={{0,2},{1,3},{2,0},{3,1},{4,6},{5,7},{6,4},{7,5},{8,10},{9,11},{10,... | collective-permute-start | bytes 1966088 | tf_op jit(solution)/shard_map/ppermute | solution.py:17
  203.9 31.1 %copy-start.1 = (bf16[320,1024]{1,0:T(8,128)(2,1)S(1)}, bf16[320,1024]{1,0:T(8,128)(2,1)}, u32[]{:S(2)}) copy-start(bf16[320,1024]{1,0:T(8,128)(2,1)} %copy-done) | copy-start | bytes 1966084
  203.9 31.1 %copy-start.6 = (bf16[320,1024]{1,0:T(8,128)(2,1)S(1)}, bf16[320,1024]{1,0:T(8,128)(2,1)}, u32[]{:S(2)}) copy-start(bf16[320,1024]{1,0:T(8,128)(2,1)} %copy-done.5) | copy-start | bytes 1966084
  208.8 14.7 %copy-start.38 = (f32[8,640]{1,0:T(8,128)}, f32[8,640]{1,0:T(8,128)S(1)}, u32[]{:S(2)}) copy-start(f32[8,640]{1,0:T(8,128)S(1)} %get-tuple-element.56.own) | copy-start | bytes 61444
  208.8 11.3 %collective-permute-start.14 = (f32[8,640]{1,0:T(8,128)S(1)}, f32[8,640]{1,0:T(8,128)S(1)}, u32[]{:S(2)}, u32[]{:S(2)}) collective-permute-start(f32[8,640]{1,0:T(8,128)S(1)} %get-tuple-element.56.own), channel_id=1, source_target_pairs={{0,2},{1,3},{2,0},{3,1},{4,6},{5,7},{6,4},{7,5},{8,10},{9,11},{10,... | collective-permute-start | bytes 61448 | tf_op jit(solution)/shard_map/ppermute | solution.py:17
  209.3 11.5 %collective-permute-start.15 = (f32[8,640]{1,0:T(8,128)S(1)}, f32[8,640]{1,0:T(8,128)S(1)}, u32[]{:S(2)}, u32[]{:S(2)}) collective-permute-start(f32[8,640]{1,0:T(8,128)S(1)} %get-tuple-element.56.own), channel_id=1, source_target_pairs={{0,1},{1,0},{2,3},{3,2},{4,5},{5,4},{6,7},{7,6},{8,9},{9,8},{10,11... | collective-permute-start | bytes 61448 | tf_op jit(solution)/shard_map/ppermute | solution.py:17
  220.1 3.4 %collective-permute-start.16 = (f32[8,640]{1,0:T(8,128)S(1)}, f32[8,640]{1,0:T(8,128)S(1)}, u32[]{:S(2)}, u32[]{:S(2)}) collective-permute-start(f32[8,640]{1,0:T(8,128)S(1)} %get-tuple-element.56.own), channel_id=1, source_target_pairs={{0,3},{1,2},{2,1},{3,0},{4,7},{5,6},{6,5},{7,4},{8,11},{9,10},{10,... | collective-permute-start | bytes 61448 | tf_op jit(solution)/shard_map/ppermute | solution.py:17
  225.6 4.2 %collective-permute-start.17 = (f32[24,320]{1,0:T(8,128)}, f32[24,320]{1,0:T(8,128)S(1)}, u32[]{:S(2)}, u32[]{:S(2)}) collective-permute-start(f32[24,320]{1,0:T(8,128)} %shard_map.64.refs_0_), channel_id=1, source_target_pairs={{0,28},{4,0},{8,4},{12,8},{16,12},{20,16},{24,20},{28,24},{1,29},{... | collective-permute-start | bytes 92168 | tf_op jit(solution)/shard_map/ppermute | solution.py:17
  226.7 5.6 %collective-permute-start.18 = (f32[24,320]{1,0:T(8,128)}, f32[24,320]{1,0:T(8,128)S(1)}, u32[]{:S(2)}, u32[]{:S(2)}) collective-permute-start(f32[24,320]{1,0:T(8,128)} %shard_map.64.refs_0_), channel_id=1, source_target_pairs={{0,24},{4,28},{8,0},{12,4},{16,8},{20,12},{24,16},{28,20},{1,25},{... | collective-permute-start | bytes 92168 | tf_op jit(solution)/shard_map/ppermute | solution.py:17
  227.1 6.1 %collective-permute-start.19 = (f32[24,320]{1,0:T(8,128)}, f32[24,320]{1,0:T(8,128)S(1)}, u32[]{:S(2)}, u32[]{:S(2)}) collective-permute-start(f32[24,320]{1,0:T(8,128)} %shard_map.64.refs_0_), channel_id=1, source_target_pairs={{0,20},{4,24},{8,28},{12,0},{16,4},{20,8},{24,12},{28,16},{1,21},{... | collective-permute-start | bytes 92168 | tf_op jit(solution)/shard_map/ppermute | solution.py:17
  229.8 15.7 %copy-start.40 = (f32[24,320]{1,0:T(8,128)}, f32[24,320]{1,0:T(8,128)S(1)}, u32[]{:S(2)}) copy-start(f32[24,320]{1,0:T(8,128)S(1)} %collective-permute-done.17.refs_1_) | copy-start | bytes 92164
  229.8 15.7 %collective-permute-start.20 = (f32[24,320]{1,0:T(8,128)}, f32[24,320]{1,0:T(8,128)S(1)}, u32[]{:S(2)}, u32[]{:S(2)}) collective-permute-start(f32[24,320]{1,0:T(8,128)} %shard_map.64.refs_0_), channel_id=1, source_target_pairs={{0,4},{4,8},{8,12},{12,16},{16,20},{20,24},{24,28},{28,0},{1,5},{5... | collective-permute-start | bytes 92168 | tf_op jit(solution)/shard_map/ppermute | solution.py:17
  232.3 13.1 %copy-start.41 = (f32[24,320]{1,0:T(8,128)}, f32[24,320]{1,0:T(8,128)S(1)}, u32[]{:S(2)}) copy-start(f32[24,320]{1,0:T(8,128)S(1)} %collective-permute-done.18.refs_2_) | copy-start | bytes 92164
  232.3 13.1 %collective-permute-start.21 = (f32[24,320]{1,0:T(8,128)}, f32[24,320]{1,0:T(8,128)S(1)}, u32[]{:S(2)}, u32[]{:S(2)}) collective-permute-start(f32[24,320]{1,0:T(8,128)} %shard_map.64.refs_0_), channel_id=1, source_target_pairs={{0,8},{4,12},{8,16},{12,20},{16,24},{20,28},{24,0},{28,4},{1,9},{5... | collective-permute-start | bytes 92168 | tf_op jit(solution)/shard_map/ppermute | solution.py:17
  233.1 12.3 %copy-start.42 = (f32[24,320]{1,0:T(8,128)}, f32[24,320]{1,0:T(8,128)S(1)}, u32[]{:S(2)}) copy-start(f32[24,320]{1,0:T(8,128)S(1)} %collective-permute-done.19.refs_3_) | copy-start | bytes 92164
  233.1 12.4 %collective-permute-start.22 = (f32[24,320]{1,0:T(8,128)}, f32[24,320]{1,0:T(8,128)S(1)}, u32[]{:S(2)}, u32[]{:S(2)}) collective-permute-start(f32[24,320]{1,0:T(8,128)} %shard_map.64.refs_0_), channel_id=1, source_target_pairs={{0,12},{4,16},{8,20},{12,24},{16,28},{20,0},{24,4},{28,8},{1,13},{... | collective-permute-start | bytes 92168 | tf_op jit(solution)/shard_map/ppermute | solution.py:17
  261.5 4.4 %copy-start.9 = (bf16[320,1024]{1,0:T(8,128)(2,1)S(1)}, bf16[320,1024]{1,0:T(8,128)(2,1)}, u32[]{:S(2)}) copy-start(bf16[320,1024]{1,0:T(8,128)(2,1)} %shard_map.69.refs_7_.refs_11_) | copy-start | bytes 1966084
  261.5 4.4 %copy-start.14 = (bf16[320,1024]{1,0:T(8,128)(2,1)S(1)}, bf16[320,1024]{1,0:T(8,128)(2,1)}, u32[]{:S(2)}) copy-start(bf16[320,1024]{1,0:T(8,128)(2,1)} %copy-done.12) | copy-start | bytes 1966084
  261.5 4.4 %copy-start.35 = (f32[8,640]{1,0:T(8,128)S(1)}, f32[8,640]{1,0:T(8,128)}, u32[]{:S(2)}) copy-start(f32[8,640]{1,0:T(8,128)} %get-tuple-element.61.refs_3_.refs_2_) | copy-start | bytes 61444
  261.5 11.3 %collective-permute-start.23 = (f32[320,1024]{1,0:T(8,128)}, f32[320,1024]{1,0:T(8,128)}, u32[]{:S(2)}, u32[]{:S(2)}) collective-permute-start(f32[320,1024]{1,0:T(8,128)} %shard_map.66), channel_id=1, source_target_pairs={{0,1},{1,0},{2,3},{3,2},{4,5},{5,4},{6,7},{7,6},{8,9},{9,8},{10,11... | collective-permute-start | bytes 3932168 | tf_op jit(solution)/shard_map/ppermute | solution.py:17
  265.9 6.4 %copy-start.50 = (f32[1,320]{1,0:T(1,128)S(1)}, f32[1,320]{1,0:T(1,128)}, u32[]{:S(2)}) copy-start(f32[1,320]{1,0:T(1,128)} %get-tuple-element.57) | copy-start | bytes 3844
  271.8 13.8 %collective-permute-start.28 = (f32[320,1024]{1,0:T(8,128)}, f32[320,1024]{1,0:T(8,128)}, u32[]{:S(2)}, u32[]{:S(2)}) collective-permute-start(f32[320,1024]{1,0:T(8,128)} %shard_map.72), channel_id=1, source_target_pairs={{0,1},{1,0},{2,3},{3,2},{4,5},{5,4},{6,7},{7,6},{8,9},{9,8},{10,11... | collective-permute-start | bytes 3932168 | tf_op jit(solution)/shard_map/ppermute | solution.py:17
  272.8 12.7 %copy-start.10 = (bf16[320,1024]{1,0:T(8,128)(2,1)S(1)}, bf16[320,1024]{1,0:T(8,128)(2,1)}, u32[]{:S(2)}) copy-start(bf16[320,1024]{1,0:T(8,128)(2,1)} %shard_map.69.refs_7_.refs_11_) | copy-start | bytes 1966084
  272.8 12.7 %copy-start.15 = (bf16[320,1024]{1,0:T(8,128)(2,1)S(1)}, bf16[320,1024]{1,0:T(8,128)(2,1)}, u32[]{:S(2)}) copy-start(bf16[320,1024]{1,0:T(8,128)(2,1)} %copy-done.12) | copy-start | bytes 1966084
  (32 other events, 38.3 us)

commit v3 on v2

--- a/solution.py
+++ b/solution.py
@@ -8,7 +8,9 @@
 from jax.sharding import PartitionSpec as P
 
 F32 = jnp.float32
-VMEM_LIMIT = 48 * 1024 * 1024
+VMEM_LIMIT = 20 * 1024 * 1024
+ANYWHERE = pl.BlockSpec(memory_space=pl.ANY)
+WHOLE = pl.BlockSpec(memory_space=pltpu.VMEM)
 NT = (((1,), (1,)), ((), ()))
 
 
@@ -53,20 +55,27 @@
 
 
 def choose(flag, first, second):
-    anywhere = pl.BlockSpec(memory_space=pl.ANY)
     return pl.pallas_call(
         choose_kernel,
         out_shape=jax.ShapeDtypeStruct(first.shape, first.dtype),
-        in_specs=[pl.BlockSpec(memory_space=pltpu.SMEM), anywhere, anywhere],
-        out_specs=anywhere,
+        in_specs=[pl.BlockSpec(memory_space=pltpu.SMEM), ANYWHERE, ANYWHERE],
+        out_specs=WHOLE,
         scratch_shapes=[pltpu.SemaphoreType.DMA],
+        compiler_params=pltpu.CompilerParams(vmem_limit_bytes=VMEM_LIMIT),
         cost_estimate=pl.CostEstimate(flops=0, bytes_accessed=2 * first.size * 2, transcendentals=0),
     )(flag, first, second)
 
 
-def after(values, landed):
-    done = lax.optimization_barrier((values, landed))
-    return done[0], done[1]
+def after(value, landed):
+    return lax.optimization_barrier((value, landed))[0]
+
+
+def kept(shape, dtype):
+    return pltpu.VMEM(shape, dtype)
+
+
+def in_vmem(array):
+    return pltpu.with_memory_space_constraint(array, pltpu.VMEM)
 
 
 def score_kernel(tokens, early, stats, factor, *refs):
@@ -75,10 +84,10 @@
     rest = list(refs[2 + tokens :])
     if stats:
         side = [rest.pop(0) for _ in range(2 if early else 1)]
-    out = rest.pop(0)
+    out, right = rest.pop(0), rest.pop(0)
     if stats:
         info = rest.pop(0)
-    left, right, sems = rest
+    left, sems = rest
     copies = fetch(mine, left, sems) + fetch(shards, right, sems.at[pl.ds(2, tokens)])
     for copy in copies[:2]:
         copy.wait()
@@ -118,19 +127,16 @@
 def score(mine, shards, early, stats, factor, side=()):
     rows, width = mine[0].shape
     tokens = len(shards)
-    anywhere = pl.BlockSpec(memory_space=pl.ANY)
-    whole = pl.BlockSpec(memory_space=pltpu.VMEM)
-    shapes = [jax.ShapeDtypeStruct((2 * rows, tokens * rows), F32)]
+    shapes = [kept((2 * rows, tokens * rows), F32), kept((tokens * rows, width), jnp.bfloat16)]
     if stats:
         shapes.append(jax.ShapeDtypeStruct((8, 2 * rows), F32))
     return pl.pallas_call(
         functools.partial(score_kernel, tokens, early, stats, factor),
         out_shape=tuple(shapes),
-        in_specs=[anywhere] * (2 + tokens) + [whole] * len(side),
-        out_specs=(whole,) * len(shapes),
+        in_specs=[ANYWHERE] * (2 + tokens) + [WHOLE] * len(side),
+        out_specs=(WHOLE,) * len(shapes),
         scratch_shapes=[
             pltpu.VMEM((2 * rows, width), jnp.bfloat16),
-            pltpu.VMEM((tokens * rows, width), jnp.bfloat16),
             pltpu.SemaphoreType.DMA((2 + tokens,)),
         ],
         compiler_params=pltpu.CompilerParams(vmem_limit_bytes=VMEM_LIMIT),
@@ -221,78 +227,55 @@
 
 
 def small_call(kernel, shapes, *args, scalars=0):
-    whole = pl.BlockSpec(memory_space=pltpu.VMEM)
     return pl.pallas_call(
         kernel,
         out_shape=tuple(jax.ShapeDtypeStruct(s, F32) for s in shapes),
-        in_specs=[pl.BlockSpec(memory_space=pltpu.SMEM)] * scalars + [whole] * (len(args) - scalars),
-        out_specs=(whole,) * len(shapes),
+        in_specs=[pl.BlockSpec(memory_space=pltpu.SMEM)] * scalars + [WHOLE] * (len(args) - scalars),
+        out_specs=(WHOLE,) * len(shapes),
+        compiler_params=pltpu.CompilerParams(vmem_limit_bytes=VMEM_LIMIT),
         cost_estimate=pl.CostEstimate(flops=100000, bytes_accessed=400000, transcendentals=20000),
     )(*args)
 
 
 def grad_kernel(group, factor, add, *refs):
-    early, late, row_info, col_info, row_ids, col_ids = refs[:6]
-    shards = refs[6:14]
-    rest = list(refs[14:])
-    received = rest.pop(0) if add else None
-    out, s_early, s_late, held, weights, sems, s_sems = rest
+    early, late, held_early, held_late, row_info, col_info, row_ids, col_ids = refs[:8]
+    received = refs[8] if add else None
+    out, weights = refs[-2:]
     rows = out.shape[0]
     pair = 2 * rows
     here = pl.ds(group * rows, rows)
-    s_copies = [
-        pltpu.make_async_copy(early.at[here], s_early, s_sems.at[0]),
-        pltpu.make_async_copy(late.at[here], s_late, s_sems.at[1]),
-    ]
-    for copy in s_copies:
-        copy.start()
-    copies = fetch(shards, held, sems)
     row = as_column(row_info[pl.ds(4, 1), :])[group * rows : (group + 1) * rows]
     own = as_column(row_ids[...])[group * rows : (group + 1) * rows]
-    s_copies[0].wait()
     for p in range(4):
-        if p < 3:
-            s = s_early[:, pl.ds(p * pair, pair)]
-        else:
-            s_copies[1].wait()
-            s = s_late[...]
+        s = early[here, pl.ds(p * pair, pair)] if p < 3 else late[here, :]
         w = 0.5 * jnp.exp(s - row) + 0.5 * jnp.exp(s - col_info[pl.ds(p, 1), :])
         if p == 0:
             w = w - jnp.where(own == col_ids[...], 1.0, 0.0)
         weights[:, pl.ds(p * pair, pair)] = w.astype(jnp.bfloat16)
-    for copy in copies:
-        copy.wait()
-    total = jnp.dot(weights[...], held[...], preferred_element_type=F32) * factor
+    total = jnp.dot(weights[:, pl.ds(0, 3 * pair)], held_early[...], preferred_element_type=F32)
+    total = total + jnp.dot(weights[:, pl.ds(3 * pair, pair)], held_late[...], preferred_element_type=F32)
+    total = total * factor
     if add:
         total = total + received[...]
     out[...] = total
 
 
-def grad(group, factor, early, late, row_info, col_info, row_ids, col_ids, shards, received=None):
-    rows, width = shards[0].shape
-    anywhere = pl.BlockSpec(memory_space=pl.ANY)
-    whole = pl.BlockSpec(memory_space=pltpu.VMEM)
+def grad(group, factor, parts, row_info, col_info, row_ids, col_ids, received=None):
+    rows, width = parts[0].shape[0] // 2, parts[2].shape[1]
     add = received is not None
     return pl.pallas_call(
         functools.partial(grad_kernel, group, factor, add),
         out_shape=jax.ShapeDtypeStruct((rows, width), F32),
-        in_specs=[anywhere] * 2 + [whole] * 4 + [anywhere] * 8 + ([whole] if add else []),
-        out_specs=whole,
-        scratch_shapes=[
-            pltpu.VMEM((rows, 6 * rows), F32),
-            pltpu.VMEM((rows, 2 * rows), F32),
-            pltpu.VMEM((8 * rows, width), jnp.bfloat16),
-            pltpu.VMEM((rows, 8 * rows), jnp.bfloat16),
-            pltpu.SemaphoreType.DMA((8,)),
-            pltpu.SemaphoreType.DMA((2,)),
-        ],
+        in_specs=[WHOLE] * (9 if add else 8),
+        out_specs=WHOLE,
+        scratch_shapes=[pltpu.VMEM((rows, 8 * rows), jnp.bfloat16)],
         compiler_params=pltpu.CompilerParams(vmem_limit_bytes=VMEM_LIMIT),
         cost_estimate=pl.CostEstimate(
             flops=16 * rows * rows * width,
             bytes_accessed=8 * rows * width * 2 + 32 * rows * rows + rows * width * 4,
             transcendentals=16 * rows * rows,
         ),
-    )(early, late, row_info, col_info, row_ids, col_ids, *shards, *((received,) if add else ()))
+    )(*map(in_vmem, parts), row_info, col_info, row_ids, col_ids, *((received,) if add else ()))
 
 
 def local(query_rows, key_rows, partner):
@@ -316,16 +299,23 @@
     kx, kz, y1 = across(k0), ahead(k0), beside(pick(k0, q0))
     ks, qs = core(k0), core(q0)
     partner_core, partner_across = core(partner), across(partner)
-    (q0b, kzb), (kx, kz, y1) = after((q0, kz), (kx, kz, y1))
-    qx, kzy, qz = across(q0b), beside(kzb), back(q0b)
-    (kzb, qzb, kzyb, qxb), (qx, kzy, qz) = after((kz, qz, kzy, qx), (qx, kzy, qz))
-    kzx, qzy, m1 = across(kzb), beside(qzb), apart(pick(kzyb, qxb))
-    (m1b, y1b, kzxb, qxb, qzyb), (kzx, qzy, m1) = after((m1, y1, kzx, qx, qzy), (kzx, qzy, m1))
-    kd0 = pick(m1b, y1b)
-    kd1, kzxy, m2 = across(kd0), beside(kzxb), back(pick(qxb, qzyb))
-    (y1b, m1b, m2b), (kd1, kzxy, m2) = after((y1, m1, m2), (kd1, kzxy, m2))
-    qd0, qzx = pick(y1b, m2b), pick(m2b, m1b)
-    qd1, qzxy = across(qd0), beside(qzx)
+
+    qx = across(after(q0, kx))
+    kzy = beside(after(kz, y1))
+    qz = back(after(q0, kz))
+
+    kzx = across(after(kz, qx))
+    qzy = beside(after(qz, kzy))
+    m1 = apart(after(pick(kzy, qx), qz))
+
+    kd0 = pick(m1, y1)
+    kd1 = across(after(kd0, kzx))
+    kzxy = beside(after(kzx, qzy))
+    m2 = back(after(pick(qx, qzy), m1))
+
+    qd0, qzx = pick(y1, m2), pick(m2, m1)
+    qd1 = across(after(qd0, kd1))
+    qzxy = beside(after(qzx, kzxy))
 
     lanes = jnp.arange(rows, dtype=jnp.int32)[None, :]
     id_own = place * rows + lanes
@@ -340,8 +330,8 @@
 
     k_shards = (k0, kx, kz, kzx, kzy, kd0, kzxy, kd1)
     q_shards = (q0, qx, qz, qzx, qzy, qd0, qzxy, qd1)
-    s_early, info = score((q0, qs), k_shards[:6], True, True, factor, (q_row_ids, q_col_ids))
-    s_late, info = score((q0, qs), k_shards[6:], False, True, factor, (info,))
+    s_early, k_early, info = score((q0, qs), k_shards[:6], True, True, factor, (q_row_ids, q_col_ids))
+    s_late, k_late, info = score((q0, qs), k_shards[6:], False, True, factor, (info,))
 
     in_block = small_call(
         block_kernel, [(24, rows)], info, across(info), core(info), corner(info)
@@ -350,11 +340,11 @@
     col_info, row_info, loss = small_call(
         window_kernel, [(8, 2 * rows), (8, 2 * rows), (1, rows)], flag, ids, partner, *near, scalars=1
     )
-    (t_early,) = score((k0, ks), q_shards[:6], True, False, factor)
-    (t_late,) = score((k0, ks), q_shards[6:], False, False, factor)
-
-    q_args = (factor, s_early, s_late, row_info, col_info, q_row_ids, q_col_ids, k_shards)
-    k_args = (factor, t_early, t_late, col_info, row_info, k_row_ids, k_col_ids, q_shards)
+    t_early, q_early = score((k0, ks), q_shards[:6], True, False, factor)
+    t_late, q_late = score((k0, ks), q_shards[6:], False, False, factor)
+
+    q_args = (factor, (s_early, s_late, k_early, k_late), row_info, col_info, q_row_ids, q_col_ids)
+    k_args = (factor, (t_early, t_late, q_early, q_late), col_info, row_info, k_row_ids, k_col_ids)
     q_other = core(grad(1, *q_args))
     k_other = core(grad(1, *k_args))
     grad_queries = grad(0, *q_args, q_other)

time: 294 us -> 146 us (0.50)
  Pallas kernels: 179 us -> 44.5 us
  local copies, waits for them, and re-layouts: 26.1 us -> 12.2 us
  waiting for transfers between devices: 52.7 us -> 56.1 us
    pallas_call x6, Pallas kernels: 126 us -> 6.62 us  [choose(): pl.pallas_call(choose_kernel, out_shape=jax.ShapeDtypeStruct(first.shape,...]
    unnamed x102 -> x44, local copies, waits for them, and re-layouts: 26.1 us -> 12.2 us
    pallas_call x4, Pallas kernels: 26.1 us -> 17.2 us  [grad(): pl.pallas_call(functools.partial(grad_kernel, group, factor, add), out_sh...]
    pallas_call x4, Pallas kernels: 24 us -> 20.1 us  [score(): pl.pallas_call(functools.partial(score_kernel, tokens, early, stats, fact...]
    ppermute x29, waiting for transfers between devices: 52.7 us -> 56.1 us  [shift(): lax.ppermute(array, axis, [(i, move(i) % peers) for i in range(peers)])]
  transfers between devices with their start and end apart: 29 -> 29, of which waited for: 9 -> 10; matrix products, arithmetic and copies ran while one was open for 0% -> 1% of each run, Pallas kernels for 52% -> 27%
where the time goes in v3:
time: 146 us; the launch traced here: 145 us
  waiting for transfers between devices  56.1 us (38%)
  Pallas kernels  44.5 us (30%)
  starting transfers between devices  30.8 us (21%)
  local copies, waits for them, and re-layouts  12.2 us (8%)
    ppermute x29, waiting for transfers between devices, shift(): lax.ppermute(array, axis, [(i, move(i) % peers) for i in range(peers)])  56.1 us
    ppermute x29, starting transfers between devices, shift(): lax.ppermute(array, axis, [(i, move(i) % peers) for i in range(peers)])  30.8 us
    pallas_call x4, Pallas kernels, score(): pl.pallas_call(functools.partial(score_kernel, tokens, early, stats, fact...  20.1 us
    pallas_call x4, Pallas kernels, grad(): pl.pallas_call(functools.partial(grad_kernel, group, factor, add), out_sh...  17.2 us
    unnamed x44, local copies, waits for them, and re-layouts  12.2 us
    pallas_call x6, Pallas kernels, choose(): pl.pallas_call(choose_kernel, out_shape=jax.ShapeDtypeStruct(first.shape,...  6.62 us
  transfers between devices with their start and end apart: 29, of which 10 were waited for; matrix products, arithmetic and copies ran while one was open for 1% of the time, Pallas kernels for 27%

profile of v3, /device:TPU:0, one launch (start us, length us, event | category | flops | bytes accessed | tf_op | source)
XLA Modules:
  0.0 145.4 jit_solution(2279075441504701064)
XLA Ops:
  0.6 3.1 %collective-permute-start.1 = (bf16[320,1024]{1,0:T(8,128)(2,1)}, bf16[320,1024]{1,0:T(8,128)(2,1)}, u32[]{:S(2)}, u32[]{:S(2)}) collective-permute-start(bf16[320,1024]{1,0:T(8,128)(2,1)} %refs_0_.7), channel_id=1, source_target_pairs={{0,8},{4,12},{8,16},{12,20},{16,24},{20,28},{24,0},{28,4},{1,9},{5... | collective-permute-start | bytes 1966088 | tf_op jit(solution)/shard_map/ppermute | solution.py:19
  3.7 1.5 %collective-permute-start.2 = (bf16[320,1024]{1,0:T(8,128)(2,1)}, bf16[320,1024]{1,0:T(8,128)(2,1)S(1)}, u32[]{:S(2)}, u32[]{:S(2)}) collective-permute-start(bf16[320,1024]{1,0:T(8,128)(2,1)} %refs_0_.7), channel_id=1, source_target_pairs={{0,2},{1,3},{2,0},{3,1},{4,6},{5,7},{6,4},{7,5},{8,10},{9,11},{10,... | collective-permute-start | bytes 1966088 | tf_op jit(solution)/shard_map/ppermute | solution.py:19
  5.2 1.1 shard_map.58
  6.3 1.6 %collective-permute-start.6 = (bf16[320,1024]{1,0:T(8,128)(2,1)S(1)}, bf16[320,1024]{1,0:T(8,128)(2,1)S(1)}, u32[]{:S(2)}, u32[]{:S(2)}) collective-permute-start(bf16[320,1024]{1,0:T(8,128)(2,1)S(1)} %shard_map.58), channel_id=1, source_target_pairs={{0,4},{4,0},{8,12},{12,8},{16,20},{20,16},{24,28},{28,24},{1,5},{5... | collective-permute-start | bytes 1966088 | tf_op jit(solution)/shard_map/ppermute | solution.py:19
  7.9 12.2 %collective-permute-done.2.refs_3_ = bf16[320,1024]{1,0:T(8,128)(2,1)S(1)} collective-permute-done((bf16[320,1024]{1,0:T(8,128)(2,1)}, bf16[320,1024]{1,0:T(8,128)(2,1)S(1)}, u32[]{:S(2)}, u32[]{:S(2)}) %collective-permute-start.2) | collective-permute-done | bytes 655392 | tf_op jit(solution)/shard_map/ppermute | solution.py:19
  20.1 0.8 copy-done.18
  20.9 1.5 %collective-permute-start.3 = (bf16[320,1024]{1,0:T(8,128)(2,1)}, bf16[320,1024]{1,0:T(8,128)(2,1)S(1)}, u32[]{:S(2)}, u32[]{:S(2)}) collective-permute-start(bf16[320,1024]{1,0:T(8,128)(2,1)} %refs_2_.3), channel_id=1, source_target_pairs={{0,2},{1,3},{2,0},{3,1},{4,6},{5,7},{6,4},{7,5},{8,10},{9,11},{10,... | collective-permute-start | bytes 1966088 | tf_op jit(solution)/shard_map/ppermute | solution.py:19
  22.4 2.4 %collective-permute-start.5 = (bf16[320,1024]{1,0:T(8,128)(2,1)}, bf16[320,1024]{1,0:T(8,128)(2,1)}, u32[]{:S(2)}, u32[]{:S(2)}) collective-permute-start(bf16[320,1024]{1,0:T(8,128)(2,1)} %refs_2_.3), channel_id=1, source_target_pairs={{0,24},{4,28},{8,0},{12,4},{16,8},{20,12},{24,16},{28,20},{1,25},{... | collective-permute-start | bytes 1966088 | tf_op jit(solution)/shard_map/ppermute | solution.py:19
  24.8 1.5 %collective-permute-start.7 = (bf16[320,1024]{1,0:T(8,128)(2,1)}, bf16[320,1024]{1,0:T(8,128)(2,1)S(1)}, u32[]{:S(2)}, u32[]{:S(2)}) collective-permute-start(bf16[320,1024]{1,0:T(8,128)(2,1)} %collective-permute-done.1.refs_4_), channel_id=1, source_target_pairs={{0,4},{4,0},{8,12},{12,8},{16,20},{20,16},{24,28},{28,24},{1,5},{5... | collective-permute-start | bytes 1966088 | tf_op jit(solution)/shard_map/ppermute | solution.py:19
  26.4 10.2 %collective-permute-done.3.second.first.refs_3_ = bf16[320,1024]{1,0:T(8,128)(2,1)S(1)} collective-permute-done((bf16[320,1024]{1,0:T(8,128)(2,1)}, bf16[320,1024]{1,0:T(8,128)(2,1)S(1)}, u32[]{:S(2)}, u32[]{:S(2)}) %collective-permute-start.3) | collective-permute-done | bytes 655392 | tf_op jit(solution)/shard_map/ppermute | solution.py:19
  36.5 1.5 %collective-permute-start.4 = (bf16[320,1024]{1,0:T(8,128)(2,1)}, bf16[320,1024]{1,0:T(8,128)(2,1)}, u32[]{:S(2)}, u32[]{:S(2)}) collective-permute-start(bf16[320,1024]{1,0:T(8,128)(2,1)} %collective-permute-done.1.refs_4_), channel_id=1, source_target_pairs={{0,2},{1,3},{2,0},{3,1},{4,6},{5,7},{6,4},{7,5},{8,10},{9,11},{10,... | collective-permute-start | bytes 1966088 | tf_op jit(solution)/shard_map/ppermute | solution.py:19
  38.0 2.0 %collective-permute-done.7.first.refs_6_ = bf16[320,1024]{1,0:T(8,128)(2,1)S(1)} collective-permute-done((bf16[320,1024]{1,0:T(8,128)(2,1)}, bf16[320,1024]{1,0:T(8,128)(2,1)S(1)}, u32[]{:S(2)}, u32[]{:S(2)}) %collective-permute-start.7) | collective-permute-done | bytes 655392 | tf_op jit(solution)/shard_map/ppermute | solution.py:19
  40.0 1.5 %collective-permute-start.8 = (bf16[320,1024]{1,0:T(8,128)(2,1)}, bf16[320,1024]{1,0:T(8,128)(2,1)S(1)}, u32[]{:S(2)}, u32[]{:S(2)}) collective-permute-start(bf16[320,1024]{1,0:T(8,128)(2,1)} %collective-permute-done.5.refs_4_), channel_id=1, source_target_pairs={{0,4},{4,0},{8,12},{12,8},{16,20},{20,16},{24,28},{28,24},{1,5},{5... | collective-permute-start | bytes 1966088 | tf_op jit(solution)/shard_map/ppermute | solution.py:19
  41.5 1.1 shard_map.59
  43.4 8.1 %collective-permute-done.4.refs_5_ = bf16[320,1024]{1,0:T(8,128)(2,1)} collective-permute-done((bf16[320,1024]{1,0:T(8,128)(2,1)}, bf16[320,1024]{1,0:T(8,128)(2,1)}, u32[]{:S(2)}, u32[]{:S(2)}) %collective-permute-start.4) | collective-permute-done | bytes 655392 | tf_op jit(solution)/shard_map/ppermute | solution.py:19
  51.5 3.4 %collective-permute-done.8.second.refs_6_ = bf16[320,1024]{1,0:T(8,128)(2,1)S(1)} collective-permute-done((bf16[320,1024]{1,0:T(8,128)(2,1)}, bf16[320,1024]{1,0:T(8,128)(2,1)S(1)}, u32[]{:S(2)}, u32[]{:S(2)}) %collective-permute-start.8) | collective-permute-done | bytes 655392 | tf_op jit(solution)/shard_map/ppermute | solution.py:19
  54.8 1.5 %collective-permute-start.9 = (bf16[320,1024]{1,0:T(8,128)(2,1)}, bf16[320,1024]{1,0:T(8,128)(2,1)}, u32[]{:S(2)}, u32[]{:S(2)}) collective-permute-start(bf16[320,1024]{1,0:T(8,128)(2,1)} %collective-permute-done.4.refs_5_), channel_id=1, source_target_pairs={{0,4},{4,0},{8,12},{12,8},{16,20},{20,16},{24,28},{28,24},{1,5},{5... | collective-permute-start | bytes 1966088 | tf_op jit(solution)/shard_map/ppermute | solution.py:19
  56.3 2.2 %collective-permute-done.10.first.second = bf16[320,1024]{1,0:T(8,128)(2,1)S(1)} collective-permute-done((bf16[320,1024]{1,0:T(8,128)(2,1)}, bf16[320,1024]{1,0:T(8,128)(2,1)S(1)}, u32[]{:S(2)}, u32[]{:S(2)}) %collective-permute-start.10) | collective-permute-done | bytes 655392 | tf_op jit(solution)/shard_map/ppermute | solution.py:19
  58.6 1.1 shard_map.60.refs_7_
  60.2 1.1 shard_map.67
  62.0 1.1 collective-permute-done.12
  63.5 1.1 copy-done.19
  64.6 7.6 %shard_map.61 = (f32[640,1920]{1,0:T(8,128)S(1)}, bf16[1920,1024]{1,0:T(8,128)(2,1)S(1)}, f32[8,640]{1,0:T(8,128)S(1)}) custom-call(bf16[320,1024]{1,0:T(8,128)(2,1)} %refs_2_.3, bf16[320,1024]{1,0:T(8,128)(2,1)} %collective-permute-done.refs_1_, bf16[320,1024]{1,0:T(8,128)(2,1)} %refs_0_.7, bf16[320,1024]{1,0:T(8,128)(2,1)S(1)} %copy-done.19, ...), custom_call_target="tpu_custom_call" | custom-call | flops 2516582400 | bytes 10158080 | tf_op jit(solution)/shard_map/pallas_call | solution.py:133
  72.2 2.2 %copy-done = f32[640,1920]{1,0:T(8,128)} copy-done((f32[640,1920]{1,0:T(8,128)}, f32[640,1920]{1,0:T(8,128)S(1)}, u32[]{:S(2)}) %copy-start) | copy-done | bytes 4915224
  74.4 1.3 shard_map.68.refs_5_
  75.7 2.6 %collective-permute-start.25 = (bf16[320,1024]{1,0:T(8,128)(2,1)}, bf16[320,1024]{1,0:T(8,128)(2,1)}, u32[]{:S(2)}, u32[]{:S(2)}) collective-permute-start(bf16[320,1024]{1,0:T(8,128)(2,1)} %shard_map.68.refs_5_), channel_id=1, source_target_pairs={{0,4},{4,0},{8,12},{12,8},{16,20},{20,16},{24,28},{28,24},{1,5},{5... | collective-permute-start | bytes 1966088 | tf_op jit(solution)/shard_map/ppermute | solution.py:19
  78.3 1.1 shard_map.69.refs_7_
  79.4 1.2 collective-permute-start.26
  80.6 3.5 %shard_map.62 = (f32[640,640]{1,0:T(8,128)S(1)}, bf16[640,1024]{1,0:T(8,128)(2,1)S(1)}, f32[8,640]{1,0:T(8,128)S(1)}) custom-call(bf16[320,1024]{1,0:T(8,128)(2,1)} %refs_2_.3, bf16[320,1024]{1,0:T(8,128)(2,1)} %collective-permute-done.refs_1_, bf16[320,1024]{1,0:T(8,128)(2,1)} %collective-permute-done.9.refs_2_, ...), custom_call_target="tpu_custom_call" | custom-call | flops 838860800 | bytes 4259840 | tf_op jit(solution)/shard_map/pallas_call | solution.py:133
  84.2 0.9 collective-permute-start.13
  85.1 11.7 %collective-permute-done.13.across = f32[8,640]{1,0:T(8,128)S(1)} collective-permute-done((f32[8,640]{1,0:T(8,128)S(1)}, f32[8,640]{1,0:T(8,128)S(1)}, u32[]{:S(2)}, u32[]{:S(2)}) %collective-permute-start.13) | collective-permute-done | bytes 20512 | tf_op jit(solution)/shard_map/ppermute | solution.py:19
  96.9 3.1 %collective-permute-done.15.corner = f32[8,640]{1,0:T(8,128)S(1)} collective-permute-done((f32[8,640]{1,0:T(8,128)S(1)}, f32[8,640]{1,0:T(8,128)S(1)}, u32[]{:S(2)}, u32[]{:S(2)}) %collective-permute-start.15) | collective-permute-done | bytes 20512 | tf_op jit(solution)/shard_map/ppermute | solution.py:19
  100.3 2.2 %collective-permute-start.18 = (f32[24,320]{1,0:T(8,128)S(1)}, f32[24,320]{1,0:T(8,128)S(1)}, u32[]{:S(2)}, u32[]{:S(2)}) collective-permute-start(f32[24,320]{1,0:T(8,128)S(1)} %shard_map.63.refs_0_), channel_id=1, source_target_pairs={{0,20},{4,24},{8,28},{12,0},{16,4},{20,8},{24,12},{28,16},{1,21},{... | collective-permute-start | bytes 92168 | tf_op jit(solution)/shard_map/ppermute | solution.py:19
  102.5 2.0 %collective-permute-done.16.refs_1_ = f32[24,320]{1,0:T(8,128)S(1)} collective-permute-done((f32[24,320]{1,0:T(8,128)S(1)}, f32[24,320]{1,0:T(8,128)S(1)}, u32[]{:S(2)}, u32[]{:S(2)}) %collective-permute-start.16) | collective-permute-done | bytes 30752 | tf_op jit(solution)/shard_map/ppermute | solution.py:19
  104.5 0.9 collective-permute-start.19
  105.4 1.1 collective-permute-start.20
  106.5 2.9 %collective-permute-start.21 = (f32[24,320]{1,0:T(8,128)S(1)}, f32[24,320]{1,0:T(8,128)S(1)}, u32[]{:S(2)}, u32[]{:S(2)}) collective-permute-start(f32[24,320]{1,0:T(8,128)S(1)} %shard_map.63.refs_0_), channel_id=1, source_target_pairs={{0,12},{4,16},{8,20},{12,24},{16,28},{20,0},{24,4},{28,8},{1,13},{... | collective-permute-start | bytes 92168 | tf_op jit(solution)/shard_map/ppermute | solution.py:19
  109.4 1.1 copy-done.14
  110.5 1.1 copy-done.16
  111.6 6.0 %shard_map.70 = (f32[640,1920]{1,0:T(8,128)S(1)}, bf16[1920,1024]{1,0:T(8,128)(2,1)S(1)}) custom-call(bf16[320,1024]{1,0:T(8,128)(2,1)} %refs_0_.7, bf16[320,1024]{1,0:T(8,128)(2,1)} %collective-permute-done.23.refs_1_, bf16[320,1024]{1,0:T(8,128)(2,1)} %refs_2_.3, bf16[320,1024]{1,0:T(8,128)(2,1)S(1)} %copy-done.14, ...), custom_call_target="tpu_custom_call" | custom-call | flops 2516582400 | bytes 10158080 | tf_op jit(solution)/shard_map/pallas_call | solution.py:133
  118.3 3.6 %shard_map.65 = f32[320,1024]{1,0:T(8,128)} custom-call(f32[640,1920]{1,0:T(8,128)S(1)} %bitcast.2, f32[640,640]{1,0:T(8,128)S(1)} %get-tuple-element.39.refs_1_, bf16[1920,1024]{1,0:T(8,128)(2,1)S(1)} %copy-done.5, bf16[640,1024]{1,0:T(8,128)(2,1)S(1)} %get-tuple-element.41.refs_3_, f32[8,640]{1,0:T(8,128)S(1)} %get-tuple-element.42.refs_4_.refs_5_, ...), custom_call_target="tpu_custom_call" | custom-call | flops 1677721600 | bytes 9830400 | tf_op jit(solution)/shard_map/pallas_call | solution.py:266
  121.9 2.9 %shard_map.71 = (f32[640,640]{1,0:T(8,128)S(1)}, bf16[640,1024]{1,0:T(8,128)(2,1)S(1)}) custom-call(bf16[320,1024]{1,0:T(8,128)(2,1)} %refs_0_.7, bf16[320,1024]{1,0:T(8,128)(2,1)} %collective-permute-done.23.refs_1_, bf16[320,1024]{1,0:T(8,128)(2,1)} %collective-permute-done.25.refs_2_, bf16[320,1024]{1,0:T(8,128)(2,1)} %collective-permute-done.26.refs_3_), custom_call_target="tpu_custom_call" | custom-call | flops 838860800 | bytes 4259840 | tf_op jit(solution)/shard_map/pallas_call | solution.py:133
  124.8 3.6 %shard_map.72 = f32[320,1024]{1,0:T(8,128)} custom-call(f32[640,1920]{1,0:T(8,128)S(1)} %get-tuple-element.45.refs_0_, f32[640,640]{1,0:T(8,128)S(1)} %get-tuple-element.48.refs_1_, bf16[1920,1024]{1,0:T(8,128)(2,1)S(1)} %get-tuple-element.49.refs_2_, bf16[640,1024]{1,0:T(8,128)(2,1)S(1)} %get-tuple-element.50.refs_3_, ...), custom_call_target="tpu_custom_call" | custom-call | flops 1677721600 | bytes 9830400 | tf_op jit(solution)/shard_map/pallas_call | solution.py:266
  129.6 2.4 %copy-done.1 = f32[640,1920]{1,0:T(8,128)S(1)} copy-done((f32[640,1920]{1,0:T(8,128)S(1)}, f32[640,1920]{1,0:T(8,128)}, u32[]{:S(2)}) %copy-start.1) | copy-done | bytes 4915224
  131.9 2.1 %copy-done.6 = bf16[1920,1024]{1,0:T(8,128)(2,1)S(1)} copy-done((bf16[1920,1024]{1,0:T(8,128)(2,1)S(1)}, bf16[1920,1024]{1,0:T(8,128)(2,1)}, u32[]{:S(2)}) %copy-start.6) | copy-done | bytes 3932184
  134.1 1.3 copy-done.10
  135.4 5.1 %shard_map.66 = f32[320,1024]{1,0:T(8,128)} custom-call(f32[640,1920]{1,0:T(8,128)S(1)} %copy-done.1, f32[640,640]{1,0:T(8,128)S(1)} %get-tuple-element.39.refs_1_, bf16[1920,1024]{1,0:T(8,128)(2,1)S(1)} %copy-done.6, bf16[640,1024]{1,0:T(8,128)(2,1)S(1)} %copy-done.10, f32[8,640]{1,0:T(8,128)S(1)} %get-tuple-element.42.refs_4_.refs_5_, ...), custom_call_target="tpu_custom_call" | custom-call | flops 1677721600 | bytes 9830400 | tf_op jit(solution)/shard_map/pallas_call | solution.py:266
  140.5 4.9 %shard_map.73 = f32[320,1024]{1,0:T(8,128)} custom-call(f32[640,1920]{1,0:T(8,128)S(1)} %copy-done.3, f32[640,640]{1,0:T(8,128)S(1)} %get-tuple-element.48.refs_1_, bf16[1920,1024]{1,0:T(8,128)(2,1)S(1)} %copy-done.8, bf16[640,1024]{1,0:T(8,128)(2,1)S(1)} %copy-done.12, f32[8,640]{1,0:T(8,128)S(1)} %get-tuple-element.43.refs_5_.refs_4_, ...), custom_call_target="tpu_custom_call" | custom-call | flops 1677721600 | bytes 9830400 | tf_op jit(solution)/shard_map/pallas_call | solution.py:266
  (78 shorter events, 4.4 us)
Async XLA Ops:
  0.6 21.8 %collective-permute-start.1 = (bf16[320,1024]{1,0:T(8,128)(2,1)}, bf16[320,1024]{1,0:T(8,128)(2,1)}, u32[]{:S(2)}, u32[]{:S(2)}) collective-permute-start(bf16[320,1024]{1,0:T(8,128)(2,1)} %refs_0_.7), channel_id=1, source_target_pairs={{0,8},{4,12},{8,16},{12,20},{16,24},{20,28},{24,0},{28,4},{1,9},{5... | collective-permute-start | bytes 1966088 | tf_op jit(solution)/shard_map/ppermute | solution.py:19
  3.7 16.4 %collective-permute-start.2 = (bf16[320,1024]{1,0:T(8,128)(2,1)}, bf16[320,1024]{1,0:T(8,128)(2,1)S(1)}, u32[]{:S(2)}, u32[]{:S(2)}) collective-permute-start(bf16[320,1024]{1,0:T(8,128)(2,1)} %refs_0_.7), channel_id=1, source_target_pairs={{0,2},{1,3},{2,0},{3,1},{4,6},{5,7},{6,4},{7,5},{8,10},{9,11},{10,... | collective-permute-start | bytes 1966088 | tf_op jit(solution)/shard_map/ppermute | solution.py:19
  6.3 36.4 %copy-start.17 = (s32[1,320]{1,0:T(1,128)S(1)}, s32[1,320]{1,0:T(1,128)}, u32[]{:S(2)}) copy-start(s32[1,320]{1,0:T(1,128)} %partner.1) | copy-start | bytes 3844
  6.3 18.5 %collective-permute-start.6 = (bf16[320,1024]{1,0:T(8,128)(2,1)S(1)}, bf16[320,1024]{1,0:T(8,128)(2,1)S(1)}, u32[]{:S(2)}, u32[]{:S(2)}) collective-permute-start(bf16[320,1024]{1,0:T(8,128)(2,1)S(1)} %shard_map.58), channel_id=1, source_target_pairs={{0,4},{4,0},{8,12},{12,8},{16,20},{20,16},{24,28},{28,24},{1,5},{5... | collective-permute-start | bytes 1966088 | tf_op jit(solution)/shard_map/ppermute | solution.py:19
  20.9 15.6 %collective-permute-start.3 = (bf16[320,1024]{1,0:T(8,128)(2,1)}, bf16[320,1024]{1,0:T(8,128)(2,1)S(1)}, u32[]{:S(2)}, u32[]{:S(2)}) collective-permute-start(bf16[320,1024]{1,0:T(8,128)(2,1)} %refs_2_.3), channel_id=1, source_target_pairs={{0,2},{1,3},{2,0},{3,1},{4,6},{5,7},{6,4},{7,5},{8,10},{9,11},{10,... | collective-permute-start | bytes 1966088 | tf_op jit(solution)/shard_map/ppermute | solution.py:19
  22.4 15.6 %collective-permute-start.5 = (bf16[320,1024]{1,0:T(8,128)(2,1)}, bf16[320,1024]{1,0:T(8,128)(2,1)}, u32[]{:S(2)}, u32[]{:S(2)}) collective-permute-start(bf16[320,1024]{1,0:T(8,128)(2,1)} %refs_2_.3), channel_id=1, source_target_pairs={{0,24},{4,28},{8,0},{12,4},{16,8},{20,12},{24,16},{28,20},{1,25},{... | collective-permute-start | bytes 1966088 | tf_op jit(solution)/shard_map/ppermute | solution.py:19
  24.8 15.2 %collective-permute-start.7 = (bf16[320,1024]{1,0:T(8,128)(2,1)}, bf16[320,1024]{1,0:T(8,128)(2,1)S(1)}, u32[]{:S(2)}, u32[]{:S(2)}) collective-permute-start(bf16[320,1024]{1,0:T(8,128)(2,1)} %collective-permute-done.1.refs_4_), channel_id=1, source_target_pairs={{0,4},{4,0},{8,12},{12,8},{16,20},{20,16},{24,28},{28,24},{1,5},{5... | collective-permute-start | bytes 1966088 | tf_op jit(solution)/shard_map/ppermute | solution.py:19
  36.5 23.7 %copy-start.13 = (bf16[320,1024]{1,0:T(8,128)(2,1)}, bf16[320,1024]{1,0:T(8,128)(2,1)S(1)}, u32[]{:S(2)}) copy-start(bf16[320,1024]{1,0:T(8,128)(2,1)S(1)} %collective-permute-done.3.second.first.refs_3_) | copy-start | bytes 1966084
  36.5 14.9 %collective-permute-start.4 = (bf16[320,1024]{1,0:T(8,128)(2,1)}, bf16[320,1024]{1,0:T(8,128)(2,1)}, u32[]{:S(2)}, u32[]{:S(2)}) collective-permute-start(bf16[320,1024]{1,0:T(8,128)(2,1)} %collective-permute-done.1.refs_4_), channel_id=1, source_target_pairs={{0,2},{1,3},{2,0},{3,1},{4,6},{5,7},{6,4},{7,5},{8,10},{9,11},{10,... | collective-permute-start | bytes 1966088 | tf_op jit(solution)/shard_map/ppermute | solution.py:19
  40.0 14.8 %collective-permute-start.8 = (bf16[320,1024]{1,0:T(8,128)(2,1)}, bf16[320,1024]{1,0:T(8,128)(2,1)S(1)}, u32[]{:S(2)}, u32[]{:S(2)}) collective-permute-start(bf16[320,1024]{1,0:T(8,128)(2,1)} %collective-permute-done.5.refs_4_), channel_id=1, source_target_pairs={{0,4},{4,0},{8,12},{12,8},{16,20},{20,16},{24,28},{28,24},{1,5},{5... | collective-permute-start | bytes 1966088 | tf_op jit(solution)/shard_map/ppermute | solution.py:19
  42.6 15.9 %collective-permute-start.10 = (bf16[320,1024]{1,0:T(8,128)(2,1)}, bf16[320,1024]{1,0:T(8,128)(2,1)S(1)}, u32[]{:S(2)}, u32[]{:S(2)}) collective-permute-start(bf16[320,1024]{1,0:T(8,128)(2,1)} %shard_map.59), channel_id=1, source_target_pairs={{0,8},{4,28},{8,16},{12,4},{16,24},{20,12},{24,0},{28,20},{1,9},{5... | collective-permute-start | bytes 1966088 | tf_op jit(solution)/shard_map/ppermute | solution.py:19
  42.7 20.8 %collective-permute-start = (bf16[320,1024]{1,0:T(8,128)(2,1)}, bf16[320,1024]{1,0:T(8,128)(2,1)}, u32[]{:S(2)}, u32[]{:S(2)}) collective-permute-start(bf16[320,1024]{1,0:T(8,128)(2,1)} %refs_2_.3), channel_id=1, source_target_pairs={{0,1},{1,0},{2,3},{3,2},{4,5},{5,4},{6,7},{7,6},{8,9},{9,8},{10,11... | collective-permute-start | bytes 1966088 | tf_op jit(solution)/shard_map/ppermute | solution.py:19
  42.8 19.2 %collective-permute-start.27 = (s32[1,320]{1,0:T(1,128)S(1)}, s32[1,320]{1,0:T(1,128)S(1)}, u32[]{:S(2)}, u32[]{:S(2)}) collective-permute-start(s32[1,320]{1,0:T(1,128)S(1)} %copy-done.17), channel_id=1, source_target_pairs={{0,2},{1,3},{2,0},{3,1},{4,6},{5,7},{6,4},{7,5},{8,10},{9,11},{10,... | collective-permute-start | bytes 3848 | tf_op jit(solution)/shard_map/ppermute | solution.py:19
  54.8 6.5 %copy-start.15 = (bf16[320,1024]{1,0:T(8,128)(2,1)}, bf16[320,1024]{1,0:T(8,128)(2,1)S(1)}, u32[]{:S(2)}) copy-start(bf16[320,1024]{1,0:T(8,128)(2,1)S(1)} %collective-permute-done.8.second.refs_6_) | copy-start | bytes 1966084
  54.8 20.9 %collective-permute-start.9 = (bf16[320,1024]{1,0:T(8,128)(2,1)}, bf16[320,1024]{1,0:T(8,128)(2,1)}, u32[]{:S(2)}, u32[]{:S(2)}) collective-permute-start(bf16[320,1024]{1,0:T(8,128)(2,1)} %collective-permute-done.4.refs_5_), channel_id=1, source_target_pairs={{0,4},{4,0},{8,12},{12,8},{16,20},{20,16},{24,28},{28,24},{1,5},{5... | collective-permute-start | bytes 1966088 | tf_op jit(solution)/shard_map/ppermute | solution.py:19
  59.6 19.8 %collective-permute-start.11 = (bf16[320,1024]{1,0:T(8,128)(2,1)}, bf16[320,1024]{1,0:T(8,128)(2,1)}, u32[]{:S(2)}, u32[]{:S(2)}) collective-permute-start(bf16[320,1024]{1,0:T(8,128)(2,1)} %shard_map.60.refs_7_), channel_id=1, source_target_pairs={{0,2},{1,3},{2,0},{3,1},{4,6},{5,7},{6,4},{7,5},{8,10},{9,11},{10,... | collective-permute-start | bytes 1966088 | tf_op jit(solution)/shard_map/ppermute | solution.py:19
  61.3 13.1 %collective-permute-start.24 = (bf16[320,1024]{1,0:T(8,128)(2,1)}, bf16[320,1024]{1,0:T(8,128)(2,1)S(1)}, u32[]{:S(2)}, u32[]{:S(2)}) collective-permute-start(bf16[320,1024]{1,0:T(8,128)(2,1)} %shard_map.67), channel_id=1, source_target_pairs={{0,24},{4,28},{8,0},{12,4},{16,8},{20,12},{24,16},{28,20},{1,25},{... | collective-permute-start | bytes 1966088 | tf_op jit(solution)/shard_map/ppermute | solution.py:19
  61.9 1.2 collective-permute-start.12
  63.1 37.1 %collective-permute-start.23 = (bf16[320,1024]{1,0:T(8,128)(2,1)}, bf16[320,1024]{1,0:T(8,128)(2,1)}, u32[]{:S(2)}, u32[]{:S(2)}) collective-permute-start(bf16[320,1024]{1,0:T(8,128)(2,1)} %refs_0_.7), channel_id=1, source_target_pairs={{0,1},{1,0},{2,3},{3,2},{4,5},{5,4},{6,7},{7,6},{8,9},{9,8},{10,11... | collective-permute-start | bytes 1966088 | tf_op jit(solution)/shard_map/ppermute | solution.py:19
  63.5 1.1 copy-start.19
  72.2 2.2 %copy-start = (f32[640,1920]{1,0:T(8,128)}, f32[640,1920]{1,0:T(8,128)S(1)}, u32[]{:S(2)}) copy-start(f32[640,1920]{1,0:T(8,128)S(1)} %get-tuple-element.38.refs_0_) | copy-start | bytes 14745604
  74.4 5.0 %copy-start.4 = (bf16[1920,1024]{1,0:T(8,128)(2,1)}, bf16[1920,1024]{1,0:T(8,128)(2,1)S(1)}, u32[]{:S(2)}) copy-start(bf16[1920,1024]{1,0:T(8,128)(2,1)S(1)} %get-tuple-element.40.refs_2_) | copy-start | bytes 11796484
  75.7 46.2 %collective-permute-start.25 = (bf16[320,1024]{1,0:T(8,128)(2,1)}, bf16[320,1024]{1,0:T(8,128)(2,1)}, u32[]{:S(2)}, u32[]{:S(2)}) collective-permute-start(bf16[320,1024]{1,0:T(8,128)(2,1)} %shard_map.68.refs_5_), channel_id=1, source_target_pairs={{0,4},{4,0},{8,12},{12,8},{16,20},{20,16},{24,28},{28,24},{1,5},{5... | collective-permute-start | bytes 1966088 | tf_op jit(solution)/shard_map/ppermute | solution.py:19
  79.4 42.5 %collective-permute-start.26 = (bf16[320,1024]{1,0:T(8,128)(2,1)}, bf16[320,1024]{1,0:T(8,128)(2,1)}, u32[]{:S(2)}, u32[]{:S(2)}) collective-permute-start(bf16[320,1024]{1,0:T(8,128)(2,1)} %shard_map.69.refs_7_), channel_id=1, source_target_pairs={{0,2},{1,3},{2,0},{3,1},{4,6},{5,7},{6,4},{7,5},{8,10},{9,11},{10,... | collective-permute-start | bytes 1966088 | tf_op jit(solution)/shard_map/ppermute | solution.py:19
  84.2 34.0 %copy-start.9 = (bf16[640,1024]{1,0:T(8,128)(2,1)}, bf16[640,1024]{1,0:T(8,128)(2,1)S(1)}, u32[]{:S(2)}) copy-start(bf16[640,1024]{1,0:T(8,128)(2,1)S(1)} %get-tuple-element.41.refs_3_) | copy-start | bytes 3932164
  84.2 12.6 %collective-permute-start.13 = (f32[8,640]{1,0:T(8,128)S(1)}, f32[8,640]{1,0:T(8,128)S(1)}, u32[]{:S(2)}, u32[]{:S(2)}) collective-permute-start(f32[8,640]{1,0:T(8,128)S(1)} %get-tuple-element.36.own), channel_id=1, source_target_pairs={{0,2},{1,3},{2,0},{3,1},{4,6},{5,7},{6,4},{7,5},{8,10},{9,11},{10,... | collective-permute-start | bytes 61448 | tf_op jit(solution)/shard_map/ppermute | solution.py:19
  85.1 11.8 %collective-permute-start.14 = (f32[8,640]{1,0:T(8,128)S(1)}, f32[8,640]{1,0:T(8,128)S(1)}, u32[]{:S(2)}, u32[]{:S(2)}) collective-permute-start(f32[8,640]{1,0:T(8,128)S(1)} %get-tuple-element.36.own), channel_id=1, source_target_pairs={{0,1},{1,0},{2,3},{3,2},{4,5},{5,4},{6,7},{7,6},{8,9},{9,8},{10,11... | collective-permute-start | bytes 61448 | tf_op jit(solution)/shard_map/ppermute | solution.py:19
  96.8 3.2 %collective-permute-start.15 = (f32[8,640]{1,0:T(8,128)S(1)}, f32[8,640]{1,0:T(8,128)S(1)}, u32[]{:S(2)}, u32[]{:S(2)}) collective-permute-start(f32[8,640]{1,0:T(8,128)S(1)} %get-tuple-element.36.own), channel_id=1, source_target_pairs={{0,3},{1,2},{2,1},{3,0},{4,7},{5,6},{6,5},{7,4},{8,11},{9,10},{10,... | collective-permute-start | bytes 61448 | tf_op jit(solution)/shard_map/ppermute | solution.py:19
  100.1 4.4 %collective-permute-start.16 = (f32[24,320]{1,0:T(8,128)S(1)}, f32[24,320]{1,0:T(8,128)S(1)}, u32[]{:S(2)}, u32[]{:S(2)}) collective-permute-start(f32[24,320]{1,0:T(8,128)S(1)} %shard_map.63.refs_0_), channel_id=1, source_target_pairs={{0,28},{4,0},{8,4},{12,8},{16,12},{20,16},{24,20},{28,24},{1,29},{... | collective-permute-start | bytes 92168 | tf_op jit(solution)/shard_map/ppermute | solution.py:19
  100.2 5.2 %collective-permute-start.17 = (f32[24,320]{1,0:T(8,128)S(1)}, f32[24,320]{1,0:T(8,128)S(1)}, u32[]{:S(2)}, u32[]{:S(2)}) collective-permute-start(f32[24,320]{1,0:T(8,128)S(1)} %shard_map.63.refs_0_), channel_id=1, source_target_pairs={{0,24},{4,28},{8,0},{12,4},{16,8},{20,12},{24,16},{28,20},{1,25},{... | collective-permute-start | bytes 92168 | tf_op jit(solution)/shard_map/ppermute | solution.py:19
  100.3 6.2 %collective-permute-start.18 = (f32[24,320]{1,0:T(8,128)S(1)}, f32[24,320]{1,0:T(8,128)S(1)}, u32[]{:S(2)}, u32[]{:S(2)}) collective-permute-start(f32[24,320]{1,0:T(8,128)S(1)} %shard_map.63.refs_0_), channel_id=1, source_target_pairs={{0,20},{4,24},{8,28},{12,0},{16,4},{20,8},{24,12},{28,16},{1,21},{... | collective-permute-start | bytes 92168 | tf_op jit(solution)/shard_map/ppermute | solution.py:19
  102.5 15.7 %slice-start = ((s8[4915200]{0:T(1024)(128)(4,1)}), s8[4194304]{0:T(1024)(128)(4,1)S(1)}, s32[]{:S(2)}) async-start(s8[4915200]{0:T(1024)(128)(4,1)} %bitcast.1), calls=%async_computation | async-start | bytes 8388608
  102.5 15.7 %slice-start.1 = ((s8[4915200]{0:T(1024)(128)(4,1)}), s8[720896]{0:T(1024)(128)(4,1)S(1)}, s32[]{:S(2)}) async-start(s8[4915200]{0:T(1024)(128)(4,1)} %bitcast.1), calls=%async_computation.1 | async-start | bytes 1441792
  104.5 13.1 %collective-permute-start.19 = (f32[24,320]{1,0:T(8,128)S(1)}, f32[24,320]{1,0:T(8,128)S(1)}, u32[]{:S(2)}, u32[]{:S(2)}) collective-permute-start(f32[24,320]{1,0:T(8,128)S(1)} %shard_map.63.refs_0_), channel_id=1, source_target_pairs={{0,4},{4,8},{8,12},{12,16},{16,20},{20,24},{24,28},{28,0},{1,5},{5... | collective-permute-start | bytes 92168 | tf_op jit(solution)/shard_map/ppermute | solution.py:19
  105.4 12.3 %collective-permute-start.20 = (f32[24,320]{1,0:T(8,128)S(1)}, f32[24,320]{1,0:T(8,128)S(1)}, u32[]{:S(2)}, u32[]{:S(2)}) collective-permute-start(f32[24,320]{1,0:T(8,128)S(1)} %shard_map.63.refs_0_), channel_id=1, source_target_pairs={{0,8},{4,12},{8,16},{12,20},{16,24},{20,28},{24,0},{28,4},{1,9},{5... | collective-permute-start | bytes 92168 | tf_op jit(solution)/shard_map/ppermute | solution.py:19
  106.5 11.2 %collective-permute-start.21 = (f32[24,320]{1,0:T(8,128)S(1)}, f32[24,320]{1,0:T(8,128)S(1)}, u32[]{:S(2)}, u32[]{:S(2)}) collective-permute-start(f32[24,320]{1,0:T(8,128)S(1)} %shard_map.63.refs_0_), channel_id=1, source_target_pairs={{0,12},{4,16},{8,20},{12,24},{16,28},{20,0},{24,4},{28,8},{1,13},{... | collective-permute-start | bytes 92168 | tf_op jit(solution)/shard_map/ppermute | solution.py:19
  111.6 6.6 %copy-start.5 = (bf16[1920,1024]{1,0:T(8,128)(2,1)S(1)}, bf16[1920,1024]{1,0:T(8,128)(2,1)}, u32[]{:S(2)}) copy-start(bf16[1920,1024]{1,0:T(8,128)(2,1)} %copy-done.4) | copy-start | bytes 11796484
  117.6 7.2 %copy-start.2 = (f32[640,1920]{1,0:T(8,128)}, f32[640,1920]{1,0:T(8,128)S(1)}, u32[]{:S(2)}) copy-start(f32[640,1920]{1,0:T(8,128)S(1)} %get-tuple-element.45.refs_0_) | copy-start | bytes 14745604
  117.6 7.2 %copy-start.7 = (bf16[1920,1024]{1,0:T(8,128)(2,1)}, bf16[1920,1024]{1,0:T(8,128)(2,1)S(1)}, u32[]{:S(2)}) copy-start(bf16[1920,1024]{1,0:T(8,128)(2,1)S(1)} %get-tuple-element.49.refs_2_) | copy-start | bytes 11796484
  121.9 7.7 %collective-permute-start.22 = (f32[320,1024]{1,0:T(8,128)}, f32[320,1024]{1,0:T(8,128)}, u32[]{:S(2)}, u32[]{:S(2)}) collective-permute-start(f32[320,1024]{1,0:T(8,128)} %shard_map.65), channel_id=1, source_target_pairs={{0,1},{1,0},{2,3},{3,2},{4,5},{5,4},{6,7},{7,6},{8,9},{9,8},{10,11... | collective-permute-start | bytes 3932168 | tf_op jit(solution)/shard_map/ppermute | solution.py:19
  124.8 3.6 %copy-start.11 = (bf16[640,1024]{1,0:T(8,128)(2,1)}, bf16[640,1024]{1,0:T(8,128)(2,1)S(1)}, u32[]{:S(2)}) copy-start(bf16[640,1024]{1,0:T(8,128)(2,1)S(1)} %get-tuple-element.50.refs_3_) | copy-start | bytes 3932164
  128.4 12.0 %collective-permute-start.28 = (f32[320,1024]{1,0:T(8,128)}, f32[320,1024]{1,0:T(8,128)}, u32[]{:S(2)}, u32[]{:S(2)}) collective-permute-start(f32[320,1024]{1,0:T(8,128)} %shard_map.72), channel_id=1, source_target_pairs={{0,1},{1,0},{2,3},{3,2},{4,5},{5,4},{6,7},{7,6},{8,9},{9,8},{10,11... | collective-permute-start | bytes 3932168 | tf_op jit(solution)/shard_map/ppermute | solution.py:19
  129.6 2.4 %copy-start.1 = (f32[640,1920]{1,0:T(8,128)S(1)}, f32[640,1920]{1,0:T(8,128)}, u32[]{:S(2)}) copy-start(f32[640,1920]{1,0:T(8,128)} %copy-done) | copy-start | bytes 14745604
  131.9 2.1 %copy-start.6 = (bf16[1920,1024]{1,0:T(8,128)(2,1)S(1)}, bf16[1920,1024]{1,0:T(8,128)(2,1)}, u32[]{:S(2)}) copy-start(bf16[1920,1024]{1,0:T(8,128)(2,1)} %copy-done.4) | copy-start | bytes 11796484
  134.1 1.3 copy-start.10
  135.4 5.1 %copy-start.3 = (f32[640,1920]{1,0:T(8,128)S(1)}, f32[640,1920]{1,0:T(8,128)}, u32[]{:S(2)}) copy-start(f32[640,1920]{1,0:T(8,128)} %copy-done.2) | copy-start | bytes 14745604
  135.4 5.1 %copy-start.8 = (bf16[1920,1024]{1,0:T(8,128)(2,1)S(1)}, bf16[1920,1024]{1,0:T(8,128)(2,1)}, u32[]{:S(2)}) copy-start(bf16[1920,1024]{1,0:T(8,128)(2,1)} %copy-done.7) | copy-start | bytes 11796484
  135.4 5.1 %copy-start.12 = (bf16[640,1024]{1,0:T(8,128)(2,1)S(1)}, bf16[640,1024]{1,0:T(8,128)(2,1)}, u32[]{:S(2)}) copy-start(bf16[640,1024]{1,0:T(8,128)(2,1)} %copy-done.11) | copy-start | bytes 3932164
  (3 other events, 3.0 us)

commit v4 on v3

v4 whole, which is shorter than its diff:
```python
import functools

import jax
import jax.numpy as jnp
from jax import lax
from jax.experimental import pallas as pl
from jax.experimental.pallas import tpu as pltpu
from jax.sharding import PartitionSpec as P

F32 = jnp.float32
BLOCK_AXIS, PART_AXIS = "blk", "pb"
CUTS = (96, 192)
VMEM_LIMIT = 16 * 1024 * 1024
ANYWHERE = pl.BlockSpec(memory_space=pl.ANY)
WHOLE = pl.BlockSpec(memory_space=pltpu.VMEM)
SCALAR = pl.BlockSpec(memory_space=pltpu.SMEM)
NT = (((1,), (1,)), ((), ()))


def shift(array, axis, move):
    peers = lax.axis_size(axis)
    return lax.ppermute(array, axis, [(i, move(i) % peers) for i in range(peers)])


def as_column(row):
    return jnp.broadcast_to(row, (128, row.shape[1])).T[:, 0:1]


def as_row(column):
    return jnp.broadcast_to(column, (column.shape[0], 128)).T[0:1, :]


def log_join(*parts):
    top = functools.reduce(jnp.maximum, parts)
    return top + jnp.log(sum(jnp.exp(part - top) for part in parts))


def flat(entries):
    return [array for entry in entries for array in (entry if isinstance(entry, tuple) else (entry,))]


def like(entries, refs):
    refs = list(refs)
    return [tuple(refs.pop(0) for _ in entry) if isinstance(entry, tuple) else refs.pop(0) for entry in entries]


def fetch(flag, sources, target, sems):
    copies, row = [], 0
    for i, source in enumerate(sources):
        both = source if isinstance(source, tuple) else (source,)
        rows = both[0].shape[0]
        here = [pltpu.make_async_copy(one, target.at[pl.ds(row, rows)], sems.at[i]) for one in both]
        if len(here) == 1:
            here[0].start()
        else:
            pl.when(flag[0] == 1)(here[0].start)
            pl.when(flag[0] != 1)(here[1].start)
        copies.append(here[0])
        row += rows
    return copies


def choose_kernel(flag, first, second, out, sem):
    @pl.when(flag[0] == 1)
    def _():
        pltpu.make_async_copy(first, out, sem).start()

    @pl.when(flag[0] != 1)
    def _():
        pltpu.make_async_copy(second, out, sem).start()

    pltpu.make_async_copy(first, out, sem).wait()


def choose(flag, first, second):
    return pl.pallas_call(
        choose_kernel,
        out_shape=jax.ShapeDtypeStruct(first.shape, first.dtype),
        in_specs=[SCALAR, ANYWHERE, ANYWHERE],
        out_specs=WHOLE,
        scratch_shapes=[pltpu.SemaphoreType.DMA],
        compiler_params=pltpu.CompilerParams(vmem_limit_bytes=VMEM_LIMIT),
        cost_estimate=pl.CostEstimate(flops=0, bytes_accessed=2 * first.size * 2, transcendentals=0),
    )(flag, first, second)


def after(value, *landed):
    return lax.optimization_barrier((value, landed))[0]


def kept(shape, dtype):
    return pltpu.VMEM(shape, dtype)


def in_vmem(array):
    return pltpu.with_memory_space_constraint(array, pltpu.VMEM)


def ids(scalars, which, rows):
    return scalars[which] + lax.broadcasted_iota(jnp.int32, (1, rows), 1)


def side_by_side(first, second):
    return jnp.concatenate([first, second], axis=1)


def score_kernel(form, pairs, early, stats, factor, scalars, *refs):
    mine = refs[:2]
    count = len(flat(form))
    shards = like(form, refs[2 : 2 + count])
    rest = list(refs[2 + count :])
    if stats:
        side = [rest.pop(0) for _ in range(2 if early else 1)]
    out, right = rest.pop(0), rest.pop(0)
    if stats:
        info = rest.pop(0)
    left, sems = rest
    copies = fetch(scalars, mine, left, sems) + fetch(scalars, shards, right, sems.at[pl.ds(2, len(form))])
    for copy in copies[:2]:
        copy.wait()
    rows = mine[0].shape[0]
    pair = 2 * rows
    per_pair = len(form) // pairs
    lhs = left[...]
    row_parts = []
    for p in range(pairs):
        for copy in copies[2 + p * per_pair : 2 + (p + 1) * per_pair]:
            copy.wait()
        s = lax.dot_general(
            lhs, right[pl.ds(p * pair, pair), :], NT, preferred_element_type=F32
        ) * factor
        out[:, pl.ds(p * pair, pair)] = s
        if stats:
            col_max = jnp.max(s, axis=0, keepdims=True)
            col = col_max + jnp.log(jnp.sum(jnp.exp(s - col_max), axis=0, keepdims=True))
            row_max = jnp.max(s, axis=1, keepdims=True)
            row_sum = jnp.sum(jnp.exp(s - row_max), axis=1, keepdims=True)
            row_parts.append(row_max + jnp.log(row_sum))
            info[pl.ds(p if early else 3, 1), :] = col
            if early and p == 0:
                chosen = as_column(side_by_side(side[0][...], side[1][...]))
                hit = chosen == side_by_side(ids(scalars, 1, rows), ids(scalars, 2, rows))
                info[pl.ds(5, 1), :] = as_row(jnp.sum(jnp.where(hit, s, 0.0), axis=1, keepdims=True))
    if stats:
        row = as_row(log_join(*row_parts) if len(row_parts) > 1 else row_parts[0])
        if early:
            info[pl.ds(3, 1), :] = jnp.zeros((1, pair), F32)
            info[pl.ds(4, 1), :] = row
            info[pl.ds(6, 2), :] = jnp.zeros((2, pair), F32)
        else:
            info[pl.ds(0, 3), :] = side[0][pl.ds(0, 3), :]
            info[pl.ds(4, 1), :] = log_join(row, side[0][pl.ds(4, 1), :])
            info[pl.ds(5, 3), :] = side[0][pl.ds(5, 3), :]


def score(scalars, mine, shards, pairs, early, stats, factor, side=()):
    rows, width = mine[0].shape
    tokens = 2 * pairs
    shapes = [kept((2 * rows, tokens * rows), F32), kept((tokens * rows, width), jnp.bfloat16)]
    if stats:
        shapes.append(jax.ShapeDtypeStruct((8, 2 * rows), F32))
    arrays = flat(shards)
    return pl.pallas_call(
        functools.partial(score_kernel, shards, pairs, early, stats, factor),
        out_shape=tuple(shapes),
        in_specs=[SCALAR] + [ANYWHERE] * (2 + len(arrays)) + [WHOLE] * len(side),
        out_specs=(WHOLE,) * len(shapes),
        scratch_shapes=[
            pltpu.VMEM((2 * rows, width), jnp.bfloat16),
            pltpu.SemaphoreType.DMA((2 + len(shards),)),
        ],
        compiler_params=pltpu.CompilerParams(vmem_limit_bytes=VMEM_LIMIT),
        cost_estimate=pl.CostEstimate(
            flops=4 * rows * rows * tokens * width,
            bytes_accessed=(tokens + 2) * rows * width * 2 + 8 * rows * rows * tokens,
            transcendentals=4 * rows * rows * tokens if stats else 0,
        ),
    )(scalars, *mine, *arrays, *side)


def halves(ref, row):
    n = ref.shape[1] // 2
    both = ref[pl.ds(row, 1), :]
    return both[:, :n], both[:, n:]


def by_shard(ref):
    a, b, early, late = (halves(ref, i) for i in range(4))
    return [a[0], a[1], b[0], b[1], early[0], late[0], early[1], late[1]]


def block_kernel(own, across, core, corner, out):
    for base, near, far in ((0, own, across), (8, core, corner)):
        near, far = by_shard(near), by_shard(far)
        for i in range(8):
            out[pl.ds(base + i, 1), :] = log_join(near[i], far[i ^ 1])
    own_row, core_row = halves(own, 4), halves(core, 4)
    across_row, corner_row = halves(across, 4), halves(corner, 4)
    out[pl.ds(16, 1), :] = log_join(own_row[0], core_row[1])
    out[pl.ds(17, 1), :] = log_join(across_row[0], corner_row[1])
    out[pl.ds(18, 1), :] = log_join(own_row[1], core_row[0])
    out[pl.ds(19, 1), :] = halves(own, 5)[0] + halves(core, 5)[1]
    out[pl.ds(20, 4), :] = jnp.zeros((4, out.shape[1]), F32)


def window_kernel(scalars, partner, own, beside, far, ahead, behind, col_out, row_out, loss_out):
    even = scalars[0] == 1
    size = own.shape[0]

    def pick(first, second):
        return jnp.where(even, first, second)

    def line(d, i):
        one = lambda ref, at=0: ref[pl.ds(at + i, 1), :]
        if d == 0:
            return one(own)
        if d in (2, -2):
            return one(ahead if d == 2 else behind)
        if d == 1:
            return pick(one(beside), one(ahead, size))
        if d == -1:
            return pick(one(behind, size), one(beside))
        if d == 3:
            return pick(one(ahead, size), one(far))
        return pick(one(far), one(behind, size))

    def total(step, base, half):
        parts = []
        for other in range(4):
            d = other - step
            if other % 2 == 0:
                parts.append(line(d, base + other + half))
            else:
                c, e = line(d, base + 4 + half), line(d, base + 6 + half)
                c_first = (other == 1) == (d % 2 == 0)
                parts.append(pick(c, e) if c_first else pick(e, c))
        return log_join(*parts)

    sums = [[total(step, 0, half) for half in range(2)] for step in range(4)]
    core_sums = [total(0, 8, half) for half in range(2)]
    c = [pick(sums[1][h], sums[3][h]) for h in range(2)]
    e = [pick(sums[3][h], sums[1][h]) for h in range(2)]
    col_out[pl.ds(0, 1), :] = side_by_side(*sums[0])
    col_out[pl.ds(1, 1), :] = side_by_side(*sums[2])
    col_out[pl.ds(2, 1), :] = side_by_side(c[0], e[0])
    col_out[pl.ds(3, 1), :] = side_by_side(c[1], e[1])
    col_out[pl.ds(4, 1), :] = side_by_side(sums[0][0], core_sums[0])
    near = [line(1, 16 + h) for h in range(2)]
    third = [line(3, 16 + h) for h in range(2)]
    c = [pick(third[h], near[h]) for h in range(2)]
    e = [pick(near[h], third[h]) for h in range(2)]
    row_out[pl.ds(0, 1), :] = side_by_side(line(0, 16), line(0, 17))
    row_out[pl.ds(1, 1), :] = side_by_side(line(2, 16), line(2, 17))
    row_out[pl.ds(2, 1), :] = side_by_side(c[0], e[0])
    row_out[pl.ds(3, 1), :] = side_by_side(c[1], e[1])
    row_out[pl.ds(4, 1), :] = side_by_side(line(0, 16), line(0, 18))
    zeros = jnp.zeros((3, col_out.shape[1]), F32)
    col_out[pl.ds(5, 3), :] = zeros
    row_out[pl.ds(5, 3), :] = zeros
    chosen = as_column(partner[...])
    found = jnp.zeros(chosen.shape, F32)
    for i, value in enumerate((sums[0][0], sums[0][1], core_sums[0], core_sums[1])):
        hit = chosen == ids(scalars, i + 1, value.shape[1])
        found = found + jnp.sum(jnp.where(hit, value, 0.0), axis=1, keepdims=True)
    loss_out[...] = 0.5 * line(0, 16) + 0.5 * as_row(found) - line(0, 19)


def small_call(kernel, shapes, *args, scalars=0):
    return pl.pallas_call(
        kernel,
        out_shape=tuple(jax.ShapeDtypeStruct(s, F32) for s in shapes),
        in_specs=[SCALAR] * scalars + [WHOLE] * (len(args) - scalars),
        out_specs=(WHOLE,) * len(shapes),
        compiler_params=pltpu.CompilerParams(vmem_limit_bytes=VMEM_LIMIT),
        cost_estimate=pl.CostEstimate(flops=100000, bytes_accessed=400000, transcendentals=20000),
    )(*args)


def grad_kernel(form, keys, factor, scalars, early, held_early, row_info, col_info, first, second, *refs):
    rows = first.shape[1]
    pair = 2 * rows
    refs = list(refs)
    if form is None:
        late, held_late = refs.pop(0), refs.pop(0)
    else:
        lhs_parts = [refs.pop(0), refs.pop(0)]
        shards = like(form, [refs.pop(0) for _ in flat(form)])
    own_out, other_out, weights = refs[:3]
    if form is not None:
        held_late, lhs, sems = refs[3:]
        copies = fetch(scalars, lhs_parts, lhs, sems)
        copies += fetch(scalars, shards, held_late, sems.at[pl.ds(2, len(form))])
    row = as_column(row_info[pl.ds(4, 1), :])
    partners = side_by_side(first[...], second[...])
    across = side_by_side(ids(scalars, 1, rows), ids(scalars, 2, rows))
    if keys:
        row_ids, col_ids = as_column(side_by_side(ids(scalars, 1, rows), ids(scalars, 3, rows))), partners
    else:
        row_ids, col_ids = as_column(partners), across
    for p in range(4):
        if p == 3 and form is not None:
            for copy in copies:
                copy.wait()
        for group in (1, 0):
            here = slice(group * rows, (group + 1) * rows)
            there = pl.ds(group * rows, rows)
            if p < 3:
                s = early[there, pl.ds(p * pair, pair)]
            elif form is None:
                s = late[there, :]
            else:
                s = lax.dot_general(
                    lhs[there, :], held_late[...], NT, preferred_element_type=F32
                ) * factor
            w = 0.5 * jnp.exp(s - row[here]) + 0.5 * jnp.exp(s - col_info[pl.ds(p, 1), :])
            if p == 0:
                w = w - jnp.where(row_ids[here] == col_ids, 1.0, 0.0)
            weights[there, pl.ds(p * pair, pair)] = w.astype(jnp.bfloat16)
    for group, out in ((1, other_out), (0, own_out)):
        there = pl.ds(group * rows, rows)
        total = jnp.dot(weights[there, pl.ds(0, 3 * pair)], held_early[...], preferred_element_type=F32)
        total = total + jnp.dot(weights[there, pl.ds(3 * pair, pair)], held_late[...], preferred_element_type=F32)
        out[...] = total * factor


def grad(scalars, keys, factor, early, held_early, row_info, col_info, first, second, late, form=None):
    rows, width = first.shape[1], held_early.shape[1]
    if form is None:
        late = tuple(map(in_vmem, late))
        late_specs, scratch = [WHOLE] * 2, []
    else:
        late = tuple(late) + tuple(flat(form))
        late_specs = [ANYWHERE] * len(late)
        scratch = [
            pltpu.VMEM((2 * rows, width), jnp.bfloat16),
            pltpu.VMEM((2 * rows, width), jnp.bfloat16),
            pltpu.SemaphoreType.DMA((2 + len(form),)),
        ]
    return pl.pallas_call(
        functools.partial(grad_kernel, form, keys, factor),
        out_shape=(jax.ShapeDtypeStruct((rows, width), F32),) * 2,
        in_specs=[SCALAR] + [WHOLE] * 6 + late_specs,
        out_specs=(WHOLE,) * 2,
        scratch_shapes=[pltpu.VMEM((2 * rows, 8 * rows), jnp.bfloat16)] + scratch,
        compiler_params=pltpu.CompilerParams(vmem_limit_bytes=VMEM_LIMIT),
        cost_estimate=pl.CostEstimate(
            flops=32 * rows * rows * width,
            bytes_accessed=8 * rows * width * 2 + 64 * rows * rows + rows * width * 8,
            transcendentals=32 * rows * rows,
        ),
    )(scalars, in_vmem(early), in_vmem(held_early), row_info, col_info, first, second, *late)


def local(query_rows, key_rows, partner):
    rows, features = query_rows.shape
    factor = float(features) ** (-0.5)
    block = lax.axis_index("blk")
    place = lax.axis_index("pb")
    even = block % 2 == 0
    starts = [(place ^ other) * rows for other in (0, 2, 1, 3)]
    scalars = jnp.stack([even.astype(jnp.int32), *starts])
    pick = functools.partial(choose, scalars)

    across = lambda a: shift(a, PART_AXIS, lambda i: i ^ 2)
    core = lambda a: shift(a, PART_AXIS, lambda i: i ^ 1)
    corner = lambda a: shift(a, PART_AXIS, lambda i: i ^ 3)
    beside = lambda a: shift(a, BLOCK_AXIS, lambda i: i ^ 1)
    ahead = lambda a: shift(a, BLOCK_AXIS, lambda i: i + 2)
    back = lambda a: shift(a, BLOCK_AXIS, lambda i: i - 2)
    apart = lambda a: shift(a, BLOCK_AXIS, lambda i: i + 2 if i % 2 == 0 else i - 2)

    k0, q0 = key_rows, query_rows
    y1_in = pick(k0, q0)
    y1, kz, kx = beside(y1_in), ahead(after(k0, y1_in)), across(after(k0, y1_in))
    ks, qs = core(k0), core(q0)
    partner_core = core(partner)

    qx = across(after(q0, kx))
    kzy = beside(after(kz, y1))
    qz = back(after(q0, kz))

    kzx = across(after(kz, qx))
    qzy = beside(after(qz, kzy))
    m1 = apart(after(pick(kzy, qx), qz))

    kd0 = pick(m1, y1)
    kd1 = across(after(kd0, kzx))
    kzxy = beside(after(kzx, qzy))
    m2 = back(after(pick(qx, qzy), m1))
    qd0, qzx = pick(y1, m2), pick(m2, m1)

    k_shards = (k0, kx, kz, kzx, kzy, kd0, kzxy, kd1)
    s_early, k_early, info = score(
        scalars, (q0, qs), k_shards[:6], 3, True, True, factor, (partner, partner_core)
    )
    x_cut, y_cut = CUTS
    qd1_0 = across(after(qd0[:x_cut], kd1, info))
    qzxy_0 = beside(after(qzx[:y_cut], kzxy, info))
    s_late, k_late, info = score(scalars, (q0, qs), k_shards[6:], 1, False, True, factor, (info,))
    info = after(info, qd1_0)
    own = small_call(block_kernel, [(24, rows)], info, across(info), core(info), corner(info))[0]
    qd1_1 = across(after(qd0[x_cut:], own))
    own = after(own, qzxy_0)
    next_to = beside(own)
    far = shift(own, BLOCK_AXIS, lambda i: i - 3 if i % 2 == 0 else i + 3)
    both = jnp.concatenate([own, next_to], axis=0)
    col_info, row_info, loss = small_call(
        window_kernel,
        [(8, 2 * rows), (8, 2 * rows), (1, rows)],
        scalars, partner, own, next_to, far, back(both), ahead(both),
        scalars=1,
    )
    qzxy_1 = beside(after(qzx[y_cut:], next_to))
    partner_across = across(after(partner, own))
    t_early, q_early = score(
        scalars, (after(k0, next_to), ks), (q0, qx, qz, qzx, qzy, qd0), 3, True, False, factor
    )
    q_own, q_other = grad(
        scalars, False, factor, s_early, k_early, row_info, col_info, partner, partner_core, (s_late, k_late)
    )
    k_own, k_other = grad(
        scalars, True, factor, t_early, q_early, col_info, row_info, partner, partner_across,
        (k0, ks), (qzxy_0, qzxy_1, qd1_0, qd1_1),
    )
    grad_queries = q_own + core(q_other)
    grad_keys = k_own + core(k_other)
    return (loss[0], grad_queries, grad_keys)


def solution(mesh):
    return jax.shard_map(
        local,
        mesh=mesh,
        in_specs=(P(("blk", "pb"), None), P(("blk", "pb"), None), P("blk", "pb")),
        out_specs=(P(("blk", "pb")), P(("blk", "pb"), None), P(("blk", "pb"), None)),
        check_vma=False,
    )
```

time: 146 us -> 124 us (0.85)
  local copies, waits for them, and re-layouts: 12.2 us -> 1.28 us
  waiting for transfers between devices: 56.1 us -> 46.2 us
  Pallas kernels: 44.5 us -> 38.3 us
  other arithmetic: 0.77 us -> 5.72 us
    unnamed x44 -> x7, local copies, waits for them, and re-layouts: 12.2 us -> 1.1 us
    ppermute x29, waiting for transfers between devices: 56.1 us -> 46.2 us  [shift(): lax.ppermute(array, axis, [(i, move(i) % peers) for i in range(peers)])]
    add x3 -> x2, other arithmetic: 0.02 us -> 5.13 us  [the longest x1 2.56 us: local(): grad_queries = q_own + core(q_other)]
    pallas_call x8 -> x5, Pallas kernels: 37.2 us -> 32.5 us  [the longest x3 18.2 us: score(): pl.pallas_call(functools.partial(score_kernel, shards, pairs, early, stat...]
    pallas_call x6, Pallas kernels: 6.62 us -> 4.61 us  [choose(): pl.pallas_call(choose_kernel, out_shape=jax.ShapeDtypeStruct(first.shape,...]
  transfers between devices with their start and end apart: 29 -> 29, of which waited for: 10 -> 9; matrix products, arithmetic and copies ran while one was open for 1% -> 3% of each run, Pallas kernels for 27% -> 30%
where the time goes in v4:
time: 124 us
  waiting for transfers between devices  46.2 us (37%)
  Pallas kernels  38.3 us (31%)
  starting transfers between devices  31.4 us (25%)
  other arithmetic  5.72 us (5%)
  local copies, waits for them, and re-layouts  1.28 us (1%)
    ppermute x29, waiting for transfers between devices, shift(): lax.ppermute(array, axis, [(i, move(i) % peers) for i in range(peers)])  46.2 us
    ppermute x29, starting transfers between devices, shift(): lax.ppermute(array, axis, [(i, move(i) % peers) for i in range(peers)])  31.4 us
    pallas_call x3, Pallas kernels, score(): pl.pallas_call(functools.partial(score_kernel, shards, pairs, early, stat...  18.2 us
    pallas_call x2, Pallas kernels, grad(): pl.pallas_call(functools.partial(grad_kernel, form, keys, factor), out_sh...  14.3 us
    pallas_call x6, Pallas kernels, choose(): pl.pallas_call(choose_kernel, out_shape=jax.ShapeDtypeStruct(first.shape,...  4.61 us
    add x1, other arithmetic, local(): grad_queries = q_own + core(q_other)  2.56 us
    add x1, other arithmetic, local(): grad_keys = k_own + core(k_other)  2.56 us
  transfers between devices with their start and end apart: 29, of which 9 were waited for; matrix products, arithmetic and copies ran while one was open for 3% of the time, Pallas kernels for 30%

profile of v4, /device:TPU:0, one launch (start us, length us, event | category | flops | bytes accessed | tf_op | source)
XLA Modules:
  0.0 123.8 jit_solution(14111478698660135055)
XLA Ops:
  0.7 1.1 copy-done
  1.8 0.8 shard_map.58
  2.6 3.1 %collective-permute-start.1 = (bf16[320,1024]{1,0:T(8,128)(2,1)S(1)}, bf16[320,1024]{1,0:T(8,128)(2,1)S(1)}, u32[]{:S(2)}, u32[]{:S(2)}) collective-permute-start(bf16[320,1024]{1,0:T(8,128)(2,1)S(1)} %copy-done), channel_id=1, source_target_pairs={{0,8},{4,12},{8,16},{12,20},{16,24},{20,28},{24,0},{28,4},{1,9},{5... | collective-permute-start | bytes 1966088 | tf_op jit(solution)/shard_map/ppermute | solution.py:22
  5.7 2.4 %collective-permute-start.6 = (bf16[320,1024]{1,0:T(8,128)(2,1)S(1)}, bf16[320,1024]{1,0:T(8,128)(2,1)S(1)}, u32[]{:S(2)}, u32[]{:S(2)}) collective-permute-start(bf16[320,1024]{1,0:T(8,128)(2,1)S(1)} %shard_map.58), channel_id=1, source_target_pairs={{0,4},{4,0},{8,12},{12,8},{16,20},{20,16},{24,28},{28,24},{1,5},{5... | collective-permute-start | bytes 1966088 | tf_op jit(solution)/shard_map/ppermute | solution.py:22
  8.1 1.5 %collective-permute-start.2 = (bf16[320,1024]{1,0:T(8,128)(2,1)S(1)}, bf16[320,1024]{1,0:T(8,128)(2,1)S(1)}, u32[]{:S(2)}, u32[]{:S(2)}) collective-permute-start(bf16[320,1024]{1,0:T(8,128)(2,1)S(1)} %copy-done), channel_id=1, source_target_pairs={{0,2},{1,3},{2,0},{3,1},{4,6},{5,7},{6,4},{7,5},{8,10},{9,11},{10,... | collective-permute-start | bytes 1966088 | tf_op jit(solution)/shard_map/ppermute | solution.py:22
  9.6 12.9 %collective-permute-done.1.refs_4_ = bf16[320,1024]{1,0:T(8,128)(2,1)S(1)} collective-permute-done((bf16[320,1024]{1,0:T(8,128)(2,1)S(1)}, bf16[320,1024]{1,0:T(8,128)(2,1)S(1)}, u32[]{:S(2)}, u32[]{:S(2)}) %collective-permute-start.1) | collective-permute-done | bytes 655392 | tf_op jit(solution)/shard_map/ppermute | solution.py:22
  22.4 1.7 %collective-permute-start.5 = (bf16[320,1024]{1,0:T(8,128)(2,1)}, bf16[320,1024]{1,0:T(8,128)(2,1)S(1)}, u32[]{:S(2)}, u32[]{:S(2)}) collective-permute-start(bf16[320,1024]{1,0:T(8,128)(2,1)} %refs_2_.3), channel_id=1, source_target_pairs={{0,24},{4,28},{8,0},{12,4},{16,8},{20,12},{24,16},{28,20},{1,25},{... | collective-permute-start | bytes 1966088 | tf_op jit(solution)/shard_map/ppermute | solution.py:22
  24.2 2.4 %collective-permute-start.7 = (bf16[320,1024]{1,0:T(8,128)(2,1)S(1)}, bf16[320,1024]{1,0:T(8,128)(2,1)S(1)}, u32[]{:S(2)}, u32[]{:S(2)}) collective-permute-start(bf16[320,1024]{1,0:T(8,128)(2,1)S(1)} %collective-permute-done.1.refs_4_), channel_id=1, source_target_pairs={{0,4},{4,0},{8,12},{12,8},{16,20},{20,16},{24,28},{28,24},{1,5},{5... | collective-permute-start | bytes 1966088 | tf_op jit(solution)/shard_map/ppermute | solution.py:22
  26.6 1.5 %collective-permute-start.3 = (bf16[320,1024]{1,0:T(8,128)(2,1)}, bf16[320,1024]{1,0:T(8,128)(2,1)S(1)}, u32[]{:S(2)}, u32[]{:S(2)}) collective-permute-start(bf16[320,1024]{1,0:T(8,128)(2,1)} %refs_2_.3), channel_id=1, source_target_pairs={{0,2},{1,3},{2,0},{3,1},{4,6},{5,7},{6,4},{7,5},{8,10},{9,11},{10,... | collective-permute-start | bytes 1966088 | tf_op jit(solution)/shard_map/ppermute | solution.py:22
  28.1 10.5 %collective-permute-done.5.refs_4_ = bf16[320,1024]{1,0:T(8,128)(2,1)S(1)} collective-permute-done((bf16[320,1024]{1,0:T(8,128)(2,1)}, bf16[320,1024]{1,0:T(8,128)(2,1)S(1)}, u32[]{:S(2)}, u32[]{:S(2)}) %collective-permute-start.5) | collective-permute-done | bytes 655392 | tf_op jit(solution)/shard_map/ppermute | solution.py:22
  38.6 1.6 %collective-permute-done.7.first.refs_6_ = bf16[320,1024]{1,0:T(8,128)(2,1)S(1)} collective-permute-done((bf16[320,1024]{1,0:T(8,128)(2,1)S(1)}, bf16[320,1024]{1,0:T(8,128)(2,1)S(1)}, u32[]{:S(2)}, u32[]{:S(2)}) %collective-permute-start.7) | collective-permute-done | bytes 655392 | tf_op jit(solution)/shard_map/ppermute | solution.py:22
  40.2 1.7 %collective-permute-start.8 = (bf16[320,1024]{1,0:T(8,128)(2,1)S(1)}, bf16[320,1024]{1,0:T(8,128)(2,1)S(1)}, u32[]{:S(2)}, u32[]{:S(2)}) collective-permute-start(bf16[320,1024]{1,0:T(8,128)(2,1)S(1)} %collective-permute-done.5.refs_4_), channel_id=1, source_target_pairs={{0,4},{4,0},{8,12},{12,8},{16,20},{20,16},{24,28},{28,24},{1,5},{5... | collective-permute-start | bytes 1966088 | tf_op jit(solution)/shard_map/ppermute | solution.py:22
  41.9 0.8 shard_map.59
  42.7 0.4 collective-permute-start.10
  43.1 1.5 %collective-permute-start.4 = (bf16[320,1024]{1,0:T(8,128)(2,1)S(1)}, bf16[320,1024]{1,0:T(8,128)(2,1)S(1)}, u32[]{:S(2)}, u32[]{:S(2)}) collective-permute-start(bf16[320,1024]{1,0:T(8,128)(2,1)S(1)} %collective-permute-done.1.refs_4_), channel_id=1, source_target_pairs={{0,2},{1,3},{2,0},{3,1},{4,6},{5,7},{6,4},{7,5},{8,10},{9,11},{10,... | collective-permute-start | bytes 1966088 | tf_op jit(solution)/shard_map/ppermute | solution.py:22
  44.6 10.3 %collective-permute-done.8.second.refs_6_ = bf16[320,1024]{1,0:T(8,128)(2,1)S(1)} collective-permute-done((bf16[320,1024]{1,0:T(8,128)(2,1)S(1)}, bf16[320,1024]{1,0:T(8,128)(2,1)S(1)}, u32[]{:S(2)}, u32[]{:S(2)}) %collective-permute-start.8) | collective-permute-done | bytes 655392 | tf_op jit(solution)/shard_map/ppermute | solution.py:22
  54.8 0.8 shard_map.63
  55.6 4.5 %collective-permute-done.10.first.second = bf16[320,1024]{1,0:T(8,128)(2,1)S(1)} collective-permute-done((bf16[320,1024]{1,0:T(8,128)(2,1)S(1)}, bf16[320,1024]{1,0:T(8,128)(2,1)S(1)}, u32[]{:S(2)}, u32[]{:S(2)}) %collective-permute-start.10) | collective-permute-done | bytes 655392 | tf_op jit(solution)/shard_map/ppermute | solution.py:22
  60.1 1.4 %collective-permute-start.9 = (bf16[320,1024]{1,0:T(8,128)(2,1)S(1)}, bf16[320,1024]{1,0:T(8,128)(2,1)S(1)}, u32[]{:S(2)}, u32[]{:S(2)}) collective-permute-start(bf16[320,1024]{1,0:T(8,128)(2,1)S(1)} %collective-permute-done.4.refs_5_), channel_id=1, source_target_pairs={{0,4},{4,0},{8,12},{12,8},{16,20},{20,16},{24,28},{28,24},{1,5},{5... | collective-permute-start | bytes 1966088 | tf_op jit(solution)/shard_map/ppermute | solution.py:22
  61.5 0.8 shard_map.60.refs_7_
  62.3 1.6 %collective-permute-start.11 = (bf16[320,1024]{1,0:T(8,128)(2,1)S(1)}, bf16[320,1024]{1,0:T(8,128)(2,1)S(1)}, u32[]{:S(2)}, u32[]{:S(2)}) collective-permute-start(bf16[320,1024]{1,0:T(8,128)(2,1)S(1)} %shard_map.60.refs_7_), channel_id=1, source_target_pairs={{0,2},{1,3},{2,0},{3,1},{4,6},{5,7},{6,4},{7,5},{8,10},{9,11},{10,... | collective-permute-start | bytes 1966088 | tf_op jit(solution)/shard_map/ppermute | solution.py:22
  63.8 1.1 collective-permute-done.12.refs_9_.second
  65.0 0.2 collective-permute-start.24
  65.2 8.2 %shard_map.61 = (f32[640,1920]{1,0:T(8,128)S(1)}, bf16[1920,1024]{1,0:T(8,128)(2,1)S(1)}, f32[8,640]{1,0:T(8,128)S(1)}) custom-call(s32[5]{0:T(128)S(1)} %stack.27.flag.scalars, bf16[320,1024]{1,0:T(8,128)(2,1)} %refs_2_.3, bf16[320,1024]{1,0:T(8,128)(2,1)S(1)} %collective-permute-done.refs_1_, bf16[320,1024]{1,0:T(8,128)(2,1)S(1)} %copy-done.1, ...), custom_call_target="tpu_custom_call" | custom-call | flops 2516582400 | bytes 10158080 | tf_op jit(solution)/shard_map/pallas_call | solution.py:163
  73.4 0.8 shard_map.66.refs_5_
  74.2 0.8 collective-permute-start.18
  75.0 0.8 shard_map.64.refs_7_
  75.8 1.6 %collective-permute-start.14 = (bf16[96,1024]{1,0:T(8,128)(2,1)S(1)}, bf16[96,1024]{1,0:T(8,128)(2,1)S(1)}, u32[]{:S(2)}, u32[]{:S(2)}) collective-permute-start(bf16[96,1024]{1,0:T(8,128)(2,1)S(1)} %slice.16), channel_id=1, source_target_pairs={{0,2},{1,3},{2,0},{3,1},{4,6},{5,7},{6,4},{7,5},{8,10},{9,11},{10,... | collective-permute-start | bytes 589832 | tf_op jit(solution)/shard_map/ppermute | solution.py:22
  77.3 3.6 %shard_map.62 = (f32[640,640]{1,0:T(8,128)S(1)}, bf16[640,1024]{1,0:T(8,128)(2,1)S(1)}, f32[8,640]{1,0:T(8,128)S(1)}) custom-call(s32[5]{0:T(128)S(1)} %stack.27.flag.scalars, bf16[320,1024]{1,0:T(8,128)(2,1)} %refs_2_.3, bf16[320,1024]{1,0:T(8,128)(2,1)S(1)} %collective-permute-done.refs_1_, bf16[320,1024]{1,0:T(8,128)(2,1)S(1)} %collective-permute-done.9.refs_2_, ...), custom_call_target="tpu_custom_call" | custom-call | flops 838860800 | bytes 4259840 | tf_op jit(solution)/shard_map/pallas_call | solution.py:163
  80.9 1.7 %collective-permute-done.14.refs_4_ = bf16[96,1024]{1,0:T(8,128)(2,1)S(1)} collective-permute-done((bf16[96,1024]{1,0:T(8,128)(2,1)S(1)}, bf16[96,1024]{1,0:T(8,128)(2,1)S(1)}, u32[]{:S(2)}, u32[]{:S(2)}) %collective-permute-start.14) | collective-permute-done | bytes 196640 | tf_op jit(solution)/shard_map/ppermute | solution.py:22
  82.6 0.5 collective-permute-start.15
  83.2 1.6 %collective-permute-start.17 = (f32[8,640]{1,0:T(8,128)S(1)}, f32[8,640]{1,0:T(8,128)S(1)}, u32[]{:S(2)}, u32[]{:S(2)}) collective-permute-start(f32[8,640]{1,0:T(8,128)S(1)} %get-tuple-element.49.own), channel_id=1, source_target_pairs={{0,3},{1,2},{2,1},{3,0},{4,7},{5,6},{6,5},{7,4},{8,11},{9,10},{10,... | collective-permute-start | bytes 61448 | tf_op jit(solution)/shard_map/ppermute | solution.py:22
  84.9 1.8 %collective-permute-done.15.across = f32[8,640]{1,0:T(8,128)S(1)} collective-permute-done((f32[8,640]{1,0:T(8,128)S(1)}, f32[8,640]{1,0:T(8,128)S(1)}, u32[]{:S(2)}, u32[]{:S(2)}) %collective-permute-start.15) | collective-permute-done | bytes 20512 | tf_op jit(solution)/shard_map/ppermute | solution.py:22
  86.6 0.1 shard_map.65.own
  86.7 1.3 %collective-permute-start.27 = (bf16[224,1024]{1,0:T(8,128)(2,1)S(1)}, bf16[224,1024]{1,0:T(8,128)(2,1)S(1)}, u32[]{:S(2)}, u32[]{:S(2)}) collective-permute-start(bf16[224,1024]{1,0:T(8,128)(2,1)S(1)} %slice.19), channel_id=1, source_target_pairs={{0,2},{1,3},{2,0},{3,1},{4,6},{5,7},{6,4},{7,5},{8,10},{9,11},{10,... | collective-permute-start | bytes 1376264 | tf_op jit(solution)/shard_map/ppermute | solution.py:22
  88.1 1.4 %collective-permute-start.19 = (f32[24,320]{1,0:T(8,128)S(1)}, f32[24,320]{1,0:T(8,128)S(1)}, u32[]{:S(2)}, u32[]{:S(2)}) collective-permute-start(f32[24,320]{1,0:T(8,128)S(1)} %shard_map.65.own), channel_id=1, source_target_pairs={{0,4},{4,0},{8,12},{12,8},{16,20},{20,16},{24,28},{28,24},{1,5},{5... | collective-permute-start | bytes 92168 | tf_op jit(solution)/shard_map/ppermute | solution.py:22
  89.5 0.8 collective-permute-start.25
  90.2 1.8 %collective-permute-done.19.beside = f32[24,320]{1,0:T(8,128)S(1)} collective-permute-done((f32[24,320]{1,0:T(8,128)S(1)}, f32[24,320]{1,0:T(8,128)S(1)}, u32[]{:S(2)}, u32[]{:S(2)}) %collective-permute-start.19) | collective-permute-done | bytes 30752 | tf_op jit(solution)/shard_map/ppermute | solution.py:22
  92.0 2.7 %collective-permute-start.21 = (f32[48,320]{1,0:T(8,128)S(1)}, f32[48,320]{1,0:T(8,128)S(1)}, u32[]{:S(2)}, u32[]{:S(2)}) collective-permute-start(f32[48,320]{1,0:T(8,128)S(1)} %constant_dynamic-update-slice_fusion), channel_id=1, source_target_pairs={{0,24},{4,28},{8,0},{12,4},{16,8},{20,12},{24,16},{28,20},{1,25},{... | collective-permute-start | bytes 184328 | tf_op jit(solution)/shard_map/ppermute | solution.py:22
  94.7 6.4 %shard_map.69 = (f32[640,1920]{1,0:T(8,128)S(1)}, bf16[1920,1024]{1,0:T(8,128)(2,1)S(1)}) custom-call(s32[5]{0:T(128)S(1)} %stack.27.flag.scalars, bf16[320,1024]{1,0:T(8,128)(2,1)S(1)} %copy-done.1, bf16[320,1024]{1,0:T(8,128)(2,1)S(1)} %collective-permute-done.24.refs_1_, bf16[320,1024]{1,0:T(8,128)(2,1)} %refs_2_.3, ...), custom_call_target="tpu_custom_call" | custom-call | flops 2516582400 | bytes 10158080 | tf_op jit(solution)/shard_map/pallas_call | solution.py:163
  101.2 0.8 collective-permute-start.26
  102.0 1.1 shard_map.67
  103.0 5.3 %shard_map.68 = (f32[320,1024]{1,0:T(8,128)S(1)}, f32[320,1024]{1,0:T(8,128)}) custom-call(s32[5]{0:T(128)S(1)} %stack.27.flag.scalars, f32[640,1920]{1,0:T(8,128)S(1)} %get-tuple-element.53.early, bf16[1920,1024]{1,0:T(8,128)(2,1)S(1)} %get-tuple-element.54.held_early, f32[8,640]{1,0:T(8,128)S(1)} %get-tuple-element.55.row_info.col_info, ...), custom_call_target="tpu_custom_call" | custom-call | flops 3355443200 | bytes 14417920 | tf_op jit(solution)/shard_map/pallas_call | solution.py:339
  108.5 9.0 %shard_map.70 = (f32[320,1024]{1,0:T(8,128)S(1)}, f32[320,1024]{1,0:T(8,128)}) custom-call(s32[5]{0:T(128)S(1)} %stack.27.flag.scalars, f32[640,1920]{1,0:T(8,128)S(1)} %get-tuple-element.62.early, bf16[1920,1024]{1,0:T(8,128)(2,1)S(1)} %get-tuple-element.63.held_early, f32[8,640]{1,0:T(8,128)S(1)} %get-tuple-element.56.col_info.row_info, ...), custom_call_target="tpu_custom_call" | custom-call | flops 3355443200 | bytes 14417920 | tf_op jit(solution)/shard_map/pallas_call | solution.py:339
  117.5 0.5 collective-permute-start.28
  118.0 0.6 reduce
  118.6 2.6 %add.11 = f32[320,1024]{1,0:T(8,128)} add(f32[320,1024]{1,0:T(8,128)S(1)} %get-tuple-element.59, f32[320,1024]{1,0:T(8,128)} %collective-permute-done.23) | non-fusion elementwise | flops 327680 | bytes 3932160 | tf_op jit(solution)/shard_map/add | solution.py:425
  121.2 2.6 %add.12 = f32[320,1024]{1,0:T(8,128)} add(f32[320,1024]{1,0:T(8,128)S(1)} %get-tuple-element.67, f32[320,1024]{1,0:T(8,128)} %collective-permute-done.28) | non-fusion elementwise | flops 327680 | bytes 3932160 | tf_op jit(solution)/shard_map/add | solution.py:426
  (39 shorter events, 0.3 us)
Async XLA Ops:
  0.7 1.1 copy-start
  2.6 19.8 %collective-permute-start.1 = (bf16[320,1024]{1,0:T(8,128)(2,1)S(1)}, bf16[320,1024]{1,0:T(8,128)(2,1)S(1)}, u32[]{:S(2)}, u32[]{:S(2)}) collective-permute-start(bf16[320,1024]{1,0:T(8,128)(2,1)S(1)} %copy-done), channel_id=1, source_target_pairs={{0,8},{4,12},{8,16},{12,20},{16,24},{20,28},{24,0},{28,4},{1,9},{5... | collective-permute-start | bytes 1966088 | tf_op jit(solution)/shard_map/ppermute | solution.py:22
  5.7 18.5 %collective-permute-start.6 = (bf16[320,1024]{1,0:T(8,128)(2,1)S(1)}, bf16[320,1024]{1,0:T(8,128)(2,1)S(1)}, u32[]{:S(2)}, u32[]{:S(2)}) collective-permute-start(bf16[320,1024]{1,0:T(8,128)(2,1)S(1)} %shard_map.58), channel_id=1, source_target_pairs={{0,4},{4,0},{8,12},{12,8},{16,20},{20,16},{24,28},{28,24},{1,5},{5... | collective-permute-start | bytes 1966088 | tf_op jit(solution)/shard_map/ppermute | solution.py:22
  8.1 18.5 %collective-permute-start.2 = (bf16[320,1024]{1,0:T(8,128)(2,1)S(1)}, bf16[320,1024]{1,0:T(8,128)(2,1)S(1)}, u32[]{:S(2)}, u32[]{:S(2)}) collective-permute-start(bf16[320,1024]{1,0:T(8,128)(2,1)S(1)} %copy-done), channel_id=1, source_target_pairs={{0,2},{1,3},{2,0},{3,1},{4,6},{5,7},{6,4},{7,5},{8,10},{9,11},{10,... | collective-permute-start | bytes 1966088 | tf_op jit(solution)/shard_map/ppermute | solution.py:22
  22.4 16.1 %collective-permute-start.5 = (bf16[320,1024]{1,0:T(8,128)(2,1)}, bf16[320,1024]{1,0:T(8,128)(2,1)S(1)}, u32[]{:S(2)}, u32[]{:S(2)}) collective-permute-start(bf16[320,1024]{1,0:T(8,128)(2,1)} %refs_2_.3), channel_id=1, source_target_pairs={{0,24},{4,28},{8,0},{12,4},{16,8},{20,12},{24,16},{28,20},{1,25},{... | collective-permute-start | bytes 1966088 | tf_op jit(solution)/shard_map/ppermute | solution.py:22
  24.2 16.0 %collective-permute-start.7 = (bf16[320,1024]{1,0:T(8,128)(2,1)S(1)}, bf16[320,1024]{1,0:T(8,128)(2,1)S(1)}, u32[]{:S(2)}, u32[]{:S(2)}) collective-permute-start(bf16[320,1024]{1,0:T(8,128)(2,1)S(1)} %collective-permute-done.1.refs_4_), channel_id=1, source_target_pairs={{0,4},{4,0},{8,12},{12,8},{16,20},{20,16},{24,28},{28,24},{1,5},{5... | collective-permute-start | bytes 1966088 | tf_op jit(solution)/shard_map/ppermute | solution.py:22
  26.6 15.3 %collective-permute-start.3 = (bf16[320,1024]{1,0:T(8,128)(2,1)}, bf16[320,1024]{1,0:T(8,128)(2,1)S(1)}, u32[]{:S(2)}, u32[]{:S(2)}) collective-permute-start(bf16[320,1024]{1,0:T(8,128)(2,1)} %refs_2_.3), channel_id=1, source_target_pairs={{0,2},{1,3},{2,0},{3,1},{4,6},{5,7},{6,4},{7,5},{8,10},{9,11},{10,... | collective-permute-start | bytes 1966088 | tf_op jit(solution)/shard_map/ppermute | solution.py:22
  40.2 14.7 %collective-permute-start.8 = (bf16[320,1024]{1,0:T(8,128)(2,1)S(1)}, bf16[320,1024]{1,0:T(8,128)(2,1)S(1)}, u32[]{:S(2)}, u32[]{:S(2)}) collective-permute-start(bf16[320,1024]{1,0:T(8,128)(2,1)S(1)} %collective-permute-done.5.refs_4_), channel_id=1, source_target_pairs={{0,4},{4,0},{8,12},{12,8},{16,20},{20,16},{24,28},{28,24},{1,5},{5... | collective-permute-start | bytes 1966088 | tf_op jit(solution)/shard_map/ppermute | solution.py:22
  42.7 17.4 %collective-permute-start.10 = (bf16[320,1024]{1,0:T(8,128)(2,1)S(1)}, bf16[320,1024]{1,0:T(8,128)(2,1)S(1)}, u32[]{:S(2)}, u32[]{:S(2)}) collective-permute-start(bf16[320,1024]{1,0:T(8,128)(2,1)S(1)} %shard_map.59), channel_id=1, source_target_pairs={{0,8},{4,28},{8,16},{12,4},{16,24},{20,12},{24,0},{28,20},{1,9},{5... | collective-permute-start | bytes 1966088 | tf_op jit(solution)/shard_map/ppermute | solution.py:22
  43.1 17.0 %collective-permute-start.4 = (bf16[320,1024]{1,0:T(8,128)(2,1)S(1)}, bf16[320,1024]{1,0:T(8,128)(2,1)S(1)}, u32[]{:S(2)}, u32[]{:S(2)}) collective-permute-start(bf16[320,1024]{1,0:T(8,128)(2,1)S(1)} %collective-permute-done.1.refs_4_), channel_id=1, source_target_pairs={{0,2},{1,3},{2,0},{3,1},{4,6},{5,7},{6,4},{7,5},{8,10},{9,11},{10,... | collective-permute-start | bytes 1966088 | tf_op jit(solution)/shard_map/ppermute | solution.py:22
  44.6 20.6 %collective-permute-start = (bf16[320,1024]{1,0:T(8,128)(2,1)}, bf16[320,1024]{1,0:T(8,128)(2,1)S(1)}, u32[]{:S(2)}, u32[]{:S(2)}) collective-permute-start(bf16[320,1024]{1,0:T(8,128)(2,1)} %refs_2_.3), channel_id=1, source_target_pairs={{0,1},{1,0},{2,3},{3,2},{4,5},{5,4},{6,7},{7,6},{8,9},{9,8},{10,11... | collective-permute-start | bytes 1966088 | tf_op jit(solution)/shard_map/ppermute | solution.py:22
  55.6 8.2 %copy-start.2 = (s32[1,320]{1,0:T(1,128)S(1)}, s32[1,320]{1,0:T(1,128)}, u32[]{:S(2)}) copy-start(s32[1,320]{1,0:T(1,128)} %first.5) | copy-start | bytes 3844
  55.6 9.4 %copy-start.1 = (bf16[320,1024]{1,0:T(8,128)(2,1)S(1)}, bf16[320,1024]{1,0:T(8,128)(2,1)}, u32[]{:S(2)}) copy-start(bf16[320,1024]{1,0:T(8,128)(2,1)} %refs_0_.6) | copy-start | bytes 1966084
  60.1 13.3 %collective-permute-start.13 = (bf16[320,1024]{1,0:T(8,128)(2,1)S(1)}, bf16[320,1024]{1,0:T(8,128)(2,1)S(1)}, u32[]{:S(2)}, u32[]{:S(2)}) collective-permute-start(bf16[320,1024]{1,0:T(8,128)(2,1)S(1)} %shard_map.63), channel_id=1, source_target_pairs={{0,24},{4,28},{8,0},{12,4},{16,8},{20,12},{24,16},{28,20},{1,25},{... | collective-permute-start | bytes 1966088 | tf_op jit(solution)/shard_map/ppermute | solution.py:22
  60.1 14.1 %collective-permute-start.9 = (bf16[320,1024]{1,0:T(8,128)(2,1)S(1)}, bf16[320,1024]{1,0:T(8,128)(2,1)S(1)}, u32[]{:S(2)}, u32[]{:S(2)}) collective-permute-start(bf16[320,1024]{1,0:T(8,128)(2,1)S(1)} %collective-permute-done.4.refs_5_), channel_id=1, source_target_pairs={{0,4},{4,0},{8,12},{12,8},{16,20},{20,16},{24,28},{28,24},{1,5},{5... | collective-permute-start | bytes 1966088 | tf_op jit(solution)/shard_map/ppermute | solution.py:22
  62.3 13.5 %collective-permute-start.11 = (bf16[320,1024]{1,0:T(8,128)(2,1)S(1)}, bf16[320,1024]{1,0:T(8,128)(2,1)S(1)}, u32[]{:S(2)}, u32[]{:S(2)}) collective-permute-start(bf16[320,1024]{1,0:T(8,128)(2,1)S(1)} %shard_map.60.refs_7_), channel_id=1, source_target_pairs={{0,2},{1,3},{2,0},{3,1},{4,6},{5,7},{6,4},{7,5},{8,10},{9,11},{10,... | collective-permute-start | bytes 1966088 | tf_op jit(solution)/shard_map/ppermute | solution.py:22
  63.8 1.2 collective-permute-start.12
  65.0 29.7 %collective-permute-start.24 = (bf16[320,1024]{1,0:T(8,128)(2,1)S(1)}, bf16[320,1024]{1,0:T(8,128)(2,1)S(1)}, u32[]{:S(2)}, u32[]{:S(2)}) collective-permute-start(bf16[320,1024]{1,0:T(8,128)(2,1)S(1)} %copy-done.1), channel_id=1, source_target_pairs={{0,1},{1,0},{2,3},{3,2},{4,5},{5,4},{6,7},{7,6},{8,9},{9,8},{10,11... | collective-permute-start | bytes 1966088 | tf_op jit(solution)/shard_map/ppermute | solution.py:22
  74.2 13.9 %collective-permute-start.18 = (bf16[192,1024]{1,0:T(8,128)(2,1)S(1)}, bf16[192,1024]{1,0:T(8,128)(2,1)S(1)}, u32[]{:S(2)}, u32[]{:S(2)}) collective-permute-start(bf16[192,1024]{1,0:T(8,128)(2,1)S(1)} %slice.17), channel_id=1, source_target_pairs={{0,4},{4,0},{8,12},{12,8},{16,20},{20,16},{24,28},{28,24},{1,5},{5... | collective-permute-start | bytes 1179656 | tf_op jit(solution)/shard_map/ppermute | solution.py:22
  75.8 6.9 %collective-permute-start.14 = (bf16[96,1024]{1,0:T(8,128)(2,1)S(1)}, bf16[96,1024]{1,0:T(8,128)(2,1)S(1)}, u32[]{:S(2)}, u32[]{:S(2)}) collective-permute-start(bf16[96,1024]{1,0:T(8,128)(2,1)S(1)} %slice.16), channel_id=1, source_target_pairs={{0,2},{1,3},{2,0},{3,1},{4,6},{5,7},{6,4},{7,5},{8,10},{9,11},{10,... | collective-permute-start | bytes 589832 | tf_op jit(solution)/shard_map/ppermute | solution.py:22
  82.6 4.0 %collective-permute-start.15 = (f32[8,640]{1,0:T(8,128)S(1)}, f32[8,640]{1,0:T(8,128)S(1)}, u32[]{:S(2)}, u32[]{:S(2)}) collective-permute-start(f32[8,640]{1,0:T(8,128)S(1)} %get-tuple-element.49.own), channel_id=1, source_target_pairs={{0,2},{1,3},{2,0},{3,1},{4,6},{5,7},{6,4},{7,5},{8,10},{9,11},{10,... | collective-permute-start | bytes 61448 | tf_op jit(solution)/shard_map/ppermute | solution.py:22
  83.2 3.4 %collective-permute-start.16 = (f32[8,640]{1,0:T(8,128)S(1)}, f32[8,640]{1,0:T(8,128)S(1)}, u32[]{:S(2)}, u32[]{:S(2)}) collective-permute-start(f32[8,640]{1,0:T(8,128)S(1)} %get-tuple-element.49.own), channel_id=1, source_target_pairs={{0,1},{1,0},{2,3},{3,2},{4,5},{5,4},{6,7},{7,6},{8,9},{9,8},{10,11... | collective-permute-start | bytes 61448 | tf_op jit(solution)/shard_map/ppermute | solution.py:22
  83.2 3.4 %collective-permute-start.17 = (f32[8,640]{1,0:T(8,128)S(1)}, f32[8,640]{1,0:T(8,128)S(1)}, u32[]{:S(2)}, u32[]{:S(2)}) collective-permute-start(f32[8,640]{1,0:T(8,128)S(1)} %get-tuple-element.49.own), channel_id=1, source_target_pairs={{0,3},{1,2},{2,1},{3,0},{4,7},{5,6},{6,5},{7,4},{8,11},{9,10},{10,... | collective-permute-start | bytes 61448 | tf_op jit(solution)/shard_map/ppermute | solution.py:22
  86.7 21.7 %collective-permute-start.27 = (bf16[224,1024]{1,0:T(8,128)(2,1)S(1)}, bf16[224,1024]{1,0:T(8,128)(2,1)S(1)}, u32[]{:S(2)}, u32[]{:S(2)}) collective-permute-start(bf16[224,1024]{1,0:T(8,128)(2,1)S(1)} %slice.19), channel_id=1, source_target_pairs={{0,2},{1,3},{2,0},{3,1},{4,6},{5,7},{6,4},{7,5},{8,10},{9,11},{10,... | collective-permute-start | bytes 1376264 | tf_op jit(solution)/shard_map/ppermute | solution.py:22
  88.1 4.0 %collective-permute-start.19 = (f32[24,320]{1,0:T(8,128)S(1)}, f32[24,320]{1,0:T(8,128)S(1)}, u32[]{:S(2)}, u32[]{:S(2)}) collective-permute-start(f32[24,320]{1,0:T(8,128)S(1)} %shard_map.65.own), channel_id=1, source_target_pairs={{0,4},{4,0},{8,12},{12,8},{16,20},{20,16},{24,28},{28,24},{1,5},{5... | collective-permute-start | bytes 92168 | tf_op jit(solution)/shard_map/ppermute | solution.py:22
  89.5 11.7 %collective-permute-start.20 = (f32[24,320]{1,0:T(8,128)S(1)}, f32[24,320]{1,0:T(8,128)S(1)}, u32[]{:S(2)}, u32[]{:S(2)}) collective-permute-start(f32[24,320]{1,0:T(8,128)S(1)} %shard_map.65.own), channel_id=1, source_target_pairs={{0,20},{4,16},{8,28},{12,24},{16,4},{20,0},{24,12},{28,8},{1,21},{... | collective-permute-start | bytes 92168 | tf_op jit(solution)/shard_map/ppermute | solution.py:22
  89.5 19.0 %collective-permute-start.25 = (s32[1,320]{1,0:T(1,128)S(1)}, s32[1,320]{1,0:T(1,128)S(1)}, u32[]{:S(2)}, u32[]{:S(2)}) collective-permute-start(s32[1,320]{1,0:T(1,128)S(1)} %copy-done.2), channel_id=1, source_target_pairs={{0,2},{1,3},{2,0},{3,1},{4,6},{5,7},{6,4},{7,5},{8,10},{9,11},{10,... | collective-permute-start | bytes 3848 | tf_op jit(solution)/shard_map/ppermute | solution.py:22
  92.0 9.9 %collective-permute-start.21 = (f32[48,320]{1,0:T(8,128)S(1)}, f32[48,320]{1,0:T(8,128)S(1)}, u32[]{:S(2)}, u32[]{:S(2)}) collective-permute-start(f32[48,320]{1,0:T(8,128)S(1)} %constant_dynamic-update-slice_fusion), channel_id=1, source_target_pairs={{0,24},{4,28},{8,0},{12,4},{16,8},{20,12},{24,16},{28,20},{1,25},{... | collective-permute-start | bytes 184328 | tf_op jit(solution)/shard_map/ppermute | solution.py:22
  94.7 7.3 %collective-permute-start.22 = (f32[48,320]{1,0:T(8,128)S(1)}, f32[48,320]{1,0:T(8,128)S(1)}, u32[]{:S(2)}, u32[]{:S(2)}) collective-permute-start(f32[48,320]{1,0:T(8,128)S(1)} %constant_dynamic-update-slice_fusion), channel_id=1, source_target_pairs={{0,8},{4,12},{8,16},{12,20},{16,24},{20,28},{24,0},{28,4},{1,9},{5... | collective-permute-start | bytes 184328 | tf_op jit(solution)/shard_map/ppermute | solution.py:22
  101.2 7.3 %collective-permute-start.26 = (bf16[128,1024]{1,0:T(8,128)(2,1)S(1)}, bf16[128,1024]{1,0:T(8,128)(2,1)S(1)}, u32[]{:S(2)}, u32[]{:S(2)}) collective-permute-start(bf16[128,1024]{1,0:T(8,128)(2,1)S(1)} %slice.18), channel_id=1, source_target_pairs={{0,4},{4,0},{8,12},{12,8},{16,20},{20,16},{24,28},{28,24},{1,5},{5... | collective-permute-start | bytes 786440 | tf_op jit(solution)/shard_map/ppermute | solution.py:22
  108.4 10.3 %collective-permute-start.23 = (f32[320,1024]{1,0:T(8,128)}, f32[320,1024]{1,0:T(8,128)}, u32[]{:S(2)}, u32[]{:S(2)}) collective-permute-start(f32[320,1024]{1,0:T(8,128)} %get-tuple-element.60), channel_id=1, source_target_pairs={{0,1},{1,0},{2,3},{3,2},{4,5},{5,4},{6,7},{7,6},{8,9},{9,8},{10,11... | collective-permute-start | bytes 3932168 | tf_op jit(solution)/shard_map/ppermute | solution.py:22
  117.5 3.7 %collective-permute-start.28 = (f32[320,1024]{1,0:T(8,128)}, f32[320,1024]{1,0:T(8,128)}, u32[]{:S(2)}, u32[]{:S(2)}) collective-permute-start(f32[320,1024]{1,0:T(8,128)} %get-tuple-element.68), channel_id=1, source_target_pairs={{0,1},{1,0},{2,3},{3,2},{4,5},{5,4},{6,7},{7,6},{8,9},{9,8},{10,11... | collective-permute-start | bytes 3932168 | tf_op jit(solution)/shard_map/ppermute | solution.py:22

commit v5 on v4

v5 whole, which is shorter than its diff:
```python
import functools

import jax
import jax.numpy as jnp
from jax import lax
from jax.experimental import pallas as pl
from jax.experimental.pallas import tpu as pltpu
from jax.sharding import PartitionSpec as P

F32 = jnp.float32
BLOCK_AXIS, PART_AXIS = "blk", "pb"
VMEM_LIMIT = 16 * 1024 * 1024
ANYWHERE = pl.BlockSpec(memory_space=pl.ANY)
WHOLE = pl.BlockSpec(memory_space=pltpu.VMEM)
SCALAR = pl.BlockSpec(memory_space=pltpu.SMEM)
NT = (((1,), (1,)), ((), ()))


def shift(array, axis, move, among=None):
    peers = lax.axis_size(axis)
    pairs = [(i, move(i) % peers) for i in range(peers) if among is None or among(i)]
    return lax.ppermute(array, axis, pairs)


def as_column(row):
    return jnp.broadcast_to(row, (128, row.shape[1])).T[:, 0:1]


def as_row(column):
    return jnp.broadcast_to(column, (column.shape[0], 128)).T[0:1, :]


def log_join(*parts):
    top = functools.reduce(jnp.maximum, parts)
    return top + jnp.log(sum(jnp.exp(part - top) for part in parts))


def fetch(sources, target, sems):
    copies, row = [], 0
    for i, source in enumerate(sources):
        rows = source.shape[0]
        copy = pltpu.make_async_copy(source, target.at[pl.ds(row, rows)], sems.at[i])
        copy.start()
        copies.append(copy)
        row += rows
    return copies


def choose_kernel(flag, first, second, out, sem):
    @pl.when(flag[0] == 1)
    def _():
        pltpu.make_async_copy(first, out, sem).start()

    @pl.when(flag[0] != 1)
    def _():
        pltpu.make_async_copy(second, out, sem).start()

    pltpu.make_async_copy(first, out, sem).wait()


def choose(flag, first, second):
    return pl.pallas_call(
        choose_kernel,
        out_shape=jax.ShapeDtypeStruct(first.shape, first.dtype),
        in_specs=[SCALAR, ANYWHERE, ANYWHERE],
        out_specs=WHOLE,
        scratch_shapes=[pltpu.SemaphoreType.DMA],
        compiler_params=pltpu.CompilerParams(vmem_limit_bytes=VMEM_LIMIT),
        cost_estimate=pl.CostEstimate(flops=0, bytes_accessed=2 * first.size * 2, transcendentals=0),
    )(flag, first, second)


def after(value, *landed):
    return lax.optimization_barrier((value, landed))[0]


def kept(shape, dtype):
    return pltpu.VMEM(shape, dtype)


def in_vmem(array):
    return pltpu.with_memory_space_constraint(array, pltpu.VMEM)


def ids(scalars, which, rows):
    return scalars[which] + lax.broadcasted_iota(jnp.int32, (1, rows), 1)


def side_by_side(first, second):
    return jnp.concatenate([first, second], axis=1)


def score_kernel(count, start, stats, factor, scalars, *refs):
    mine = refs[:2]
    shards = refs[2 : 2 + count]
    rest = list(refs[2 + count :])
    *side, out, right, info, left, sems = rest
    copies = fetch(mine, left, sems) + fetch(shards, right, sems.at[pl.ds(2, count)])
    for copy in copies[:2]:
        copy.wait()
    rows = mine[0].shape[0]
    pair = 2 * rows
    lhs = left[...]
    row_parts = []
    if not stats:
        info[...] = jnp.zeros(info.shape, F32)
    elif start:
        info[...] = side[0][...]
    waiting = copies[2:]
    ends = [sum(shard.shape[0] for shard in shards[: i + 1]) for i in range(count)]
    for p in range(ends[-1] // pair):
        while waiting and ends[-len(waiting)] - shards[-len(waiting)].shape[0] < (p + 1) * pair:
            waiting.pop(0).wait()
        s = lax.dot_general(
            lhs, right[pl.ds(p * pair, pair), :], NT, preferred_element_type=F32
        ) * factor
        out[:, pl.ds(p * pair, pair)] = s
        if stats:
            col_max = jnp.max(s, axis=0, keepdims=True)
            col = col_max + jnp.log(jnp.sum(jnp.exp(s - col_max), axis=0, keepdims=True))
            row_max = jnp.max(s, axis=1, keepdims=True)
            row_sum = jnp.sum(jnp.exp(s - row_max), axis=1, keepdims=True)
            row_parts.append(row_max + jnp.log(row_sum))
            info[pl.ds(start + p, 1), :] = col
            if start + p == 0:
                chosen = as_column(side_by_side(side[0][...], side[1][...]))
                hit = chosen == side_by_side(ids(scalars, 1, rows), ids(scalars, 2, rows))
                info[pl.ds(5, 1), :] = as_row(jnp.sum(jnp.where(hit, s, 0.0), axis=1, keepdims=True))
    if stats:
        row = as_row(log_join(*row_parts) if len(row_parts) > 1 else row_parts[0])
        if start:
            row = log_join(row, side[0][pl.ds(4, 1), :])
        else:
            info[pl.ds(2, 2), :] = jnp.zeros((2, pair), F32)
            info[pl.ds(6, 2), :] = jnp.zeros((2, pair), F32)
        info[pl.ds(4, 1), :] = row


def score(scalars, mine, shards, start, stats, factor, side=()):
    rows, width = mine[0].shape
    tokens = sum(shard.shape[0] for shard in shards) // rows
    info = (8, 2 * rows) if stats else (8, 128)
    shapes = [
        kept((2 * rows, tokens * rows), F32),
        kept((tokens * rows, width), jnp.bfloat16),
        jax.ShapeDtypeStruct(info, F32),
    ]
    return pl.pallas_call(
        functools.partial(score_kernel, len(shards), start, stats, factor),
        out_shape=tuple(shapes),
        in_specs=[SCALAR] + [ANYWHERE] * (2 + len(shards)) + [WHOLE] * len(side),
        out_specs=(WHOLE,) * len(shapes),
        scratch_shapes=[
            pltpu.VMEM((2 * rows, width), jnp.bfloat16),
            pltpu.SemaphoreType.DMA((2 + len(shards),)),
        ],
        compiler_params=pltpu.CompilerParams(vmem_limit_bytes=VMEM_LIMIT),
        cost_estimate=pl.CostEstimate(
            flops=4 * rows * rows * tokens * width,
            bytes_accessed=(tokens + 2) * rows * width * 2 + 8 * rows * rows * tokens,
            transcendentals=4 * rows * rows * tokens if stats else 0,
        ),
    )(scalars, *mine, *shards, *side)


def halves(line):
    n = line.shape[1] // 2
    return line[:, :n], line[:, n:]


def by_shard(lines):
    p = [halves(line) for line in lines]
    return [p[0][0], p[0][1], p[1][0], p[2][0], p[1][1], p[3][0], p[2][1], p[3][1]]


def chain_kernel(scalars, own, beside, far, ahead, behind, out):
    even = scalars[0] == 1
    size = own.shape[0]

    def pick(first, second):
        return jnp.where(even, first, second)

    def line(d, i):
        one = lambda ref, at=0: ref[pl.ds(at + i, 1), :]
        if d == 0:
            return one(own)
        if d in (2, -2):
            return one(ahead if d == 2 else behind)
        if d == 1:
            return pick(one(beside), one(ahead, size))
        if d == -1:
            return pick(one(behind, size), one(beside))
        if d == 3:
            return pick(one(ahead, size), one(far))
        return pick(one(far), one(behind, size))

    shards = {d: by_shard([line(d, i) for i in range(4)]) for d in range(-3, 4)}

    def total(step, half):
        parts = []
        for other in range(4):
            d = other - step
            if other % 2 == 0:
                parts.append(shards[d][other + half])
            else:
                c, e = shards[d][4 + half], shards[d][6 + half]
                c_first = (other == 1) == (d % 2 == 0)
                parts.append(pick(c, e) if c_first else pick(e, c))
        return log_join(*parts)

    sums = [[total(step, half) for half in range(2)] for step in range(4)]
    for half in range(2):
        out[pl.ds(half, 1), :] = sums[0][half]
        out[pl.ds(2 + half, 1), :] = sums[2][half]
        out[pl.ds(4 + half, 1), :] = pick(sums[1][half], sums[3][half])
        out[pl.ds(6 + half, 1), :] = pick(sums[3][half], sums[1][half])
    row = {d: halves(line(d, 4)) for d in range(4)}
    for half in range(2):
        at = 8 + 4 * half
        out[pl.ds(at, 1), :] = row[0][half]
        out[pl.ds(at + 1, 1), :] = row[2][half]
        out[pl.ds(at + 2, 1), :] = pick(row[3][half], row[1][half])
        out[pl.ds(at + 3, 1), :] = pick(row[1][half], row[3][half])
    positive = halves(line(0, 5))
    out[pl.ds(16, 1), :] = positive[0]
    out[pl.ds(17, 1), :] = positive[1]
    out[pl.ds(18, 6), :] = jnp.zeros((6, out.shape[1]), F32)


def block_kernel(scalars, partner, own, across, core, corner, col_out, row_out, loss_out):
    line = lambda ref, i: ref[pl.ds(i, 1), :]
    col = [[log_join(line(own, 2 * i + h), line(across, 2 * i + 1 - h)) for h in range(2)] for i in range(4)]
    core_col = [log_join(line(core, h), line(corner, 1 - h)) for h in range(2)]
    row = [
        [log_join(line(own, 8 + i), line(core, 12 + i)), log_join(line(across, 8 + i), line(corner, 12 + i))]
        for i in range(4)
    ]
    core_row = log_join(line(own, 12), line(core, 8))
    zeros = jnp.zeros((3, col_out.shape[1]), F32)
    for out, part, more in ((col_out, col, core_col[0]), (row_out, row, core_row)):
        a, b, c, d = part
        out[pl.ds(0, 1), :] = side_by_side(a[0], a[1])
        out[pl.ds(1, 1), :] = side_by_side(b[0], c[0])
        out[pl.ds(2, 1), :] = side_by_side(b[1], d[0])
        out[pl.ds(3, 1), :] = side_by_side(c[1], d[1])
        out[pl.ds(4, 1), :] = side_by_side(a[0], more)
        out[pl.ds(5, 3), :] = zeros
    chosen = as_column(partner[...])
    found = jnp.zeros(chosen.shape, F32)
    for i, value in enumerate((col[0][0], col[0][1], core_col[0], core_col[1])):
        hit = chosen == ids(scalars, i + 1, value.shape[1])
        found = found + jnp.sum(jnp.where(hit, value, 0.0), axis=1, keepdims=True)
    score = line(own, 16) + line(core, 17)
    loss_out[...] = (0.5 * row[0][0] + 0.5 * as_row(found) - score)[0]


def small_call(kernel, shapes, *args, scalars=0):
    return pl.pallas_call(
        kernel,
        out_shape=tuple(jax.ShapeDtypeStruct(s, F32) for s in shapes),
        in_specs=[SCALAR] * scalars + [WHOLE] * (len(args) - scalars),
        out_specs=(WHOLE,) * len(shapes),
        compiler_params=pltpu.CompilerParams(vmem_limit_bytes=VMEM_LIMIT),
        cost_estimate=pl.CostEstimate(flops=100000, bytes_accessed=400000, transcendentals=20000),
    )(*args)


def grad_kernel(keys, factor, scalars, first, second, row_info, col_info, *refs):
    rows = first.shape[1]
    pair = 2 * rows
    *made, own_out, other_out, weights = refs
    made = list(zip(made[::2], made[1::2]))
    row = as_column(row_info[pl.ds(4, 1), :])
    partners = side_by_side(first[...], second[...])
    across = side_by_side(ids(scalars, 1, rows), ids(scalars, 2, rows))
    if keys:
        row_ids, col_ids = as_column(side_by_side(ids(scalars, 1, rows), ids(scalars, 3, rows))), partners
    else:
        row_ids, col_ids = as_column(partners), across

    def weigh(p, group, s):
        here = slice(group * rows, (group + 1) * rows)
        w = 0.5 * jnp.exp(s - row[here]) + 0.5 * jnp.exp(s - col_info[pl.ds(p, 1), :])
        if p == 0:
            w = w - jnp.where(row_ids[here] == col_ids, 1.0, 0.0)
        weights[pl.ds(group * rows, rows), pl.ds(p * pair, pair)] = w.astype(jnp.bfloat16)

    p = 0
    for scores, _ in made:
        for at in range(0, scores.shape[1], pair):
            for group in (1, 0):
                weigh(p, group, scores[pl.ds(group * rows, rows), pl.ds(at, pair)])
            p += 1
    for group, out in ((1, other_out), (0, own_out)):
        there = pl.ds(group * rows, rows)
        total, at = None, 0
        for _, held in made:
            span = held.shape[0]
            part = jnp.dot(weights[there, pl.ds(at, span)], held[...], preferred_element_type=F32)
            total = part if total is None else total + part
            at += span
        out[...] = total * factor


def grad(scalars, keys, factor, first, second, row_info, col_info, made):
    rows, width = first.shape[1], made[0][1].shape[1]
    made = [in_vmem(array) for part in made for array in part]
    return pl.pallas_call(
        functools.partial(grad_kernel, keys, factor),
        out_shape=(kept((rows, width), F32), kept((rows, width), F32)),
        in_specs=[SCALAR] + [WHOLE] * (4 + len(made)),
        out_specs=(WHOLE,) * 2,
        scratch_shapes=[pltpu.VMEM((2 * rows, 8 * rows), jnp.bfloat16)],
        compiler_params=pltpu.CompilerParams(vmem_limit_bytes=VMEM_LIMIT),
        cost_estimate=pl.CostEstimate(
            flops=32 * rows * rows * width,
            bytes_accessed=8 * rows * width * 2 + 64 * rows * rows + rows * width * 8,
            transcendentals=32 * rows * rows,
        ),
    )(scalars, first, second, row_info, col_info, *made)


def add_kernel(own, received, out, total, sems):
    parts = sems.shape[0]
    step = own.shape[0] // parts
    writes = []
    for i in range(parts):
        here = pl.ds(i * step, step)
        total[here, :] = own[here, :] + received[here, :]
        writes.append(pltpu.make_async_copy(total.at[here], out.at[here], sems.at[i]))
        writes[-1].start()
    for write in writes:
        write.wait()


def add(own, received):
    return pl.pallas_call(
        add_kernel,
        out_shape=jax.ShapeDtypeStruct(own.shape, F32),
        in_specs=[WHOLE] * 2,
        out_specs=ANYWHERE,
        scratch_shapes=[pltpu.VMEM(own.shape, F32), pltpu.SemaphoreType.DMA((4,))],
        compiler_params=pltpu.CompilerParams(vmem_limit_bytes=VMEM_LIMIT),
        cost_estimate=pl.CostEstimate(flops=own.size, bytes_accessed=12 * own.size, transcendentals=0),
    )(in_vmem(own), in_vmem(received))


def local(query_rows, key_rows, partner):
    rows, features = query_rows.shape
    factor = float(features) ** (-0.5)
    block = lax.axis_index("blk")
    place = lax.axis_index("pb")
    even = block % 2 == 0
    starts = [(place ^ other) * rows for other in (0, 2, 1, 3)]
    scalars = jnp.stack([even.astype(jnp.int32), *starts])
    pick = functools.partial(choose, scalars)

    across = lambda a: shift(a, PART_AXIS, lambda i: i ^ 2)
    core = lambda a: shift(a, PART_AXIS, lambda i: i ^ 1)
    corner = lambda a: shift(a, PART_AXIS, lambda i: i ^ 3)
    beside = lambda a, among=None: shift(a, BLOCK_AXIS, lambda i: i ^ 1, among)
    ahead = lambda a: shift(a, BLOCK_AXIS, lambda i: i + 2)
    back = lambda a: shift(a, BLOCK_AXIS, lambda i: i - 2)
    apart = lambda a: shift(a, BLOCK_AXIS, lambda i: i + 2 if i % 2 == 0 else i - 2)

    k0, q0 = key_rows, query_rows
    kz, partner_core, partner_across = ahead(k0), core(partner), across(partner)
    kx = across(after(k0, partner_across))
    y1_odd = beside(after(k0, partner_core), lambda i: i % 2 == 0)
    y1_even = beside(after(q0, partner_core), lambda i: i % 2 == 1)
    ks, qs = core(k0), core(q0)

    qx = across(after(q0, kx))
    kzy = beside(after(kz, y1_odd, y1_even))
    qz = back(after(q0, kz))

    kzx = across(after(kz, qx))
    qzy = beside(after(qz, kzy))
    m1 = apart(after(pick(kzy, qx), qz))

    kd0 = pick(m1, y1_odd)
    kzxy = beside(after(kzx, qzy))
    m2 = back(after(pick(qx, qzy), m1))
    qd0, qzx = pick(y1_even, m2), pick(m2, m1)

    mine = (q0, qs)
    *k_made_0, info = score(scalars, mine, (k0, kx, kz, kzy), 0, True, factor, (partner, partner_core))
    *q_made_0, tick = score(scalars, (k0, ks), (q0, qx, qz, qzy), 0, False, factor, (partner_across,))
    kd1 = across(after(kd0, kzx, info))
    *k_made_1, info = score(scalars, mine, (kzx, kd0), 2, True, factor, (info, tick))
    qd1 = across(after(qd0, info))
    *k_made_2, info = score(scalars, mine, (kzxy, kd1), 3, True, factor, (info,))

    next_to = beside(info)
    far = shift(info, BLOCK_AXIS, lambda i: i - 3 if i % 2 == 0 else i + 3)
    both = jnp.concatenate([info, next_to], axis=0)
    chain = small_call(chain_kernel, [(24, rows)], scalars, info, next_to, far, back(both), ahead(both), scalars=1)[0]
    *q_made_1, tick = score(scalars, (after(k0, next_to), ks), (qzx, qd0), 2, False, factor)
    qzxy = beside(after(qzx, next_to))
    chain = after(chain, qd1)
    col_info, row_info, loss = small_call(
        block_kernel,
        [(8, 2 * rows), (8, 2 * rows), (rows,)],
        scalars, partner, chain, across(chain), core(chain), corner(chain),
        scalars=1,
    )
    *q_made_2, _ = score(scalars, (k0, ks), (qzxy, qd1), 3, False, factor)
    q_own, q_other = grad(
        scalars, False, factor, partner, partner_core, row_info, col_info, (k_made_0, k_made_1, k_made_2)
    )
    k_own, k_other = grad(
        scalars, True, factor, partner, partner_across, col_info, row_info, (q_made_0, q_made_1, q_made_2)
    )
    grad_queries = add(q_own, core(q_other))
    grad_keys = add(k_own, core(k_other))
    return (loss, grad_queries, grad_keys)


def solution(mesh):
    return jax.shard_map(
        local,
        mesh=mesh,
        in_specs=(P(("blk", "pb"), None), P(("blk", "pb"), None), P("blk", "pb")),
        out_specs=(P(("blk", "pb")), P(("blk", "pb"), None), P(("blk", "pb"), None)),
        check_vma=False,
    )
```

time: 124 us -> 114 us (0.919)
  waiting for transfers between devices: 46.2 us -> 38.6 us
  other arithmetic: 5.72 us -> 0 us
  Pallas kernels: 38.3 us -> 43 us
    ppermute x29 -> x28, waiting for transfers between devices: 46.2 us -> 38.6 us  [shift(): return lax.ppermute(array, axis, pairs)]
    add x2 -> x0, other arithmetic: 5.13 us -> none  [the longest x1 2.56 us: local(): grad_queries = q_own + core(q_other)]
    pallas_call x5 -> x10, Pallas kernels: 32.5 us -> 36.9 us  [the longest x6 24 us: score(): pl.pallas_call(functools.partial(score_kernel, len(shards), start, stats,...]
    ppermute x29 -> x28, starting transfers between devices: 31.4 us -> 30.3 us  [shift(): return lax.ppermute(array, axis, pairs)]
    pallas_call x6 -> x5, Pallas kernels: 4.61 us -> 3.84 us  [choose(): pl.pallas_call(choose_kernel, out_shape=jax.ShapeDtypeStruct(first.shape,...]
  transfers between devices with their start and end apart: 29 -> 28, of which waited for: 9 -> 11; matrix products, arithmetic and copies ran while one was open for 3% -> 0% of each run, Pallas kernels for 30% -> 31%
where the time goes in v5:
time: 114 us
  Pallas kernels  43 us (38%)
  waiting for transfers between devices  38.6 us (34%)
  starting transfers between devices  30.3 us (27%)
    ppermute x28, waiting for transfers between devices, shift(): return lax.ppermute(array, axis, pairs)  38.6 us
    ppermute x28, starting transfers between devices, shift(): return lax.ppermute(array, axis, pairs)  30.3 us
    pallas_call x6, Pallas kernels, score(): pl.pallas_call(functools.partial(score_kernel, len(shards), start, stats,...  24 us
    pallas_call x2, Pallas kernels, grad(): pl.pallas_call(functools.partial(grad_kernel, keys, factor), out_shape=(k...  10.6 us
    pallas_call x5, Pallas kernels, choose(): pl.pallas_call(choose_kernel, out_shape=jax.ShapeDtypeStruct(first.shape,...  3.84 us
    pallas_call x2, Pallas kernels, small_call(): pl.pallas_call(kernel, out_shape=tuple((jax.ShapeDtypeStruct(s, F32) for...  2.29 us
  transfers between devices with their start and end apart: 28, of which 11 were waited for; matrix products, arithmetic and copies ran while one was open for 0% of the time, Pallas kernels for 31%

profile of v5, /device:TPU:0, one launch (start us, length us, event | category | flops | bytes accessed | tf_op | source)
XLA Modules:
  0.0 113.9 jit_solution(5968198924283859132)
XLA Ops:
  1.2 2.6 %collective-permute-start.2 = (s32[1,320]{1,0:T(1,128)}, s32[1,320]{1,0:T(1,128)S(1)}, u32[]{:S(2)}, u32[]{:S(2)}) collective-permute-start(s32[1,320]{1,0:T(1,128)} %first.3), channel_id=1, source_target_pairs={{0,2},{1,3},{2,0},{3,1},{4,6},{5,7},{6,4},{7,5},{8,10},{9,11},{10,... | collective-permute-start | bytes 3848 | tf_op jit(solution)/shard_map/ppermute | solution.py:22
  3.7 1.6 %collective-permute-start.1 = (bf16[320,1024]{1,0:T(8,128)(2,1)}, bf16[320,1024]{1,0:T(8,128)(2,1)}, u32[]{:S(2)}, u32[]{:S(2)}) collective-permute-start(bf16[320,1024]{1,0:T(8,128)(2,1)} %refs_0_.10), channel_id=1, source_target_pairs={{0,8},{4,12},{8,16},{12,20},{16,24},{20,28},{24,0},{28,4},{1,9},{5... | collective-permute-start | bytes 1966088 | tf_op jit(solution)/shard_map/ppermute | solution.py:22
  5.5 2.0 %collective-permute-start.3 = (bf16[320,1024]{1,0:T(8,128)(2,1)}, bf16[320,1024]{1,0:T(8,128)(2,1)S(1)}, u32[]{:S(2)}, u32[]{:S(2)}) collective-permute-start(bf16[320,1024]{1,0:T(8,128)(2,1)} %refs_0_.10), channel_id=1, source_target_pairs={{0,2},{1,3},{2,0},{3,1},{4,6},{5,7},{6,4},{7,5},{8,10},{9,11},{10,... | collective-permute-start | bytes 1966088 | tf_op jit(solution)/shard_map/ppermute | solution.py:22
  7.5 3.5 %collective-permute-start.8 = (bf16[320,1024]{1,0:T(8,128)(2,1)}, bf16[320,1024]{1,0:T(8,128)(2,1)S(1)}, u32[]{:S(2)}, u32[]{:S(2)}) collective-permute-start(bf16[320,1024]{1,0:T(8,128)(2,1)} %refs_0_.10), channel_id=1, source_target_pairs={{0,4},{8,12},{16,20},{24,28},{1,5},{9,13},{17,21},{25,29},{2,6},{1... | collective-permute-start | bytes 1966088 | tf_op jit(solution)/shard_map/ppermute | solution.py:22
  11.0 1.3 %collective-permute-start.9 = (bf16[320,1024]{1,0:T(8,128)(2,1)}, bf16[320,1024]{1,0:T(8,128)(2,1)S(1)}, u32[]{:S(2)}, u32[]{:S(2)}) collective-permute-start(bf16[320,1024]{1,0:T(8,128)(2,1)} %refs_0_.8), channel_id=1, source_target_pairs={{4,0},{12,8},{20,16},{28,24},{5,1},{13,9},{21,17},{29,25},{6,2},{1... | collective-permute-start | bytes 1966088 | tf_op jit(solution)/shard_map/ppermute | solution.py:22
  12.3 10.4 %collective-permute-done.1.refs_4_ = bf16[320,1024]{1,0:T(8,128)(2,1)} collective-permute-done((bf16[320,1024]{1,0:T(8,128)(2,1)}, bf16[320,1024]{1,0:T(8,128)(2,1)}, u32[]{:S(2)}, u32[]{:S(2)}) %collective-permute-start.1) | collective-permute-done | bytes 655392 | tf_op jit(solution)/shard_map/ppermute | solution.py:22
  22.7 1.7 %collective-permute-start.6 = (bf16[320,1024]{1,0:T(8,128)(2,1)}, bf16[320,1024]{1,0:T(8,128)(2,1)}, u32[]{:S(2)}, u32[]{:S(2)}) collective-permute-start(bf16[320,1024]{1,0:T(8,128)(2,1)} %refs_0_.8), channel_id=1, source_target_pairs={{0,24},{4,28},{8,0},{12,4},{16,8},{20,12},{24,16},{28,20},{1,25},{... | collective-permute-start | bytes 1966088 | tf_op jit(solution)/shard_map/ppermute | solution.py:22
  24.5 0.8 copy-done.3
  25.3 0.5 collective-permute-start.4
  25.8 2.6 %collective-permute-done.9.first = bf16[320,1024]{1,0:T(8,128)(2,1)S(1)} collective-permute-done((bf16[320,1024]{1,0:T(8,128)(2,1)}, bf16[320,1024]{1,0:T(8,128)(2,1)S(1)}, u32[]{:S(2)}, u32[]{:S(2)}) %collective-permute-start.9) | collective-permute-done | bytes 655392 | tf_op jit(solution)/shard_map/ppermute | solution.py:22
  28.6 12.6 %collective-permute-done.4.second.refs_3_.first = bf16[320,1024]{1,0:T(8,128)(2,1)S(1)} collective-permute-done((bf16[320,1024]{1,0:T(8,128)(2,1)}, bf16[320,1024]{1,0:T(8,128)(2,1)S(1)}, u32[]{:S(2)}, u32[]{:S(2)}) %collective-permute-start.4) | collective-permute-done | bytes 655392 | tf_op jit(solution)/shard_map/ppermute | solution.py:22
  41.2 0.5 collective-permute-start.5
  41.7 1.6 %collective-permute-done.10.first.refs_5_ = bf16[320,1024]{1,0:T(8,128)(2,1)S(1)} collective-permute-done((bf16[320,1024]{1,0:T(8,128)(2,1)}, bf16[320,1024]{1,0:T(8,128)(2,1)S(1)}, u32[]{:S(2)}, u32[]{:S(2)}) %collective-permute-start.10) | collective-permute-done | bytes 655392 | tf_op jit(solution)/shard_map/ppermute | solution.py:22
  43.4 0.8 shard_map.58
  44.2 1.7 %collective-permute-start.13 = (bf16[320,1024]{1,0:T(8,128)(2,1)S(1)}, bf16[320,1024]{1,0:T(8,128)(2,1)S(1)}, u32[]{:S(2)}, u32[]{:S(2)}) collective-permute-start(bf16[320,1024]{1,0:T(8,128)(2,1)S(1)} %shard_map.58), channel_id=1, source_target_pairs={{0,8},{4,28},{8,16},{12,4},{16,24},{20,12},{24,0},{28,20},{1,9},{5... | collective-permute-start | bytes 1966088 | tf_op jit(solution)/shard_map/ppermute | solution.py:22
  46.0 6.2 %shard_map.60 = (f32[640,1280]{1,0:T(8,128)S(1)}, bf16[1280,1024]{1,0:T(8,128)(2,1)S(1)}, f32[8,640]{1,0:T(8,128)S(1)}) custom-call(s32[5]{0:T(128)S(1)} %stack.27.flag.scalars, bf16[320,1024]{1,0:T(8,128)(2,1)S(1)} %copy-done.1, bf16[320,1024]{1,0:T(8,128)(2,1)} %collective-permute-done.refs_1_, bf16[320,1024]{1,0:T(8,128)(2,1)S(1)} %copy-done.2, ...), custom_call_target="tpu_custom_call" | custom-call | flops 1677721600 | bytes 7208960 | tf_op jit(solution)/shard_map/pallas_call | solution.py:148
  52.2 4.0 %collective-permute-done.5.refs_2_ = bf16[320,1024]{1,0:T(8,128)(2,1)S(1)} collective-permute-done((bf16[320,1024]{1,0:T(8,128)(2,1)}, bf16[320,1024]{1,0:T(8,128)(2,1)S(1)}, u32[]{:S(2)}, u32[]{:S(2)}) %collective-permute-start.5) | collective-permute-done | bytes 655392 | tf_op jit(solution)/shard_map/ppermute | solution.py:22
  56.2 1.0 collective-permute-done.11.refs_5_.second
  57.2 0.8 collective-permute-start.12
  58.0 2.2 %collective-permute-done.13.first.second = bf16[320,1024]{1,0:T(8,128)(2,1)S(1)} collective-permute-done((bf16[320,1024]{1,0:T(8,128)(2,1)S(1)}, bf16[320,1024]{1,0:T(8,128)(2,1)S(1)}, u32[]{:S(2)}, u32[]{:S(2)}) %collective-permute-start.13) | collective-permute-done | bytes 655392 | tf_op jit(solution)/shard_map/ppermute | solution.py:22
  60.1 0.8 shard_map.59.refs_3_
  60.9 1.6 %collective-permute-start.14 = (bf16[320,1024]{1,0:T(8,128)(2,1)S(1)}, bf16[320,1024]{1,0:T(8,128)(2,1)S(1)}, u32[]{:S(2)}, u32[]{:S(2)}) collective-permute-start(bf16[320,1024]{1,0:T(8,128)(2,1)S(1)} %shard_map.59.refs_3_), channel_id=1, source_target_pairs={{0,2},{1,3},{2,0},{3,1},{4,6},{5,7},{6,4},{7,5},{8,10},{9,11},{10,... | collective-permute-start | bytes 1966088 | tf_op jit(solution)/shard_map/ppermute | solution.py:22
  62.5 0.8 shard_map.65
  63.3 1.1 collective-permute-start.20
  64.3 4.8 %shard_map.61 = (f32[640,1280]{1,0:T(8,128)S(1)}, bf16[1280,1024]{1,0:T(8,128)(2,1)S(1)}, f32[8,128]{1,0:T(8,128)S(1)}) custom-call(s32[5]{0:T(128)S(1)} %stack.27.flag.scalars, bf16[320,1024]{1,0:T(8,128)(2,1)S(1)} %copy-done.2, bf16[320,1024]{1,0:T(8,128)(2,1)S(1)} %collective-permute-done.15.refs_1_, bf16[320,1024]{1,0:T(8,128)(2,1)S(1)} %copy-done.1, ...), custom_call_target="tpu_custom_call" | custom-call | flops 1677721600 | bytes 7208960 | tf_op jit(solution)/shard_map/pallas_call | solution.py:148
  69.1 3.8 %shard_map.62 = (f32[640,640]{1,0:T(8,128)S(1)}, bf16[640,1024]{1,0:T(8,128)(2,1)S(1)}, f32[8,640]{1,0:T(8,128)S(1)}) custom-call(s32[5]{0:T(128)S(1)} %stack.27.flag.scalars, bf16[320,1024]{1,0:T(8,128)(2,1)S(1)} %copy-done.1, bf16[320,1024]{1,0:T(8,128)(2,1)} %collective-permute-done.refs_1_, bf16[320,1024]{1,0:T(8,128)(2,1)S(1)} %collective-permute-done.5.refs_2_, ...), custom_call_target="tpu_custom_call" | custom-call | flops 838860800 | bytes 4259840 | tf_op jit(solution)/shard_map/pallas_call | solution.py:148
  72.9 1.1 %collective-permute-done.14.refs_3_ = bf16[320,1024]{1,0:T(8,128)(2,1)S(1)} collective-permute-done((bf16[320,1024]{1,0:T(8,128)(2,1)S(1)}, bf16[320,1024]{1,0:T(8,128)(2,1)S(1)}, u32[]{:S(2)}, u32[]{:S(2)}) %collective-permute-start.14) | collective-permute-done | bytes 655392 | tf_op jit(solution)/shard_map/ppermute | solution.py:22
  74.1 3.8 %shard_map.63 = (f32[640,640]{1,0:T(8,128)S(1)}, bf16[640,1024]{1,0:T(8,128)(2,1)S(1)}, f32[8,640]{1,0:T(8,128)S(1)}) custom-call(s32[5]{0:T(128)S(1)} %stack.27.flag.scalars, bf16[320,1024]{1,0:T(8,128)(2,1)S(1)} %copy-done.1, bf16[320,1024]{1,0:T(8,128)(2,1)} %collective-permute-done.refs_1_, bf16[320,1024]{1,0:T(8,128)(2,1)S(1)} %collective-permute-done.12.refs_2_, ...), custom_call_target="tpu_custom_call" | custom-call | flops 838860800 | bytes 4259840 | tf_op jit(solution)/shard_map/pallas_call | solution.py:148
  77.9 1.4 %collective-permute-start.16 = (f32[8,640]{1,0:T(8,128)S(1)}, f32[8,640]{1,0:T(8,128)S(1)}, u32[]{:S(2)}, u32[]{:S(2)}) collective-permute-start(f32[8,640]{1,0:T(8,128)S(1)} %get-tuple-element.56.own), channel_id=1, source_target_pairs={{0,4},{4,0},{8,12},{12,8},{16,20},{20,16},{24,28},{28,24},{1,5},{5... | collective-permute-start | bytes 61448 | tf_op jit(solution)/shard_map/ppermute | solution.py:22
  79.3 0.8 shard_map.66.refs_3_
  80.1 1.6 %collective-permute-start.21 = (bf16[320,1024]{1,0:T(8,128)(2,1)S(1)}, bf16[320,1024]{1,0:T(8,128)(2,1)S(1)}, u32[]{:S(2)}, u32[]{:S(2)}) collective-permute-start(bf16[320,1024]{1,0:T(8,128)(2,1)S(1)} %shard_map.66.refs_3_), channel_id=1, source_target_pairs={{0,2},{1,3},{2,0},{3,1},{4,6},{5,7},{6,4},{7,5},{8,10},{9,11},{10,... | collective-permute-start | bytes 1966088 | tf_op jit(solution)/shard_map/ppermute | solution.py:22
  81.7 0.8 shard_map.70.refs_2_
  82.4 1.2 %collective-permute-start.26 = (bf16[320,1024]{1,0:T(8,128)(2,1)S(1)}, bf16[320,1024]{1,0:T(8,128)(2,1)S(1)}, u32[]{:S(2)}, u32[]{:S(2)}) collective-permute-start(bf16[320,1024]{1,0:T(8,128)(2,1)S(1)} %shard_map.70.refs_2_), channel_id=1, source_target_pairs={{0,4},{4,0},{8,12},{12,8},{16,20},{20,16},{24,28},{28,24},{1,5},{5... | collective-permute-start | bytes 1966088 | tf_op jit(solution)/shard_map/ppermute | solution.py:22
  83.7 2.0 %collective-permute-start.19 = (f32[16,640]{1,0:T(8,128)S(1)}, f32[16,640]{1,0:T(8,128)S(1)}, u32[]{:S(2)}, u32[]{:S(2)}) collective-permute-start(f32[16,640]{1,0:T(8,128)S(1)} %constant_dynamic-update-slice_fusion), channel_id=1, source_target_pairs={{0,8},{4,12},{8,16},{12,20},{16,24},{20,28},{24,0},{28,4},{1,9},{5... | collective-permute-start | bytes 122888 | tf_op jit(solution)/shard_map/ppermute | solution.py:22
  85.7 1.8 %collective-permute-start.18 = (f32[16,640]{1,0:T(8,128)S(1)}, f32[16,640]{1,0:T(8,128)S(1)}, u32[]{:S(2)}, u32[]{:S(2)}) collective-permute-start(f32[16,640]{1,0:T(8,128)S(1)} %constant_dynamic-update-slice_fusion), channel_id=1, source_target_pairs={{0,24},{4,28},{8,0},{12,4},{16,8},{20,12},{24,16},{28,20},{1,25},{... | collective-permute-start | bytes 122888 | tf_op jit(solution)/shard_map/ppermute | solution.py:22
  87.6 2.7 %shard_map.71 = (f32[640,640]{1,0:T(8,128)S(1)}, bf16[640,1024]{1,0:T(8,128)(2,1)S(1)}, f32[8,128]{1,0:T(8,128)}) custom-call(s32[5]{0:T(128)S(1)} %stack.27.flag.scalars, bf16[320,1024]{1,0:T(8,128)(2,1)S(1)} %copy-done.2, bf16[320,1024]{1,0:T(8,128)(2,1)S(1)} %collective-permute-done.15.refs_1_, bf16[320,1024]{1,0:T(8,128)(2,1)S(1)} %shard_map.70.refs_2_, ...), custom_call_target="tpu_custom_call" | custom-call | flops 838860800 | bytes 4259840 | tf_op jit(solution)/shard_map/pallas_call | solution.py:148
  90.3 0.7 shard_map.64.own
  91.0 1.2 %collective-permute-done.21.refs_3_ = bf16[320,1024]{1,0:T(8,128)(2,1)S(1)} collective-permute-done((bf16[320,1024]{1,0:T(8,128)(2,1)S(1)}, bf16[320,1024]{1,0:T(8,128)(2,1)S(1)}, u32[]{:S(2)}, u32[]{:S(2)}) %collective-permute-start.21) | collective-permute-done | bytes 655392 | tf_op jit(solution)/shard_map/ppermute | solution.py:22
  92.2 0.8 collective-permute-start.23
  93.0 1.3 %collective-permute-start.22 = (f32[24,320]{1,0:T(8,128)S(1)}, f32[24,320]{1,0:T(8,128)S(1)}, u32[]{:S(2)}, u32[]{:S(2)}) collective-permute-start(f32[24,320]{1,0:T(8,128)S(1)} %shard_map.64.own), channel_id=1, source_target_pairs={{0,2},{1,3},{2,0},{3,1},{4,6},{5,7},{6,4},{7,5},{8,10},{9,11},{10,... | collective-permute-start | bytes 92168 | tf_op jit(solution)/shard_map/ppermute | solution.py:22
  94.3 2.7 %shard_map.72 = (f32[640,640]{1,0:T(8,128)S(1)}, bf16[640,1024]{1,0:T(8,128)(2,1)S(1)}, f32[8,128]{1,0:T(8,128)}) custom-call(s32[5]{0:T(128)S(1)} %stack.27.flag.scalars, bf16[320,1024]{1,0:T(8,128)(2,1)S(1)} %copy-done.2, bf16[320,1024]{1,0:T(8,128)(2,1)S(1)} %collective-permute-done.15.refs_1_, bf16[320,1024]{1,0:T(8,128)(2,1)S(1)} %collective-permute-done.26.refs_2_, ...), custom_call_target="tpu_custom_call" | custom-call | flops 838860800 | bytes 4259840 | tf_op jit(solution)/shard_map/pallas_call | solution.py:148
  97.1 1.6 %shard_map.67 = (f32[8,640]{1,0:T(8,128)S(1)}, f32[8,640]{1,0:T(8,128)S(1)}, f32[320]{0:T(512)}) custom-call(s32[5]{0:T(128)S(1)} %stack.27.flag.scalars, s32[1,320]{1,0:T(1,128)S(1)} %copy-done, f32[24,320]{1,0:T(8,128)S(1)} %shard_map.64.own, f32[24,320]{1,0:T(8,128)S(1)} %collective-permute-done.22.across, f32[24,320]{1,0:T(8,128)S(1)} %collective-permute-done.23.core, ...), custom_call_target="tpu_custom_call" | custom-call | flops 100000 | bytes 400000 | tf_op jit(solution)/shard_map/pallas_call | solution.py:258
  98.7 5.3 %shard_map.68 = (f32[320,1024]{1,0:T(8,128)S(1)}, f32[320,1024]{1,0:T(8,128)S(1)}) custom-call(s32[5]{0:T(128)S(1)} %stack.27.flag.scalars, s32[1,320]{1,0:T(1,128)S(1)} %copy-done, s32[1,320]{1,0:T(1,128)S(1)} %collective-permute-done.7.refs_7_.second, f32[8,640]{1,0:T(8,128)S(1)} %get-tuple-element.61.row_info.col_info, ...), custom_call_target="tpu_custom_call" | custom-call | flops 3355443200 | bytes 14417920 | tf_op jit(solution)/shard_map/pallas_call | solution.py:308
  104.1 5.3 %shard_map.73 = (f32[320,1024]{1,0:T(8,128)S(1)}, f32[320,1024]{1,0:T(8,128)S(1)}) custom-call(s32[5]{0:T(128)S(1)} %stack.27.flag.scalars, s32[1,320]{1,0:T(1,128)S(1)} %copy-done, s32[1,320]{1,0:T(1,128)S(1)} %collective-permute-done.2.refs_6_.second, f32[8,640]{1,0:T(8,128)S(1)} %get-tuple-element.62.col_info.row_info, ...), custom_call_target="tpu_custom_call" | custom-call | flops 3355443200 | bytes 14417920 | tf_op jit(solution)/shard_map/pallas_call | solution.py:308
  109.4 0.6 collective-permute-start.27
  110.0 1.1 shard_map.69
  111.1 1.5 %collective-permute-done.27.received = f32[320,1024]{1,0:T(8,128)S(1)} collective-permute-done((f32[320,1024]{1,0:T(8,128)S(1)}, f32[320,1024]{1,0:T(8,128)S(1)}, u32[]{:S(2)}, u32[]{:S(2)}) %collective-permute-start.27) | collective-permute-done | bytes 1310752 | tf_op jit(solution)/shard_map/ppermute | solution.py:22
  112.6 1.1 shard_map.74
  (38 shorter events, 1.1 us)
Async XLA Ops:
  0.6 45.3 %copy-start = (s32[1,320]{1,0:T(1,128)S(1)}, s32[1,320]{1,0:T(1,128)}, u32[]{:S(2)}) copy-start(s32[1,320]{1,0:T(1,128)} %first.3) | copy-start | bytes 3844
  0.6 45.3 %copy-start.1 = (bf16[320,1024]{1,0:T(8,128)(2,1)S(1)}, bf16[320,1024]{1,0:T(8,128)(2,1)}, u32[]{:S(2)}) copy-start(bf16[320,1024]{1,0:T(8,128)(2,1)} %refs_0_.8) | copy-start | bytes 1966084
  0.6 4.7 %collective-permute-start.7 = (s32[1,320]{1,0:T(1,128)}, s32[1,320]{1,0:T(1,128)S(1)}, u32[]{:S(2)}, u32[]{:S(2)}) collective-permute-start(s32[1,320]{1,0:T(1,128)} %first.3), channel_id=1, source_target_pairs={{0,1},{1,0},{2,3},{3,2},{4,5},{5,4},{6,7},{7,6},{8,9},{9,8},{10,11... | collective-permute-start | bytes 3848 | tf_op jit(solution)/shard_map/ppermute | solution.py:22
  1.2 4.3 %collective-permute-start.2 = (s32[1,320]{1,0:T(1,128)}, s32[1,320]{1,0:T(1,128)S(1)}, u32[]{:S(2)}, u32[]{:S(2)}) collective-permute-start(s32[1,320]{1,0:T(1,128)} %first.3), channel_id=1, source_target_pairs={{0,2},{1,3},{2,0},{3,1},{4,6},{5,7},{6,4},{7,5},{8,10},{9,11},{10,... | collective-permute-start | bytes 3848 | tf_op jit(solution)/shard_map/ppermute | solution.py:22
  3.7 19.0 %collective-permute-start.1 = (bf16[320,1024]{1,0:T(8,128)(2,1)}, bf16[320,1024]{1,0:T(8,128)(2,1)}, u32[]{:S(2)}, u32[]{:S(2)}) collective-permute-start(bf16[320,1024]{1,0:T(8,128)(2,1)} %refs_0_.10), channel_id=1, source_target_pairs={{0,8},{4,12},{8,16},{12,20},{16,24},{20,28},{24,0},{28,4},{1,9},{5... | collective-permute-start | bytes 1966088 | tf_op jit(solution)/shard_map/ppermute | solution.py:22
  5.5 19.0 %collective-permute-start.3 = (bf16[320,1024]{1,0:T(8,128)(2,1)}, bf16[320,1024]{1,0:T(8,128)(2,1)S(1)}, u32[]{:S(2)}, u32[]{:S(2)}) collective-permute-start(bf16[320,1024]{1,0:T(8,128)(2,1)} %refs_0_.10), channel_id=1, source_target_pairs={{0,2},{1,3},{2,0},{3,1},{4,6},{5,7},{6,4},{7,5},{8,10},{9,11},{10,... | collective-permute-start | bytes 1966088 | tf_op jit(solution)/shard_map/ppermute | solution.py:22
  7.5 18.3 %collective-permute-start.8 = (bf16[320,1024]{1,0:T(8,128)(2,1)}, bf16[320,1024]{1,0:T(8,128)(2,1)S(1)}, u32[]{:S(2)}, u32[]{:S(2)}) collective-permute-start(bf16[320,1024]{1,0:T(8,128)(2,1)} %refs_0_.10), channel_id=1, source_target_pairs={{0,4},{8,12},{16,20},{24,28},{1,5},{9,13},{17,21},{25,29},{2,6},{1... | collective-permute-start | bytes 1966088 | tf_op jit(solution)/shard_map/ppermute | solution.py:22
  11.0 17.5 %collective-permute-start.9 = (bf16[320,1024]{1,0:T(8,128)(2,1)}, bf16[320,1024]{1,0:T(8,128)(2,1)S(1)}, u32[]{:S(2)}, u32[]{:S(2)}) collective-permute-start(bf16[320,1024]{1,0:T(8,128)(2,1)} %refs_0_.8), channel_id=1, source_target_pairs={{4,0},{12,8},{20,16},{28,24},{5,1},{13,9},{21,17},{29,25},{6,2},{1... | collective-permute-start | bytes 1966088 | tf_op jit(solution)/shard_map/ppermute | solution.py:22
  22.7 19.0 %collective-permute-start.6 = (bf16[320,1024]{1,0:T(8,128)(2,1)}, bf16[320,1024]{1,0:T(8,128)(2,1)}, u32[]{:S(2)}, u32[]{:S(2)}) collective-permute-start(bf16[320,1024]{1,0:T(8,128)(2,1)} %refs_0_.8), channel_id=1, source_target_pairs={{0,24},{4,28},{8,0},{12,4},{16,8},{20,12},{24,16},{28,20},{1,25},{... | collective-permute-start | bytes 1966088 | tf_op jit(solution)/shard_map/ppermute | solution.py:22
  24.5 0.8 copy-start.3
  25.3 15.9 %collective-permute-start.4 = (bf16[320,1024]{1,0:T(8,128)(2,1)}, bf16[320,1024]{1,0:T(8,128)(2,1)S(1)}, u32[]{:S(2)}, u32[]{:S(2)}) collective-permute-start(bf16[320,1024]{1,0:T(8,128)(2,1)} %refs_0_.8), channel_id=1, source_target_pairs={{0,2},{1,3},{2,0},{3,1},{4,6},{5,7},{6,4},{7,5},{8,10},{9,11},{10,... | collective-permute-start | bytes 1966088 | tf_op jit(solution)/shard_map/ppermute | solution.py:22
  28.5 14.9 %collective-permute-start.10 = (bf16[320,1024]{1,0:T(8,128)(2,1)}, bf16[320,1024]{1,0:T(8,128)(2,1)S(1)}, u32[]{:S(2)}, u32[]{:S(2)}) collective-permute-start(bf16[320,1024]{1,0:T(8,128)(2,1)} %collective-permute-done.1.refs_4_), channel_id=1, source_target_pairs={{0,4},{4,0},{8,12},{12,8},{16,20},{20,16},{24,28},{28,24},{1,5},{5... | collective-permute-start | bytes 1966088 | tf_op jit(solution)/shard_map/ppermute | solution.py:22
  28.5 17.5 %collective-permute-start = (bf16[320,1024]{1,0:T(8,128)(2,1)}, bf16[320,1024]{1,0:T(8,128)(2,1)}, u32[]{:S(2)}, u32[]{:S(2)}) collective-permute-start(bf16[320,1024]{1,0:T(8,128)(2,1)} %refs_0_.8), channel_id=1, source_target_pairs={{0,1},{1,0},{2,3},{3,2},{4,5},{5,4},{6,7},{7,6},{8,9},{9,8},{10,11... | collective-permute-start | bytes 1966088 | tf_op jit(solution)/shard_map/ppermute | solution.py:22
  28.6 17.4 %copy-start.2 = (bf16[320,1024]{1,0:T(8,128)(2,1)S(1)}, bf16[320,1024]{1,0:T(8,128)(2,1)}, u32[]{:S(2)}) copy-start(bf16[320,1024]{1,0:T(8,128)(2,1)} %refs_0_.10) | copy-start | bytes 1966084
  28.6 17.4 %copy-start.4 = (bf16[320,1024]{1,0:T(8,128)(2,1)S(1)}, bf16[320,1024]{1,0:T(8,128)(2,1)}, u32[]{:S(2)}) copy-start(bf16[320,1024]{1,0:T(8,128)(2,1)} %copy-done.3) | copy-start | bytes 1966084
  41.2 15.0 %collective-permute-start.5 = (bf16[320,1024]{1,0:T(8,128)(2,1)}, bf16[320,1024]{1,0:T(8,128)(2,1)S(1)}, u32[]{:S(2)}, u32[]{:S(2)}) collective-permute-start(bf16[320,1024]{1,0:T(8,128)(2,1)} %collective-permute-done.1.refs_4_), channel_id=1, source_target_pairs={{0,2},{1,3},{2,0},{3,1},{4,6},{5,7},{6,4},{7,5},{8,10},{9,11},{10,... | collective-permute-start | bytes 1966088 | tf_op jit(solution)/shard_map/ppermute | solution.py:22
  43.4 13.8 %collective-permute-start.11 = (bf16[320,1024]{1,0:T(8,128)(2,1)}, bf16[320,1024]{1,0:T(8,128)(2,1)S(1)}, u32[]{:S(2)}, u32[]{:S(2)}) collective-permute-start(bf16[320,1024]{1,0:T(8,128)(2,1)} %collective-permute-done.6.refs_4_), channel_id=1, source_target_pairs={{0,4},{4,0},{8,12},{12,8},{16,20},{20,16},{24,28},{28,24},{1,5},{5... | collective-permute-start | bytes 1966088 | tf_op jit(solution)/shard_map/ppermute | solution.py:22
  44.2 15.9 %collective-permute-start.13 = (bf16[320,1024]{1,0:T(8,128)(2,1)S(1)}, bf16[320,1024]{1,0:T(8,128)(2,1)S(1)}, u32[]{:S(2)}, u32[]{:S(2)}) collective-permute-start(bf16[320,1024]{1,0:T(8,128)(2,1)S(1)} %shard_map.58), channel_id=1, source_target_pairs={{0,8},{4,28},{8,16},{12,4},{16,24},{20,12},{24,0},{28,20},{1,9},{5... | collective-permute-start | bytes 1966088 | tf_op jit(solution)/shard_map/ppermute | solution.py:22
  45.9 18.4 %collective-permute-start.15 = (bf16[320,1024]{1,0:T(8,128)(2,1)S(1)}, bf16[320,1024]{1,0:T(8,128)(2,1)S(1)}, u32[]{:S(2)}, u32[]{:S(2)}) collective-permute-start(bf16[320,1024]{1,0:T(8,128)(2,1)S(1)} %copy-done.2), channel_id=1, source_target_pairs={{0,1},{1,0},{2,3},{3,2},{4,5},{5,4},{6,7},{7,6},{8,9},{9,8},{10,11... | collective-permute-start | bytes 1966088 | tf_op jit(solution)/shard_map/ppermute | solution.py:22
  57.2 15.8 %collective-permute-start.12 = (bf16[320,1024]{1,0:T(8,128)(2,1)S(1)}, bf16[320,1024]{1,0:T(8,128)(2,1)S(1)}, u32[]{:S(2)}, u32[]{:S(2)}) collective-permute-start(bf16[320,1024]{1,0:T(8,128)(2,1)S(1)} %collective-permute-done.5.refs_2_), channel_id=1, source_target_pairs={{0,4},{4,0},{8,12},{12,8},{16,20},{20,16},{24,28},{28,24},{1,5},{5... | collective-permute-start | bytes 1966088 | tf_op jit(solution)/shard_map/ppermute | solution.py:22
  60.9 13.2 %collective-permute-start.14 = (bf16[320,1024]{1,0:T(8,128)(2,1)S(1)}, bf16[320,1024]{1,0:T(8,128)(2,1)S(1)}, u32[]{:S(2)}, u32[]{:S(2)}) collective-permute-start(bf16[320,1024]{1,0:T(8,128)(2,1)S(1)} %shard_map.59.refs_3_), channel_id=1, source_target_pairs={{0,2},{1,3},{2,0},{3,1},{4,6},{5,7},{6,4},{7,5},{8,10},{9,11},{10,... | collective-permute-start | bytes 1966088 | tf_op jit(solution)/shard_map/ppermute | solution.py:22
  63.3 16.1 %collective-permute-start.20 = (bf16[320,1024]{1,0:T(8,128)(2,1)S(1)}, bf16[320,1024]{1,0:T(8,128)(2,1)S(1)}, u32[]{:S(2)}, u32[]{:S(2)}) collective-permute-start(bf16[320,1024]{1,0:T(8,128)(2,1)S(1)} %shard_map.65), channel_id=1, source_target_pairs={{0,24},{4,28},{8,0},{12,4},{16,8},{20,12},{24,16},{28,20},{1,25},{... | collective-permute-start | bytes 1966088 | tf_op jit(solution)/shard_map/ppermute | solution.py:22
  77.9 4.5 %collective-permute-start.16 = (f32[8,640]{1,0:T(8,128)S(1)}, f32[8,640]{1,0:T(8,128)S(1)}, u32[]{:S(2)}, u32[]{:S(2)}) collective-permute-start(f32[8,640]{1,0:T(8,128)S(1)} %get-tuple-element.56.own), channel_id=1, source_target_pairs={{0,4},{4,0},{8,12},{12,8},{16,20},{20,16},{24,28},{28,24},{1,5},{5... | collective-permute-start | bytes 61448 | tf_op jit(solution)/shard_map/ppermute | solution.py:22
  80.1 12.1 %collective-permute-start.21 = (bf16[320,1024]{1,0:T(8,128)(2,1)S(1)}, bf16[320,1024]{1,0:T(8,128)(2,1)S(1)}, u32[]{:S(2)}, u32[]{:S(2)}) collective-permute-start(bf16[320,1024]{1,0:T(8,128)(2,1)S(1)} %shard_map.66.refs_3_), channel_id=1, source_target_pairs={{0,2},{1,3},{2,0},{3,1},{4,6},{5,7},{6,4},{7,5},{8,10},{9,11},{10,... | collective-permute-start | bytes 1966088 | tf_op jit(solution)/shard_map/ppermute | solution.py:22
  82.4 11.9 %collective-permute-start.26 = (bf16[320,1024]{1,0:T(8,128)(2,1)S(1)}, bf16[320,1024]{1,0:T(8,128)(2,1)S(1)}, u32[]{:S(2)}, u32[]{:S(2)}) collective-permute-start(bf16[320,1024]{1,0:T(8,128)(2,1)S(1)} %shard_map.70.refs_2_), channel_id=1, source_target_pairs={{0,4},{4,0},{8,12},{12,8},{16,20},{20,16},{24,28},{28,24},{1,5},{5... | collective-permute-start | bytes 1966088 | tf_op jit(solution)/shard_map/ppermute | solution.py:22
  83.6 6.7 %collective-permute-start.17 = (f32[8,640]{1,0:T(8,128)S(1)}, f32[8,640]{1,0:T(8,128)S(1)}, u32[]{:S(2)}, u32[]{:S(2)}) collective-permute-start(f32[8,640]{1,0:T(8,128)S(1)} %get-tuple-element.56.own), channel_id=1, source_target_pairs={{0,20},{4,16},{8,28},{12,24},{16,4},{20,0},{24,12},{28,8},{1,21},{... | collective-permute-start | bytes 61448 | tf_op jit(solution)/shard_map/ppermute | solution.py:22
  83.7 6.5 %collective-permute-start.19 = (f32[16,640]{1,0:T(8,128)S(1)}, f32[16,640]{1,0:T(8,128)S(1)}, u32[]{:S(2)}, u32[]{:S(2)}) collective-permute-start(f32[16,640]{1,0:T(8,128)S(1)} %constant_dynamic-update-slice_fusion), channel_id=1, source_target_pairs={{0,8},{4,12},{8,16},{12,20},{16,24},{20,28},{24,0},{28,4},{1,9},{5... | collective-permute-start | bytes 122888 | tf_op jit(solution)/shard_map/ppermute | solution.py:22
  85.7 4.6 %collective-permute-start.18 = (f32[16,640]{1,0:T(8,128)S(1)}, f32[16,640]{1,0:T(8,128)S(1)}, u32[]{:S(2)}, u32[]{:S(2)}) collective-permute-start(f32[16,640]{1,0:T(8,128)S(1)} %constant_dynamic-update-slice_fusion), channel_id=1, source_target_pairs={{0,24},{4,28},{8,0},{12,4},{16,8},{20,12},{24,16},{28,20},{1,25},{... | collective-permute-start | bytes 122888 | tf_op jit(solution)/shard_map/ppermute | solution.py:22
  92.2 4.9 %collective-permute-start.24 = (f32[24,320]{1,0:T(8,128)S(1)}, f32[24,320]{1,0:T(8,128)S(1)}, u32[]{:S(2)}, u32[]{:S(2)}) collective-permute-start(f32[24,320]{1,0:T(8,128)S(1)} %shard_map.64.own), channel_id=1, source_target_pairs={{0,3},{1,2},{2,1},{3,0},{4,7},{5,6},{6,5},{7,4},{8,11},{9,10},{10,... | collective-permute-start | bytes 92168 | tf_op jit(solution)/shard_map/ppermute | solution.py:22
  92.2 4.9 %collective-permute-start.23 = (f32[24,320]{1,0:T(8,128)S(1)}, f32[24,320]{1,0:T(8,128)S(1)}, u32[]{:S(2)}, u32[]{:S(2)}) collective-permute-start(f32[24,320]{1,0:T(8,128)S(1)} %shard_map.64.own), channel_id=1, source_target_pairs={{0,1},{1,0},{2,3},{3,2},{4,5},{5,4},{6,7},{7,6},{8,9},{9,8},{10,11... | collective-permute-start | bytes 92168 | tf_op jit(solution)/shard_map/ppermute | solution.py:22
  93.0 4.0 %collective-permute-start.22 = (f32[24,320]{1,0:T(8,128)S(1)}, f32[24,320]{1,0:T(8,128)S(1)}, u32[]{:S(2)}, u32[]{:S(2)}) collective-permute-start(f32[24,320]{1,0:T(8,128)S(1)} %shard_map.64.own), channel_id=1, source_target_pairs={{0,2},{1,3},{2,0},{3,1},{4,6},{5,7},{6,4},{7,5},{8,10},{9,11},{10,... | collective-permute-start | bytes 92168 | tf_op jit(solution)/shard_map/ppermute | solution.py:22
  104.0 5.9 %collective-permute-start.25 = (f32[320,1024]{1,0:T(8,128)S(1)}, f32[320,1024]{1,0:T(8,128)S(1)}, u32[]{:S(2)}, u32[]{:S(2)}) collective-permute-start(f32[320,1024]{1,0:T(8,128)S(1)} %get-tuple-element.70), channel_id=1, source_target_pairs={{0,1},{1,0},{2,3},{3,2},{4,5},{5,4},{6,7},{7,6},{8,9},{9,8},{10,11... | collective-permute-start | bytes 3932168 | tf_op jit(solution)/shard_map/ppermute | solution.py:22
  109.4 3.2 %collective-permute-start.27 = (f32[320,1024]{1,0:T(8,128)S(1)}, f32[320,1024]{1,0:T(8,128)S(1)}, u32[]{:S(2)}, u32[]{:S(2)}) collective-permute-start(f32[320,1024]{1,0:T(8,128)S(1)} %get-tuple-element.80), channel_id=1, source_target_pairs={{0,1},{1,0},{2,3},{3,2},{4,5},{5,4},{6,7},{7,6},{8,9},{9,8},{10,11... | collective-permute-start | bytes 3932168 | tf_op jit(solution)/shard_map/ppermute | solution.py:22

commit v6 on v5

--- a/solution.py
+++ b/solution.py
@@ -90,23 +90,28 @@
     return jnp.concatenate([first, second], axis=1)
 
 
-def score_kernel(count, start, stats, factor, scalars, *refs):
-    mine = refs[:2]
-    shards = refs[2 : 2 + count]
-    rest = list(refs[2 + count :])
-    *side, out, right, info, left, sems = rest
-    copies = fetch(mine, left, sems) + fetch(shards, right, sems.at[pl.ds(2, count)])
-    for copy in copies[:2]:
-        copy.wait()
-    rows = mine[0].shape[0]
-    pair = 2 * rows
+def score_kernel(count, given, start, stats, factor, scalars, *refs):
+    refs = list(refs)
+    mine = refs.pop(0) if given else (refs.pop(0), refs.pop(0))
+    shards = [refs.pop(0) for _ in range(count)]
+    if given:
+        *side, out, right, info, sems = refs
+        left = mine
+    else:
+        *side, out, right, info, left, sems = refs
+    copies = fetch(shards, right, sems.at[pl.ds(2, count)])
+    if not given:
+        for copy in fetch(mine, left, sems):
+            copy.wait()
+    pair = left.shape[0]
+    rows = pair // 2
     lhs = left[...]
     row_parts = []
     if not stats:
         info[...] = jnp.zeros(info.shape, F32)
     elif start:
         info[...] = side[0][...]
-    waiting = copies[2:]
+    waiting = copies
     ends = [sum(shard.shape[0] for shard in shards[: i + 1]) for i in range(count)]
     for p in range(ends[-1] // pair):
         while waiting and ends[-len(waiting)] - shards[-len(waiting)].shape[0] < (p + 1) * pair:
@@ -136,8 +141,10 @@
         info[pl.ds(4, 1), :] = row
 
 
-def score(scalars, mine, shards, start, stats, factor, side=()):
-    rows, width = mine[0].shape
+def score(scalars, mine, shards, start, stats, factor, side=(), keep=False):
+    given = not isinstance(mine, tuple)
+    width = shards[0].shape[1]
+    rows = mine.shape[0] // 2 if given else mine[0].shape[0]
     tokens = sum(shard.shape[0] for shard in shards) // rows
     info = (8, 2 * rows) if stats else (8, 128)
     shapes = [
@@ -145,22 +152,24 @@
         kept((tokens * rows, width), jnp.bfloat16),
         jax.ShapeDtypeStruct(info, F32),
     ]
+    left = (2 * rows, width)
+    if keep:
+        shapes.append(kept(left, jnp.bfloat16))
+    lhs, lhs_specs = ([in_vmem(mine)], [WHOLE]) if given else (mine, [ANYWHERE] * 2)
     return pl.pallas_call(
-        functools.partial(score_kernel, len(shards), start, stats, factor),
+        functools.partial(score_kernel, len(shards), given, start, stats, factor),
         out_shape=tuple(shapes),
-        in_specs=[SCALAR] + [ANYWHERE] * (2 + len(shards)) + [WHOLE] * len(side),
+        in_specs=[SCALAR] + lhs_specs + [ANYWHERE] * len(shards) + [WHOLE] * len(side),
         out_specs=(WHOLE,) * len(shapes),
-        scratch_shapes=[
-            pltpu.VMEM((2 * rows, width), jnp.bfloat16),
-            pltpu.SemaphoreType.DMA((2 + len(shards),)),
-        ],
+        scratch_shapes=([] if given or keep else [pltpu.VMEM(left, jnp.bfloat16)])
+        + [pltpu.SemaphoreType.DMA((2 + len(shards),))],
         compiler_params=pltpu.CompilerParams(vmem_limit_bytes=VMEM_LIMIT),
         cost_estimate=pl.CostEstimate(
             flops=4 * rows * rows * tokens * width,
             bytes_accessed=(tokens + 2) * rows * width * 2 + 8 * rows * rows * tokens,
             transcendentals=4 * rows * rows * tokens if stats else 0,
         ),
-    )(scalars, *mine, *shards, *side)
+    )(scalars, *lhs, *shards, *side)
 
 
 def halves(line):
@@ -227,7 +236,7 @@
     out[pl.ds(18, 6), :] = jnp.zeros((6, out.shape[1]), F32)
 
 
-def block_kernel(scalars, partner, own, across, core, corner, col_out, row_out, loss_out):
+def block_sums(own, across, core, corner):
     line = lambda ref, i: ref[pl.ds(i, 1), :]
     col = [[log_join(line(own, 2 * i + h), line(across, 2 * i + 1 - h)) for h in range(2)] for i in range(4)]
     core_col = [log_join(line(core, h), line(corner, 1 - h)) for h in range(2)]
@@ -236,6 +245,11 @@
         for i in range(4)
     ]
     core_row = log_join(line(own, 12), line(core, 8))
+    return col, core_col, row, core_row
+
+
+def fill_info(sums, col_out, row_out):
+    col, core_col, row, core_row = sums
     zeros = jnp.zeros((3, col_out.shape[1]), F32)
     for out, part, more in ((col_out, col, core_col[0]), (row_out, row, core_row)):
         a, b, c, d = part
@@ -245,13 +259,17 @@
         out[pl.ds(3, 1), :] = side_by_side(c[1], d[1])
         out[pl.ds(4, 1), :] = side_by_side(a[0], more)
         out[pl.ds(5, 3), :] = zeros
+
+
+def loss_kernel(scalars, partner, own, across, core, corner, out):
+    col, core_col, row, _ = block_sums(own, across, core, corner)
     chosen = as_column(partner[...])
     found = jnp.zeros(chosen.shape, F32)
     for i, value in enumerate((col[0][0], col[0][1], core_col[0], core_col[1])):
         hit = chosen == ids(scalars, i + 1, value.shape[1])
         found = found + jnp.sum(jnp.where(hit, value, 0.0), axis=1, keepdims=True)
-    score = line(own, 16) + line(core, 17)
-    loss_out[...] = (0.5 * row[0][0] + 0.5 * as_row(found) - score)[0]
+    score = own[pl.ds(16, 1), :] + core[pl.ds(17, 1), :]
+    out[...] = (0.5 * row[0][0] + 0.5 * as_row(found) - score)[0]
 
 
 def small_call(kernel, shapes, *args, scalars=0):
@@ -265,10 +283,14 @@
     )(*args)
 
 
-def grad_kernel(keys, factor, scalars, first, second, row_info, col_info, *refs):
+def grad_kernel(keys, factor, scalars, first, second, *refs):
     rows = first.shape[1]
     pair = 2 * rows
-    *made, own_out, other_out, weights = refs
+    if keys:
+        row_info, col_info, *made, own_out, other_out, weights = refs
+    else:
+        *made, own_out, other_out, col_info, row_info, weights = refs[4:]
+        fill_info(block_sums(*refs[:4]), col_info, row_info)
     made = list(zip(made[::2], made[1::2]))
     row = as_column(row_info[pl.ds(4, 1), :])
     partners = side_by_side(first[...], second[...])
@@ -302,14 +324,15 @@
         out[...] = total * factor
 
 
-def grad(scalars, keys, factor, first, second, row_info, col_info, made):
+def grad(scalars, keys, factor, first, second, sums, made):
     rows, width = first.shape[1], made[0][1].shape[1]
     made = [in_vmem(array) for part in made for array in part]
+    more = () if keys else (jax.ShapeDtypeStruct((8, 2 * rows), F32),) * 2
     return pl.pallas_call(
         functools.partial(grad_kernel, keys, factor),
-        out_shape=(kept((rows, width), F32), kept((rows, width), F32)),
-        in_specs=[SCALAR] + [WHOLE] * (4 + len(made)),
-        out_specs=(WHOLE,) * 2,
+        out_shape=(kept((rows, width), F32),) * 2 + more,
+        in_specs=[SCALAR] + [WHOLE] * (2 + len(sums) + len(made)),
+        out_specs=(WHOLE,) * (2 + len(more)),
         scratch_shapes=[pltpu.VMEM((2 * rows, 8 * rows), jnp.bfloat16)],
         compiler_params=pltpu.CompilerParams(vmem_limit_bytes=VMEM_LIMIT),
         cost_estimate=pl.CostEstimate(
@@ -317,7 +340,7 @@
             bytes_accessed=8 * rows * width * 2 + 64 * rows * rows + rows * width * 8,
             transcendentals=32 * rows * rows,
         ),
-    )(scalars, first, second, row_info, col_info, *made)
+    )(scalars, first, second, *sums, *made)
 
 
 def add_kernel(own, received, out, total, sems):
@@ -387,7 +410,7 @@
     *k_made_0, info = score(scalars, mine, (k0, kx, kz, kzy), 0, True, factor, (partner, partner_core))
     *q_made_0, tick = score(scalars, (k0, ks), (q0, qx, qz, qzy), 0, False, factor, (partner_across,))
     kd1 = across(after(kd0, kzx, info))
-    *k_made_1, info = score(scalars, mine, (kzx, kd0), 2, True, factor, (info, tick))
+    *k_made_1, info, mine = score(scalars, mine, (kzx, kd0), 2, True, factor, (info, tick), keep=True)
     qd1 = across(after(qd0, info))
     *k_made_2, info = score(scalars, mine, (kzxy, kd1), 3, True, factor, (info,))
 
@@ -398,19 +421,15 @@
     *q_made_1, tick = score(scalars, (after(k0, next_to), ks), (qzx, qd0), 2, False, factor)
     qzxy = beside(after(qzx, next_to))
     chain = after(chain, qd1)
-    col_info, row_info, loss = small_call(
-        block_kernel,
-        [(8, 2 * rows), (8, 2 * rows), (rows,)],
-        scalars, partner, chain, across(chain), core(chain), corner(chain),
-        scalars=1,
-    )
+    sums = (chain, across(chain), core(chain), corner(chain))
     *q_made_2, _ = score(scalars, (k0, ks), (qzxy, qd1), 3, False, factor)
-    q_own, q_other = grad(
-        scalars, False, factor, partner, partner_core, row_info, col_info, (k_made_0, k_made_1, k_made_2)
+    q_own, q_other, col_info, row_info = grad(
+        scalars, False, factor, partner, partner_core, sums, (k_made_0, k_made_1, k_made_2)
     )
     k_own, k_other = grad(
-        scalars, True, factor, partner, partner_across, col_info, row_info, (q_made_0, q_made_1, q_made_2)
+        scalars, True, factor, partner, partner_across, (col_info, row_info), (q_made_0, q_made_1, q_made_2)
     )
+    loss = small_call(loss_kernel, [(rows,)], scalars, after(partner, k_other), *sums, scalars=1)[0]
     grad_queries = add(q_own, core(q_other))
     grad_keys = add(k_own, core(k_other))
     return (loss, grad_queries, grad_keys)

time: 114 us -> 113 us (level)
  transfers between devices with their start and end apart: 28 -> 28, of which waited for: 11 -> 10; matrix products, arithmetic and copies ran while one was open for 0% -> 0% of each run, Pallas kernels for 31% -> 32%
where the time goes in v6:
time: 113 us
  Pallas kernels  43.5 us (38%)
  waiting for transfers between devices  37.7 us (33%)
  starting transfers between devices  30 us (27%)
    ppermute x28, waiting for transfers between devices, shift(): return lax.ppermute(array, axis, pairs)  37.7 us
    ppermute x28, starting transfers between devices, shift(): return lax.ppermute(array, axis, pairs)  30 us
    pallas_call x6, Pallas kernels, score(): pl.pallas_call(functools.partial(score_kernel, len(shards), given, start,...  24.2 us
    pallas_call x2, Pallas kernels, grad(): pl.pallas_call(functools.partial(grad_kernel, keys, factor), out_shape=(k...  11 us
    pallas_call x5, Pallas kernels, choose(): pl.pallas_call(choose_kernel, out_shape=jax.ShapeDtypeStruct(first.shape,...  3.84 us
    pallas_call x2, Pallas kernels, small_call(): pl.pallas_call(kernel, out_shape=tuple((jax.ShapeDtypeStruct(s, F32) for...  2.26 us
  transfers between devices with their start and end apart: 28, of which 10 were waited for; matrix products, arithmetic and copies ran while one was open for 0% of the time, Pallas kernels for 32%

profile of v6, /device:TPU:0, one launch (start us, length us, event | category | flops | bytes accessed | tf_op | source)
XLA Modules:
  0.0 113.2 jit_solution(10607992250354919866)
XLA Ops:
  0.6 0.5 collective-permute-start.1
  1.2 2.6 %collective-permute-start = (s32[1,320]{1,0:T(1,128)}, s32[1,320]{1,0:T(1,128)S(1)}, u32[]{:S(2)}, u32[]{:S(2)}) collective-permute-start(s32[1,320]{1,0:T(1,128)} %partner), channel_id=1, source_target_pairs={{0,2},{1,3},{2,0},{3,1},{4,6},{5,7},{6,4},{7,5},{8,10},{9,11},{10,... | collective-permute-start | bytes 3848 | tf_op jit(solution)/shard_map/ppermute | solution.py:22
  3.7 1.6 %collective-permute-start.3 = (bf16[320,1024]{1,0:T(8,128)(2,1)}, bf16[320,1024]{1,0:T(8,128)(2,1)}, u32[]{:S(2)}, u32[]{:S(2)}) collective-permute-start(bf16[320,1024]{1,0:T(8,128)(2,1)} %refs_0_.8), channel_id=1, source_target_pairs={{0,8},{4,12},{8,16},{12,20},{16,24},{20,28},{24,0},{28,4},{1,9},{5... | collective-permute-start | bytes 1966088 | tf_op jit(solution)/shard_map/ppermute | solution.py:22
  5.5 2.0 %collective-permute-start.4 = (bf16[320,1024]{1,0:T(8,128)(2,1)}, bf16[320,1024]{1,0:T(8,128)(2,1)S(1)}, u32[]{:S(2)}, u32[]{:S(2)}) collective-permute-start(bf16[320,1024]{1,0:T(8,128)(2,1)} %refs_0_.8), channel_id=1, source_target_pairs={{0,2},{1,3},{2,0},{3,1},{4,6},{5,7},{6,4},{7,5},{8,10},{9,11},{10,... | collective-permute-start | bytes 1966088 | tf_op jit(solution)/shard_map/ppermute | solution.py:22
  7.5 3.5 %collective-permute-start.7 = (bf16[320,1024]{1,0:T(8,128)(2,1)}, bf16[320,1024]{1,0:T(8,128)(2,1)S(1)}, u32[]{:S(2)}, u32[]{:S(2)}) collective-permute-start(bf16[320,1024]{1,0:T(8,128)(2,1)} %refs_0_.8), channel_id=1, source_target_pairs={{0,4},{8,12},{16,20},{24,28},{1,5},{9,13},{17,21},{25,29},{2,6},{1... | collective-permute-start | bytes 1966088 | tf_op jit(solution)/shard_map/ppermute | solution.py:22
  11.0 1.3 %collective-permute-start.8 = (bf16[320,1024]{1,0:T(8,128)(2,1)}, bf16[320,1024]{1,0:T(8,128)(2,1)S(1)}, u32[]{:S(2)}, u32[]{:S(2)}) collective-permute-start(bf16[320,1024]{1,0:T(8,128)(2,1)} %refs_0_.6), channel_id=1, source_target_pairs={{4,0},{12,8},{20,16},{28,24},{5,1},{13,9},{21,17},{29,25},{6,2},{1... | collective-permute-start | bytes 1966088 | tf_op jit(solution)/shard_map/ppermute | solution.py:22
  12.3 10.4 %collective-permute-done.3.refs_4_ = bf16[320,1024]{1,0:T(8,128)(2,1)} collective-permute-done((bf16[320,1024]{1,0:T(8,128)(2,1)}, bf16[320,1024]{1,0:T(8,128)(2,1)}, u32[]{:S(2)}, u32[]{:S(2)}) %collective-permute-start.3) | collective-permute-done | bytes 655392 | tf_op jit(solution)/shard_map/ppermute | solution.py:22
  22.7 1.7 %collective-permute-start.10 = (bf16[320,1024]{1,0:T(8,128)(2,1)}, bf16[320,1024]{1,0:T(8,128)(2,1)}, u32[]{:S(2)}, u32[]{:S(2)}) collective-permute-start(bf16[320,1024]{1,0:T(8,128)(2,1)} %refs_0_.6), channel_id=1, source_target_pairs={{0,24},{4,28},{8,0},{12,4},{16,8},{20,12},{24,16},{28,20},{1,25},{... | collective-permute-start | bytes 1966088 | tf_op jit(solution)/shard_map/ppermute | solution.py:22
  24.5 0.8 copy-done.3
  25.3 0.5 collective-permute-start.5
  25.8 2.6 %collective-permute-done.8.first = bf16[320,1024]{1,0:T(8,128)(2,1)S(1)} collective-permute-done((bf16[320,1024]{1,0:T(8,128)(2,1)}, bf16[320,1024]{1,0:T(8,128)(2,1)S(1)}, u32[]{:S(2)}, u32[]{:S(2)}) %collective-permute-start.8) | collective-permute-done | bytes 655392 | tf_op jit(solution)/shard_map/ppermute | solution.py:22
  28.6 12.6 %collective-permute-done.5.second.refs_3_.first = bf16[320,1024]{1,0:T(8,128)(2,1)S(1)} collective-permute-done((bf16[320,1024]{1,0:T(8,128)(2,1)}, bf16[320,1024]{1,0:T(8,128)(2,1)S(1)}, u32[]{:S(2)}, u32[]{:S(2)}) %collective-permute-start.5) | collective-permute-done | bytes 655392 | tf_op jit(solution)/shard_map/ppermute | solution.py:22
  41.2 0.5 collective-permute-start.6
  41.7 1.6 %collective-permute-done.9.first.refs_5_ = bf16[320,1024]{1,0:T(8,128)(2,1)S(1)} collective-permute-done((bf16[320,1024]{1,0:T(8,128)(2,1)}, bf16[320,1024]{1,0:T(8,128)(2,1)S(1)}, u32[]{:S(2)}, u32[]{:S(2)}) %collective-permute-start.9) | collective-permute-done | bytes 655392 | tf_op jit(solution)/shard_map/ppermute | solution.py:22
  43.4 0.8 shard_map.58
  44.2 1.7 %collective-permute-start.11 = (bf16[320,1024]{1,0:T(8,128)(2,1)S(1)}, bf16[320,1024]{1,0:T(8,128)(2,1)S(1)}, u32[]{:S(2)}, u32[]{:S(2)}) collective-permute-start(bf16[320,1024]{1,0:T(8,128)(2,1)S(1)} %shard_map.58), channel_id=1, source_target_pairs={{0,8},{4,28},{8,16},{12,4},{16,24},{20,12},{24,0},{28,20},{1,9},{5... | collective-permute-start | bytes 1966088 | tf_op jit(solution)/shard_map/ppermute | solution.py:22
  46.0 6.9 %shard_map.60 = (f32[640,1280]{1,0:T(8,128)S(1)}, bf16[1280,1024]{1,0:T(8,128)(2,1)S(1)}, f32[8,640]{1,0:T(8,128)S(1)}) custom-call(s32[5]{0:T(128)S(1)} %stack.27.flag.scalars, bf16[320,1024]{1,0:T(8,128)(2,1)S(1)} %copy-done.1, bf16[320,1024]{1,0:T(8,128)(2,1)} %collective-permute-done.2.refs_1_, bf16[320,1024]{1,0:T(8,128)(2,1)S(1)} %copy-done.2, ...), custom_call_target="tpu_custom_call" | custom-call | flops 1677721600 | bytes 7208960 | tf_op jit(solution)/shard_map/pallas_call | solution.py:159
  52.9 3.3 %collective-permute-done.6.refs_2_ = bf16[320,1024]{1,0:T(8,128)(2,1)S(1)} collective-permute-done((bf16[320,1024]{1,0:T(8,128)(2,1)}, bf16[320,1024]{1,0:T(8,128)(2,1)S(1)}, u32[]{:S(2)}, u32[]{:S(2)}) %collective-permute-start.6) | collective-permute-done | bytes 655392 | tf_op jit(solution)/shard_map/ppermute | solution.py:22
  56.2 1.0 collective-permute-done.13.refs_5_.second
  57.2 0.8 collective-permute-start.14
  58.0 2.2 %collective-permute-done.11.first.second = bf16[320,1024]{1,0:T(8,128)(2,1)S(1)} collective-permute-done((bf16[320,1024]{1,0:T(8,128)(2,1)S(1)}, bf16[320,1024]{1,0:T(8,128)(2,1)S(1)}, u32[]{:S(2)}, u32[]{:S(2)}) %collective-permute-start.11) | collective-permute-done | bytes 655392 | tf_op jit(solution)/shard_map/ppermute | solution.py:22
  60.1 0.8 shard_map.59.refs_3_
  60.9 1.6 %collective-permute-start.15 = (bf16[320,1024]{1,0:T(8,128)(2,1)S(1)}, bf16[320,1024]{1,0:T(8,128)(2,1)S(1)}, u32[]{:S(2)}, u32[]{:S(2)}) collective-permute-start(bf16[320,1024]{1,0:T(8,128)(2,1)S(1)} %shard_map.59.refs_3_), channel_id=1, source_target_pairs={{0,2},{1,3},{2,0},{3,1},{4,6},{5,7},{6,4},{7,5},{8,10},{9,11},{10,... | collective-permute-start | bytes 1966088 | tf_op jit(solution)/shard_map/ppermute | solution.py:22
  62.5 0.8 shard_map.65
  63.3 1.0 collective-permute-start.20
  64.3 4.8 %shard_map.61 = (f32[640,1280]{1,0:T(8,128)S(1)}, bf16[1280,1024]{1,0:T(8,128)(2,1)S(1)}, f32[8,128]{1,0:T(8,128)S(1)}) custom-call(s32[5]{0:T(128)S(1)} %stack.27.flag.scalars, bf16[320,1024]{1,0:T(8,128)(2,1)S(1)} %copy-done.2, bf16[320,1024]{1,0:T(8,128)(2,1)S(1)} %collective-permute-done.12.refs_1_, bf16[320,1024]{1,0:T(8,128)(2,1)S(1)} %copy-done.1, ...), custom_call_target="tpu_custom_call" | custom-call | flops 1677721600 | bytes 7208960 | tf_op jit(solution)/shard_map/pallas_call | solution.py:159
  69.1 4.2 %shard_map.62 = (f32[640,640]{1,0:T(8,128)S(1)}, bf16[640,1024]{1,0:T(8,128)(2,1)S(1)}, f32[8,640]{1,0:T(8,128)S(1)}, bf16[640,1024]{1,0:T(8,128)(2,1)S(1)}) custom-call(s32[5]{0:T(128)S(1)} %stack.27.flag.scalars, bf16[320,1024]{1,0:T(8,128)(2,1)S(1)} %copy-done.1, bf16[320,1024]{1,0:T(8,128)(2,1)} %collective-permute-done.2.refs_1_, ...), custom_call_target="tpu_custom_call" | custom-call | flops 838860800 | bytes 4259840 | tf_op jit(solution)/shard_map/pallas_call | solution.py:159
  73.3 1.2 %collective-permute-done.15.refs_2_ = bf16[320,1024]{1,0:T(8,128)(2,1)S(1)} collective-permute-done((bf16[320,1024]{1,0:T(8,128)(2,1)S(1)}, bf16[320,1024]{1,0:T(8,128)(2,1)S(1)}, u32[]{:S(2)}, u32[]{:S(2)}) %collective-permute-start.15) | collective-permute-done | bytes 655392 | tf_op jit(solution)/shard_map/ppermute | solution.py:22
  74.6 2.9 %shard_map.63 = (f32[640,640]{1,0:T(8,128)S(1)}, bf16[640,1024]{1,0:T(8,128)(2,1)S(1)}, f32[8,640]{1,0:T(8,128)S(1)}) custom-call(s32[5]{0:T(128)S(1)} %stack.27.flag.scalars, bf16[640,1024]{1,0:T(8,128)(2,1)S(1)} %get-tuple-element.54.refs_0_, bf16[320,1024]{1,0:T(8,128)(2,1)S(1)} %collective-permute-done.14.refs_1_, ...), custom_call_target="tpu_custom_call" | custom-call | flops 838860800 | bytes 4259840 | tf_op jit(solution)/shard_map/pallas_call | solution.py:159
  77.5 1.4 %collective-permute-start.16 = (f32[8,640]{1,0:T(8,128)S(1)}, f32[8,640]{1,0:T(8,128)S(1)}, u32[]{:S(2)}, u32[]{:S(2)}) collective-permute-start(f32[8,640]{1,0:T(8,128)S(1)} %get-tuple-element.58.own), channel_id=1, source_target_pairs={{0,4},{4,0},{8,12},{12,8},{16,20},{20,16},{24,28},{28,24},{1,5},{5... | collective-permute-start | bytes 61448 | tf_op jit(solution)/shard_map/ppermute | solution.py:22
  78.9 0.8 shard_map.66.refs_3_
  79.6 1.6 %collective-permute-start.21 = (bf16[320,1024]{1,0:T(8,128)(2,1)S(1)}, bf16[320,1024]{1,0:T(8,128)(2,1)S(1)}, u32[]{:S(2)}, u32[]{:S(2)}) collective-permute-start(bf16[320,1024]{1,0:T(8,128)(2,1)S(1)} %shard_map.66.refs_3_), channel_id=1, source_target_pairs={{0,2},{1,3},{2,0},{3,1},{4,6},{5,7},{6,4},{7,5},{8,10},{9,11},{10,... | collective-permute-start | bytes 1966088 | tf_op jit(solution)/shard_map/ppermute | solution.py:22
  81.2 0.8 shard_map.68.refs_2_
  82.0 0.9 collective-permute-start.25
  82.9 1.9 %collective-permute-start.19 = (f32[16,640]{1,0:T(8,128)S(1)}, f32[16,640]{1,0:T(8,128)S(1)}, u32[]{:S(2)}, u32[]{:S(2)}) collective-permute-start(f32[16,640]{1,0:T(8,128)S(1)} %constant_dynamic-update-slice_fusion), channel_id=1, source_target_pairs={{0,8},{4,12},{8,16},{12,20},{16,24},{20,28},{24,0},{28,4},{1,9},{5... | collective-permute-start | bytes 122888 | tf_op jit(solution)/shard_map/ppermute | solution.py:22
  84.8 2.0 %collective-permute-start.18 = (f32[16,640]{1,0:T(8,128)S(1)}, f32[16,640]{1,0:T(8,128)S(1)}, u32[]{:S(2)}, u32[]{:S(2)}) collective-permute-start(f32[16,640]{1,0:T(8,128)S(1)} %constant_dynamic-update-slice_fusion), channel_id=1, source_target_pairs={{0,24},{4,28},{8,0},{12,4},{16,8},{20,12},{24,16},{28,20},{1,25},{... | collective-permute-start | bytes 122888 | tf_op jit(solution)/shard_map/ppermute | solution.py:22
  86.8 2.7 %shard_map.69 = (f32[640,640]{1,0:T(8,128)S(1)}, bf16[640,1024]{1,0:T(8,128)(2,1)S(1)}, f32[8,128]{1,0:T(8,128)}) custom-call(s32[5]{0:T(128)S(1)} %stack.27.flag.scalars, bf16[320,1024]{1,0:T(8,128)(2,1)S(1)} %copy-done.2, bf16[320,1024]{1,0:T(8,128)(2,1)S(1)} %collective-permute-done.12.refs_1_, bf16[320,1024]{1,0:T(8,128)(2,1)S(1)} %shard_map.68.refs_2_, ...), custom_call_target="tpu_custom_call" | custom-call | flops 838860800 | bytes 4259840 | tf_op jit(solution)/shard_map/pallas_call | solution.py:159
  89.5 0.7 shard_map.64.refs_0_.own
  90.2 2.4 %collective-permute-done.21.refs_3_ = bf16[320,1024]{1,0:T(8,128)(2,1)S(1)} collective-permute-done((bf16[320,1024]{1,0:T(8,128)(2,1)S(1)}, bf16[320,1024]{1,0:T(8,128)(2,1)S(1)}, u32[]{:S(2)}, u32[]{:S(2)}) %collective-permute-start.21) | collective-permute-done | bytes 655392 | tf_op jit(solution)/shard_map/ppermute | solution.py:22
  92.6 0.4 collective-permute-start.23
  93.0 1.7 %collective-permute-start.22 = (f32[24,320]{1,0:T(8,128)S(1)}, f32[24,320]{1,0:T(8,128)S(1)}, u32[]{:S(2)}, u32[]{:S(2)}) collective-permute-start(f32[24,320]{1,0:T(8,128)S(1)} %shard_map.64.refs_0_.own), channel_id=1, source_target_pairs={{0,2},{1,3},{2,0},{3,1},{4,6},{5,7},{6,4},{7,5},{8,10},{9,11},{10,... | collective-permute-start | bytes 92168 | tf_op jit(solution)/shard_map/ppermute | solution.py:22
  94.8 2.7 %shard_map.70 = (f32[640,640]{1,0:T(8,128)S(1)}, bf16[640,1024]{1,0:T(8,128)(2,1)S(1)}, f32[8,128]{1,0:T(8,128)}) custom-call(s32[5]{0:T(128)S(1)} %stack.27.flag.scalars, bf16[320,1024]{1,0:T(8,128)(2,1)S(1)} %copy-done.2, bf16[320,1024]{1,0:T(8,128)(2,1)S(1)} %collective-permute-done.12.refs_1_, bf16[320,1024]{1,0:T(8,128)(2,1)S(1)} %collective-permute-done.25.refs_2_, ...), custom_call_target="tpu_custom_call" | custom-call | flops 838860800 | bytes 4259840 | tf_op jit(solution)/shard_map/pallas_call | solution.py:159
  97.5 5.7 %shard_map.67 = (f32[320,1024]{1,0:T(8,128)S(1)}, f32[320,1024]{1,0:T(8,128)S(1)}, f32[8,640]{1,0:T(8,128)S(1)}, f32[8,640]{1,0:T(8,128)S(1)}) custom-call(s32[5]{0:T(128)S(1)} %stack.27.flag.scalars, s32[1,320]{1,0:T(1,128)S(1)} %copy-done, s32[1,320]{1,0:T(1,128)S(1)} %collective-permute-done.1.refs_7_.second, f32[24,320]{1,0:T(8,128)S(1)} %shard_map.64.refs_0_.own, ...), custom_call_target="tpu_custom_call" | custom-call | flops 3355443200 | bytes 14417920 | tf_op jit(solution)/shard_map/pallas_call | solution.py:331
  103.3 5.3 %shard_map.71 = (f32[320,1024]{1,0:T(8,128)S(1)}, f32[320,1024]{1,0:T(8,128)S(1)}) custom-call(s32[5]{0:T(128)S(1)} %stack.27.flag.scalars, s32[1,320]{1,0:T(1,128)S(1)} %copy-done, s32[1,320]{1,0:T(1,128)S(1)} %collective-permute-done.refs_6_.second, f32[8,640]{1,0:T(8,128)S(1)} %get-tuple-element.68.refs_0_, f32[8,640]{1,0:T(8,128)S(1)} %get-tuple-element.69.refs_1_, ...), custom_call_target="tpu_custom_call" | custom-call | flops 3355443200 | bytes 14417920 | tf_op jit(solution)/shard_map/pallas_call | solution.py:331
  108.6 0.5 collective-permute-start.27
  109.1 1.6 %shard_map.72 = f32[320]{0:T(512)} custom-call(s32[5]{0:T(128)S(1)} %stack.27.flag.scalars, s32[1,320]{1,0:T(1,128)S(1)} %copy-done, f32[24,320]{1,0:T(8,128)S(1)} %shard_map.64.refs_0_.own, f32[24,320]{1,0:T(8,128)S(1)} %collective-permute-done.22.refs_1_.across, f32[24,320]{1,0:T(8,128)S(1)} %collective-permute-done.23.refs_2_.core, ...), custom_call_target="tpu_custom_call" | custom-call | flops 100000 | bytes 400000 | tf_op jit(solution)/shard_map/pallas_call | solution.py:276
  110.8 1.1 shard_map.73
  111.9 1.1 shard_map.74
  (38 shorter events, 0.5 us)
Async XLA Ops:
  0.6 45.3 %copy-start = (s32[1,320]{1,0:T(1,128)S(1)}, s32[1,320]{1,0:T(1,128)}, u32[]{:S(2)}) copy-start(s32[1,320]{1,0:T(1,128)} %partner) | copy-start | bytes 3844
  0.6 45.3 %copy-start.1 = (bf16[320,1024]{1,0:T(8,128)(2,1)S(1)}, bf16[320,1024]{1,0:T(8,128)(2,1)}, u32[]{:S(2)}) copy-start(bf16[320,1024]{1,0:T(8,128)(2,1)} %refs_0_.6) | copy-start | bytes 1966084
  0.6 4.7 %collective-permute-start.1 = (s32[1,320]{1,0:T(1,128)}, s32[1,320]{1,0:T(1,128)S(1)}, u32[]{:S(2)}, u32[]{:S(2)}) collective-permute-start(s32[1,320]{1,0:T(1,128)} %partner), channel_id=1, source_target_pairs={{0,1},{1,0},{2,3},{3,2},{4,5},{5,4},{6,7},{7,6},{8,9},{9,8},{10,11... | collective-permute-start | bytes 3848 | tf_op jit(solution)/shard_map/ppermute | solution.py:22
  1.2 4.3 %collective-permute-start = (s32[1,320]{1,0:T(1,128)}, s32[1,320]{1,0:T(1,128)S(1)}, u32[]{:S(2)}, u32[]{:S(2)}) collective-permute-start(s32[1,320]{1,0:T(1,128)} %partner), channel_id=1, source_target_pairs={{0,2},{1,3},{2,0},{3,1},{4,6},{5,7},{6,4},{7,5},{8,10},{9,11},{10,... | collective-permute-start | bytes 3848 | tf_op jit(solution)/shard_map/ppermute | solution.py:22
  3.7 19.0 %collective-permute-start.3 = (bf16[320,1024]{1,0:T(8,128)(2,1)}, bf16[320,1024]{1,0:T(8,128)(2,1)}, u32[]{:S(2)}, u32[]{:S(2)}) collective-permute-start(bf16[320,1024]{1,0:T(8,128)(2,1)} %refs_0_.8), channel_id=1, source_target_pairs={{0,8},{4,12},{8,16},{12,20},{16,24},{20,28},{24,0},{28,4},{1,9},{5... | collective-permute-start | bytes 1966088 | tf_op jit(solution)/shard_map/ppermute | solution.py:22
  5.5 19.0 %collective-permute-start.4 = (bf16[320,1024]{1,0:T(8,128)(2,1)}, bf16[320,1024]{1,0:T(8,128)(2,1)S(1)}, u32[]{:S(2)}, u32[]{:S(2)}) collective-permute-start(bf16[320,1024]{1,0:T(8,128)(2,1)} %refs_0_.8), channel_id=1, source_target_pairs={{0,2},{1,3},{2,0},{3,1},{4,6},{5,7},{6,4},{7,5},{8,10},{9,11},{10,... | collective-permute-start | bytes 1966088 | tf_op jit(solution)/shard_map/ppermute | solution.py:22
  7.5 18.3 %collective-permute-start.7 = (bf16[320,1024]{1,0:T(8,128)(2,1)}, bf16[320,1024]{1,0:T(8,128)(2,1)S(1)}, u32[]{:S(2)}, u32[]{:S(2)}) collective-permute-start(bf16[320,1024]{1,0:T(8,128)(2,1)} %refs_0_.8), channel_id=1, source_target_pairs={{0,4},{8,12},{16,20},{24,28},{1,5},{9,13},{17,21},{25,29},{2,6},{1... | collective-permute-start | bytes 1966088 | tf_op jit(solution)/shard_map/ppermute | solution.py:22
  11.0 17.5 %collective-permute-start.8 = (bf16[320,1024]{1,0:T(8,128)(2,1)}, bf16[320,1024]{1,0:T(8,128)(2,1)S(1)}, u32[]{:S(2)}, u32[]{:S(2)}) collective-permute-start(bf16[320,1024]{1,0:T(8,128)(2,1)} %refs_0_.6), channel_id=1, source_target_pairs={{4,0},{12,8},{20,16},{28,24},{5,1},{13,9},{21,17},{29,25},{6,2},{1... | collective-permute-start | bytes 1966088 | tf_op jit(solution)/shard_map/ppermute | solution.py:22
  22.7 19.0 %collective-permute-start.10 = (bf16[320,1024]{1,0:T(8,128)(2,1)}, bf16[320,1024]{1,0:T(8,128)(2,1)}, u32[]{:S(2)}, u32[]{:S(2)}) collective-permute-start(bf16[320,1024]{1,0:T(8,128)(2,1)} %refs_0_.6), channel_id=1, source_target_pairs={{0,24},{4,28},{8,0},{12,4},{16,8},{20,12},{24,16},{28,20},{1,25},{... | collective-permute-start | bytes 1966088 | tf_op jit(solution)/shard_map/ppermute | solution.py:22
  24.5 0.8 copy-start.3
  25.3 15.9 %collective-permute-start.5 = (bf16[320,1024]{1,0:T(8,128)(2,1)}, bf16[320,1024]{1,0:T(8,128)(2,1)S(1)}, u32[]{:S(2)}, u32[]{:S(2)}) collective-permute-start(bf16[320,1024]{1,0:T(8,128)(2,1)} %refs_0_.6), channel_id=1, source_target_pairs={{0,2},{1,3},{2,0},{3,1},{4,6},{5,7},{6,4},{7,5},{8,10},{9,11},{10,... | collective-permute-start | bytes 1966088 | tf_op jit(solution)/shard_map/ppermute | solution.py:22
  28.5 14.9 %collective-permute-start.9 = (bf16[320,1024]{1,0:T(8,128)(2,1)}, bf16[320,1024]{1,0:T(8,128)(2,1)S(1)}, u32[]{:S(2)}, u32[]{:S(2)}) collective-permute-start(bf16[320,1024]{1,0:T(8,128)(2,1)} %collective-permute-done.3.refs_4_), channel_id=1, source_target_pairs={{0,4},{4,0},{8,12},{12,8},{16,20},{20,16},{24,28},{28,24},{1,5},{5... | collective-permute-start | bytes 1966088 | tf_op jit(solution)/shard_map/ppermute | solution.py:22
  28.5 17.5 %collective-permute-start.2 = (bf16[320,1024]{1,0:T(8,128)(2,1)}, bf16[320,1024]{1,0:T(8,128)(2,1)}, u32[]{:S(2)}, u32[]{:S(2)}) collective-permute-start(bf16[320,1024]{1,0:T(8,128)(2,1)} %refs_0_.6), channel_id=1, source_target_pairs={{0,1},{1,0},{2,3},{3,2},{4,5},{5,4},{6,7},{7,6},{8,9},{9,8},{10,11... | collective-permute-start | bytes 1966088 | tf_op jit(solution)/shard_map/ppermute | solution.py:22
  28.6 17.4 %copy-start.2 = (bf16[320,1024]{1,0:T(8,128)(2,1)S(1)}, bf16[320,1024]{1,0:T(8,128)(2,1)}, u32[]{:S(2)}) copy-start(bf16[320,1024]{1,0:T(8,128)(2,1)} %refs_0_.8) | copy-start | bytes 1966084
  28.6 17.4 %copy-start.4 = (bf16[320,1024]{1,0:T(8,128)(2,1)S(1)}, bf16[320,1024]{1,0:T(8,128)(2,1)}, u32[]{:S(2)}) copy-start(bf16[320,1024]{1,0:T(8,128)(2,1)} %copy-done.3) | copy-start | bytes 1966084
  41.2 15.0 %collective-permute-start.6 = (bf16[320,1024]{1,0:T(8,128)(2,1)}, bf16[320,1024]{1,0:T(8,128)(2,1)S(1)}, u32[]{:S(2)}, u32[]{:S(2)}) collective-permute-start(bf16[320,1024]{1,0:T(8,128)(2,1)} %collective-permute-done.3.refs_4_), channel_id=1, source_target_pairs={{0,2},{1,3},{2,0},{3,1},{4,6},{5,7},{6,4},{7,5},{8,10},{9,11},{10,... | collective-permute-start | bytes 1966088 | tf_op jit(solution)/shard_map/ppermute | solution.py:22
  43.4 13.8 %collective-permute-start.13 = (bf16[320,1024]{1,0:T(8,128)(2,1)}, bf16[320,1024]{1,0:T(8,128)(2,1)S(1)}, u32[]{:S(2)}, u32[]{:S(2)}) collective-permute-start(bf16[320,1024]{1,0:T(8,128)(2,1)} %collective-permute-done.10.refs_4_), channel_id=1, source_target_pairs={{0,4},{4,0},{8,12},{12,8},{16,20},{20,16},{24,28},{28,24},{1,5},{5... | collective-permute-start | bytes 1966088 | tf_op jit(solution)/shard_map/ppermute | solution.py:22
  44.2 15.9 %collective-permute-start.11 = (bf16[320,1024]{1,0:T(8,128)(2,1)S(1)}, bf16[320,1024]{1,0:T(8,128)(2,1)S(1)}, u32[]{:S(2)}, u32[]{:S(2)}) collective-permute-start(bf16[320,1024]{1,0:T(8,128)(2,1)S(1)} %shard_map.58), channel_id=1, source_target_pairs={{0,8},{4,28},{8,16},{12,4},{16,24},{20,12},{24,0},{28,20},{1,9},{5... | collective-permute-start | bytes 1966088 | tf_op jit(solution)/shard_map/ppermute | solution.py:22
  45.9 18.4 %collective-permute-start.12 = (bf16[320,1024]{1,0:T(8,128)(2,1)S(1)}, bf16[320,1024]{1,0:T(8,128)(2,1)S(1)}, u32[]{:S(2)}, u32[]{:S(2)}) collective-permute-start(bf16[320,1024]{1,0:T(8,128)(2,1)S(1)} %copy-done.2), channel_id=1, source_target_pairs={{0,1},{1,0},{2,3},{3,2},{4,5},{5,4},{6,7},{7,6},{8,9},{9,8},{10,11... | collective-permute-start | bytes 1966088 | tf_op jit(solution)/shard_map/ppermute | solution.py:22
  57.2 16.1 %collective-permute-start.14 = (bf16[320,1024]{1,0:T(8,128)(2,1)S(1)}, bf16[320,1024]{1,0:T(8,128)(2,1)S(1)}, u32[]{:S(2)}, u32[]{:S(2)}) collective-permute-start(bf16[320,1024]{1,0:T(8,128)(2,1)S(1)} %collective-permute-done.6.refs_2_), channel_id=1, source_target_pairs={{0,4},{4,0},{8,12},{12,8},{16,20},{20,16},{24,28},{28,24},{1,5},{5... | collective-permute-start | bytes 1966088 | tf_op jit(solution)/shard_map/ppermute | solution.py:22
  60.9 13.7 %collective-permute-start.15 = (bf16[320,1024]{1,0:T(8,128)(2,1)S(1)}, bf16[320,1024]{1,0:T(8,128)(2,1)S(1)}, u32[]{:S(2)}, u32[]{:S(2)}) collective-permute-start(bf16[320,1024]{1,0:T(8,128)(2,1)S(1)} %shard_map.59.refs_3_), channel_id=1, source_target_pairs={{0,2},{1,3},{2,0},{3,1},{4,6},{5,7},{6,4},{7,5},{8,10},{9,11},{10,... | collective-permute-start | bytes 1966088 | tf_op jit(solution)/shard_map/ppermute | solution.py:22
  63.3 15.6 %collective-permute-start.20 = (bf16[320,1024]{1,0:T(8,128)(2,1)S(1)}, bf16[320,1024]{1,0:T(8,128)(2,1)S(1)}, u32[]{:S(2)}, u32[]{:S(2)}) collective-permute-start(bf16[320,1024]{1,0:T(8,128)(2,1)S(1)} %shard_map.65), channel_id=1, source_target_pairs={{0,24},{4,28},{8,0},{12,4},{16,8},{20,12},{24,16},{28,20},{1,25},{... | collective-permute-start | bytes 1966088 | tf_op jit(solution)/shard_map/ppermute | solution.py:22
  77.5 4.5 %collective-permute-start.16 = (f32[8,640]{1,0:T(8,128)S(1)}, f32[8,640]{1,0:T(8,128)S(1)}, u32[]{:S(2)}, u32[]{:S(2)}) collective-permute-start(f32[8,640]{1,0:T(8,128)S(1)} %get-tuple-element.58.own), channel_id=1, source_target_pairs={{0,4},{4,0},{8,12},{12,8},{16,20},{20,16},{24,28},{28,24},{1,5},{5... | collective-permute-start | bytes 61448 | tf_op jit(solution)/shard_map/ppermute | solution.py:22
  79.6 13.0 %collective-permute-start.21 = (bf16[320,1024]{1,0:T(8,128)(2,1)S(1)}, bf16[320,1024]{1,0:T(8,128)(2,1)S(1)}, u32[]{:S(2)}, u32[]{:S(2)}) collective-permute-start(bf16[320,1024]{1,0:T(8,128)(2,1)S(1)} %shard_map.66.refs_3_), channel_id=1, source_target_pairs={{0,2},{1,3},{2,0},{3,1},{4,6},{5,7},{6,4},{7,5},{8,10},{9,11},{10,... | collective-permute-start | bytes 1966088 | tf_op jit(solution)/shard_map/ppermute | solution.py:22
  82.0 12.8 %collective-permute-start.25 = (bf16[320,1024]{1,0:T(8,128)(2,1)S(1)}, bf16[320,1024]{1,0:T(8,128)(2,1)S(1)}, u32[]{:S(2)}, u32[]{:S(2)}) collective-permute-start(bf16[320,1024]{1,0:T(8,128)(2,1)S(1)} %shard_map.68.refs_2_), channel_id=1, source_target_pairs={{0,4},{4,0},{8,12},{12,8},{16,20},{20,16},{24,28},{28,24},{1,5},{5... | collective-permute-start | bytes 1966088 | tf_op jit(solution)/shard_map/ppermute | solution.py:22
  82.9 6.6 %collective-permute-start.17 = (f32[8,640]{1,0:T(8,128)S(1)}, f32[8,640]{1,0:T(8,128)S(1)}, u32[]{:S(2)}, u32[]{:S(2)}) collective-permute-start(f32[8,640]{1,0:T(8,128)S(1)} %get-tuple-element.58.own), channel_id=1, source_target_pairs={{0,20},{4,16},{8,28},{12,24},{16,4},{20,0},{24,12},{28,8},{1,21},{... | collective-permute-start | bytes 61448 | tf_op jit(solution)/shard_map/ppermute | solution.py:22
  82.9 6.6 %collective-permute-start.19 = (f32[16,640]{1,0:T(8,128)S(1)}, f32[16,640]{1,0:T(8,128)S(1)}, u32[]{:S(2)}, u32[]{:S(2)}) collective-permute-start(f32[16,640]{1,0:T(8,128)S(1)} %constant_dynamic-update-slice_fusion), channel_id=1, source_target_pairs={{0,8},{4,12},{8,16},{12,20},{16,24},{20,28},{24,0},{28,4},{1,9},{5... | collective-permute-start | bytes 122888 | tf_op jit(solution)/shard_map/ppermute | solution.py:22
  84.8 4.7 %collective-permute-start.18 = (f32[16,640]{1,0:T(8,128)S(1)}, f32[16,640]{1,0:T(8,128)S(1)}, u32[]{:S(2)}, u32[]{:S(2)}) collective-permute-start(f32[16,640]{1,0:T(8,128)S(1)} %constant_dynamic-update-slice_fusion), channel_id=1, source_target_pairs={{0,24},{4,28},{8,0},{12,4},{16,8},{20,12},{24,16},{28,20},{1,25},{... | collective-permute-start | bytes 122888 | tf_op jit(solution)/shard_map/ppermute | solution.py:22
  92.6 4.9 %collective-permute-start.24 = (f32[24,320]{1,0:T(8,128)S(1)}, f32[24,320]{1,0:T(8,128)S(1)}, u32[]{:S(2)}, u32[]{:S(2)}) collective-permute-start(f32[24,320]{1,0:T(8,128)S(1)} %shard_map.64.refs_0_.own), channel_id=1, source_target_pairs={{0,3},{1,2},{2,1},{3,0},{4,7},{5,6},{6,5},{7,4},{8,11},{9,10},{10,... | collective-permute-start | bytes 92168 | tf_op jit(solution)/shard_map/ppermute | solution.py:22
  92.6 4.9 %collective-permute-start.23 = (f32[24,320]{1,0:T(8,128)S(1)}, f32[24,320]{1,0:T(8,128)S(1)}, u32[]{:S(2)}, u32[]{:S(2)}) collective-permute-start(f32[24,320]{1,0:T(8,128)S(1)} %shard_map.64.refs_0_.own), channel_id=1, source_target_pairs={{0,1},{1,0},{2,3},{3,2},{4,5},{5,4},{6,7},{7,6},{8,9},{9,8},{10,11... | collective-permute-start | bytes 92168 | tf_op jit(solution)/shard_map/ppermute | solution.py:22
  93.0 4.5 %collective-permute-start.22 = (f32[24,320]{1,0:T(8,128)S(1)}, f32[24,320]{1,0:T(8,128)S(1)}, u32[]{:S(2)}, u32[]{:S(2)}) collective-permute-start(f32[24,320]{1,0:T(8,128)S(1)} %shard_map.64.refs_0_.own), channel_id=1, source_target_pairs={{0,2},{1,3},{2,0},{3,1},{4,6},{5,7},{6,4},{7,5},{8,10},{9,11},{10,... | collective-permute-start | bytes 92168 | tf_op jit(solution)/shard_map/ppermute | solution.py:22
  103.2 7.5 %collective-permute-start.26 = (f32[320,1024]{1,0:T(8,128)S(1)}, f32[320,1024]{1,0:T(8,128)S(1)}, u32[]{:S(2)}, u32[]{:S(2)}) collective-permute-start(f32[320,1024]{1,0:T(8,128)S(1)} %get-tuple-element.81), channel_id=1, source_target_pairs={{0,1},{1,0},{2,3},{3,2},{4,5},{5,4},{6,7},{7,6},{8,9},{9,8},{10,11... | collective-permute-start | bytes 3932168 | tf_op jit(solution)/shard_map/ppermute | solution.py:22
  108.6 3.3 %collective-permute-start.27 = (f32[320,1024]{1,0:T(8,128)S(1)}, f32[320,1024]{1,0:T(8,128)S(1)}, u32[]{:S(2)}, u32[]{:S(2)}) collective-permute-start(f32[320,1024]{1,0:T(8,128)S(1)} %get-tuple-element.78), channel_id=1, source_target_pairs={{0,1},{1,0},{2,3},{3,2},{4,5},{5,4},{6,7},{7,6},{8,9},{9,8},{10,11... | collective-permute-start | bytes 3932168 | tf_op jit(solution)/shard_map/ppermute | solution.py:22

commit v7 on v6

--- a/solution.py
+++ b/solution.py
@@ -398,7 +398,7 @@
     qz = back(after(q0, kz))
 
     kzx = across(after(kz, qx))
-    qzy = beside(after(qz, kzy))
+    qzy = beside(qz)
     m1 = apart(after(pick(kzy, qx), qz))
 
     kd0 = pick(m1, y1_odd)
@@ -429,7 +429,7 @@
     k_own, k_other = grad(
         scalars, True, factor, partner, partner_across, (col_info, row_info), (q_made_0, q_made_1, q_made_2)
     )
-    loss = small_call(loss_kernel, [(rows,)], scalars, after(partner, k_other), *sums, scalars=1)[0]
+    loss = small_call(loss_kernel, [(rows,)], scalars, after(partner, q_other), *sums, scalars=1)[0]
     grad_queries = add(q_own, core(q_other))
     grad_keys = add(k_own, core(k_other))
     return (loss, grad_queries, grad_keys)

time: 113 us -> 113 us (level)
  waiting for transfers between devices: 37.7 us -> 33.7 us
  starting transfers between devices: 30 us -> 33.5 us
    ppermute x28, waiting for transfers between devices: 37.7 us -> 33.7 us  [shift(): return lax.ppermute(array, axis, pairs)]
    ppermute x28, starting transfers between devices: 30 us -> 33.5 us  [shift(): return lax.ppermute(array, axis, pairs)]
  transfers between devices with their start and end apart: 28 -> 28, of which waited for: 10 -> 14; matrix products, arithmetic and copies ran while one was open for 0% -> 0% of each run, Pallas kernels for 32% -> 33%
where the time goes in v7:
time: 113 us
  Pallas kernels  43.5 us (38%)
  waiting for transfers between devices  33.7 us (30%)
  starting transfers between devices  33.5 us (30%)
    ppermute x28, waiting for transfers between devices, shift(): return lax.ppermute(array, axis, pairs)  33.7 us
    ppermute x28, starting transfers between devices, shift(): return lax.ppermute(array, axis, pairs)  33.5 us
    pallas_call x6, Pallas kernels, score(): pl.pallas_call(functools.partial(score_kernel, len(shards), given, start,...  24.2 us
    pallas_call x2, Pallas kernels, grad(): pl.pallas_call(functools.partial(grad_kernel, keys, factor), out_shape=(k...  11 us
    pallas_call x5, Pallas kernels, choose(): pl.pallas_call(choose_kernel, out_shape=jax.ShapeDtypeStruct(first.shape,...  3.84 us
    pallas_call x2, Pallas kernels, small_call(): pl.pallas_call(kernel, out_shape=tuple((jax.ShapeDtypeStruct(s, F32) for...  2.26 us
  transfers between devices with their start and end apart: 28, of which 14 were waited for; matrix products, arithmetic and copies ran while one was open for 0% of the time, Pallas kernels for 33%

profile of v7, /device:TPU:0, one launch (start us, length us, event | category | flops | bytes accessed | tf_op | source)
XLA Modules:
  0.0 112.8 jit_solution(13418751448177305578)
XLA Ops:
  0.6 3.0 %collective-permute-start.3 = (s32[1,320]{1,0:T(1,128)}, s32[1,320]{1,0:T(1,128)S(1)}, u32[]{:S(2)}, u32[]{:S(2)}) collective-permute-start(s32[1,320]{1,0:T(1,128)} %first.3), channel_id=1, source_target_pairs={{0,2},{1,3},{2,0},{3,1},{4,6},{5,7},{6,4},{7,5},{8,10},{9,11},{10,... | collective-permute-start | bytes 3848 | tf_op jit(solution)/shard_map/ppermute | solution.py:22
  3.7 1.6 %collective-permute-start.2 = (bf16[320,1024]{1,0:T(8,128)(2,1)}, bf16[320,1024]{1,0:T(8,128)(2,1)}, u32[]{:S(2)}, u32[]{:S(2)}) collective-permute-start(bf16[320,1024]{1,0:T(8,128)(2,1)} %refs_0_.8), channel_id=1, source_target_pairs={{0,8},{4,12},{8,16},{12,20},{16,24},{20,28},{24,0},{28,4},{1,9},{5... | collective-permute-start | bytes 1966088 | tf_op jit(solution)/shard_map/ppermute | solution.py:22
  5.4 2.0 %collective-permute-start.4 = (bf16[320,1024]{1,0:T(8,128)(2,1)}, bf16[320,1024]{1,0:T(8,128)(2,1)S(1)}, u32[]{:S(2)}, u32[]{:S(2)}) collective-permute-start(bf16[320,1024]{1,0:T(8,128)(2,1)} %refs_0_.8), channel_id=1, source_target_pairs={{0,2},{1,3},{2,0},{3,1},{4,6},{5,7},{6,4},{7,5},{8,10},{9,11},{10,... | collective-permute-start | bytes 1966088 | tf_op jit(solution)/shard_map/ppermute | solution.py:22
  7.4 3.5 %collective-permute-start.7 = (bf16[320,1024]{1,0:T(8,128)(2,1)}, bf16[320,1024]{1,0:T(8,128)(2,1)S(1)}, u32[]{:S(2)}, u32[]{:S(2)}) collective-permute-start(bf16[320,1024]{1,0:T(8,128)(2,1)} %refs_0_.8), channel_id=1, source_target_pairs={{0,4},{8,12},{16,20},{24,28},{1,5},{9,13},{17,21},{25,29},{2,6},{1... | collective-permute-start | bytes 1966088 | tf_op jit(solution)/shard_map/ppermute | solution.py:22
  10.9 1.3 %collective-permute-start.8 = (bf16[320,1024]{1,0:T(8,128)(2,1)}, bf16[320,1024]{1,0:T(8,128)(2,1)S(1)}, u32[]{:S(2)}, u32[]{:S(2)}) collective-permute-start(bf16[320,1024]{1,0:T(8,128)(2,1)} %refs_0_.6), channel_id=1, source_target_pairs={{4,0},{12,8},{20,16},{28,24},{5,1},{13,9},{21,17},{29,25},{6,2},{1... | collective-permute-start | bytes 1966088 | tf_op jit(solution)/shard_map/ppermute | solution.py:22
  12.2 10.8 %collective-permute-done.2.refs_4_ = bf16[320,1024]{1,0:T(8,128)(2,1)} collective-permute-done((bf16[320,1024]{1,0:T(8,128)(2,1)}, bf16[320,1024]{1,0:T(8,128)(2,1)}, u32[]{:S(2)}, u32[]{:S(2)}) %collective-permute-start.2) | collective-permute-done | bytes 655392 | tf_op jit(solution)/shard_map/ppermute | solution.py:22
  23.0 1.7 %collective-permute-start.10 = (bf16[320,1024]{1,0:T(8,128)(2,1)}, bf16[320,1024]{1,0:T(8,128)(2,1)}, u32[]{:S(2)}, u32[]{:S(2)}) collective-permute-start(bf16[320,1024]{1,0:T(8,128)(2,1)} %refs_0_.6), channel_id=1, source_target_pairs={{0,24},{4,28},{8,0},{12,4},{16,8},{20,12},{24,16},{28,20},{1,25},{... | collective-permute-start | bytes 1966088 | tf_op jit(solution)/shard_map/ppermute | solution.py:22
  24.7 0.8 copy-done.3
  26.1 1.7 %collective-permute-done.8.first = bf16[320,1024]{1,0:T(8,128)(2,1)S(1)} collective-permute-done((bf16[320,1024]{1,0:T(8,128)(2,1)}, bf16[320,1024]{1,0:T(8,128)(2,1)S(1)}, u32[]{:S(2)}, u32[]{:S(2)}) %collective-permute-start.8) | collective-permute-done | bytes 655392 | tf_op jit(solution)/shard_map/ppermute | solution.py:22
  27.9 11.9 %collective-permute-done.10.refs_4_ = bf16[320,1024]{1,0:T(8,128)(2,1)} collective-permute-done((bf16[320,1024]{1,0:T(8,128)(2,1)}, bf16[320,1024]{1,0:T(8,128)(2,1)}, u32[]{:S(2)}, u32[]{:S(2)}) %collective-permute-start.10) | collective-permute-done | bytes 655392 | tf_op jit(solution)/shard_map/ppermute | solution.py:22
  39.7 1.5 %collective-permute-start.13 = (bf16[320,1024]{1,0:T(8,128)(2,1)}, bf16[320,1024]{1,0:T(8,128)(2,1)S(1)}, u32[]{:S(2)}, u32[]{:S(2)}) collective-permute-start(bf16[320,1024]{1,0:T(8,128)(2,1)} %collective-permute-done.10.refs_4_), channel_id=1, source_target_pairs={{0,4},{4,0},{8,12},{12,8},{16,20},{20,16},{24,28},{28,24},{1,5},{5... | collective-permute-start | bytes 1966088 | tf_op jit(solution)/shard_map/ppermute | solution.py:22
  41.2 0.6 collective-permute-done.5.second.refs_3_.first
  42.7 0.8 shard_map.58
  43.5 3.1 %collective-permute-start.11 = (bf16[320,1024]{1,0:T(8,128)(2,1)S(1)}, bf16[320,1024]{1,0:T(8,128)(2,1)S(1)}, u32[]{:S(2)}, u32[]{:S(2)}) collective-permute-start(bf16[320,1024]{1,0:T(8,128)(2,1)S(1)} %shard_map.58), channel_id=1, source_target_pairs={{0,8},{4,28},{8,16},{12,4},{16,24},{20,12},{24,0},{28,20},{1,9},{5... | collective-permute-start | bytes 1966088 | tf_op jit(solution)/shard_map/ppermute | solution.py:22
  46.6 6.9 %shard_map.60 = (f32[640,1280]{1,0:T(8,128)S(1)}, bf16[1280,1024]{1,0:T(8,128)(2,1)S(1)}, f32[8,640]{1,0:T(8,128)S(1)}) custom-call(s32[5]{0:T(128)S(1)} %stack.27.flag.scalars, bf16[320,1024]{1,0:T(8,128)(2,1)S(1)} %copy-done.1, bf16[320,1024]{1,0:T(8,128)(2,1)} %collective-permute-done.1.refs_1_, bf16[320,1024]{1,0:T(8,128)(2,1)S(1)} %copy-done.2, ...), custom_call_target="tpu_custom_call" | custom-call | flops 1677721600 | bytes 7208960 | tf_op jit(solution)/shard_map/pallas_call | solution.py:159
  53.5 2.7 %collective-permute-done.13.refs_5_.second = bf16[320,1024]{1,0:T(8,128)(2,1)S(1)} collective-permute-done((bf16[320,1024]{1,0:T(8,128)(2,1)}, bf16[320,1024]{1,0:T(8,128)(2,1)S(1)}, u32[]{:S(2)}, u32[]{:S(2)}) %collective-permute-start.13) | collective-permute-done | bytes 655392 | tf_op jit(solution)/shard_map/ppermute | solution.py:22
  56.2 1.1 collective-permute-done.6.refs_2_
  57.2 1.5 %collective-permute-start.14 = (bf16[320,1024]{1,0:T(8,128)(2,1)S(1)}, bf16[320,1024]{1,0:T(8,128)(2,1)S(1)}, u32[]{:S(2)}, u32[]{:S(2)}) collective-permute-start(bf16[320,1024]{1,0:T(8,128)(2,1)S(1)} %collective-permute-done.6.refs_2_), channel_id=1, source_target_pairs={{0,4},{4,0},{8,12},{12,8},{16,20},{20,16},{24,28},{28,24},{1,5},{5... | collective-permute-start | bytes 1966088 | tf_op jit(solution)/shard_map/ppermute | solution.py:22
  58.7 1.2 %collective-permute-done.11.first.second = bf16[320,1024]{1,0:T(8,128)(2,1)S(1)} collective-permute-done((bf16[320,1024]{1,0:T(8,128)(2,1)S(1)}, bf16[320,1024]{1,0:T(8,128)(2,1)S(1)}, u32[]{:S(2)}, u32[]{:S(2)}) %collective-permute-start.11) | collective-permute-done | bytes 655392 | tf_op jit(solution)/shard_map/ppermute | solution.py:22
  59.9 0.8 shard_map.59.refs_3_
  60.7 1.6 %collective-permute-start.15 = (bf16[320,1024]{1,0:T(8,128)(2,1)S(1)}, bf16[320,1024]{1,0:T(8,128)(2,1)S(1)}, u32[]{:S(2)}, u32[]{:S(2)}) collective-permute-start(bf16[320,1024]{1,0:T(8,128)(2,1)S(1)} %shard_map.59.refs_3_), channel_id=1, source_target_pairs={{0,2},{1,3},{2,0},{3,1},{4,6},{5,7},{6,4},{7,5},{8,10},{9,11},{10,... | collective-permute-start | bytes 1966088 | tf_op jit(solution)/shard_map/ppermute | solution.py:22
  62.2 0.8 shard_map.65
  63.0 1.2 %collective-permute-start.20 = (bf16[320,1024]{1,0:T(8,128)(2,1)S(1)}, bf16[320,1024]{1,0:T(8,128)(2,1)S(1)}, u32[]{:S(2)}, u32[]{:S(2)}) collective-permute-start(bf16[320,1024]{1,0:T(8,128)(2,1)S(1)} %shard_map.65), channel_id=1, source_target_pairs={{0,24},{4,28},{8,0},{12,4},{16,8},{20,12},{24,16},{28,20},{1,25},{... | collective-permute-start | bytes 1966088 | tf_op jit(solution)/shard_map/ppermute | solution.py:22
  64.2 4.8 %shard_map.61 = (f32[640,1280]{1,0:T(8,128)S(1)}, bf16[1280,1024]{1,0:T(8,128)(2,1)S(1)}, f32[8,128]{1,0:T(8,128)S(1)}) custom-call(s32[5]{0:T(128)S(1)} %stack.27.flag.scalars, bf16[320,1024]{1,0:T(8,128)(2,1)S(1)} %copy-done.2, bf16[320,1024]{1,0:T(8,128)(2,1)S(1)} %collective-permute-done.12.refs_1_, bf16[320,1024]{1,0:T(8,128)(2,1)S(1)} %copy-done.1, ...), custom_call_target="tpu_custom_call" | custom-call | flops 1677721600 | bytes 7208960 | tf_op jit(solution)/shard_map/pallas_call | solution.py:159
  69.0 4.2 %shard_map.62 = (f32[640,640]{1,0:T(8,128)S(1)}, bf16[640,1024]{1,0:T(8,128)(2,1)S(1)}, f32[8,640]{1,0:T(8,128)S(1)}, bf16[640,1024]{1,0:T(8,128)(2,1)S(1)}) custom-call(s32[5]{0:T(128)S(1)} %stack.27.flag.scalars, bf16[320,1024]{1,0:T(8,128)(2,1)S(1)} %copy-done.1, bf16[320,1024]{1,0:T(8,128)(2,1)} %collective-permute-done.1.refs_1_, ...), custom_call_target="tpu_custom_call" | custom-call | flops 838860800 | bytes 4259840 | tf_op jit(solution)/shard_map/pallas_call | solution.py:159
  73.2 1.2 %collective-permute-done.15.refs_2_ = bf16[320,1024]{1,0:T(8,128)(2,1)S(1)} collective-permute-done((bf16[320,1024]{1,0:T(8,128)(2,1)S(1)}, bf16[320,1024]{1,0:T(8,128)(2,1)S(1)}, u32[]{:S(2)}, u32[]{:S(2)}) %collective-permute-start.15) | collective-permute-done | bytes 655392 | tf_op jit(solution)/shard_map/ppermute | solution.py:22
  74.4 2.9 %shard_map.63 = (f32[640,640]{1,0:T(8,128)S(1)}, bf16[640,1024]{1,0:T(8,128)(2,1)S(1)}, f32[8,640]{1,0:T(8,128)S(1)}) custom-call(s32[5]{0:T(128)S(1)} %stack.27.flag.scalars, bf16[640,1024]{1,0:T(8,128)(2,1)S(1)} %get-tuple-element.52.refs_0_, bf16[320,1024]{1,0:T(8,128)(2,1)S(1)} %collective-permute-done.14.refs_1_, ...), custom_call_target="tpu_custom_call" | custom-call | flops 838860800 | bytes 4259840 | tf_op jit(solution)/shard_map/pallas_call | solution.py:159
  77.3 1.2 %collective-permute-start.16 = (f32[8,640]{1,0:T(8,128)S(1)}, f32[8,640]{1,0:T(8,128)S(1)}, u32[]{:S(2)}, u32[]{:S(2)}) collective-permute-start(f32[8,640]{1,0:T(8,128)S(1)} %get-tuple-element.56.own), channel_id=1, source_target_pairs={{0,4},{4,0},{8,12},{12,8},{16,20},{20,16},{24,28},{28,24},{1,5},{5... | collective-permute-start | bytes 61448 | tf_op jit(solution)/shard_map/ppermute | solution.py:22
  78.5 0.8 shard_map.66.refs_3_
  79.3 0.7 collective-permute-start.21
  80.0 0.8 shard_map.70.refs_2_
  80.8 0.6 collective-permute-done.16.beside
  81.4 1.1 %collective-permute-start.26 = (bf16[320,1024]{1,0:T(8,128)(2,1)S(1)}, bf16[320,1024]{1,0:T(8,128)(2,1)S(1)}, u32[]{:S(2)}, u32[]{:S(2)}) collective-permute-start(bf16[320,1024]{1,0:T(8,128)(2,1)S(1)} %shard_map.70.refs_2_), channel_id=1, source_target_pairs={{0,4},{4,0},{8,12},{12,8},{16,20},{20,16},{24,28},{28,24},{1,5},{5... | collective-permute-start | bytes 1966088 | tf_op jit(solution)/shard_map/ppermute | solution.py:22
  82.6 0.9 collective-permute-start.17
  83.4 2.1 %collective-permute-start.19 = (f32[16,640]{1,0:T(8,128)S(1)}, f32[16,640]{1,0:T(8,128)S(1)}, u32[]{:S(2)}, u32[]{:S(2)}) collective-permute-start(f32[16,640]{1,0:T(8,128)S(1)} %constant_dynamic-update-slice_fusion), channel_id=1, source_target_pairs={{0,8},{4,12},{8,16},{12,20},{16,24},{20,28},{24,0},{28,4},{1,9},{5... | collective-permute-start | bytes 122888 | tf_op jit(solution)/shard_map/ppermute | solution.py:22
  85.5 1.7 %collective-permute-start.18 = (f32[16,640]{1,0:T(8,128)S(1)}, f32[16,640]{1,0:T(8,128)S(1)}, u32[]{:S(2)}, u32[]{:S(2)}) collective-permute-start(f32[16,640]{1,0:T(8,128)S(1)} %constant_dynamic-update-slice_fusion), channel_id=1, source_target_pairs={{0,24},{4,28},{8,0},{12,4},{16,8},{20,12},{24,16},{28,20},{1,25},{... | collective-permute-start | bytes 122888 | tf_op jit(solution)/shard_map/ppermute | solution.py:22
  87.3 2.7 %shard_map.71 = (f32[640,640]{1,0:T(8,128)S(1)}, bf16[640,1024]{1,0:T(8,128)(2,1)S(1)}, f32[8,128]{1,0:T(8,128)}) custom-call(s32[5]{0:T(128)S(1)} %stack.27.flag.scalars, bf16[320,1024]{1,0:T(8,128)(2,1)S(1)} %copy-done.2, bf16[320,1024]{1,0:T(8,128)(2,1)S(1)} %collective-permute-done.12.refs_1_, bf16[320,1024]{1,0:T(8,128)(2,1)S(1)} %shard_map.70.refs_2_, ...), custom_call_target="tpu_custom_call" | custom-call | flops 838860800 | bytes 4259840 | tf_op jit(solution)/shard_map/pallas_call | solution.py:159
  90.0 0.7 shard_map.64.refs_0_.own
  90.7 1.0 collective-permute-done.21.refs_3_
  91.7 1.5 %collective-permute-start.23 = (f32[24,320]{1,0:T(8,128)S(1)}, f32[24,320]{1,0:T(8,128)S(1)}, u32[]{:S(2)}, u32[]{:S(2)}) collective-permute-start(f32[24,320]{1,0:T(8,128)S(1)} %shard_map.64.refs_0_.own), channel_id=1, source_target_pairs={{0,1},{1,0},{2,3},{3,2},{4,5},{5,4},{6,7},{7,6},{8,9},{9,8},{10,11... | collective-permute-start | bytes 92168 | tf_op jit(solution)/shard_map/ppermute | solution.py:22
  93.1 0.7 collective-permute-start.22
  94.3 2.7 %shard_map.72 = (f32[640,640]{1,0:T(8,128)S(1)}, bf16[640,1024]{1,0:T(8,128)(2,1)S(1)}, f32[8,128]{1,0:T(8,128)}) custom-call(s32[5]{0:T(128)S(1)} %stack.27.flag.scalars, bf16[320,1024]{1,0:T(8,128)(2,1)S(1)} %copy-done.2, bf16[320,1024]{1,0:T(8,128)(2,1)S(1)} %collective-permute-done.12.refs_1_, bf16[320,1024]{1,0:T(8,128)(2,1)S(1)} %collective-permute-done.26.refs_2_, ...), custom_call_target="tpu_custom_call" | custom-call | flops 838860800 | bytes 4259840 | tf_op jit(solution)/shard_map/pallas_call | solution.py:159
  97.1 5.7 %shard_map.67 = (f32[320,1024]{1,0:T(8,128)S(1)}, f32[320,1024]{1,0:T(8,128)S(1)}, f32[8,640]{1,0:T(8,128)S(1)}, f32[8,640]{1,0:T(8,128)S(1)}) custom-call(s32[5]{0:T(128)S(1)} %stack.27.flag.scalars, s32[1,320]{1,0:T(1,128)S(1)} %copy-done, s32[1,320]{1,0:T(1,128)S(1)} %collective-permute-done.refs_7_.second, f32[24,320]{1,0:T(8,128)S(1)} %shard_map.64.refs_0_.own, ...), custom_call_target="tpu_custom_call" | custom-call | flops 3355443200 | bytes 14417920 | tf_op jit(solution)/shard_map/pallas_call | solution.py:331
  102.9 5.3 %shard_map.73 = (f32[320,1024]{1,0:T(8,128)S(1)}, f32[320,1024]{1,0:T(8,128)S(1)}) custom-call(s32[5]{0:T(128)S(1)} %stack.27.flag.scalars, s32[1,320]{1,0:T(1,128)S(1)} %copy-done, s32[1,320]{1,0:T(1,128)S(1)} %collective-permute-done.3.refs_6_.second, f32[8,640]{1,0:T(8,128)S(1)} %get-tuple-element.69.refs_0_, f32[8,640]{1,0:T(8,128)S(1)} %get-tuple-element.70.refs_1_, ...), custom_call_target="tpu_custom_call" | custom-call | flops 3355443200 | bytes 14417920 | tf_op jit(solution)/shard_map/pallas_call | solution.py:331
  108.2 0.6 collective-permute-start.27
  108.7 1.6 %shard_map.68 = f32[320]{0:T(512)} custom-call(s32[5]{0:T(128)S(1)} %stack.27.flag.scalars, s32[1,320]{1,0:T(1,128)S(1)} %copy-done, f32[24,320]{1,0:T(8,128)S(1)} %shard_map.64.refs_0_.own, f32[24,320]{1,0:T(8,128)S(1)} %collective-permute-done.22.refs_1_.across, f32[24,320]{1,0:T(8,128)S(1)} %collective-permute-done.23.refs_2_.core, ...), custom_call_target="tpu_custom_call" | custom-call | flops 100000 | bytes 400000 | tf_op jit(solution)/shard_map/pallas_call | solution.py:276
  110.3 1.1 shard_map.69
  111.5 1.1 shard_map.74
  (38 shorter events, 2.4 us)
Async XLA Ops:
  0.6 45.9 %copy-start = (s32[1,320]{1,0:T(1,128)S(1)}, s32[1,320]{1,0:T(1,128)}, u32[]{:S(2)}) copy-start(s32[1,320]{1,0:T(1,128)} %first.3) | copy-start | bytes 3844
  0.6 45.9 %copy-start.1 = (bf16[320,1024]{1,0:T(8,128)(2,1)S(1)}, bf16[320,1024]{1,0:T(8,128)(2,1)}, u32[]{:S(2)}) copy-start(bf16[320,1024]{1,0:T(8,128)(2,1)} %refs_0_.6) | copy-start | bytes 1966084
  0.6 4.8 %collective-permute-start.3 = (s32[1,320]{1,0:T(1,128)}, s32[1,320]{1,0:T(1,128)S(1)}, u32[]{:S(2)}, u32[]{:S(2)}) collective-permute-start(s32[1,320]{1,0:T(1,128)} %first.3), channel_id=1, source_target_pairs={{0,2},{1,3},{2,0},{3,1},{4,6},{5,7},{6,4},{7,5},{8,10},{9,11},{10,... | collective-permute-start | bytes 3848 | tf_op jit(solution)/shard_map/ppermute | solution.py:22
  3.7 1.8 %collective-permute-start = (s32[1,320]{1,0:T(1,128)}, s32[1,320]{1,0:T(1,128)S(1)}, u32[]{:S(2)}, u32[]{:S(2)}) collective-permute-start(s32[1,320]{1,0:T(1,128)} %first.3), channel_id=1, source_target_pairs={{0,1},{1,0},{2,3},{3,2},{4,5},{5,4},{6,7},{7,6},{8,9},{9,8},{10,11... | collective-permute-start | bytes 3848 | tf_op jit(solution)/shard_map/ppermute | solution.py:22
  3.7 19.3 %collective-permute-start.2 = (bf16[320,1024]{1,0:T(8,128)(2,1)}, bf16[320,1024]{1,0:T(8,128)(2,1)}, u32[]{:S(2)}, u32[]{:S(2)}) collective-permute-start(bf16[320,1024]{1,0:T(8,128)(2,1)} %refs_0_.8), channel_id=1, source_target_pairs={{0,8},{4,12},{8,16},{12,20},{16,24},{20,28},{24,0},{28,4},{1,9},{5... | collective-permute-start | bytes 1966088 | tf_op jit(solution)/shard_map/ppermute | solution.py:22
  5.4 19.3 %collective-permute-start.4 = (bf16[320,1024]{1,0:T(8,128)(2,1)}, bf16[320,1024]{1,0:T(8,128)(2,1)S(1)}, u32[]{:S(2)}, u32[]{:S(2)}) collective-permute-start(bf16[320,1024]{1,0:T(8,128)(2,1)} %refs_0_.8), channel_id=1, source_target_pairs={{0,2},{1,3},{2,0},{3,1},{4,6},{5,7},{6,4},{7,5},{8,10},{9,11},{10,... | collective-permute-start | bytes 1966088 | tf_op jit(solution)/shard_map/ppermute | solution.py:22
  7.4 18.7 %collective-permute-start.7 = (bf16[320,1024]{1,0:T(8,128)(2,1)}, bf16[320,1024]{1,0:T(8,128)(2,1)S(1)}, u32[]{:S(2)}, u32[]{:S(2)}) collective-permute-start(bf16[320,1024]{1,0:T(8,128)(2,1)} %refs_0_.8), channel_id=1, source_target_pairs={{0,4},{8,12},{16,20},{24,28},{1,5},{9,13},{17,21},{25,29},{2,6},{1... | collective-permute-start | bytes 1966088 | tf_op jit(solution)/shard_map/ppermute | solution.py:22
  10.9 16.9 %collective-permute-start.8 = (bf16[320,1024]{1,0:T(8,128)(2,1)}, bf16[320,1024]{1,0:T(8,128)(2,1)S(1)}, u32[]{:S(2)}, u32[]{:S(2)}) collective-permute-start(bf16[320,1024]{1,0:T(8,128)(2,1)} %refs_0_.6), channel_id=1, source_target_pairs={{4,0},{12,8},{20,16},{28,24},{5,1},{13,9},{21,17},{29,25},{6,2},{1... | collective-permute-start | bytes 1966088 | tf_op jit(solution)/shard_map/ppermute | solution.py:22
  23.0 16.8 %collective-permute-start.10 = (bf16[320,1024]{1,0:T(8,128)(2,1)}, bf16[320,1024]{1,0:T(8,128)(2,1)}, u32[]{:S(2)}, u32[]{:S(2)}) collective-permute-start(bf16[320,1024]{1,0:T(8,128)(2,1)} %refs_0_.6), channel_id=1, source_target_pairs={{0,24},{4,28},{8,0},{12,4},{16,8},{20,12},{24,16},{28,20},{1,25},{... | collective-permute-start | bytes 1966088 | tf_op jit(solution)/shard_map/ppermute | solution.py:22
  24.7 0.8 copy-start.3
  25.6 16.3 %collective-permute-start.5 = (bf16[320,1024]{1,0:T(8,128)(2,1)}, bf16[320,1024]{1,0:T(8,128)(2,1)S(1)}, u32[]{:S(2)}, u32[]{:S(2)}) collective-permute-start(bf16[320,1024]{1,0:T(8,128)(2,1)} %refs_0_.6), channel_id=1, source_target_pairs={{0,2},{1,3},{2,0},{3,1},{4,6},{5,7},{6,4},{7,5},{8,10},{9,11},{10,... | collective-permute-start | bytes 1966088 | tf_op jit(solution)/shard_map/ppermute | solution.py:22
  27.8 14.9 %collective-permute-start.9 = (bf16[320,1024]{1,0:T(8,128)(2,1)}, bf16[320,1024]{1,0:T(8,128)(2,1)S(1)}, u32[]{:S(2)}, u32[]{:S(2)}) collective-permute-start(bf16[320,1024]{1,0:T(8,128)(2,1)} %collective-permute-done.2.refs_4_), channel_id=1, source_target_pairs={{0,4},{4,0},{8,12},{12,8},{16,20},{20,16},{24,28},{28,24},{1,5},{5... | collective-permute-start | bytes 1966088 | tf_op jit(solution)/shard_map/ppermute | solution.py:22
  27.8 18.8 %collective-permute-start.1 = (bf16[320,1024]{1,0:T(8,128)(2,1)}, bf16[320,1024]{1,0:T(8,128)(2,1)}, u32[]{:S(2)}, u32[]{:S(2)}) collective-permute-start(bf16[320,1024]{1,0:T(8,128)(2,1)} %refs_0_.6), channel_id=1, source_target_pairs={{0,1},{1,0},{2,3},{3,2},{4,5},{5,4},{6,7},{7,6},{8,9},{9,8},{10,11... | collective-permute-start | bytes 1966088 | tf_op jit(solution)/shard_map/ppermute | solution.py:22
  27.9 18.7 %copy-start.2 = (bf16[320,1024]{1,0:T(8,128)(2,1)S(1)}, bf16[320,1024]{1,0:T(8,128)(2,1)}, u32[]{:S(2)}) copy-start(bf16[320,1024]{1,0:T(8,128)(2,1)} %refs_0_.8) | copy-start | bytes 1966084
  27.9 18.7 %copy-start.4 = (bf16[320,1024]{1,0:T(8,128)(2,1)S(1)}, bf16[320,1024]{1,0:T(8,128)(2,1)}, u32[]{:S(2)}) copy-start(bf16[320,1024]{1,0:T(8,128)(2,1)} %copy-done.3) | copy-start | bytes 1966084
  39.7 16.4 %collective-permute-start.13 = (bf16[320,1024]{1,0:T(8,128)(2,1)}, bf16[320,1024]{1,0:T(8,128)(2,1)S(1)}, u32[]{:S(2)}, u32[]{:S(2)}) collective-permute-start(bf16[320,1024]{1,0:T(8,128)(2,1)} %collective-permute-done.10.refs_4_), channel_id=1, source_target_pairs={{0,4},{4,0},{8,12},{12,8},{16,20},{20,16},{24,28},{28,24},{1,5},{5... | collective-permute-start | bytes 1966088 | tf_op jit(solution)/shard_map/ppermute | solution.py:22
  41.9 15.4 %collective-permute-start.6 = (bf16[320,1024]{1,0:T(8,128)(2,1)}, bf16[320,1024]{1,0:T(8,128)(2,1)S(1)}, u32[]{:S(2)}, u32[]{:S(2)}) collective-permute-start(bf16[320,1024]{1,0:T(8,128)(2,1)} %collective-permute-done.2.refs_4_), channel_id=1, source_target_pairs={{0,2},{1,3},{2,0},{3,1},{4,6},{5,7},{6,4},{7,5},{8,10},{9,11},{10,... | collective-permute-start | bytes 1966088 | tf_op jit(solution)/shard_map/ppermute | solution.py:22
  43.5 16.4 %collective-permute-start.11 = (bf16[320,1024]{1,0:T(8,128)(2,1)S(1)}, bf16[320,1024]{1,0:T(8,128)(2,1)S(1)}, u32[]{:S(2)}, u32[]{:S(2)}) collective-permute-start(bf16[320,1024]{1,0:T(8,128)(2,1)S(1)} %shard_map.58), channel_id=1, source_target_pairs={{0,8},{4,28},{8,16},{12,4},{16,24},{20,12},{24,0},{28,20},{1,9},{5... | collective-permute-start | bytes 1966088 | tf_op jit(solution)/shard_map/ppermute | solution.py:22
  46.6 17.6 %collective-permute-start.12 = (bf16[320,1024]{1,0:T(8,128)(2,1)S(1)}, bf16[320,1024]{1,0:T(8,128)(2,1)S(1)}, u32[]{:S(2)}, u32[]{:S(2)}) collective-permute-start(bf16[320,1024]{1,0:T(8,128)(2,1)S(1)} %copy-done.2), channel_id=1, source_target_pairs={{0,1},{1,0},{2,3},{3,2},{4,5},{5,4},{6,7},{7,6},{8,9},{9,8},{10,11... | collective-permute-start | bytes 1966088 | tf_op jit(solution)/shard_map/ppermute | solution.py:22
  57.2 16.0 %collective-permute-start.14 = (bf16[320,1024]{1,0:T(8,128)(2,1)S(1)}, bf16[320,1024]{1,0:T(8,128)(2,1)S(1)}, u32[]{:S(2)}, u32[]{:S(2)}) collective-permute-start(bf16[320,1024]{1,0:T(8,128)(2,1)S(1)} %collective-permute-done.6.refs_2_), channel_id=1, source_target_pairs={{0,4},{4,0},{8,12},{12,8},{16,20},{20,16},{24,28},{28,24},{1,5},{5... | collective-permute-start | bytes 1966088 | tf_op jit(solution)/shard_map/ppermute | solution.py:22
  60.7 13.7 %collective-permute-start.15 = (bf16[320,1024]{1,0:T(8,128)(2,1)S(1)}, bf16[320,1024]{1,0:T(8,128)(2,1)S(1)}, u32[]{:S(2)}, u32[]{:S(2)}) collective-permute-start(bf16[320,1024]{1,0:T(8,128)(2,1)S(1)} %shard_map.59.refs_3_), channel_id=1, source_target_pairs={{0,2},{1,3},{2,0},{3,1},{4,6},{5,7},{6,4},{7,5},{8,10},{9,11},{10,... | collective-permute-start | bytes 1966088 | tf_op jit(solution)/shard_map/ppermute | solution.py:22
  63.0 15.5 %collective-permute-start.20 = (bf16[320,1024]{1,0:T(8,128)(2,1)S(1)}, bf16[320,1024]{1,0:T(8,128)(2,1)S(1)}, u32[]{:S(2)}, u32[]{:S(2)}) collective-permute-start(bf16[320,1024]{1,0:T(8,128)(2,1)S(1)} %shard_map.65), channel_id=1, source_target_pairs={{0,24},{4,28},{8,0},{12,4},{16,8},{20,12},{24,16},{28,20},{1,25},{... | collective-permute-start | bytes 1966088 | tf_op jit(solution)/shard_map/ppermute | solution.py:22
  77.3 4.1 %collective-permute-start.16 = (f32[8,640]{1,0:T(8,128)S(1)}, f32[8,640]{1,0:T(8,128)S(1)}, u32[]{:S(2)}, u32[]{:S(2)}) collective-permute-start(f32[8,640]{1,0:T(8,128)S(1)} %get-tuple-element.56.own), channel_id=1, source_target_pairs={{0,4},{4,0},{8,12},{12,8},{16,20},{20,16},{24,28},{28,24},{1,5},{5... | collective-permute-start | bytes 61448 | tf_op jit(solution)/shard_map/ppermute | solution.py:22
  79.3 12.4 %collective-permute-start.21 = (bf16[320,1024]{1,0:T(8,128)(2,1)S(1)}, bf16[320,1024]{1,0:T(8,128)(2,1)S(1)}, u32[]{:S(2)}, u32[]{:S(2)}) collective-permute-start(bf16[320,1024]{1,0:T(8,128)(2,1)S(1)} %shard_map.66.refs_3_), channel_id=1, source_target_pairs={{0,2},{1,3},{2,0},{3,1},{4,6},{5,7},{6,4},{7,5},{8,10},{9,11},{10,... | collective-permute-start | bytes 1966088 | tf_op jit(solution)/shard_map/ppermute | solution.py:22
  81.4 12.9 %collective-permute-start.26 = (bf16[320,1024]{1,0:T(8,128)(2,1)S(1)}, bf16[320,1024]{1,0:T(8,128)(2,1)S(1)}, u32[]{:S(2)}, u32[]{:S(2)}) collective-permute-start(bf16[320,1024]{1,0:T(8,128)(2,1)S(1)} %shard_map.70.refs_2_), channel_id=1, source_target_pairs={{0,4},{4,0},{8,12},{12,8},{16,20},{20,16},{24,28},{28,24},{1,5},{5... | collective-permute-start | bytes 1966088 | tf_op jit(solution)/shard_map/ppermute | solution.py:22
  82.6 7.4 %collective-permute-start.17 = (f32[8,640]{1,0:T(8,128)S(1)}, f32[8,640]{1,0:T(8,128)S(1)}, u32[]{:S(2)}, u32[]{:S(2)}) collective-permute-start(f32[8,640]{1,0:T(8,128)S(1)} %get-tuple-element.56.own), channel_id=1, source_target_pairs={{0,20},{4,16},{8,28},{12,24},{16,4},{20,0},{24,12},{28,8},{1,21},{... | collective-permute-start | bytes 61448 | tf_op jit(solution)/shard_map/ppermute | solution.py:22
  83.4 6.5 %collective-permute-start.19 = (f32[16,640]{1,0:T(8,128)S(1)}, f32[16,640]{1,0:T(8,128)S(1)}, u32[]{:S(2)}, u32[]{:S(2)}) collective-permute-start(f32[16,640]{1,0:T(8,128)S(1)} %constant_dynamic-update-slice_fusion), channel_id=1, source_target_pairs={{0,8},{4,12},{8,16},{12,20},{16,24},{20,28},{24,0},{28,4},{1,9},{5... | collective-permute-start | bytes 122888 | tf_op jit(solution)/shard_map/ppermute | solution.py:22
  85.5 4.5 %collective-permute-start.18 = (f32[16,640]{1,0:T(8,128)S(1)}, f32[16,640]{1,0:T(8,128)S(1)}, u32[]{:S(2)}, u32[]{:S(2)}) collective-permute-start(f32[16,640]{1,0:T(8,128)S(1)} %constant_dynamic-update-slice_fusion), channel_id=1, source_target_pairs={{0,24},{4,28},{8,0},{12,4},{16,8},{20,12},{24,16},{28,20},{1,25},{... | collective-permute-start | bytes 122888 | tf_op jit(solution)/shard_map/ppermute | solution.py:22
  91.7 5.3 %collective-permute-start.24 = (f32[24,320]{1,0:T(8,128)S(1)}, f32[24,320]{1,0:T(8,128)S(1)}, u32[]{:S(2)}, u32[]{:S(2)}) collective-permute-start(f32[24,320]{1,0:T(8,128)S(1)} %shard_map.64.refs_0_.own), channel_id=1, source_target_pairs={{0,3},{1,2},{2,1},{3,0},{4,7},{5,6},{6,5},{7,4},{8,11},{9,10},{10,... | collective-permute-start | bytes 92168 | tf_op jit(solution)/shard_map/ppermute | solution.py:22
  91.7 5.3 %collective-permute-start.23 = (f32[24,320]{1,0:T(8,128)S(1)}, f32[24,320]{1,0:T(8,128)S(1)}, u32[]{:S(2)}, u32[]{:S(2)}) collective-permute-start(f32[24,320]{1,0:T(8,128)S(1)} %shard_map.64.refs_0_.own), channel_id=1, source_target_pairs={{0,1},{1,0},{2,3},{3,2},{4,5},{5,4},{6,7},{7,6},{8,9},{9,8},{10,11... | collective-permute-start | bytes 92168 | tf_op jit(solution)/shard_map/ppermute | solution.py:22
  93.1 4.0 %collective-permute-start.22 = (f32[24,320]{1,0:T(8,128)S(1)}, f32[24,320]{1,0:T(8,128)S(1)}, u32[]{:S(2)}, u32[]{:S(2)}) collective-permute-start(f32[24,320]{1,0:T(8,128)S(1)} %shard_map.64.refs_0_.own), channel_id=1, source_target_pairs={{0,2},{1,3},{2,0},{3,1},{4,6},{5,7},{6,4},{7,5},{8,10},{9,11},{10,... | collective-permute-start | bytes 92168 | tf_op jit(solution)/shard_map/ppermute | solution.py:22
  102.8 7.5 %collective-permute-start.25 = (f32[320,1024]{1,0:T(8,128)S(1)}, f32[320,1024]{1,0:T(8,128)S(1)}, u32[]{:S(2)}, u32[]{:S(2)}) collective-permute-start(f32[320,1024]{1,0:T(8,128)S(1)} %get-tuple-element.66), channel_id=1, source_target_pairs={{0,1},{1,0},{2,3},{3,2},{4,5},{5,4},{6,7},{7,6},{8,9},{9,8},{10,11... | collective-permute-start | bytes 3932168 | tf_op jit(solution)/shard_map/ppermute | solution.py:22
  108.2 3.3 %collective-permute-start.27 = (f32[320,1024]{1,0:T(8,128)S(1)}, f32[320,1024]{1,0:T(8,128)S(1)}, u32[]{:S(2)}, u32[]{:S(2)}) collective-permute-start(f32[320,1024]{1,0:T(8,128)S(1)} %get-tuple-element.80), channel_id=1, source_target_pairs={{0,1},{1,0},{2,3},{3,2},{4,5},{5,4},{6,7},{7,6},{8,9},{9,8},{10,11... | collective-permute-start | bytes 3932168 | tf_op jit(solution)/shard_map/ppermute | solution.py:22

commit v8 on v7

--- a/solution.py
+++ b/solution.py
@@ -248,28 +248,35 @@
     return col, core_col, row, core_row
 
 
-def fill_info(sums, col_out, row_out):
+def fill_info(sums, score, col_out, row_out):
     col, core_col, row, core_row = sums
-    zeros = jnp.zeros((3, col_out.shape[1]), F32)
-    for out, part, more in ((col_out, col, core_col[0]), (row_out, row, core_row)):
+    none = jnp.zeros(score.shape, F32)
+    zeros = jnp.zeros((2, col_out.shape[1]), F32)
+    for out, part, more, fifth in (
+        (col_out, col, core_col[0], side_by_side(core_col[1], score)),
+        (row_out, row, core_row, side_by_side(none, none)),
+    ):
         a, b, c, d = part
         out[pl.ds(0, 1), :] = side_by_side(a[0], a[1])
         out[pl.ds(1, 1), :] = side_by_side(b[0], c[0])
         out[pl.ds(2, 1), :] = side_by_side(b[1], d[0])
         out[pl.ds(3, 1), :] = side_by_side(c[1], d[1])
         out[pl.ds(4, 1), :] = side_by_side(a[0], more)
-        out[pl.ds(5, 3), :] = zeros
-
-
-def loss_kernel(scalars, partner, own, across, core, corner, out):
-    col, core_col, row, _ = block_sums(own, across, core, corner)
+        out[pl.ds(5, 1), :] = fifth
+        out[pl.ds(6, 2), :] = zeros
+
+
+def loss_kernel(scalars, partner, col_info, row_info, out):
+    own, across = halves(col_info[pl.ds(0, 1), :])
+    core = halves(col_info[pl.ds(4, 1), :])[1]
+    corner, score = halves(col_info[pl.ds(5, 1), :])
+    row = halves(row_info[pl.ds(4, 1), :])[0]
     chosen = as_column(partner[...])
     found = jnp.zeros(chosen.shape, F32)
-    for i, value in enumerate((col[0][0], col[0][1], core_col[0], core_col[1])):
+    for i, value in enumerate((own, across, core, corner)):
         hit = chosen == ids(scalars, i + 1, value.shape[1])
         found = found + jnp.sum(jnp.where(hit, value, 0.0), axis=1, keepdims=True)
-    score = own[pl.ds(16, 1), :] + core[pl.ds(17, 1), :]
-    out[...] = (0.5 * row[0][0] + 0.5 * as_row(found) - score)[0]
+    out[...] = (0.5 * row + 0.5 * as_row(found) - score)[0]
 
 
 def small_call(kernel, shapes, *args, scalars=0):
@@ -290,7 +297,8 @@
         row_info, col_info, *made, own_out, other_out, weights = refs
     else:
         *made, own_out, other_out, col_info, row_info, weights = refs[4:]
-        fill_info(block_sums(*refs[:4]), col_info, row_info)
+        score = refs[0][pl.ds(16, 1), :] + refs[2][pl.ds(17, 1), :]
+        fill_info(block_sums(*refs[:4]), score, col_info, row_info)
     made = list(zip(made[::2], made[1::2]))
     row = as_column(row_info[pl.ds(4, 1), :])
     partners = side_by_side(first[...], second[...])
@@ -429,7 +437,7 @@
     k_own, k_other = grad(
         scalars, True, factor, partner, partner_across, (col_info, row_info), (q_made_0, q_made_1, q_made_2)
     )
-    loss = small_call(loss_kernel, [(rows,)], scalars, after(partner, q_other), *sums, scalars=1)[0]
+    loss = small_call(loss_kernel, [(rows,)], scalars, partner, col_info, row_info, scalars=1)[0]
     grad_queries = add(q_own, core(q_other))
     grad_keys = add(k_own, core(k_other))
     return (loss, grad_queries, grad_keys)

time: 113 us -> 113 us (level)
  no operation moved by 1% of the time
where the time goes in v8:
time: 113 us
  Pallas kernels  43.7 us (39%)
  waiting for transfers between devices  33.7 us (30%)
  starting transfers between devices  33.5 us (30%)
    ppermute x28, waiting for transfers between devices, shift(): return lax.ppermute(array, axis, pairs)  33.7 us
    ppermute x28, starting transfers between devices, shift(): return lax.ppermute(array, axis, pairs)  33.5 us
    pallas_call x6, Pallas kernels, score(): pl.pallas_call(functools.partial(score_kernel, len(shards), given, start,...  24.2 us
    pallas_call x2, Pallas kernels, grad(): pl.pallas_call(functools.partial(grad_kernel, keys, factor), out_shape=(k...  10.9 us
    pallas_call x5, Pallas kernels, choose(): pl.pallas_call(choose_kernel, out_shape=jax.ShapeDtypeStruct(first.shape,...  3.84 us
    pallas_call x2, Pallas kernels, small_call(): pl.pallas_call(kernel, out_shape=tuple((jax.ShapeDtypeStruct(s, F32) for...  2.43 us
  transfers between devices with their start and end apart: 28, of which 14 were waited for; matrix products, arithmetic and copies ran while one was open for 0% of the time, Pallas kernels for 33%

profile of v8, /device:TPU:0, one launch (start us, length us, event | category | flops | bytes accessed | tf_op | source)
XLA Modules:
  0.0 112.9 jit_solution(18009295900054289965)
XLA Ops:
  0.6 3.0 %collective-permute-start.3 = (s32[1,320]{1,0:T(1,128)}, s32[1,320]{1,0:T(1,128)S(1)}, u32[]{:S(2)}, u32[]{:S(2)}) collective-permute-start(s32[1,320]{1,0:T(1,128)} %first.3), channel_id=1, source_target_pairs={{0,2},{1,3},{2,0},{3,1},{4,6},{5,7},{6,4},{7,5},{8,10},{9,11},{10,... | collective-permute-start | bytes 3848 | tf_op jit(solution)/shard_map/ppermute | solution.py:22
  3.7 1.6 %collective-permute-start.2 = (bf16[320,1024]{1,0:T(8,128)(2,1)}, bf16[320,1024]{1,0:T(8,128)(2,1)}, u32[]{:S(2)}, u32[]{:S(2)}) collective-permute-start(bf16[320,1024]{1,0:T(8,128)(2,1)} %refs_0_.8), channel_id=1, source_target_pairs={{0,8},{4,12},{8,16},{12,20},{16,24},{20,28},{24,0},{28,4},{1,9},{5... | collective-permute-start | bytes 1966088 | tf_op jit(solution)/shard_map/ppermute | solution.py:22
  5.4 2.0 %collective-permute-start.4 = (bf16[320,1024]{1,0:T(8,128)(2,1)}, bf16[320,1024]{1,0:T(8,128)(2,1)S(1)}, u32[]{:S(2)}, u32[]{:S(2)}) collective-permute-start(bf16[320,1024]{1,0:T(8,128)(2,1)} %refs_0_.8), channel_id=1, source_target_pairs={{0,2},{1,3},{2,0},{3,1},{4,6},{5,7},{6,4},{7,5},{8,10},{9,11},{10,... | collective-permute-start | bytes 1966088 | tf_op jit(solution)/shard_map/ppermute | solution.py:22
  7.4 3.5 %collective-permute-start.7 = (bf16[320,1024]{1,0:T(8,128)(2,1)}, bf16[320,1024]{1,0:T(8,128)(2,1)S(1)}, u32[]{:S(2)}, u32[]{:S(2)}) collective-permute-start(bf16[320,1024]{1,0:T(8,128)(2,1)} %refs_0_.8), channel_id=1, source_target_pairs={{0,4},{8,12},{16,20},{24,28},{1,5},{9,13},{17,21},{25,29},{2,6},{1... | collective-permute-start | bytes 1966088 | tf_op jit(solution)/shard_map/ppermute | solution.py:22
  10.9 1.3 %collective-permute-start.8 = (bf16[320,1024]{1,0:T(8,128)(2,1)}, bf16[320,1024]{1,0:T(8,128)(2,1)S(1)}, u32[]{:S(2)}, u32[]{:S(2)}) collective-permute-start(bf16[320,1024]{1,0:T(8,128)(2,1)} %refs_0_.6), channel_id=1, source_target_pairs={{4,0},{12,8},{20,16},{28,24},{5,1},{13,9},{21,17},{29,25},{6,2},{1... | collective-permute-start | bytes 1966088 | tf_op jit(solution)/shard_map/ppermute | solution.py:22
  12.2 10.8 %collective-permute-done.2.refs_4_ = bf16[320,1024]{1,0:T(8,128)(2,1)} collective-permute-done((bf16[320,1024]{1,0:T(8,128)(2,1)}, bf16[320,1024]{1,0:T(8,128)(2,1)}, u32[]{:S(2)}, u32[]{:S(2)}) %collective-permute-start.2) | collective-permute-done | bytes 655392 | tf_op jit(solution)/shard_map/ppermute | solution.py:22
  23.0 1.7 %collective-permute-start.10 = (bf16[320,1024]{1,0:T(8,128)(2,1)}, bf16[320,1024]{1,0:T(8,128)(2,1)}, u32[]{:S(2)}, u32[]{:S(2)}) collective-permute-start(bf16[320,1024]{1,0:T(8,128)(2,1)} %refs_0_.6), channel_id=1, source_target_pairs={{0,24},{4,28},{8,0},{12,4},{16,8},{20,12},{24,16},{28,20},{1,25},{... | collective-permute-start | bytes 1966088 | tf_op jit(solution)/shard_map/ppermute | solution.py:22
  24.7 0.8 copy-done.3
  26.1 1.7 %collective-permute-done.8.first = bf16[320,1024]{1,0:T(8,128)(2,1)S(1)} collective-permute-done((bf16[320,1024]{1,0:T(8,128)(2,1)}, bf16[320,1024]{1,0:T(8,128)(2,1)S(1)}, u32[]{:S(2)}, u32[]{:S(2)}) %collective-permute-start.8) | collective-permute-done | bytes 655392 | tf_op jit(solution)/shard_map/ppermute | solution.py:22
  27.9 11.9 %collective-permute-done.10.refs_4_ = bf16[320,1024]{1,0:T(8,128)(2,1)} collective-permute-done((bf16[320,1024]{1,0:T(8,128)(2,1)}, bf16[320,1024]{1,0:T(8,128)(2,1)}, u32[]{:S(2)}, u32[]{:S(2)}) %collective-permute-start.10) | collective-permute-done | bytes 655392 | tf_op jit(solution)/shard_map/ppermute | solution.py:22
  39.7 1.5 %collective-permute-start.13 = (bf16[320,1024]{1,0:T(8,128)(2,1)}, bf16[320,1024]{1,0:T(8,128)(2,1)S(1)}, u32[]{:S(2)}, u32[]{:S(2)}) collective-permute-start(bf16[320,1024]{1,0:T(8,128)(2,1)} %collective-permute-done.10.refs_4_), channel_id=1, source_target_pairs={{0,4},{4,0},{8,12},{12,8},{16,20},{20,16},{24,28},{28,24},{1,5},{5... | collective-permute-start | bytes 1966088 | tf_op jit(solution)/shard_map/ppermute | solution.py:22
  41.2 0.6 collective-permute-done.5.second.refs_3_.first
  42.7 0.8 shard_map.58
  43.5 3.1 %collective-permute-start.11 = (bf16[320,1024]{1,0:T(8,128)(2,1)S(1)}, bf16[320,1024]{1,0:T(8,128)(2,1)S(1)}, u32[]{:S(2)}, u32[]{:S(2)}) collective-permute-start(bf16[320,1024]{1,0:T(8,128)(2,1)S(1)} %shard_map.58), channel_id=1, source_target_pairs={{0,8},{4,28},{8,16},{12,4},{16,24},{20,12},{24,0},{28,20},{1,9},{5... | collective-permute-start | bytes 1966088 | tf_op jit(solution)/shard_map/ppermute | solution.py:22
  46.6 6.9 %shard_map.60 = (f32[640,1280]{1,0:T(8,128)S(1)}, bf16[1280,1024]{1,0:T(8,128)(2,1)S(1)}, f32[8,640]{1,0:T(8,128)S(1)}) custom-call(s32[5]{0:T(128)S(1)} %stack.27.flag.scalars, bf16[320,1024]{1,0:T(8,128)(2,1)S(1)} %copy-done.1, bf16[320,1024]{1,0:T(8,128)(2,1)} %collective-permute-done.1.refs_1_, bf16[320,1024]{1,0:T(8,128)(2,1)S(1)} %copy-done.2, ...), custom_call_target="tpu_custom_call" | custom-call | flops 1677721600 | bytes 7208960 | tf_op jit(solution)/shard_map/pallas_call | solution.py:159
  53.5 2.7 %collective-permute-done.13.refs_5_.second = bf16[320,1024]{1,0:T(8,128)(2,1)S(1)} collective-permute-done((bf16[320,1024]{1,0:T(8,128)(2,1)}, bf16[320,1024]{1,0:T(8,128)(2,1)S(1)}, u32[]{:S(2)}, u32[]{:S(2)}) %collective-permute-start.13) | collective-permute-done | bytes 655392 | tf_op jit(solution)/shard_map/ppermute | solution.py:22
  56.2 1.1 collective-permute-done.6.refs_2_
  57.2 1.5 %collective-permute-start.14 = (bf16[320,1024]{1,0:T(8,128)(2,1)S(1)}, bf16[320,1024]{1,0:T(8,128)(2,1)S(1)}, u32[]{:S(2)}, u32[]{:S(2)}) collective-permute-start(bf16[320,1024]{1,0:T(8,128)(2,1)S(1)} %collective-permute-done.6.refs_2_), channel_id=1, source_target_pairs={{0,4},{4,0},{8,12},{12,8},{16,20},{20,16},{24,28},{28,24},{1,5},{5... | collective-permute-start | bytes 1966088 | tf_op jit(solution)/shard_map/ppermute | solution.py:22
  58.7 1.2 %collective-permute-done.11.first.second = bf16[320,1024]{1,0:T(8,128)(2,1)S(1)} collective-permute-done((bf16[320,1024]{1,0:T(8,128)(2,1)S(1)}, bf16[320,1024]{1,0:T(8,128)(2,1)S(1)}, u32[]{:S(2)}, u32[]{:S(2)}) %collective-permute-start.11) | collective-permute-done | bytes 655392 | tf_op jit(solution)/shard_map/ppermute | solution.py:22
  59.9 0.8 shard_map.59.refs_3_
  60.7 1.6 %collective-permute-start.15 = (bf16[320,1024]{1,0:T(8,128)(2,1)S(1)}, bf16[320,1024]{1,0:T(8,128)(2,1)S(1)}, u32[]{:S(2)}, u32[]{:S(2)}) collective-permute-start(bf16[320,1024]{1,0:T(8,128)(2,1)S(1)} %shard_map.59.refs_3_), channel_id=1, source_target_pairs={{0,2},{1,3},{2,0},{3,1},{4,6},{5,7},{6,4},{7,5},{8,10},{9,11},{10,... | collective-permute-start | bytes 1966088 | tf_op jit(solution)/shard_map/ppermute | solution.py:22
  62.2 0.8 shard_map.65
  63.0 1.2 %collective-permute-start.20 = (bf16[320,1024]{1,0:T(8,128)(2,1)S(1)}, bf16[320,1024]{1,0:T(8,128)(2,1)S(1)}, u32[]{:S(2)}, u32[]{:S(2)}) collective-permute-start(bf16[320,1024]{1,0:T(8,128)(2,1)S(1)} %shard_map.65), channel_id=1, source_target_pairs={{0,24},{4,28},{8,0},{12,4},{16,8},{20,12},{24,16},{28,20},{1,25},{... | collective-permute-start | bytes 1966088 | tf_op jit(solution)/shard_map/ppermute | solution.py:22
  64.2 4.8 %shard_map.61 = (f32[640,1280]{1,0:T(8,128)S(1)}, bf16[1280,1024]{1,0:T(8,128)(2,1)S(1)}, f32[8,128]{1,0:T(8,128)S(1)}) custom-call(s32[5]{0:T(128)S(1)} %stack.27.flag.scalars, bf16[320,1024]{1,0:T(8,128)(2,1)S(1)} %copy-done.2, bf16[320,1024]{1,0:T(8,128)(2,1)S(1)} %collective-permute-done.12.refs_1_, bf16[320,1024]{1,0:T(8,128)(2,1)S(1)} %copy-done.1, ...), custom_call_target="tpu_custom_call" | custom-call | flops 1677721600 | bytes 7208960 | tf_op jit(solution)/shard_map/pallas_call | solution.py:159
  69.0 4.2 %shard_map.62 = (f32[640,640]{1,0:T(8,128)S(1)}, bf16[640,1024]{1,0:T(8,128)(2,1)S(1)}, f32[8,640]{1,0:T(8,128)S(1)}, bf16[640,1024]{1,0:T(8,128)(2,1)S(1)}) custom-call(s32[5]{0:T(128)S(1)} %stack.27.flag.scalars, bf16[320,1024]{1,0:T(8,128)(2,1)S(1)} %copy-done.1, bf16[320,1024]{1,0:T(8,128)(2,1)} %collective-permute-done.1.refs_1_, ...), custom_call_target="tpu_custom_call" | custom-call | flops 838860800 | bytes 4259840 | tf_op jit(solution)/shard_map/pallas_call | solution.py:159
  73.2 1.2 %collective-permute-done.15.refs_2_ = bf16[320,1024]{1,0:T(8,128)(2,1)S(1)} collective-permute-done((bf16[320,1024]{1,0:T(8,128)(2,1)S(1)}, bf16[320,1024]{1,0:T(8,128)(2,1)S(1)}, u32[]{:S(2)}, u32[]{:S(2)}) %collective-permute-start.15) | collective-permute-done | bytes 655392 | tf_op jit(solution)/shard_map/ppermute | solution.py:22
  74.4 2.9 %shard_map.63 = (f32[640,640]{1,0:T(8,128)S(1)}, bf16[640,1024]{1,0:T(8,128)(2,1)S(1)}, f32[8,640]{1,0:T(8,128)S(1)}) custom-call(s32[5]{0:T(128)S(1)} %stack.27.flag.scalars, bf16[640,1024]{1,0:T(8,128)(2,1)S(1)} %get-tuple-element.51.refs_0_, bf16[320,1024]{1,0:T(8,128)(2,1)S(1)} %collective-permute-done.14.refs_1_, ...), custom_call_target="tpu_custom_call" | custom-call | flops 838860800 | bytes 4259840 | tf_op jit(solution)/shard_map/pallas_call | solution.py:159
  77.3 1.2 %collective-permute-start.16 = (f32[8,640]{1,0:T(8,128)S(1)}, f32[8,640]{1,0:T(8,128)S(1)}, u32[]{:S(2)}, u32[]{:S(2)}) collective-permute-start(f32[8,640]{1,0:T(8,128)S(1)} %get-tuple-element.55.own), channel_id=1, source_target_pairs={{0,4},{4,0},{8,12},{12,8},{16,20},{20,16},{24,28},{28,24},{1,5},{5... | collective-permute-start | bytes 61448 | tf_op jit(solution)/shard_map/ppermute | solution.py:22
  78.5 0.8 shard_map.66.refs_3_
  79.3 0.7 collective-permute-start.21
  80.0 0.8 shard_map.70.refs_2_
  80.8 0.6 collective-permute-done.16.beside
  81.4 1.1 %collective-permute-start.26 = (bf16[320,1024]{1,0:T(8,128)(2,1)S(1)}, bf16[320,1024]{1,0:T(8,128)(2,1)S(1)}, u32[]{:S(2)}, u32[]{:S(2)}) collective-permute-start(bf16[320,1024]{1,0:T(8,128)(2,1)S(1)} %shard_map.70.refs_2_), channel_id=1, source_target_pairs={{0,4},{4,0},{8,12},{12,8},{16,20},{20,16},{24,28},{28,24},{1,5},{5... | collective-permute-start | bytes 1966088 | tf_op jit(solution)/shard_map/ppermute | solution.py:22
  82.6 0.9 collective-permute-start.17
  83.4 2.1 %collective-permute-start.19 = (f32[16,640]{1,0:T(8,128)S(1)}, f32[16,640]{1,0:T(8,128)S(1)}, u32[]{:S(2)}, u32[]{:S(2)}) collective-permute-start(f32[16,640]{1,0:T(8,128)S(1)} %constant_dynamic-update-slice_fusion), channel_id=1, source_target_pairs={{0,8},{4,12},{8,16},{12,20},{16,24},{20,28},{24,0},{28,4},{1,9},{5... | collective-permute-start | bytes 122888 | tf_op jit(solution)/shard_map/ppermute | solution.py:22
  85.5 1.7 %collective-permute-start.18 = (f32[16,640]{1,0:T(8,128)S(1)}, f32[16,640]{1,0:T(8,128)S(1)}, u32[]{:S(2)}, u32[]{:S(2)}) collective-permute-start(f32[16,640]{1,0:T(8,128)S(1)} %constant_dynamic-update-slice_fusion), channel_id=1, source_target_pairs={{0,24},{4,28},{8,0},{12,4},{16,8},{20,12},{24,16},{28,20},{1,25},{... | collective-permute-start | bytes 122888 | tf_op jit(solution)/shard_map/ppermute | solution.py:22
  87.3 2.7 %shard_map.71 = (f32[640,640]{1,0:T(8,128)S(1)}, bf16[640,1024]{1,0:T(8,128)(2,1)S(1)}, f32[8,128]{1,0:T(8,128)}) custom-call(s32[5]{0:T(128)S(1)} %stack.27.flag.scalars, bf16[320,1024]{1,0:T(8,128)(2,1)S(1)} %copy-done.2, bf16[320,1024]{1,0:T(8,128)(2,1)S(1)} %collective-permute-done.12.refs_1_, bf16[320,1024]{1,0:T(8,128)(2,1)S(1)} %shard_map.70.refs_2_, ...), custom_call_target="tpu_custom_call" | custom-call | flops 838860800 | bytes 4259840 | tf_op jit(solution)/shard_map/pallas_call | solution.py:159
  90.0 0.7 shard_map.64.refs_0_
  90.7 1.0 collective-permute-done.21.refs_3_
  91.7 1.5 %collective-permute-start.23 = (f32[24,320]{1,0:T(8,128)S(1)}, f32[24,320]{1,0:T(8,128)S(1)}, u32[]{:S(2)}, u32[]{:S(2)}) collective-permute-start(f32[24,320]{1,0:T(8,128)S(1)} %shard_map.64.refs_0_), channel_id=1, source_target_pairs={{0,1},{1,0},{2,3},{3,2},{4,5},{5,4},{6,7},{7,6},{8,9},{9,8},{10,11... | collective-permute-start | bytes 92168 | tf_op jit(solution)/shard_map/ppermute | solution.py:22
  93.1 0.7 collective-permute-start.22
  94.3 2.7 %shard_map.72 = (f32[640,640]{1,0:T(8,128)S(1)}, bf16[640,1024]{1,0:T(8,128)(2,1)S(1)}, f32[8,128]{1,0:T(8,128)}) custom-call(s32[5]{0:T(128)S(1)} %stack.27.flag.scalars, bf16[320,1024]{1,0:T(8,128)(2,1)S(1)} %copy-done.2, bf16[320,1024]{1,0:T(8,128)(2,1)S(1)} %collective-permute-done.12.refs_1_, bf16[320,1024]{1,0:T(8,128)(2,1)S(1)} %collective-permute-done.26.refs_2_, ...), custom_call_target="tpu_custom_call" | custom-call | flops 838860800 | bytes 4259840 | tf_op jit(solution)/shard_map/pallas_call | solution.py:159
  97.1 5.7 %shard_map.67 = (f32[320,1024]{1,0:T(8,128)S(1)}, f32[320,1024]{1,0:T(8,128)S(1)}, f32[8,640]{1,0:T(8,128)S(1)}, f32[8,640]{1,0:T(8,128)S(1)}) custom-call(s32[5]{0:T(128)S(1)} %stack.27.flag.scalars, s32[1,320]{1,0:T(1,128)S(1)} %copy-done, s32[1,320]{1,0:T(1,128)S(1)} %collective-permute-done.refs_7_.second, f32[24,320]{1,0:T(8,128)S(1)} %shard_map.64.refs_0_, ...), custom_call_target="tpu_custom_call" | custom-call | flops 3355443200 | bytes 14417920 | tf_op jit(solution)/shard_map/pallas_call | solution.py:339
  102.9 5.3 %shard_map.73 = (f32[320,1024]{1,0:T(8,128)S(1)}, f32[320,1024]{1,0:T(8,128)S(1)}) custom-call(s32[5]{0:T(128)S(1)} %stack.27.flag.scalars, s32[1,320]{1,0:T(1,128)S(1)} %copy-done, s32[1,320]{1,0:T(1,128)S(1)} %collective-permute-done.3.refs_6_.second, f32[8,640]{1,0:T(8,128)S(1)} %get-tuple-element.65.col_info.refs_0_, ...), custom_call_target="tpu_custom_call" | custom-call | flops 3355443200 | bytes 14417920 | tf_op jit(solution)/shard_map/pallas_call | solution.py:339
  108.1 0.6 collective-permute-start.27
  108.7 1.8 %shard_map.68 = f32[320]{0:T(512)} custom-call(s32[5]{0:T(128)S(1)} %stack.27.flag.scalars, s32[1,320]{1,0:T(1,128)S(1)} %copy-done, f32[8,640]{1,0:T(8,128)S(1)} %get-tuple-element.65.col_info.refs_0_, f32[8,640]{1,0:T(8,128)S(1)} %get-tuple-element.66.row_info.refs_1_), custom_call_target="tpu_custom_call" | custom-call | flops 100000 | bytes 400000 | tf_op jit(solution)/shard_map/pallas_call | solution.py:283
  110.5 1.1 shard_map.69
  111.6 1.1 shard_map.74
  (38 shorter events, 2.4 us)
Async XLA Ops:
  0.6 45.9 %copy-start = (s32[1,320]{1,0:T(1,128)S(1)}, s32[1,320]{1,0:T(1,128)}, u32[]{:S(2)}) copy-start(s32[1,320]{1,0:T(1,128)} %first.3) | copy-start | bytes 3844
  0.6 45.9 %copy-start.1 = (bf16[320,1024]{1,0:T(8,128)(2,1)S(1)}, bf16[320,1024]{1,0:T(8,128)(2,1)}, u32[]{:S(2)}) copy-start(bf16[320,1024]{1,0:T(8,128)(2,1)} %refs_0_.6) | copy-start | bytes 1966084
  0.6 4.8 %collective-permute-start.3 = (s32[1,320]{1,0:T(1,128)}, s32[1,320]{1,0:T(1,128)S(1)}, u32[]{:S(2)}, u32[]{:S(2)}) collective-permute-start(s32[1,320]{1,0:T(1,128)} %first.3), channel_id=1, source_target_pairs={{0,2},{1,3},{2,0},{3,1},{4,6},{5,7},{6,4},{7,5},{8,10},{9,11},{10,... | collective-permute-start | bytes 3848 | tf_op jit(solution)/shard_map/ppermute | solution.py:22
  3.7 1.8 %collective-permute-start = (s32[1,320]{1,0:T(1,128)}, s32[1,320]{1,0:T(1,128)S(1)}, u32[]{:S(2)}, u32[]{:S(2)}) collective-permute-start(s32[1,320]{1,0:T(1,128)} %first.3), channel_id=1, source_target_pairs={{0,1},{1,0},{2,3},{3,2},{4,5},{5,4},{6,7},{7,6},{8,9},{9,8},{10,11... | collective-permute-start | bytes 3848 | tf_op jit(solution)/shard_map/ppermute | solution.py:22
  3.7 19.3 %collective-permute-start.2 = (bf16[320,1024]{1,0:T(8,128)(2,1)}, bf16[320,1024]{1,0:T(8,128)(2,1)}, u32[]{:S(2)}, u32[]{:S(2)}) collective-permute-start(bf16[320,1024]{1,0:T(8,128)(2,1)} %refs_0_.8), channel_id=1, source_target_pairs={{0,8},{4,12},{8,16},{12,20},{16,24},{20,28},{24,0},{28,4},{1,9},{5... | collective-permute-start | bytes 1966088 | tf_op jit(solution)/shard_map/ppermute | solution.py:22
  5.4 19.3 %collective-permute-start.4 = (bf16[320,1024]{1,0:T(8,128)(2,1)}, bf16[320,1024]{1,0:T(8,128)(2,1)S(1)}, u32[]{:S(2)}, u32[]{:S(2)}) collective-permute-start(bf16[320,1024]{1,0:T(8,128)(2,1)} %refs_0_.8), channel_id=1, source_target_pairs={{0,2},{1,3},{2,0},{3,1},{4,6},{5,7},{6,4},{7,5},{8,10},{9,11},{10,... | collective-permute-start | bytes 1966088 | tf_op jit(solution)/shard_map/ppermute | solution.py:22
  7.4 18.7 %collective-permute-start.7 = (bf16[320,1024]{1,0:T(8,128)(2,1)}, bf16[320,1024]{1,0:T(8,128)(2,1)S(1)}, u32[]{:S(2)}, u32[]{:S(2)}) collective-permute-start(bf16[320,1024]{1,0:T(8,128)(2,1)} %refs_0_.8), channel_id=1, source_target_pairs={{0,4},{8,12},{16,20},{24,28},{1,5},{9,13},{17,21},{25,29},{2,6},{1... | collective-permute-start | bytes 1966088 | tf_op jit(solution)/shard_map/ppermute | solution.py:22
  10.9 16.9 %collective-permute-start.8 = (bf16[320,1024]{1,0:T(8,128)(2,1)}, bf16[320,1024]{1,0:T(8,128)(2,1)S(1)}, u32[]{:S(2)}, u32[]{:S(2)}) collective-permute-start(bf16[320,1024]{1,0:T(8,128)(2,1)} %refs_0_.6), channel_id=1, source_target_pairs={{4,0},{12,8},{20,16},{28,24},{5,1},{13,9},{21,17},{29,25},{6,2},{1... | collective-permute-start | bytes 1966088 | tf_op jit(solution)/shard_map/ppermute | solution.py:22
  23.0 16.8 %collective-permute-start.10 = (bf16[320,1024]{1,0:T(8,128)(2,1)}, bf16[320,1024]{1,0:T(8,128)(2,1)}, u32[]{:S(2)}, u32[]{:S(2)}) collective-permute-start(bf16[320,1024]{1,0:T(8,128)(2,1)} %refs_0_.6), channel_id=1, source_target_pairs={{0,24},{4,28},{8,0},{12,4},{16,8},{20,12},{24,16},{28,20},{1,25},{... | collective-permute-start | bytes 1966088 | tf_op jit(solution)/shard_map/ppermute | solution.py:22
  24.7 0.8 copy-start.3
  25.6 16.3 %collective-permute-start.5 = (bf16[320,1024]{1,0:T(8,128)(2,1)}, bf16[320,1024]{1,0:T(8,128)(2,1)S(1)}, u32[]{:S(2)}, u32[]{:S(2)}) collective-permute-start(bf16[320,1024]{1,0:T(8,128)(2,1)} %refs_0_.6), channel_id=1, source_target_pairs={{0,2},{1,3},{2,0},{3,1},{4,6},{5,7},{6,4},{7,5},{8,10},{9,11},{10,... | collective-permute-start | bytes 1966088 | tf_op jit(solution)/shard_map/ppermute | solution.py:22
  27.8 14.9 %collective-permute-start.9 = (bf16[320,1024]{1,0:T(8,128)(2,1)}, bf16[320,1024]{1,0:T(8,128)(2,1)S(1)}, u32[]{:S(2)}, u32[]{:S(2)}) collective-permute-start(bf16[320,1024]{1,0:T(8,128)(2,1)} %collective-permute-done.2.refs_4_), channel_id=1, source_target_pairs={{0,4},{4,0},{8,12},{12,8},{16,20},{20,16},{24,28},{28,24},{1,5},{5... | collective-permute-start | bytes 1966088 | tf_op jit(solution)/shard_map/ppermute | solution.py:22
  27.8 18.8 %collective-permute-start.1 = (bf16[320,1024]{1,0:T(8,128)(2,1)}, bf16[320,1024]{1,0:T(8,128)(2,1)}, u32[]{:S(2)}, u32[]{:S(2)}) collective-permute-start(bf16[320,1024]{1,0:T(8,128)(2,1)} %refs_0_.6), channel_id=1, source_target_pairs={{0,1},{1,0},{2,3},{3,2},{4,5},{5,4},{6,7},{7,6},{8,9},{9,8},{10,11... | collective-permute-start | bytes 1966088 | tf_op jit(solution)/shard_map/ppermute | solution.py:22
  27.9 18.7 %copy-start.2 = (bf16[320,1024]{1,0:T(8,128)(2,1)S(1)}, bf16[320,1024]{1,0:T(8,128)(2,1)}, u32[]{:S(2)}) copy-start(bf16[320,1024]{1,0:T(8,128)(2,1)} %refs_0_.8) | copy-start | bytes 1966084
  27.9 18.7 %copy-start.4 = (bf16[320,1024]{1,0:T(8,128)(2,1)S(1)}, bf16[320,1024]{1,0:T(8,128)(2,1)}, u32[]{:S(2)}) copy-start(bf16[320,1024]{1,0:T(8,128)(2,1)} %copy-done.3) | copy-start | bytes 1966084
  39.7 16.4 %collective-permute-start.13 = (bf16[320,1024]{1,0:T(8,128)(2,1)}, bf16[320,1024]{1,0:T(8,128)(2,1)S(1)}, u32[]{:S(2)}, u32[]{:S(2)}) collective-permute-start(bf16[320,1024]{1,0:T(8,128)(2,1)} %collective-permute-done.10.refs_4_), channel_id=1, source_target_pairs={{0,4},{4,0},{8,12},{12,8},{16,20},{20,16},{24,28},{28,24},{1,5},{5... | collective-permute-start | bytes 1966088 | tf_op jit(solution)/shard_map/ppermute | solution.py:22
  41.9 15.4 %collective-permute-start.6 = (bf16[320,1024]{1,0:T(8,128)(2,1)}, bf16[320,1024]{1,0:T(8,128)(2,1)S(1)}, u32[]{:S(2)}, u32[]{:S(2)}) collective-permute-start(bf16[320,1024]{1,0:T(8,128)(2,1)} %collective-permute-done.2.refs_4_), channel_id=1, source_target_pairs={{0,2},{1,3},{2,0},{3,1},{4,6},{5,7},{6,4},{7,5},{8,10},{9,11},{10,... | collective-permute-start | bytes 1966088 | tf_op jit(solution)/shard_map/ppermute | solution.py:22
  43.5 16.4 %collective-permute-start.11 = (bf16[320,1024]{1,0:T(8,128)(2,1)S(1)}, bf16[320,1024]{1,0:T(8,128)(2,1)S(1)}, u32[]{:S(2)}, u32[]{:S(2)}) collective-permute-start(bf16[320,1024]{1,0:T(8,128)(2,1)S(1)} %shard_map.58), channel_id=1, source_target_pairs={{0,8},{4,28},{8,16},{12,4},{16,24},{20,12},{24,0},{28,20},{1,9},{5... | collective-permute-start | bytes 1966088 | tf_op jit(solution)/shard_map/ppermute | solution.py:22
  46.6 17.6 %collective-permute-start.12 = (bf16[320,1024]{1,0:T(8,128)(2,1)S(1)}, bf16[320,1024]{1,0:T(8,128)(2,1)S(1)}, u32[]{:S(2)}, u32[]{:S(2)}) collective-permute-start(bf16[320,1024]{1,0:T(8,128)(2,1)S(1)} %copy-done.2), channel_id=1, source_target_pairs={{0,1},{1,0},{2,3},{3,2},{4,5},{5,4},{6,7},{7,6},{8,9},{9,8},{10,11... | collective-permute-start | bytes 1966088 | tf_op jit(solution)/shard_map/ppermute | solution.py:22
  57.2 16.0 %collective-permute-start.14 = (bf16[320,1024]{1,0:T(8,128)(2,1)S(1)}, bf16[320,1024]{1,0:T(8,128)(2,1)S(1)}, u32[]{:S(2)}, u32[]{:S(2)}) collective-permute-start(bf16[320,1024]{1,0:T(8,128)(2,1)S(1)} %collective-permute-done.6.refs_2_), channel_id=1, source_target_pairs={{0,4},{4,0},{8,12},{12,8},{16,20},{20,16},{24,28},{28,24},{1,5},{5... | collective-permute-start | bytes 1966088 | tf_op jit(solution)/shard_map/ppermute | solution.py:22
  60.7 13.7 %collective-permute-start.15 = (bf16[320,1024]{1,0:T(8,128)(2,1)S(1)}, bf16[320,1024]{1,0:T(8,128)(2,1)S(1)}, u32[]{:S(2)}, u32[]{:S(2)}) collective-permute-start(bf16[320,1024]{1,0:T(8,128)(2,1)S(1)} %shard_map.59.refs_3_), channel_id=1, source_target_pairs={{0,2},{1,3},{2,0},{3,1},{4,6},{5,7},{6,4},{7,5},{8,10},{9,11},{10,... | collective-permute-start | bytes 1966088 | tf_op jit(solution)/shard_map/ppermute | solution.py:22
  63.0 15.5 %collective-permute-start.20 = (bf16[320,1024]{1,0:T(8,128)(2,1)S(1)}, bf16[320,1024]{1,0:T(8,128)(2,1)S(1)}, u32[]{:S(2)}, u32[]{:S(2)}) collective-permute-start(bf16[320,1024]{1,0:T(8,128)(2,1)S(1)} %shard_map.65), channel_id=1, source_target_pairs={{0,24},{4,28},{8,0},{12,4},{16,8},{20,12},{24,16},{28,20},{1,25},{... | collective-permute-start | bytes 1966088 | tf_op jit(solution)/shard_map/ppermute | solution.py:22
  77.3 4.1 %collective-permute-start.16 = (f32[8,640]{1,0:T(8,128)S(1)}, f32[8,640]{1,0:T(8,128)S(1)}, u32[]{:S(2)}, u32[]{:S(2)}) collective-permute-start(f32[8,640]{1,0:T(8,128)S(1)} %get-tuple-element.55.own), channel_id=1, source_target_pairs={{0,4},{4,0},{8,12},{12,8},{16,20},{20,16},{24,28},{28,24},{1,5},{5... | collective-permute-start | bytes 61448 | tf_op jit(solution)/shard_map/ppermute | solution.py:22
  79.3 12.4 %collective-permute-start.21 = (bf16[320,1024]{1,0:T(8,128)(2,1)S(1)}, bf16[320,1024]{1,0:T(8,128)(2,1)S(1)}, u32[]{:S(2)}, u32[]{:S(2)}) collective-permute-start(bf16[320,1024]{1,0:T(8,128)(2,1)S(1)} %shard_map.66.refs_3_), channel_id=1, source_target_pairs={{0,2},{1,3},{2,0},{3,1},{4,6},{5,7},{6,4},{7,5},{8,10},{9,11},{10,... | collective-permute-start | bytes 1966088 | tf_op jit(solution)/shard_map/ppermute | solution.py:22
  81.4 12.9 %collective-permute-start.26 = (bf16[320,1024]{1,0:T(8,128)(2,1)S(1)}, bf16[320,1024]{1,0:T(8,128)(2,1)S(1)}, u32[]{:S(2)}, u32[]{:S(2)}) collective-permute-start(bf16[320,1024]{1,0:T(8,128)(2,1)S(1)} %shard_map.70.refs_2_), channel_id=1, source_target_pairs={{0,4},{4,0},{8,12},{12,8},{16,20},{20,16},{24,28},{28,24},{1,5},{5... | collective-permute-start | bytes 1966088 | tf_op jit(solution)/shard_map/ppermute | solution.py:22
  82.6 7.4 %collective-permute-start.17 = (f32[8,640]{1,0:T(8,128)S(1)}, f32[8,640]{1,0:T(8,128)S(1)}, u32[]{:S(2)}, u32[]{:S(2)}) collective-permute-start(f32[8,640]{1,0:T(8,128)S(1)} %get-tuple-element.55.own), channel_id=1, source_target_pairs={{0,20},{4,16},{8,28},{12,24},{16,4},{20,0},{24,12},{28,8},{1,21},{... | collective-permute-start | bytes 61448 | tf_op jit(solution)/shard_map/ppermute | solution.py:22
  83.4 6.5 %collective-permute-start.19 = (f32[16,640]{1,0:T(8,128)S(1)}, f32[16,640]{1,0:T(8,128)S(1)}, u32[]{:S(2)}, u32[]{:S(2)}) collective-permute-start(f32[16,640]{1,0:T(8,128)S(1)} %constant_dynamic-update-slice_fusion), channel_id=1, source_target_pairs={{0,8},{4,12},{8,16},{12,20},{16,24},{20,28},{24,0},{28,4},{1,9},{5... | collective-permute-start | bytes 122888 | tf_op jit(solution)/shard_map/ppermute | solution.py:22
  85.5 4.5 %collective-permute-start.18 = (f32[16,640]{1,0:T(8,128)S(1)}, f32[16,640]{1,0:T(8,128)S(1)}, u32[]{:S(2)}, u32[]{:S(2)}) collective-permute-start(f32[16,640]{1,0:T(8,128)S(1)} %constant_dynamic-update-slice_fusion), channel_id=1, source_target_pairs={{0,24},{4,28},{8,0},{12,4},{16,8},{20,12},{24,16},{28,20},{1,25},{... | collective-permute-start | bytes 122888 | tf_op jit(solution)/shard_map/ppermute | solution.py:22
  91.7 5.3 %collective-permute-start.24 = (f32[24,320]{1,0:T(8,128)S(1)}, f32[24,320]{1,0:T(8,128)S(1)}, u32[]{:S(2)}, u32[]{:S(2)}) collective-permute-start(f32[24,320]{1,0:T(8,128)S(1)} %shard_map.64.refs_0_), channel_id=1, source_target_pairs={{0,3},{1,2},{2,1},{3,0},{4,7},{5,6},{6,5},{7,4},{8,11},{9,10},{10,... | collective-permute-start | bytes 92168 | tf_op jit(solution)/shard_map/ppermute | solution.py:22
  91.7 5.3 %collective-permute-start.23 = (f32[24,320]{1,0:T(8,128)S(1)}, f32[24,320]{1,0:T(8,128)S(1)}, u32[]{:S(2)}, u32[]{:S(2)}) collective-permute-start(f32[24,320]{1,0:T(8,128)S(1)} %shard_map.64.refs_0_), channel_id=1, source_target_pairs={{0,1},{1,0},{2,3},{3,2},{4,5},{5,4},{6,7},{7,6},{8,9},{9,8},{10,11... | collective-permute-start | bytes 92168 | tf_op jit(solution)/shard_map/ppermute | solution.py:22
  93.1 4.0 %collective-permute-start.22 = (f32[24,320]{1,0:T(8,128)S(1)}, f32[24,320]{1,0:T(8,128)S(1)}, u32[]{:S(2)}, u32[]{:S(2)}) collective-permute-start(f32[24,320]{1,0:T(8,128)S(1)} %shard_map.64.refs_0_), channel_id=1, source_target_pairs={{0,2},{1,3},{2,0},{3,1},{4,6},{5,7},{6,4},{7,5},{8,10},{9,11},{10,... | collective-permute-start | bytes 92168 | tf_op jit(solution)/shard_map/ppermute | solution.py:22
  102.8 7.7 %collective-permute-start.25 = (f32[320,1024]{1,0:T(8,128)S(1)}, f32[320,1024]{1,0:T(8,128)S(1)}, u32[]{:S(2)}, u32[]{:S(2)}) collective-permute-start(f32[320,1024]{1,0:T(8,128)S(1)} %get-tuple-element.68), channel_id=1, source_target_pairs={{0,1},{1,0},{2,3},{3,2},{4,5},{5,4},{6,7},{7,6},{8,9},{9,8},{10,11... | collective-permute-start | bytes 3932168 | tf_op jit(solution)/shard_map/ppermute | solution.py:22
  108.1 3.5 %collective-permute-start.27 = (f32[320,1024]{1,0:T(8,128)S(1)}, f32[320,1024]{1,0:T(8,128)S(1)}, u32[]{:S(2)}, u32[]{:S(2)}) collective-permute-start(f32[320,1024]{1,0:T(8,128)S(1)} %get-tuple-element.78), channel_id=1, source_target_pairs={{0,1},{1,0},{2,3},{3,2},{4,5},{5,4},{6,7},{7,6},{8,9},{9,8},{10,11... | collective-permute-start | bytes 3932168 | tf_op jit(solution)/shard_map/ppermute | solution.py:22

commit v9 on v7

--- a/solution.py
+++ b/solution.py
@@ -165,8 +165,8 @@
         + [pltpu.SemaphoreType.DMA((2 + len(shards),))],
         compiler_params=pltpu.CompilerParams(vmem_limit_bytes=VMEM_LIMIT),
         cost_estimate=pl.CostEstimate(
-            flops=4 * rows * rows * tokens * width,
-            bytes_accessed=(tokens + 2) * rows * width * 2 + 8 * rows * rows * tokens,
+            flops=8 * rows * rows * tokens * width,
+            bytes_accessed=2 * ((tokens + 2) * rows * width * 2 + 8 * rows * rows * tokens),
             transcendentals=4 * rows * rows * tokens if stats else 0,
         ),
     )(scalars, *lhs, *shards, *side)

time: 113 us -> 113 us (level)
  no operation moved by 1% of the time
where the time goes in v9:
time: 113 us
  Pallas kernels  43.5 us (38%)
  waiting for transfers between devices  33.7 us (30%)
  starting transfers between devices  33.5 us (30%)
    ppermute x28, waiting for transfers between devices, shift(): return lax.ppermute(array, axis, pairs)  33.7 us
    ppermute x28, starting transfers between devices, shift(): return lax.ppermute(array, axis, pairs)  33.5 us
    pallas_call x6, Pallas kernels, score(): pl.pallas_call(functools.partial(score_kernel, len(shards), given, start,...  24.2 us
    pallas_call x2, Pallas kernels, grad(): pl.pallas_call(functools.partial(grad_kernel, keys, factor), out_shape=(k...  11 us
    pallas_call x5, Pallas kernels, choose(): pl.pallas_call(choose_kernel, out_shape=jax.ShapeDtypeStruct(first.shape,...  3.84 us
    pallas_call x2, Pallas kernels, small_call(): pl.pallas_call(kernel, out_shape=tuple((jax.ShapeDtypeStruct(s, F32) for...  2.26 us
  transfers between devices with their start and end apart: 28, of which 14 were waited for; matrix products, arithmetic and copies ran while one was open for 0% of the time, Pallas kernels for 33%

profile of v9, /device:TPU:0, one launch (start us, length us, event | category | flops | bytes accessed | tf_op | source)
XLA Modules:
  0.0 112.7 jit_solution(15764911572342710560)
XLA Ops:
  0.6 3.0 %collective-permute-start.3 = (s32[1,320]{1,0:T(1,128)}, s32[1,320]{1,0:T(1,128)S(1)}, u32[]{:S(2)}, u32[]{:S(2)}) collective-permute-start(s32[1,320]{1,0:T(1,128)} %first.3), channel_id=1, source_target_pairs={{0,2},{1,3},{2,0},{3,1},{4,6},{5,7},{6,4},{7,5},{8,10},{9,11},{10,... | collective-permute-start | bytes 3848 | tf_op jit(solution)/shard_map/ppermute | solution.py:22
  3.7 1.6 %collective-permute-start.2 = (bf16[320,1024]{1,0:T(8,128)(2,1)}, bf16[320,1024]{1,0:T(8,128)(2,1)}, u32[]{:S(2)}, u32[]{:S(2)}) collective-permute-start(bf16[320,1024]{1,0:T(8,128)(2,1)} %refs_0_.8), channel_id=1, source_target_pairs={{0,8},{4,12},{8,16},{12,20},{16,24},{20,28},{24,0},{28,4},{1,9},{5... | collective-permute-start | bytes 1966088 | tf_op jit(solution)/shard_map/ppermute | solution.py:22
  5.4 2.0 %collective-permute-start.4 = (bf16[320,1024]{1,0:T(8,128)(2,1)}, bf16[320,1024]{1,0:T(8,128)(2,1)S(1)}, u32[]{:S(2)}, u32[]{:S(2)}) collective-permute-start(bf16[320,1024]{1,0:T(8,128)(2,1)} %refs_0_.8), channel_id=1, source_target_pairs={{0,2},{1,3},{2,0},{3,1},{4,6},{5,7},{6,4},{7,5},{8,10},{9,11},{10,... | collective-permute-start | bytes 1966088 | tf_op jit(solution)/shard_map/ppermute | solution.py:22
  7.4 3.5 %collective-permute-start.7 = (bf16[320,1024]{1,0:T(8,128)(2,1)}, bf16[320,1024]{1,0:T(8,128)(2,1)S(1)}, u32[]{:S(2)}, u32[]{:S(2)}) collective-permute-start(bf16[320,1024]{1,0:T(8,128)(2,1)} %refs_0_.8), channel_id=1, source_target_pairs={{0,4},{8,12},{16,20},{24,28},{1,5},{9,13},{17,21},{25,29},{2,6},{1... | collective-permute-start | bytes 1966088 | tf_op jit(solution)/shard_map/ppermute | solution.py:22
  10.9 1.3 %collective-permute-start.8 = (bf16[320,1024]{1,0:T(8,128)(2,1)}, bf16[320,1024]{1,0:T(8,128)(2,1)S(1)}, u32[]{:S(2)}, u32[]{:S(2)}) collective-permute-start(bf16[320,1024]{1,0:T(8,128)(2,1)} %refs_0_.6), channel_id=1, source_target_pairs={{4,0},{12,8},{20,16},{28,24},{5,1},{13,9},{21,17},{29,25},{6,2},{1... | collective-permute-start | bytes 1966088 | tf_op jit(solution)/shard_map/ppermute | solution.py:22
  12.2 10.8 %collective-permute-done.2.refs_4_ = bf16[320,1024]{1,0:T(8,128)(2,1)} collective-permute-done((bf16[320,1024]{1,0:T(8,128)(2,1)}, bf16[320,1024]{1,0:T(8,128)(2,1)}, u32[]{:S(2)}, u32[]{:S(2)}) %collective-permute-start.2) | collective-permute-done | bytes 655392 | tf_op jit(solution)/shard_map/ppermute | solution.py:22
  23.0 1.7 %collective-permute-start.10 = (bf16[320,1024]{1,0:T(8,128)(2,1)}, bf16[320,1024]{1,0:T(8,128)(2,1)}, u32[]{:S(2)}, u32[]{:S(2)}) collective-permute-start(bf16[320,1024]{1,0:T(8,128)(2,1)} %refs_0_.6), channel_id=1, source_target_pairs={{0,24},{4,28},{8,0},{12,4},{16,8},{20,12},{24,16},{28,20},{1,25},{... | collective-permute-start | bytes 1966088 | tf_op jit(solution)/shard_map/ppermute | solution.py:22
  24.7 0.8 copy-done.3
  26.1 1.7 %collective-permute-done.8.first = bf16[320,1024]{1,0:T(8,128)(2,1)S(1)} collective-permute-done((bf16[320,1024]{1,0:T(8,128)(2,1)}, bf16[320,1024]{1,0:T(8,128)(2,1)S(1)}, u32[]{:S(2)}, u32[]{:S(2)}) %collective-permute-start.8) | collective-permute-done | bytes 655392 | tf_op jit(solution)/shard_map/ppermute | solution.py:22
  27.9 11.9 %collective-permute-done.10.refs_4_ = bf16[320,1024]{1,0:T(8,128)(2,1)} collective-permute-done((bf16[320,1024]{1,0:T(8,128)(2,1)}, bf16[320,1024]{1,0:T(8,128)(2,1)}, u32[]{:S(2)}, u32[]{:S(2)}) %collective-permute-start.10) | collective-permute-done | bytes 655392 | tf_op jit(solution)/shard_map/ppermute | solution.py:22
  39.7 1.5 %collective-permute-start.13 = (bf16[320,1024]{1,0:T(8,128)(2,1)}, bf16[320,1024]{1,0:T(8,128)(2,1)S(1)}, u32[]{:S(2)}, u32[]{:S(2)}) collective-permute-start(bf16[320,1024]{1,0:T(8,128)(2,1)} %collective-permute-done.10.refs_4_), channel_id=1, source_target_pairs={{0,4},{4,0},{8,12},{12,8},{16,20},{20,16},{24,28},{28,24},{1,5},{5... | collective-permute-start | bytes 1966088 | tf_op jit(solution)/shard_map/ppermute | solution.py:22
  41.2 0.6 collective-permute-done.5.second.refs_3_.first
  42.7 0.8 shard_map.58
  43.5 3.1 %collective-permute-start.11 = (bf16[320,1024]{1,0:T(8,128)(2,1)S(1)}, bf16[320,1024]{1,0:T(8,128)(2,1)S(1)}, u32[]{:S(2)}, u32[]{:S(2)}) collective-permute-start(bf16[320,1024]{1,0:T(8,128)(2,1)S(1)} %shard_map.58), channel_id=1, source_target_pairs={{0,8},{4,28},{8,16},{12,4},{16,24},{20,12},{24,0},{28,20},{1,9},{5... | collective-permute-start | bytes 1966088 | tf_op jit(solution)/shard_map/ppermute | solution.py:22
  46.6 6.9 %shard_map.60 = (f32[640,1280]{1,0:T(8,128)S(1)}, bf16[1280,1024]{1,0:T(8,128)(2,1)S(1)}, f32[8,640]{1,0:T(8,128)S(1)}) custom-call(s32[5]{0:T(128)S(1)} %stack.27.flag.scalars, bf16[320,1024]{1,0:T(8,128)(2,1)S(1)} %copy-done.1, bf16[320,1024]{1,0:T(8,128)(2,1)} %collective-permute-done.1.refs_1_, bf16[320,1024]{1,0:T(8,128)(2,1)S(1)} %copy-done.2, ...), custom_call_target="tpu_custom_call" | custom-call | flops 3355443200 | bytes 14417920 | tf_op jit(solution)/shard_map/pallas_call | solution.py:159
  53.5 2.7 %collective-permute-done.13.refs_5_.second = bf16[320,1024]{1,0:T(8,128)(2,1)S(1)} collective-permute-done((bf16[320,1024]{1,0:T(8,128)(2,1)}, bf16[320,1024]{1,0:T(8,128)(2,1)S(1)}, u32[]{:S(2)}, u32[]{:S(2)}) %collective-permute-start.13) | collective-permute-done | bytes 655392 | tf_op jit(solution)/shard_map/ppermute | solution.py:22
  56.2 1.1 collective-permute-done.6.refs_2_
  57.2 1.5 %collective-permute-start.14 = (bf16[320,1024]{1,0:T(8,128)(2,1)S(1)}, bf16[320,1024]{1,0:T(8,128)(2,1)S(1)}, u32[]{:S(2)}, u32[]{:S(2)}) collective-permute-start(bf16[320,1024]{1,0:T(8,128)(2,1)S(1)} %collective-permute-done.6.refs_2_), channel_id=1, source_target_pairs={{0,4},{4,0},{8,12},{12,8},{16,20},{20,16},{24,28},{28,24},{1,5},{5... | collective-permute-start | bytes 1966088 | tf_op jit(solution)/shard_map/ppermute | solution.py:22
  58.7 1.2 %collective-permute-done.11.first.second = bf16[320,1024]{1,0:T(8,128)(2,1)S(1)} collective-permute-done((bf16[320,1024]{1,0:T(8,128)(2,1)S(1)}, bf16[320,1024]{1,0:T(8,128)(2,1)S(1)}, u32[]{:S(2)}, u32[]{:S(2)}) %collective-permute-start.11) | collective-permute-done | bytes 655392 | tf_op jit(solution)/shard_map/ppermute | solution.py:22
  59.9 0.8 shard_map.59.refs_3_
  60.7 1.6 %collective-permute-start.15 = (bf16[320,1024]{1,0:T(8,128)(2,1)S(1)}, bf16[320,1024]{1,0:T(8,128)(2,1)S(1)}, u32[]{:S(2)}, u32[]{:S(2)}) collective-permute-start(bf16[320,1024]{1,0:T(8,128)(2,1)S(1)} %shard_map.59.refs_3_), channel_id=1, source_target_pairs={{0,2},{1,3},{2,0},{3,1},{4,6},{5,7},{6,4},{7,5},{8,10},{9,11},{10,... | collective-permute-start | bytes 1966088 | tf_op jit(solution)/shard_map/ppermute | solution.py:22
  62.2 0.8 shard_map.65
  63.0 1.2 %collective-permute-start.20 = (bf16[320,1024]{1,0:T(8,128)(2,1)S(1)}, bf16[320,1024]{1,0:T(8,128)(2,1)S(1)}, u32[]{:S(2)}, u32[]{:S(2)}) collective-permute-start(bf16[320,1024]{1,0:T(8,128)(2,1)S(1)} %shard_map.65), channel_id=1, source_target_pairs={{0,24},{4,28},{8,0},{12,4},{16,8},{20,12},{24,16},{28,20},{1,25},{... | collective-permute-start | bytes 1966088 | tf_op jit(solution)/shard_map/ppermute | solution.py:22
  64.2 4.8 %shard_map.61 = (f32[640,1280]{1,0:T(8,128)S(1)}, bf16[1280,1024]{1,0:T(8,128)(2,1)S(1)}, f32[8,128]{1,0:T(8,128)S(1)}) custom-call(s32[5]{0:T(128)S(1)} %stack.27.flag.scalars, bf16[320,1024]{1,0:T(8,128)(2,1)S(1)} %copy-done.2, bf16[320,1024]{1,0:T(8,128)(2,1)S(1)} %collective-permute-done.12.refs_1_, bf16[320,1024]{1,0:T(8,128)(2,1)S(1)} %copy-done.1, ...), custom_call_target="tpu_custom_call" | custom-call | flops 3355443200 | bytes 14417920 | tf_op jit(solution)/shard_map/pallas_call | solution.py:159
  69.0 4.2 %shard_map.62 = (f32[640,640]{1,0:T(8,128)S(1)}, bf16[640,1024]{1,0:T(8,128)(2,1)S(1)}, f32[8,640]{1,0:T(8,128)S(1)}, bf16[640,1024]{1,0:T(8,128)(2,1)S(1)}) custom-call(s32[5]{0:T(128)S(1)} %stack.27.flag.scalars, bf16[320,1024]{1,0:T(8,128)(2,1)S(1)} %copy-done.1, bf16[320,1024]{1,0:T(8,128)(2,1)} %collective-permute-done.1.refs_1_, ...), custom_call_target="tpu_custom_call" | custom-call | flops 1677721600 | bytes 8519680 | tf_op jit(solution)/shard_map/pallas_call | solution.py:159
  73.2 1.2 %collective-permute-done.15.refs_2_ = bf16[320,1024]{1,0:T(8,128)(2,1)S(1)} collective-permute-done((bf16[320,1024]{1,0:T(8,128)(2,1)S(1)}, bf16[320,1024]{1,0:T(8,128)(2,1)S(1)}, u32[]{:S(2)}, u32[]{:S(2)}) %collective-permute-start.15) | collective-permute-done | bytes 655392 | tf_op jit(solution)/shard_map/ppermute | solution.py:22
  74.4 2.9 %shard_map.63 = (f32[640,640]{1,0:T(8,128)S(1)}, bf16[640,1024]{1,0:T(8,128)(2,1)S(1)}, f32[8,640]{1,0:T(8,128)S(1)}) custom-call(s32[5]{0:T(128)S(1)} %stack.27.flag.scalars, bf16[640,1024]{1,0:T(8,128)(2,1)S(1)} %get-tuple-element.52.refs_0_, bf16[320,1024]{1,0:T(8,128)(2,1)S(1)} %collective-permute-done.14.refs_1_, ...), custom_call_target="tpu_custom_call" | custom-call | flops 1677721600 | bytes 8519680 | tf_op jit(solution)/shard_map/pallas_call | solution.py:159
  77.3 1.2 %collective-permute-start.16 = (f32[8,640]{1,0:T(8,128)S(1)}, f32[8,640]{1,0:T(8,128)S(1)}, u32[]{:S(2)}, u32[]{:S(2)}) collective-permute-start(f32[8,640]{1,0:T(8,128)S(1)} %get-tuple-element.56.own), channel_id=1, source_target_pairs={{0,4},{4,0},{8,12},{12,8},{16,20},{20,16},{24,28},{28,24},{1,5},{5... | collective-permute-start | bytes 61448 | tf_op jit(solution)/shard_map/ppermute | solution.py:22
  78.5 0.8 shard_map.66.refs_3_
  79.3 0.7 collective-permute-start.21
  80.0 0.8 shard_map.70.refs_2_
  80.8 0.6 collective-permute-done.16.beside
  81.4 1.1 %collective-permute-start.26 = (bf16[320,1024]{1,0:T(8,128)(2,1)S(1)}, bf16[320,1024]{1,0:T(8,128)(2,1)S(1)}, u32[]{:S(2)}, u32[]{:S(2)}) collective-permute-start(bf16[320,1024]{1,0:T(8,128)(2,1)S(1)} %shard_map.70.refs_2_), channel_id=1, source_target_pairs={{0,4},{4,0},{8,12},{12,8},{16,20},{20,16},{24,28},{28,24},{1,5},{5... | collective-permute-start | bytes 1966088 | tf_op jit(solution)/shard_map/ppermute | solution.py:22
  82.6 0.9 collective-permute-start.17
  83.4 2.1 %collective-permute-start.19 = (f32[16,640]{1,0:T(8,128)S(1)}, f32[16,640]{1,0:T(8,128)S(1)}, u32[]{:S(2)}, u32[]{:S(2)}) collective-permute-start(f32[16,640]{1,0:T(8,128)S(1)} %constant_dynamic-update-slice_fusion), channel_id=1, source_target_pairs={{0,8},{4,12},{8,16},{12,20},{16,24},{20,28},{24,0},{28,4},{1,9},{5... | collective-permute-start | bytes 122888 | tf_op jit(solution)/shard_map/ppermute | solution.py:22
  85.5 1.7 %collective-permute-start.18 = (f32[16,640]{1,0:T(8,128)S(1)}, f32[16,640]{1,0:T(8,128)S(1)}, u32[]{:S(2)}, u32[]{:S(2)}) collective-permute-start(f32[16,640]{1,0:T(8,128)S(1)} %constant_dynamic-update-slice_fusion), channel_id=1, source_target_pairs={{0,24},{4,28},{8,0},{12,4},{16,8},{20,12},{24,16},{28,20},{1,25},{... | collective-permute-start | bytes 122888 | tf_op jit(solution)/shard_map/ppermute | solution.py:22
  87.3 2.7 %shard_map.71 = (f32[640,640]{1,0:T(8,128)S(1)}, bf16[640,1024]{1,0:T(8,128)(2,1)S(1)}, f32[8,128]{1,0:T(8,128)}) custom-call(s32[5]{0:T(128)S(1)} %stack.27.flag.scalars, bf16[320,1024]{1,0:T(8,128)(2,1)S(1)} %copy-done.2, bf16[320,1024]{1,0:T(8,128)(2,1)S(1)} %collective-permute-done.12.refs_1_, bf16[320,1024]{1,0:T(8,128)(2,1)S(1)} %shard_map.70.refs_2_, ...), custom_call_target="tpu_custom_call" | custom-call | flops 1677721600 | bytes 8519680 | tf_op jit(solution)/shard_map/pallas_call | solution.py:159
  90.0 0.7 shard_map.64.refs_0_.own
  90.7 1.0 collective-permute-done.21.refs_3_
  91.7 1.5 %collective-permute-start.23 = (f32[24,320]{1,0:T(8,128)S(1)}, f32[24,320]{1,0:T(8,128)S(1)}, u32[]{:S(2)}, u32[]{:S(2)}) collective-permute-start(f32[24,320]{1,0:T(8,128)S(1)} %shard_map.64.refs_0_.own), channel_id=1, source_target_pairs={{0,1},{1,0},{2,3},{3,2},{4,5},{5,4},{6,7},{7,6},{8,9},{9,8},{10,11... | collective-permute-start | bytes 92168 | tf_op jit(solution)/shard_map/ppermute | solution.py:22
  93.1 0.7 collective-permute-start.22
  94.3 2.7 %shard_map.72 = (f32[640,640]{1,0:T(8,128)S(1)}, bf16[640,1024]{1,0:T(8,128)(2,1)S(1)}, f32[8,128]{1,0:T(8,128)}) custom-call(s32[5]{0:T(128)S(1)} %stack.27.flag.scalars, bf16[320,1024]{1,0:T(8,128)(2,1)S(1)} %copy-done.2, bf16[320,1024]{1,0:T(8,128)(2,1)S(1)} %collective-permute-done.12.refs_1_, bf16[320,1024]{1,0:T(8,128)(2,1)S(1)} %collective-permute-done.26.refs_2_, ...), custom_call_target="tpu_custom_call" | custom-call | flops 1677721600 | bytes 8519680 | tf_op jit(solution)/shard_map/pallas_call | solution.py:159
  97.1 5.7 %shard_map.67 = (f32[320,1024]{1,0:T(8,128)S(1)}, f32[320,1024]{1,0:T(8,128)S(1)}, f32[8,640]{1,0:T(8,128)S(1)}, f32[8,640]{1,0:T(8,128)S(1)}) custom-call(s32[5]{0:T(128)S(1)} %stack.27.flag.scalars, s32[1,320]{1,0:T(1,128)S(1)} %copy-done, s32[1,320]{1,0:T(1,128)S(1)} %collective-permute-done.refs_7_.second, f32[24,320]{1,0:T(8,128)S(1)} %shard_map.64.refs_0_.own, ...), custom_call_target="tpu_custom_call" | custom-call | flops 3355443200 | bytes 14417920 | tf_op jit(solution)/shard_map/pallas_call | solution.py:331
  102.9 5.3 %shard_map.73 = (f32[320,1024]{1,0:T(8,128)S(1)}, f32[320,1024]{1,0:T(8,128)S(1)}) custom-call(s32[5]{0:T(128)S(1)} %stack.27.flag.scalars, s32[1,320]{1,0:T(1,128)S(1)} %copy-done, s32[1,320]{1,0:T(1,128)S(1)} %collective-permute-done.3.refs_6_.second, f32[8,640]{1,0:T(8,128)S(1)} %get-tuple-element.69.refs_0_, f32[8,640]{1,0:T(8,128)S(1)} %get-tuple-element.70.refs_1_, ...), custom_call_target="tpu_custom_call" | custom-call | flops 3355443200 | bytes 14417920 | tf_op jit(solution)/shard_map/pallas_call | solution.py:331
  108.2 0.6 collective-permute-start.27
  108.7 1.6 %shard_map.68 = f32[320]{0:T(512)} custom-call(s32[5]{0:T(128)S(1)} %stack.27.flag.scalars, s32[1,320]{1,0:T(1,128)S(1)} %copy-done, f32[24,320]{1,0:T(8,128)S(1)} %shard_map.64.refs_0_.own, f32[24,320]{1,0:T(8,128)S(1)} %collective-permute-done.22.refs_1_.across, f32[24,320]{1,0:T(8,128)S(1)} %collective-permute-done.23.refs_2_.core, ...), custom_call_target="tpu_custom_call" | custom-call | flops 100000 | bytes 400000 | tf_op jit(solution)/shard_map/pallas_call | solution.py:276
  110.3 1.1 shard_map.69
  111.5 1.1 shard_map.74
  (38 shorter events, 2.4 us)
Async XLA Ops:
  0.6 45.9 %copy-start = (s32[1,320]{1,0:T(1,128)S(1)}, s32[1,320]{1,0:T(1,128)}, u32[]{:S(2)}) copy-start(s32[1,320]{1,0:T(1,128)} %first.3) | copy-start | bytes 3844
  0.6 45.9 %copy-start.1 = (bf16[320,1024]{1,0:T(8,128)(2,1)S(1)}, bf16[320,1024]{1,0:T(8,128)(2,1)}, u32[]{:S(2)}) copy-start(bf16[320,1024]{1,0:T(8,128)(2,1)} %refs_0_.6) | copy-start | bytes 1966084
  0.6 4.8 %collective-permute-start.3 = (s32[1,320]{1,0:T(1,128)}, s32[1,320]{1,0:T(1,128)S(1)}, u32[]{:S(2)}, u32[]{:S(2)}) collective-permute-start(s32[1,320]{1,0:T(1,128)} %first.3), channel_id=1, source_target_pairs={{0,2},{1,3},{2,0},{3,1},{4,6},{5,7},{6,4},{7,5},{8,10},{9,11},{10,... | collective-permute-start | bytes 3848 | tf_op jit(solution)/shard_map/ppermute | solution.py:22
  3.7 1.8 %collective-permute-start = (s32[1,320]{1,0:T(1,128)}, s32[1,320]{1,0:T(1,128)S(1)}, u32[]{:S(2)}, u32[]{:S(2)}) collective-permute-start(s32[1,320]{1,0:T(1,128)} %first.3), channel_id=1, source_target_pairs={{0,1},{1,0},{2,3},{3,2},{4,5},{5,4},{6,7},{7,6},{8,9},{9,8},{10,11... | collective-permute-start | bytes 3848 | tf_op jit(solution)/shard_map/ppermute | solution.py:22
  3.7 19.3 %collective-permute-start.2 = (bf16[320,1024]{1,0:T(8,128)(2,1)}, bf16[320,1024]{1,0:T(8,128)(2,1)}, u32[]{:S(2)}, u32[]{:S(2)}) collective-permute-start(bf16[320,1024]{1,0:T(8,128)(2,1)} %refs_0_.8), channel_id=1, source_target_pairs={{0,8},{4,12},{8,16},{12,20},{16,24},{20,28},{24,0},{28,4},{1,9},{5... | collective-permute-start | bytes 1966088 | tf_op jit(solution)/shard_map/ppermute | solution.py:22
  5.4 19.3 %collective-permute-start.4 = (bf16[320,1024]{1,0:T(8,128)(2,1)}, bf16[320,1024]{1,0:T(8,128)(2,1)S(1)}, u32[]{:S(2)}, u32[]{:S(2)}) collective-permute-start(bf16[320,1024]{1,0:T(8,128)(2,1)} %refs_0_.8), channel_id=1, source_target_pairs={{0,2},{1,3},{2,0},{3,1},{4,6},{5,7},{6,4},{7,5},{8,10},{9,11},{10,... | collective-permute-start | bytes 1966088 | tf_op jit(solution)/shard_map/ppermute | solution.py:22
  7.4 18.7 %collective-permute-start.7 = (bf16[320,1024]{1,0:T(8,128)(2,1)}, bf16[320,1024]{1,0:T(8,128)(2,1)S(1)}, u32[]{:S(2)}, u32[]{:S(2)}) collective-permute-start(bf16[320,1024]{1,0:T(8,128)(2,1)} %refs_0_.8), channel_id=1, source_target_pairs={{0,4},{8,12},{16,20},{24,28},{1,5},{9,13},{17,21},{25,29},{2,6},{1... | collective-permute-start | bytes 1966088 | tf_op jit(solution)/shard_map/ppermute | solution.py:22
  10.9 16.9 %collective-permute-start.8 = (bf16[320,1024]{1,0:T(8,128)(2,1)}, bf16[320,1024]{1,0:T(8,128)(2,1)S(1)}, u32[]{:S(2)}, u32[]{:S(2)}) collective-permute-start(bf16[320,1024]{1,0:T(8,128)(2,1)} %refs_0_.6), channel_id=1, source_target_pairs={{4,0},{12,8},{20,16},{28,24},{5,1},{13,9},{21,17},{29,25},{6,2},{1... | collective-permute-start | bytes 1966088 | tf_op jit(solution)/shard_map/ppermute | solution.py:22
  23.0 16.8 %collective-permute-start.10 = (bf16[320,1024]{1,0:T(8,128)(2,1)}, bf16[320,1024]{1,0:T(8,128)(2,1)}, u32[]{:S(2)}, u32[]{:S(2)}) collective-permute-start(bf16[320,1024]{1,0:T(8,128)(2,1)} %refs_0_.6), channel_id=1, source_target_pairs={{0,24},{4,28},{8,0},{12,4},{16,8},{20,12},{24,16},{28,20},{1,25},{... | collective-permute-start | bytes 1966088 | tf_op jit(solution)/shard_map/ppermute | solution.py:22
  24.7 0.8 copy-start.3
  25.6 16.3 %collective-permute-start.5 = (bf16[320,1024]{1,0:T(8,128)(2,1)}, bf16[320,1024]{1,0:T(8,128)(2,1)S(1)}, u32[]{:S(2)}, u32[]{:S(2)}) collective-permute-start(bf16[320,1024]{1,0:T(8,128)(2,1)} %refs_0_.6), channel_id=1, source_target_pairs={{0,2},{1,3},{2,0},{3,1},{4,6},{5,7},{6,4},{7,5},{8,10},{9,11},{10,... | collective-permute-start | bytes 1966088 | tf_op jit(solution)/shard_map/ppermute | solution.py:22
  27.8 14.9 %collective-permute-start.9 = (bf16[320,1024]{1,0:T(8,128)(2,1)}, bf16[320,1024]{1,0:T(8,128)(2,1)S(1)}, u32[]{:S(2)}, u32[]{:S(2)}) collective-permute-start(bf16[320,1024]{1,0:T(8,128)(2,1)} %collective-permute-done.2.refs_4_), channel_id=1, source_target_pairs={{0,4},{4,0},{8,12},{12,8},{16,20},{20,16},{24,28},{28,24},{1,5},{5... | collective-permute-start | bytes 1966088 | tf_op jit(solution)/shard_map/ppermute | solution.py:22
  27.8 18.8 %collective-permute-start.1 = (bf16[320,1024]{1,0:T(8,128)(2,1)}, bf16[320,1024]{1,0:T(8,128)(2,1)}, u32[]{:S(2)}, u32[]{:S(2)}) collective-permute-start(bf16[320,1024]{1,0:T(8,128)(2,1)} %refs_0_.6), channel_id=1, source_target_pairs={{0,1},{1,0},{2,3},{3,2},{4,5},{5,4},{6,7},{7,6},{8,9},{9,8},{10,11... | collective-permute-start | bytes 1966088 | tf_op jit(solution)/shard_map/ppermute | solution.py:22
  27.9 18.7 %copy-start.2 = (bf16[320,1024]{1,0:T(8,128)(2,1)S(1)}, bf16[320,1024]{1,0:T(8,128)(2,1)}, u32[]{:S(2)}) copy-start(bf16[320,1024]{1,0:T(8,128)(2,1)} %refs_0_.8) | copy-start | bytes 1966084
  27.9 18.7 %copy-start.4 = (bf16[320,1024]{1,0:T(8,128)(2,1)S(1)}, bf16[320,1024]{1,0:T(8,128)(2,1)}, u32[]{:S(2)}) copy-start(bf16[320,1024]{1,0:T(8,128)(2,1)} %copy-done.3) | copy-start | bytes 1966084
  39.7 16.4 %collective-permute-start.13 = (bf16[320,1024]{1,0:T(8,128)(2,1)}, bf16[320,1024]{1,0:T(8,128)(2,1)S(1)}, u32[]{:S(2)}, u32[]{:S(2)}) collective-permute-start(bf16[320,1024]{1,0:T(8,128)(2,1)} %collective-permute-done.10.refs_4_), channel_id=1, source_target_pairs={{0,4},{4,0},{8,12},{12,8},{16,20},{20,16},{24,28},{28,24},{1,5},{5... | collective-permute-start | bytes 1966088 | tf_op jit(solution)/shard_map/ppermute | solution.py:22
  41.9 15.4 %collective-permute-start.6 = (bf16[320,1024]{1,0:T(8,128)(2,1)}, bf16[320,1024]{1,0:T(8,128)(2,1)S(1)}, u32[]{:S(2)}, u32[]{:S(2)}) collective-permute-start(bf16[320,1024]{1,0:T(8,128)(2,1)} %collective-permute-done.2.refs_4_), channel_id=1, source_target_pairs={{0,2},{1,3},{2,0},{3,1},{4,6},{5,7},{6,4},{7,5},{8,10},{9,11},{10,... | collective-permute-start | bytes 1966088 | tf_op jit(solution)/shard_map/ppermute | solution.py:22
  43.5 16.4 %collective-permute-start.11 = (bf16[320,1024]{1,0:T(8,128)(2,1)S(1)}, bf16[320,1024]{1,0:T(8,128)(2,1)S(1)}, u32[]{:S(2)}, u32[]{:S(2)}) collective-permute-start(bf16[320,1024]{1,0:T(8,128)(2,1)S(1)} %shard_map.58), channel_id=1, source_target_pairs={{0,8},{4,28},{8,16},{12,4},{16,24},{20,12},{24,0},{28,20},{1,9},{5... | collective-permute-start | bytes 1966088 | tf_op jit(solution)/shard_map/ppermute | solution.py:22
  46.6 17.6 %collective-permute-start.12 = (bf16[320,1024]{1,0:T(8,128)(2,1)S(1)}, bf16[320,1024]{1,0:T(8,128)(2,1)S(1)}, u32[]{:S(2)}, u32[]{:S(2)}) collective-permute-start(bf16[320,1024]{1,0:T(8,128)(2,1)S(1)} %copy-done.2), channel_id=1, source_target_pairs={{0,1},{1,0},{2,3},{3,2},{4,5},{5,4},{6,7},{7,6},{8,9},{9,8},{10,11... | collective-permute-start | bytes 1966088 | tf_op jit(solution)/shard_map/ppermute | solution.py:22
  57.2 16.0 %collective-permute-start.14 = (bf16[320,1024]{1,0:T(8,128)(2,1)S(1)}, bf16[320,1024]{1,0:T(8,128)(2,1)S(1)}, u32[]{:S(2)}, u32[]{:S(2)}) collective-permute-start(bf16[320,1024]{1,0:T(8,128)(2,1)S(1)} %collective-permute-done.6.refs_2_), channel_id=1, source_target_pairs={{0,4},{4,0},{8,12},{12,8},{16,20},{20,16},{24,28},{28,24},{1,5},{5... | collective-permute-start | bytes 1966088 | tf_op jit(solution)/shard_map/ppermute | solution.py:22
  60.7 13.7 %collective-permute-start.15 = (bf16[320,1024]{1,0:T(8,128)(2,1)S(1)}, bf16[320,1024]{1,0:T(8,128)(2,1)S(1)}, u32[]{:S(2)}, u32[]{:S(2)}) collective-permute-start(bf16[320,1024]{1,0:T(8,128)(2,1)S(1)} %shard_map.59.refs_3_), channel_id=1, source_target_pairs={{0,2},{1,3},{2,0},{3,1},{4,6},{5,7},{6,4},{7,5},{8,10},{9,11},{10,... | collective-permute-start | bytes 1966088 | tf_op jit(solution)/shard_map/ppermute | solution.py:22
  63.0 15.5 %collective-permute-start.20 = (bf16[320,1024]{1,0:T(8,128)(2,1)S(1)}, bf16[320,1024]{1,0:T(8,128)(2,1)S(1)}, u32[]{:S(2)}, u32[]{:S(2)}) collective-permute-start(bf16[320,1024]{1,0:T(8,128)(2,1)S(1)} %shard_map.65), channel_id=1, source_target_pairs={{0,24},{4,28},{8,0},{12,4},{16,8},{20,12},{24,16},{28,20},{1,25},{... | collective-permute-start | bytes 1966088 | tf_op jit(solution)/shard_map/ppermute | solution.py:22
  77.3 4.1 %collective-permute-start.16 = (f32[8,640]{1,0:T(8,128)S(1)}, f32[8,640]{1,0:T(8,128)S(1)}, u32[]{:S(2)}, u32[]{:S(2)}) collective-permute-start(f32[8,640]{1,0:T(8,128)S(1)} %get-tuple-element.56.own), channel_id=1, source_target_pairs={{0,4},{4,0},{8,12},{12,8},{16,20},{20,16},{24,28},{28,24},{1,5},{5... | collective-permute-start | bytes 61448 | tf_op jit(solution)/shard_map/ppermute | solution.py:22
  79.3 12.4 %collective-permute-start.21 = (bf16[320,1024]{1,0:T(8,128)(2,1)S(1)}, bf16[320,1024]{1,0:T(8,128)(2,1)S(1)}, u32[]{:S(2)}, u32[]{:S(2)}) collective-permute-start(bf16[320,1024]{1,0:T(8,128)(2,1)S(1)} %shard_map.66.refs_3_), channel_id=1, source_target_pairs={{0,2},{1,3},{2,0},{3,1},{4,6},{5,7},{6,4},{7,5},{8,10},{9,11},{10,... | collective-permute-start | bytes 1966088 | tf_op jit(solution)/shard_map/ppermute | solution.py:22
  81.4 12.9 %collective-permute-start.26 = (bf16[320,1024]{1,0:T(8,128)(2,1)S(1)}, bf16[320,1024]{1,0:T(8,128)(2,1)S(1)}, u32[]{:S(2)}, u32[]{:S(2)}) collective-permute-start(bf16[320,1024]{1,0:T(8,128)(2,1)S(1)} %shard_map.70.refs_2_), channel_id=1, source_target_pairs={{0,4},{4,0},{8,12},{12,8},{16,20},{20,16},{24,28},{28,24},{1,5},{5... | collective-permute-start | bytes 1966088 | tf_op jit(solution)/shard_map/ppermute | solution.py:22
  82.6 7.4 %collective-permute-start.17 = (f32[8,640]{1,0:T(8,128)S(1)}, f32[8,640]{1,0:T(8,128)S(1)}, u32[]{:S(2)}, u32[]{:S(2)}) collective-permute-start(f32[8,640]{1,0:T(8,128)S(1)} %get-tuple-element.56.own), channel_id=1, source_target_pairs={{0,20},{4,16},{8,28},{12,24},{16,4},{20,0},{24,12},{28,8},{1,21},{... | collective-permute-start | bytes 61448 | tf_op jit(solution)/shard_map/ppermute | solution.py:22
  83.4 6.5 %collective-permute-start.19 = (f32[16,640]{1,0:T(8,128)S(1)}, f32[16,640]{1,0:T(8,128)S(1)}, u32[]{:S(2)}, u32[]{:S(2)}) collective-permute-start(f32[16,640]{1,0:T(8,128)S(1)} %constant_dynamic-update-slice_fusion), channel_id=1, source_target_pairs={{0,8},{4,12},{8,16},{12,20},{16,24},{20,28},{24,0},{28,4},{1,9},{5... | collective-permute-start | bytes 122888 | tf_op jit(solution)/shard_map/ppermute | solution.py:22
  85.5 4.4 %collective-permute-start.18 = (f32[16,640]{1,0:T(8,128)S(1)}, f32[16,640]{1,0:T(8,128)S(1)}, u32[]{:S(2)}, u32[]{:S(2)}) collective-permute-start(f32[16,640]{1,0:T(8,128)S(1)} %constant_dynamic-update-slice_fusion), channel_id=1, source_target_pairs={{0,24},{4,28},{8,0},{12,4},{16,8},{20,12},{24,16},{28,20},{1,25},{... | collective-permute-start | bytes 122888 | tf_op jit(solution)/shard_map/ppermute | solution.py:22
  91.7 5.3 %collective-permute-start.24 = (f32[24,320]{1,0:T(8,128)S(1)}, f32[24,320]{1,0:T(8,128)S(1)}, u32[]{:S(2)}, u32[]{:S(2)}) collective-permute-start(f32[24,320]{1,0:T(8,128)S(1)} %shard_map.64.refs_0_.own), channel_id=1, source_target_pairs={{0,3},{1,2},{2,1},{3,0},{4,7},{5,6},{6,5},{7,4},{8,11},{9,10},{10,... | collective-permute-start | bytes 92168 | tf_op jit(solution)/shard_map/ppermute | solution.py:22
  91.7 5.3 %collective-permute-start.23 = (f32[24,320]{1,0:T(8,128)S(1)}, f32[24,320]{1,0:T(8,128)S(1)}, u32[]{:S(2)}, u32[]{:S(2)}) collective-permute-start(f32[24,320]{1,0:T(8,128)S(1)} %shard_map.64.refs_0_.own), channel_id=1, source_target_pairs={{0,1},{1,0},{2,3},{3,2},{4,5},{5,4},{6,7},{7,6},{8,9},{9,8},{10,11... | collective-permute-start | bytes 92168 | tf_op jit(solution)/shard_map/ppermute | solution.py:22
  93.1 4.0 %collective-permute-start.22 = (f32[24,320]{1,0:T(8,128)S(1)}, f32[24,320]{1,0:T(8,128)S(1)}, u32[]{:S(2)}, u32[]{:S(2)}) collective-permute-start(f32[24,320]{1,0:T(8,128)S(1)} %shard_map.64.refs_0_.own), channel_id=1, source_target_pairs={{0,2},{1,3},{2,0},{3,1},{4,6},{5,7},{6,4},{7,5},{8,10},{9,11},{10,... | collective-permute-start | bytes 92168 | tf_op jit(solution)/shard_map/ppermute | solution.py:22
  102.8 7.5 %collective-permute-start.25 = (f32[320,1024]{1,0:T(8,128)S(1)}, f32[320,1024]{1,0:T(8,128)S(1)}, u32[]{:S(2)}, u32[]{:S(2)}) collective-permute-start(f32[320,1024]{1,0:T(8,128)S(1)} %get-tuple-element.66), channel_id=1, source_target_pairs={{0,1},{1,0},{2,3},{3,2},{4,5},{5,4},{6,7},{7,6},{8,9},{9,8},{10,11... | collective-permute-start | bytes 3932168 | tf_op jit(solution)/shard_map/ppermute | solution.py:22
  108.2 3.3 %collective-permute-start.27 = (f32[320,1024]{1,0:T(8,128)S(1)}, f32[320,1024]{1,0:T(8,128)S(1)}, u32[]{:S(2)}, u32[]{:S(2)}) collective-permute-start(f32[320,1024]{1,0:T(8,128)S(1)} %get-tuple-element.80), channel_id=1, source_target_pairs={{0,1},{1,0},{2,3},{3,2},{4,5},{5,4},{6,7},{7,6},{8,9},{9,8},{10,11... | collective-permute-start | bytes 3932168 | tf_op jit(solution)/shard_map/ppermute | solution.py:22
